TPU v7x, 32 devices: a whole 2x2x4 slice. The times are simulated.
32 devices in a mesh: bx: 8 (over z, y), by: 4 (over x, core).
Axes of the slice: x: 2, y: 2, z: 4, core: 2. Of those that a mesh axis runs over, the one named last changes fastest.
Arguments:
- normals: float32 [3, 131072], P(None, ('bx', 'by')), may hold values from -60 to 60
- owners: int32 [131072, 1], P(('bx', 'by')), may hold values from 0 to 31; in each aligned block of 4096 rows (0 to 4095, 4096 to 8191, ...) at most 256 rows name the same one
- cells: int32 [131072], P(('bx', 'by')), may hold values from 0 to 262143
- levels: int32 [8, 4], P('bx', 'by'), may hold values from 0 to 3
- rows_inverse: float32 [128, 128], replicated, may hold values from 0 to 0.25
- columns_inverse: float32 [256, 256], replicated, may hold values from 0 to 0.25
- depth_inverse: float32 [256, 256], replicated, may hold values from 0 to 0.25
Outputs:
- iterate: float32 [128, 256, 256], P('bx', 'by')
- implicit: float32 [131072], P(('bx', 'by'))
Inputs may be any that keep to these rules, and one draw needn't show every extreme that they name: `owners`: A brick's number is its index along bx times the number of devices along by plus its index along by. Among the 4096 points of one device at most 256 name one brick, and in every draw some brick is named by exactly 256 of them.
All inputs are finite; a program needn't handle non-finite values.
Results may differ from a plain program's by a relative error of at most 0.0001.
Values sent between devices are 32-bit elements; how exact they have to be, the bound alone decides.
No kernel may reach another device: no remote copies, remote signals or barrier semaphores. Data moves between devices by JAX's collectives and lax.ppermute only.
A program may use at most 320 MiB of HBM per device.

v0:
```python
import jax
import jax.numpy as jnp
from jax import lax
from jax.sharding import PartitionSpec as P

CX = 16
CY = 64
NZ = 256
ITERS = 4


screen_base = 1.0


def padded(shard, sides, width):
    for axis, dim in sides:
        peers, length = (lax.axis_size(axis), shard.shape[dim])
        up = [(i, (i + 1) % peers) for i in range(peers - 1)]
        down = [(j, i) for i, j in up]
        last = lax.slice_in_dim(shard, length - width, length, axis=dim)
        initial = lax.slice_in_dim(shard, 0, width, axis=dim)
        before = lax.ppermute(last, axis, up)
        after = lax.ppermute(initial, axis, down)
        shard = jnp.concatenate([before, shard, after], axis=dim)
    return shard


def remainder_of(iterate, source, screening):
    extended = padded(iterate, (("bx", 0), ("by", 1)), 1)
    z_padded = jnp.pad(iterate, ((0, 0), (0, 0), (1, 1)))
    beside = extended[2:, 1:-1] + extended[:-2, 1:-1]
    beside = beside + extended[1:-1, 2:] + extended[1:-1, :-2]
    beside = beside + z_padded[:, :, 2:] + z_padded[:, :, :-2]
    return source - ((6.0 + screening) * iterate - beside)


def sweep_first(remainder, matrix):
    highest = lax.Precision.HIGHEST
    lines = lax.all_to_all(remainder, "bx", split_axis=1, concat_axis=0, tiled=True)
    product = jnp.einsum("ab,bjk->ajk", matrix, lines, precision=highest)
    return lax.all_to_all(product, "bx", split_axis=0, concat_axis=1, tiled=True)


def sweep_second(remainder, matrix):
    highest = lax.Precision.HIGHEST
    lines = lax.all_to_all(remainder, "by", split_axis=0, concat_axis=1, tiled=True)
    product = jnp.einsum("ab,ibk->iak", matrix, lines, precision=highest)
    return lax.all_to_all(product, "by", split_axis=1, concat_axis=0, tiled=True)


def local(normals, owners, cells, levels, rows_inverse, columns_inverse, depth_inverse):
    first_count = lax.axis_size("bx")
    second_count = lax.axis_size("by")
    bricks = first_count * second_count
    point_count = cells.shape[0]
    capacity = 2 * point_count // bricks
    brick_cells = CX * CY * NZ
    target = owners[:, 0]
    onehot = (target[:, None] == jnp.arange(bricks, dtype=jnp.int32)[None, :]).astype(jnp.int32)
    ranking = jnp.sum(onehot * (jnp.cumsum(onehot, axis=0) - 1), axis=1)
    slot_index = target * capacity + ranking
    send_normals = jnp.zeros((3, bricks * capacity), jnp.float32).at[:, slot_index].set(normals)
    send_cells = jnp.zeros((bricks * capacity,), jnp.int32).at[slot_index].set(cells)
    arrived_normals, arrived_cells = (
        lax.all_to_all(
            send_normals.reshape(3, bricks, capacity),
            ("bx", "by"),
            split_axis=1,
            concat_axis=1,
            tiled=True,
        ),
        lax.all_to_all(
            send_cells.reshape(1, bricks, capacity),
            ("bx", "by"),
            split_axis=1,
            concat_axis=1,
            tiled=True,
        ),
    )
    flat_cells = arrived_cells.reshape(-1)
    vector_field = (
        jnp.zeros((3, brick_cells), jnp.float32)
        .at[:, flat_cells]
        .add(arrived_normals.reshape(3, -1))
    )
    vector_field = vector_field.reshape(3, CX, CY, NZ)
    stretched = padded(vector_field, (("bx", 1), ("by", 2)), 1)
    z_padded = jnp.pad(vector_field[2], ((0, 0), (0, 0), (1, 1)))
    source = -0.5 * (
        stretched[0, 2:, 1:-1]
        - stretched[0, :-2, 1:-1]
        + (stretched[1, 1:-1, 2:] - stretched[1, 1:-1, :-2])
        + (z_padded[:, :, 2:] - z_padded[:, :, :-2])
    )
    screening = screen_base * (1.0 + levels[0, 0].astype(jnp.float32))
    highest = lax.Precision.HIGHEST
    iterate = jnp.zeros((CX, CY, NZ), jnp.float32)
    for iteration in range(ITERS):
        remainder = remainder_of(iterate, source, screening)
        iterate = iterate + sweep_first(remainder, rows_inverse)
        remainder = remainder_of(iterate, source, screening)
        iterate = iterate + sweep_second(remainder, columns_inverse)
        remainder = remainder_of(iterate, source, screening)
        iterate = iterate + jnp.einsum("ab,ijb->ija", depth_inverse, remainder, precision=highest)
    sampled = iterate.reshape(-1)[flat_cells]
    returned = lax.all_to_all(
        sampled.reshape(1, bricks, capacity), ("bx", "by"), split_axis=1, concat_axis=1, tiled=True
    )
    implicit = returned.reshape(-1)[slot_index]
    return (iterate, implicit)


def solution(mesh):
    placed = (
        P(None, ("bx", "by")),
        P(("bx", "by"), None),
        P(("bx", "by")),
        P("bx", "by"),
        P(),
        P(),
        P(),
    )
    return jax.shard_map(
        local,
        mesh=mesh,
        in_specs=placed,
        out_specs=(P("bx", "by", None), P(("bx", "by"))),
        check_vma=False,
    )
```

profile of v0, /device:TPU:0, one launch (start us, length us, event | category | flops | bytes accessed | tf_op | source)
XLA Modules:
  0.0 1147.5 jit_solution(4864154974263732575)
XLA Ops:
  1.5 9.2 reduce-window.6
  13.7 16.3 %scatter_custom_fusion = s32[8192]{0:T(1024)} fusion(s32[4096]{0:T(1024)S(1)} %bitcast.205, s32[4096]{0:T(1024)} %param.9, s32[]{:T(128)} %constant.9.clone.1), kind=kCustom, calls=%fused_computation.346 | custom fusion | bytes 33280 | tf_op jit(solution)/shard_map/scatter | solution.py:63
  30.0 7.3 all-to-all-start
  38.8 12.8 %scatter_custom_fusion.1 = f32[3,8192]{0,1:T(8,128)} fusion(s32[4096]{0:T(1024)S(1)} %bitcast.206, f32[4096,3]{1,0:T(8,128)S(1)} %copy.102, f32[]{:T(128)} %constant.8.clone.1), kind=kCustom, calls=%fused_computation.12 | custom fusion | bytes 98308 | tf_op jit(solution)/shard_map/scatter | solution.py:62
  55.0 6.0 all-to-all-start.1
  61.1 5.9 sort
  71.9 159.8 %scatter_custom_fusion.2 = f32[3,262144]{0,1:T(8,128)} fusion(s32[8192]{0:T(1024)S(1)} %get-tuple-element.2, f32[]{:T(128)} %constant.8.clone.1, f32[8192,3]{1,0:T(8,128)} %copy.104, s32[8192]{0:T(1024)S(1)} %broadcast_clamp_fusion.1), kind=kCustom, calls=%fused_computation.7 | custom fusion | flops 24576 | bytes 3146240 | tf_op jit(solution)/shard_map/scatter-add | solution.py:84
  231.7 77.2 %copy.154 = f32[3,16,64,256]{3,2,1,0:T(8,128)} copy(f32[3,16,64,256]{0,3,2,1:T(8,128)} %bitcast.12) | data formatting | bytes 6291456 | tf_op jit(solution)/shard_map/reshape | solution.py:86
  337.0 74.8 %slice_reduce_fusion = f32[262144]{0:T(1024)S(1)} fusion(f32[3,262144]{0,1:T(8,128)} %scatter_custom_fusion.2), kind=kLoop, calls=%fused_computation.6 | loop fusion | bytes 2097152 | tf_op jit(solution)/shard_map/slice | solution.py:88
  418.4 34.1 %all_to_all.303 = f32[16,64,256]{2,0,1:T(8,128)S(1)} all-to-all(f32[16,64,256]{2,0,1:T(8,128)S(1)} %copy.106), channel_id=1, replica_groups=mesh['bx'=8,'by'=4] {'bx'}, dimensions={1} | all-to-all | bytes 2097152 | tf_op jit(solution)/shard_map/all_to_all | solution.py:39
  455.6 29.4 %all_to_all.304 = f32[128,8,256]{2,1,0:T(8,128)S(1)} all-to-all(f32[128,8,256]{2,1,0:T(8,128)S(1)} %copy.110), channel_id=1, replica_groups=mesh['bx'=8,'by'=4] {'bx'}, dimensions={0} | all-to-all | bytes 2097152 | tf_op jit(solution)/shard_map/all_to_all | solution.py:41
  498.7 17.8 %all_to_all.305 = f32[16,64,256]{2,1,0:T(8,128)S(1)} all-to-all(f32[16,64,256]{2,1,0:T(8,128)S(1)} %fusion.21), channel_id=1, replica_groups=mesh['bx'=8,'by'=4] {'by'}, dimensions={0} | all-to-all | bytes 2097152 | tf_op jit(solution)/shard_map/all_to_all | solution.py:46
  519.7 18.1 %all_to_all.306 = f32[4,256,256]{2,0,1:T(4,128)S(1)} all-to-all(f32[4,256,256]{2,0,1:T(4,128)} %copy.114), channel_id=1, replica_groups=mesh['bx'=8,'by'=4] {'by'}, dimensions={1} | all-to-all | bytes 2097152 | tf_op jit(solution)/shard_map/all_to_all | solution.py:48
  554.5 5.7 collective-permute-start.17
  569.6 33.7 %all_to_all.307 = f32[16,64,256]{2,0,1:T(8,128)S(1)} all-to-all(f32[16,64,256]{2,0,1:T(8,128)S(1)} %copy.117), channel_id=1, replica_groups=mesh['bx'=8,'by'=4] {'bx'}, dimensions={1} | all-to-all | bytes 2097152 | tf_op jit(solution)/shard_map/all_to_all | solution.py:39
  607.1 30.2 %all_to_all.308 = f32[128,8,256]{2,1,0:T(8,128)S(1)} all-to-all(f32[128,8,256]{2,1,0:T(8,128)} %copy.121), channel_id=1, replica_groups=mesh['bx'=8,'by'=4] {'bx'}, dimensions={0} | all-to-all | bytes 2097152 | tf_op jit(solution)/shard_map/all_to_all | solution.py:41
  651.1 18.1 %all_to_all.309 = f32[16,64,256]{2,1,0:T(8,128)S(1)} all-to-all(f32[16,64,256]{2,1,0:T(8,128)S(1)} %fusion.34), channel_id=1, replica_groups=mesh['bx'=8,'by'=4] {'by'}, dimensions={0} | all-to-all | bytes 2097152 | tf_op jit(solution)/shard_map/all_to_all | solution.py:46
  672.4 17.9 %all_to_all.310 = f32[4,256,256]{2,0,1:T(4,128)S(1)} all-to-all(f32[4,256,256]{2,0,1:T(4,128)} %copy.125), channel_id=1, replica_groups=mesh['bx'=8,'by'=4] {'by'}, dimensions={1} | all-to-all | bytes 2097152 | tf_op jit(solution)/shard_map/all_to_all | solution.py:48
  707.0 5.7 collective-permute-start.29
  722.1 33.7 %all_to_all.311 = f32[16,64,256]{2,0,1:T(8,128)S(1)} all-to-all(f32[16,64,256]{2,0,1:T(8,128)S(1)} %copy.128), channel_id=1, replica_groups=mesh['bx'=8,'by'=4] {'bx'}, dimensions={1} | all-to-all | bytes 2097152 | tf_op jit(solution)/shard_map/all_to_all | solution.py:39
  759.6 30.2 %all_to_all.312 = f32[128,8,256]{2,1,0:T(8,128)S(1)} all-to-all(f32[128,8,256]{2,1,0:T(8,128)} %copy.132), channel_id=1, replica_groups=mesh['bx'=8,'by'=4] {'bx'}, dimensions={0} | all-to-all | bytes 2097152 | tf_op jit(solution)/shard_map/all_to_all | solution.py:41
  803.6 18.1 %all_to_all.313 = f32[16,64,256]{2,1,0:T(8,128)S(1)} all-to-all(f32[16,64,256]{2,1,0:T(8,128)S(1)} %fusion.47), channel_id=1, replica_groups=mesh['bx'=8,'by'=4] {'by'}, dimensions={0} | all-to-all | bytes 2097152 | tf_op jit(solution)/shard_map/all_to_all | solution.py:46
  824.9 17.9 %all_to_all.314 = f32[4,256,256]{2,0,1:T(4,128)S(1)} all-to-all(f32[4,256,256]{2,0,1:T(4,128)} %copy.136), channel_id=1, replica_groups=mesh['bx'=8,'by'=4] {'by'}, dimensions={1} | all-to-all | bytes 2097152 | tf_op jit(solution)/shard_map/all_to_all | solution.py:48
  859.5 5.7 collective-permute-start.41
  874.6 33.7 %all_to_all.315 = f32[16,64,256]{2,0,1:T(8,128)S(1)} all-to-all(f32[16,64,256]{2,0,1:T(8,128)S(1)} %copy.139), channel_id=1, replica_groups=mesh['bx'=8,'by'=4] {'bx'}, dimensions={1} | all-to-all | bytes 2097152 | tf_op jit(solution)/shard_map/all_to_all | solution.py:39
  912.1 30.2 %all_to_all.316 = f32[128,8,256]{2,1,0:T(8,128)S(1)} all-to-all(f32[128,8,256]{2,1,0:T(8,128)} %copy.143), channel_id=1, replica_groups=mesh['bx'=8,'by'=4] {'bx'}, dimensions={0} | all-to-all | bytes 2097152 | tf_op jit(solution)/shard_map/all_to_all | solution.py:41
  956.1 18.1 %all_to_all.317 = f32[16,64,256]{2,1,0:T(8,128)S(1)} all-to-all(f32[16,64,256]{2,1,0:T(8,128)S(1)} %fusion.60), channel_id=1, replica_groups=mesh['bx'=8,'by'=4] {'by'}, dimensions={0} | all-to-all | bytes 2097152 | tf_op jit(solution)/shard_map/all_to_all | solution.py:46
  977.4 17.9 %all_to_all.318 = f32[4,256,256]{2,0,1:T(4,128)S(1)} all-to-all(f32[4,256,256]{2,0,1:T(4,128)} %copy.147), channel_id=1, replica_groups=mesh['bx'=8,'by'=4] {'by'}, dimensions={1} | all-to-all | bytes 2097152 | tf_op jit(solution)/shard_map/all_to_all | solution.py:48
  1011.2 80.4 %gather_fusion = f32[8192]{0:T(1024)} fusion(f32[262144]{0:T(1024)S(1)} %bitcast.164, s32[8192]{0:T(1024)S(1)} %broadcast_clamp_fusion), kind=kCustom, calls=%fused_computation | custom fusion | bytes 98304 | tf_op jit(solution)/shard_map/gather | solution.py:105
  1091.6 7.6 all-to-all-start.18
  1099.2 7.2 all-to-all-done.18
  1106.5 40.5 %gather_fusion.1 = f32[4096]{0:T(1024)} fusion(f32[8192]{0:T(1024)S(1)} %bitcast.163, s32[4096]{0:T(1024)S(1)} %broadcast_clamp_fusion.2), kind=kCustom, calls=%fused_computation.1 | custom fusion | bytes 49152 | tf_op jit(solution)/shard_map/gather | solution.py:109
  (228 shorter events, 223.1 us)
Async XLA Ops:
  30.0 25.1 %all-to-all-start = ((s32[1,32,256]{2,0,1:T(1,128)}), s32[1,32,256]{2,0,1:T(1,128)S(1)}, u32[]{:S(2)}, u32[]{:S(2)}) async-start(s32[1,32,256]{2,0,1:T(1,128)} %bitcast.5), calls=%async_computation | async-start | bytes 65536 | tf_op jit(solution)/shard_map/all_to_all | solution.py:72
  55.0 14.2 %all-to-all-start.1 = ((f32[3,32,256]{2,0,1:T(4,128)}), f32[3,32,256]{2,0,1:T(4,128)S(1)}, u32[]{:S(2)}, u32[]{:S(2)}) async-start(f32[3,32,256]{2,0,1:T(4,128)} %copy.103), calls=%async_computation.1 | async-start | bytes 262144 | tf_op jit(solution)/shard_map/all_to_all | solution.py:65
  310.0 19.4 %collective-permute-start = (f32[3,1,64,256]{3,2,1,0:T(8,128)S(1)}, f32[3,1,64,256]{3,2,1,0:T(8,128)S(1)}, u32[]{:S(2)}, u32[]{:S(2)}) collective-permute-start(f32[3,1,64,256]{3,2,1,0:T(8,128)S(1)} %get-tuple-element.9), channel_id=1, source_target_pairs={{4,0},{8,4},{12,8},{16,12},{20,16},{24,20},{28,24},{5,1},{9,5},{13... | collective-permute-start | bytes 589832 | tf_op jit(solution)/shard_map/ppermute | solution.py:23
  311.3 18.1 %collective-permute-start.1 = (f32[3,1,64,256]{3,2,1,0:T(8,128)S(1)}, f32[3,1,64,256]{3,2,1,0:T(8,128)S(1)}, u32[]{:S(2)}, u32[]{:S(2)}) collective-permute-start(f32[3,1,64,256]{3,2,1,0:T(8,128)S(1)} %get-tuple-element.8), channel_id=1, source_target_pairs={{0,4},{4,8},{8,12},{12,16},{16,20},{20,24},{24,28},{1,5},{5,9},{9,... | collective-permute-start | bytes 589832 | tf_op jit(solution)/shard_map/ppermute | solution.py:22
  315.9 6.6 collective-permute-start.4
  317.2 6.6 collective-permute-start.5
  324.5 87.6 %collective-permute-start.6 = (f32[18,1,256]{2,1,0:T(1,128)}, f32[18,1,256]{2,1,0:T(1,128)}, u32[]{:S(2)}, u32[]{:S(2)}) collective-permute-start(f32[18,1,256]{2,1,0:T(1,128)} %get-tuple-element.32), channel_id=1, source_target_pairs={{1,0},{2,1},{3,2},{5,4},{6,5},{7,6},{9,8},{10,9},{11,10},{13,12},{... | collective-permute-start | bytes 55304 | tf_op jit(solution)/shard_map/ppermute | solution.py:23
  325.8 86.3 %collective-permute-start.7 = (f32[18,1,256]{2,1,0:T(1,128)}, f32[18,1,256]{2,1,0:T(1,128)}, u32[]{:S(2)}, u32[]{:S(2)}) collective-permute-start(f32[18,1,256]{2,1,0:T(1,128)} %get-tuple-element.33), channel_id=1, source_target_pairs={{0,1},{1,2},{2,3},{4,5},{5,6},{6,7},{8,9},{9,10},{10,11},{12,13},{... | collective-permute-start | bytes 55304 | tf_op jit(solution)/shard_map/ppermute | solution.py:22
  331.4 80.7 %collective-permute-start.2 = (f32[3,18,1,256]{3,2,1,0:T(1,128)}, f32[3,18,1,256]{3,2,1,0:T(1,128)}, u32[]{:S(2)}, u32[]{:S(2)}) collective-permute-start(f32[3,18,1,256]{3,2,1,0:T(1,128)} %get-tuple-element.6), channel_id=1, source_target_pairs={{1,0},{2,1},{3,2},{5,4},{6,5},{7,6},{9,8},{10,9},{11,10},{13,12},{... | collective-permute-start | bytes 165896 | tf_op jit(solution)/shard_map/ppermute | solution.py:23
  332.7 79.4 %collective-permute-start.3 = (f32[3,18,1,256]{3,2,1,0:T(1,128)}, f32[3,18,1,256]{3,2,1,0:T(1,128)}, u32[]{:S(2)}, u32[]{:S(2)}) collective-permute-start(f32[3,18,1,256]{3,2,1,0:T(1,128)} %get-tuple-element.7), channel_id=1, source_target_pairs={{0,1},{1,2},{2,3},{4,5},{5,6},{6,7},{8,9},{9,10},{10,11},{12,13},{... | collective-permute-start | bytes 165896 | tf_op jit(solution)/shard_map/ppermute | solution.py:22
  485.0 6.2 collective-permute-start.8
  486.3 6.4 collective-permute-start.9
  538.3 6.5 collective-permute-start.12
  539.6 6.9 collective-permute-start.13
  553.2 7.7 collective-permute-start.16
  554.5 8.6 collective-permute-start.17
  637.5 6.2 collective-permute-start.20
  638.8 6.4 collective-permute-start.21
  690.9 6.5 collective-permute-start.24
  692.2 6.8 collective-permute-start.25
  705.7 7.7 collective-permute-start.28
  707.0 8.6 collective-permute-start.29
  790.0 6.2 collective-permute-start.32
  791.3 6.4 collective-permute-start.33
  843.4 6.5 collective-permute-start.36
  844.7 6.8 collective-permute-start.37
  858.2 7.7 collective-permute-start.40
  859.5 8.6 collective-permute-start.41
  943.8 6.4 collective-permute-start.45
  995.9 6.5 collective-permute-start.48
  997.2 6.8 collective-permute-start.49
  1091.6 14.8 %all-to-all-start.18 = ((f32[1,32,256]{2,0,1:T(1,128)}), f32[1,32,256]{2,0,1:T(1,128)S(1)}, u32[]{:S(2)}, u32[]{:S(2)}) async-start(f32[1,32,256]{2,0,1:T(1,128)} %bitcast.81), calls=%async_computation.18 | async-start | bytes 65536 | tf_op jit(solution)/shard_map/all_to_all | solution.py:106
  (36 other events, 1104.5 us)
where the time goes:
time: 1160 us; the launch traced here: 1150 us
  blocking collectives  399 us (34%)
  local copies, waits for them, and re-layouts  329 us (28%)
  other arithmetic  192 us (17%)
  starting transfers between devices  161 us (14%)
  waiting for transfers between devices  42.6 us (4%)
  matrix products  20.7 us (2%)
    scatter-add x3, other arithmetic, local(): vector_field = jnp.zeros((3, brick_cells), jnp.float32).at[:, flat_cells]...  166 us
    all_to_all x4, blocking collectives, sweep_first(): lax.all_to_all(remainder, 'bx', split_axis=1, concat_axis=0, tiled=True)  135 us
    all_to_all x4, blocking collectives, sweep_first(): lax.all_to_all(product, 'bx', split_axis=0, concat_axis=1, tiled=True)  120 us
    ppermute x26, starting transfers between devices, padded(): before = lax.ppermute(last, axis, up)  106 us
    gather x1, local copies, waits for them, and re-layouts, local(): sampled = iterate.reshape(-1)[flat_cells]  80.4 us
    reshape x1, local copies, waits for them, and re-layouts, local(): vector_field = vector_field.reshape(3, CX, CY, NZ)  77.2 us
    slice x1, local copies, waits for them, and re-layouts, local(): z_padded = jnp.pad(vector_field[2], ((0, 0), (0, 0), (1, 1)))  74.8 us
    all_to_all x4, blocking collectives, sweep_second(): lax.all_to_all(remainder, 'by', split_axis=0, concat_axis=1, tiled=True)  72.1 us
  transfers between devices with their start and end apart: 55, of which 36 were waited for; matrix products, arithmetic and copies ran while one was open for 9% of the time, Pallas kernels for 0%

commit v1 on v0

--- a/solution.py
+++ b/solution.py
@@ -7,6 +7,7 @@
 CY = 64
 NZ = 256
 ITERS = 4
+EVERY = ("bx", "by")
 
 
 screen_base = 1.0
@@ -25,27 +26,90 @@
     return shard
 
 
-def remainder_of(iterate, source, screening):
-    extended = padded(iterate, (("bx", 0), ("by", 1)), 1)
-    z_padded = jnp.pad(iterate, ((0, 0), (0, 0), (1, 1)))
-    beside = extended[2:, 1:-1] + extended[:-2, 1:-1]
-    beside = beside + extended[1:-1, 2:] + extended[1:-1, :-2]
-    beside = beside + z_padded[:, :, 2:] + z_padded[:, :, :-2]
-    return source - ((6.0 + screening) * iterate - beside)
+def slab_halo(slab, width):
+    devices = lax.axis_size(EVERY)
+    count = slab.shape[0]
+    before, after = [], []
+    reach = 1
+    while width > 0:
+        part = min(width, count)
+        up = [(i, i + reach) for i in range(devices - reach)]
+        down = [(j, i) for i, j in up]
+        before.insert(0, lax.ppermute(slab[count - part :], EVERY, up))
+        after.append(lax.ppermute(slab[:part], EVERY, down))
+        width, reach = width - part, reach + 1
+    return jnp.concatenate(before + [slab] + after, axis=0)
 
 
-def sweep_first(remainder, matrix):
-    highest = lax.Precision.HIGHEST
-    lines = lax.all_to_all(remainder, "bx", split_axis=1, concat_axis=0, tiled=True)
-    product = jnp.einsum("ab,bjk->ajk", matrix, lines, precision=highest)
-    return lax.all_to_all(product, "bx", split_axis=0, concat_axis=1, tiled=True)
+def turn(slab):
+    devices = lax.axis_size(EVERY)
+    n, first, second = slab.shape
+    sent = slab.transpose(2, 0, 1)
+    held = lax.all_to_all(sent, EVERY, split_axis=0, concat_axis=0, tiled=True)
+    held = held.reshape(devices, second // devices, n, first)
+    return held.transpose(1, 0, 2, 3).reshape(second // devices, devices * n, first)
 
 
-def sweep_second(remainder, matrix):
+def stencil(field, diagonal):
+    middle = field[1:-1]
+    beside = field[2:] + field[:-2]
+    wide = jnp.pad(middle, ((0, 0), (1, 1), (1, 1)))
+    beside = beside + wide[:, 2:, 1:-1] + wide[:, :-2, 1:-1]
+    beside = beside + wide[:, 1:-1, 2:] + wide[:, 1:-1, :-2]
+    return diagonal * middle - beside
+
+
+def phase(iterate, source, diagonal, inside, first_matrix, second_matrix):
     highest = lax.Precision.HIGHEST
-    lines = lax.all_to_all(remainder, "by", split_axis=0, concat_axis=1, tiled=True)
-    product = jnp.einsum("ab,ibk->iak", matrix, lines, precision=highest)
-    return lax.all_to_all(product, "by", split_axis=1, concat_axis=0, tiled=True)
+    remainder = source - stencil(iterate, diagonal)
+    step = jnp.einsum("ab,nbk->nak", first_matrix, remainder, precision=highest)
+    iterate = iterate[1:-1] + step * inside
+    remainder = source[1:-1] - stencil(iterate, diagonal[1:-1] if diagonal.shape[0] > 1 else diagonal)
+    step = jnp.einsum("ab,nkb->nka", second_matrix, remainder, precision=highest)
+    return iterate[1:-1] + step
+
+
+def relax(source, level, rows_inverse, columns_inverse, depth_inverse):
+    first_count, second_count = lax.axis_size("bx"), lax.axis_size("by")
+    devices = first_count * second_count
+    me = lax.axis_index(EVERY)
+    nx, ny = first_count * CX, second_count * CY
+    thick = (NZ // devices, ny // devices, nx // devices)
+    levels = lax.all_gather(level[0], EVERY, tiled=False).reshape(first_count, second_count)
+    diagonal = 6.0 + screen_base * (1.0 + levels.astype(jnp.float32))
+    diagonal = jnp.repeat(jnp.repeat(diagonal, CX, 0), CY, 1)
+    own = lambda n: me * n - 1 + jnp.arange(n + 2)
+    inside = []
+    for n in thick:
+        place = own(n)
+        inside.append(((place >= 0) & (place < n * devices)).astype(jnp.float32)[:, None, None])
+    wide = jnp.pad(diagonal, ((1, 1), (1, 1)), constant_values=1.0)
+    diagonals = (
+        diagonal[None],
+        lax.dynamic_slice_in_dim(wide, me * thick[1], thick[1] + 2, 1).T[:, None, 1:-1],
+        lax.dynamic_slice_in_dim(wide, me * thick[2], thick[2] + 2, 0)[:, 1:-1, None],
+    )
+    sent = source.reshape(CX, CY, devices, NZ // devices).transpose(2, 3, 0, 1)
+    held = lax.all_to_all(sent, EVERY, split_axis=0, concat_axis=0, tiled=True)
+    held = held.reshape(first_count, second_count, thick[0], CX, CY).transpose(2, 0, 3, 1, 4)
+    z_source = held.reshape(thick[0], nx, ny)
+    held = lax.all_to_all(source, "by", split_axis=0, concat_axis=1, tiled=True)
+    sources = [slab_halo(z_source, 1), slab_halo(turn(z_source), 1), slab_halo(held, 1)]
+    matrices = (rows_inverse, columns_inverse, depth_inverse)
+    iterate = jnp.zeros((thick[0], nx, ny), jnp.float32)
+    for step in range(3 * ITERS // 2):
+        at = step % 3
+        iterate = phase(
+            slab_halo(iterate, 2),
+            sources[at],
+            diagonals[at],
+            inside[at],
+            matrices[2 * step % 3],
+            matrices[(2 * step + 1) % 3],
+        )
+        if step + 1 < 3 * ITERS // 2:
+            iterate = turn(iterate)
+    return lax.all_to_all(iterate, "by", split_axis=1, concat_axis=0, tiled=True)
 
 
 def local(normals, owners, cells, levels, rows_inverse, columns_inverse, depth_inverse):
@@ -92,16 +156,7 @@
         + (stretched[1, 1:-1, 2:] - stretched[1, 1:-1, :-2])
         + (z_padded[:, :, 2:] - z_padded[:, :, :-2])
     )
-    screening = screen_base * (1.0 + levels[0, 0].astype(jnp.float32))
-    highest = lax.Precision.HIGHEST
-    iterate = jnp.zeros((CX, CY, NZ), jnp.float32)
-    for iteration in range(ITERS):
-        remainder = remainder_of(iterate, source, screening)
-        iterate = iterate + sweep_first(remainder, rows_inverse)
-        remainder = remainder_of(iterate, source, screening)
-        iterate = iterate + sweep_second(remainder, columns_inverse)
-        remainder = remainder_of(iterate, source, screening)
-        iterate = iterate + jnp.einsum("ab,ijb->ija", depth_inverse, remainder, precision=highest)
+    iterate = relax(source, levels[0], rows_inverse, columns_inverse, depth_inverse)
     sampled = iterate.reshape(-1)[flat_cells]
     returned = lax.all_to_all(
         sampled.reshape(1, bricks, capacity), ("bx", "by"), split_axis=1, concat_axis=1, tiled=True

time: 1160 us -> 984 us (0.85)
  blocking collectives: 399 us -> 183 us
  starting transfers between devices: 161 us -> 95.5 us
  local copies, waits for them, and re-layouts: 329 us -> 392 us
  waiting for transfers between devices: 42.6 us -> 85.1 us
    all_to_all x16 -> x4, blocking collectives: 399 us -> 137 us  [turn(): held = lax.all_to_all(sent, EVERY, split_axis=0, concat_axis=0, tiled=True)]
    ppermute x26 -> x2, starting transfers between devices: 106 us -> 9.26 us  [padded(): before = lax.ppermute(last, axis, up)]
    all_to_all x0 -> x5, waiting for transfers between devices: none -> 55 us  [the longest x2 40.1 us: turn(): held = lax.all_to_all(sent, EVERY, split_axis=0, concat_axis=0, tiled=True)]
    unnamed x0 -> x1, blocking collectives: none -> 45.9 us
    slice x1 -> x48, local copies, waits for them, and re-layouts: 0.79 us -> 38.7 us  [the longest x20 18.9 us: slab_halo(): before.insert(0, lax.ppermute(slab[count - part:], EVERY, up))]
    ppermute x0 -> x18, starting transfers between devices: none -> 34 us  [the longest x9 21.6 us: slab_halo(): before.insert(0, lax.ppermute(slab[count - part:], EVERY, up))]
    all_to_all x0 -> x5, starting transfers between devices: none -> 33.8 us  [the longest x2 11.8 us: turn(): held = lax.all_to_all(sent, EVERY, split_axis=0, concat_axis=0, tiled=True)]
    ppermute x26 -> x2, starting transfers between devices: 33.6 us -> 2.57 us  [padded(): after = lax.ppermute(initial, axis, down)]
  transfers between devices with their start and end apart: 55 -> 30, of which waited for: 36 -> 11; matrix products, arithmetic and copies ran while one was open for 9% -> 17% of each run, Pallas kernels for 0% -> 0%
where the time goes in v1:
time: 984 us; the launch traced here: 976 us
  local copies, waits for them, and re-layouts  392 us (40%)
  other arithmetic  186 us (19%)
  blocking collectives  183 us (19%)
  starting transfers between devices  95.5 us (10%)
  waiting for transfers between devices  85.1 us (9%)
  matrix products  31.9 us (3%)
    scatter-add x3, other arithmetic, local(): vector_field = jnp.zeros((3, brick_cells), jnp.float32).at[:, flat_cells]...  160 us
    all_to_all x4, blocking collectives, turn(): held = lax.all_to_all(sent, EVERY, split_axis=0, concat_axis=0, tiled=True)  137 us
    gather x1, local copies, waits for them, and re-layouts, local(): sampled = iterate.reshape(-1)[flat_cells]  80.4 us
    reshape x1, local copies, waits for them, and re-layouts, local(): vector_field = vector_field.reshape(3, CX, CY, NZ)  76 us
    slice x1, local copies, waits for them, and re-layouts, local(): z_padded = jnp.pad(vector_field[2], ((0, 0), (0, 0), (1, 1)))  75.7 us
    unnamed x1, blocking collectives  45.9 us
    gather x1, local copies, waits for them, and re-layouts, local(): implicit = returned.reshape(-1)[slot_index]  40.5 us
    all_to_all x2, waiting for transfers between devices, turn(): held = lax.all_to_all(sent, EVERY, split_axis=0, concat_axis=0, tiled=True)  40.1 us
  transfers between devices with their start and end apart: 30, of which 11 were waited for; matrix products, arithmetic and copies ran while one was open for 17% of the time, Pallas kernels for 0%

profile of v1, /device:TPU:0, one launch (start us, length us, event | category | flops | bytes accessed | tf_op | source)
XLA Modules:
  0.0 976.0 jit_solution(8159531307833744911)
XLA Ops:
  1.5 9.2 reduce-window.6
  12.3 16.3 %scatter_custom_fusion = s32[8192]{0:T(1024)} fusion(s32[4096]{0:T(1024)S(1)} %bitcast.237, s32[4096]{0:T(1024)} %param.9, s32[]{:T(128)} %constant.18.clone.1), kind=kCustom, calls=%fused_computation.305 | custom fusion | bytes 33280 | tf_op jit(solution)/shard_map/scatter | solution.py:127
  28.6 7.3 all-to-all-start
  36.5 12.8 %scatter_custom_fusion.1 = f32[3,8192]{0,1:T(8,128)} fusion(s32[4096]{0:T(1024)S(1)} %bitcast.238, f32[4096,3]{1,0:T(8,128)S(1)} %copy.258, f32[]{:T(128)} %constant.17.clone.1), kind=kCustom, calls=%fused_computation.58 | custom fusion | bytes 98308 | tf_op jit(solution)/shard_map/scatter | solution.py:126
  52.8 6.0 all-to-all-start.1
  58.9 5.9 sort
  69.7 154.4 %scatter_custom_fusion.2 = f32[3,262144]{0,1:T(8,128)} fusion(s32[8192]{0:T(1024)S(1)} %get-tuple-element.2, f32[]{:T(128)} %constant.17.clone.1, f32[8192,3]{1,0:T(8,128)} %copy.260, s32[8192]{0:T(1024)S(1)} %broadcast_clamp_fusion.1), kind=kCustom, calls=%fused_computation.7 | custom fusion | flops 24576 | bytes 3146240 | tf_op jit(solution)/shard_map/scatter-add | solution.py:148
  224.2 76.0 %copy.262 = f32[3,16,64,256]{3,2,1,0:T(8,128)S(1)} copy(f32[3,16,64,256]{0,3,2,1:T(8,128)} %bitcast.12) | data formatting | bytes 6291456 | tf_op jit(solution)/shard_map/reshape | solution.py:150
  301.5 5.6 collective-permute-start.3
  308.4 6.6 collective-permute-done.3
  317.0 3.6 collective-permute-start.5
  320.7 75.7 %slice_reduce_fusion = f32[262144]{0:T(1024)} fusion(f32[3,262144]{0,1:T(8,128)} %scatter_custom_fusion.2), kind=kLoop, calls=%fused_computation.6 | loop fusion | bytes 2097152 | tf_op jit(solution)/shard_map/slice | solution.py:152
  409.5 6.2 all-to-all-start.2
  421.3 45.9 %all-reduce.16 = s32[32]{0:T(128)S(1)} all-reduce(s32[32]{0:T(128)S(1)} %bitcast_dynamic-update-slice_fusion), channel_id=2, replica_groups=mesh['bx'=8,'by'=4] {'bx','by'}, use_global_device_ids=true, to_apply=%add.16 | all-reduce | flops 32 | bytes 256
  484.4 4.3 collective-permute-done.7
  495.1 8.2 all-to-all-start.3
  504.6 24.9 %all-to-all-done.3 = f32[256,8,128]{2,1,0:T(8,128)S(1)} async-done(((f32[256,8,128]{2,1,0:T(8,128)}), f32[256,8,128]{2,1,0:T(8,128)S(1)}, u32[]{:S(2)}, u32[]{:S(2)}) %all-to-all-start.3) | async-done | bytes 1048608 | tf_op jit(solution)/shard_map/all_to_all | solution.py:48
  529.5 3.6 all-to-all-start.4
  544.2 15.1 %all-to-all-done.4 = f32[256,8,128]{2,1,0:T(8,128)S(1)} async-done(((f32[256,8,128]{2,1,0:T(8,128)}), f32[256,8,128]{2,1,0:T(8,128)S(1)}, u32[]{:S(2)}, u32[]{:S(2)}) %all-to-all-start.4) | async-done | bytes 1048608 | tf_op jit(solution)/shard_map/all_to_all | solution.py:48
  581.6 32.9 %all_to_all.86 = f32[128,8,256]{2,1,0:T(8,128)S(1)} all-to-all(f32[128,8,256]{2,1,0:T(8,128)S(1)} %copy.292), channel_id=1, replica_groups=mesh['bx'=8,'by'=4] {'bx','by'}, dimensions={0} | all-to-all | bytes 2097152 | tf_op jit(solution)/shard_map/all_to_all | solution.py:48
  614.5 4.3 all-to-all-start.6
  637.9 4.1 collective-permute-start.14
  653.9 3.7 bitcast_add_fusion.1
  661.0 34.5 %all_to_all.87 = f32[256,4,256]{2,1,0:T(4,128)S(1)} all-to-all(f32[256,4,256]{2,1,0:T(4,128)S(1)} %copy.310), channel_id=1, replica_groups=mesh['bx'=8,'by'=4] {'bx','by'}, dimensions={0} | all-to-all | bytes 2097152 | tf_op jit(solution)/shard_map/all_to_all | solution.py:48
  715.5 34.7 %all_to_all.88 = f32[256,8,128]{2,1,0:T(8,128)S(1)} all-to-all(f32[256,8,128]{2,1,0:T(8,128)S(1)} %copy.312), channel_id=1, replica_groups=mesh['bx'=8,'by'=4] {'bx','by'}, dimensions={0} | all-to-all | bytes 2097152 | tf_op jit(solution)/shard_map/all_to_all | solution.py:48
  766.2 34.7 %all_to_all.89 = f32[128,8,256]{2,1,0:T(8,128)S(1)} all-to-all(f32[128,8,256]{2,1,0:T(8,128)S(1)} %copy.324), channel_id=1, replica_groups=mesh['bx'=8,'by'=4] {'bx','by'}, dimensions={0} | all-to-all | bytes 2097152 | tf_op jit(solution)/shard_map/all_to_all | solution.py:48
  806.5 3.6 collective-permute-done.21
  817.4 11.5 %all-to-all-start.10 = ((f32[4,256,256]{2,0,1:T(4,128)}), f32[4,256,256]{2,0,1:T(4,128)S(1)}, u32[]{:S(2)}, u32[]{:S(2)}) async-start(f32[4,256,256]{2,0,1:T(4,128)} %copy.336), calls=%async_computation.10 | async-start | bytes 2097152 | tf_op jit(solution)/shard_map/all_to_all | solution.py:112
  829.0 14.9 %all-to-all-done.10 = f32[4,256,256]{2,0,1:T(4,128)S(1)} async-done(((f32[4,256,256]{2,0,1:T(4,128)}), f32[4,256,256]{2,0,1:T(4,128)S(1)}, u32[]{:S(2)}, u32[]{:S(2)}) %all-to-all-start.10) | async-done | bytes 1048608 | tf_op jit(solution)/shard_map/all_to_all | solution.py:112
  844.7 80.4 %gather_fusion = f32[8192]{0:T(1024)} fusion(f32[262144]{0:T(1024)S(1)} %bitcast.185, s32[8192]{0:T(1024)S(1)} %broadcast_clamp_fusion), kind=kCustom, calls=%fused_computation | custom fusion | bytes 98304 | tf_op jit(solution)/shard_map/gather | solution.py:160
  927.7 7.2 all-to-all-done.11
  934.9 40.5 %gather_fusion.1 = f32[4096]{0:T(1024)} fusion(f32[8192]{0:T(1024)S(1)} %bitcast.184, s32[4096]{0:T(1024)S(1)} %broadcast_clamp_fusion.2), kind=kCustom, calls=%fused_computation.1 | custom fusion | bytes 49152 | tf_op jit(solution)/shard_map/gather | solution.py:164
  (231 shorter events, 178.0 us)
Async XLA Ops:
  0.6 491.6 %copy-start = (f32[256,256]{1,0:T(8,128)S(1)}, f32[256,256]{1,0:T(8,128)}, u32[]{:S(2)}) copy-start(f32[256,256]{1,0:T(8,128)} %param.12) | copy-start | bytes 786436
  28.6 24.2 %all-to-all-start = ((s32[1,32,256]{2,0,1:T(1,128)}), s32[1,32,256]{2,0,1:T(1,128)S(1)}, u32[]{:S(2)}, u32[]{:S(2)}) async-start(s32[1,32,256]{2,0,1:T(1,128)} %bitcast.5), calls=%async_computation | async-start | bytes 65536 | tf_op jit(solution)/shard_map/all_to_all | solution.py:136
  52.8 14.3 %all-to-all-start.1 = ((f32[3,32,256]{2,0,1:T(4,128)}), f32[3,32,256]{2,0,1:T(4,128)S(1)}, u32[]{:S(2)}, u32[]{:S(2)}) async-start(f32[3,32,256]{2,0,1:T(4,128)} %copy.259), calls=%async_computation.1 | async-start | bytes 262144 | tf_op jit(solution)/shard_map/all_to_all | solution.py:129
  300.2 8.1 collective-permute-start.2
  301.5 13.5 %collective-permute-start.3 = (f32[3,1,64,256]{3,2,1,0:T(8,128)S(1)}, f32[3,1,64,256]{3,2,1,0:T(8,128)S(1)}, u32[]{:S(2)}, u32[]{:S(2)}) collective-permute-start(f32[3,1,64,256]{3,2,1,0:T(8,128)S(1)} %get-tuple-element.6), channel_id=1, source_target_pairs={{0,4},{4,8},{8,12},{12,16},{16,20},{20,24},{24,28},{1,5},{5,9},{9,... | collective-permute-start | bytes 589832 | tf_op jit(solution)/shard_map/ppermute | solution.py:23
  315.7 83.2 %collective-permute-start.4 = (f32[3,18,1,256]{3,2,1,0:T(1,128)}, f32[3,18,1,256]{3,2,1,0:T(1,128)S(1)}, u32[]{:S(2)}, u32[]{:S(2)}) collective-permute-start(f32[3,18,1,256]{3,2,1,0:T(1,128)} %get-tuple-element.4), channel_id=1, source_target_pairs={{1,0},{2,1},{3,2},{5,4},{6,5},{7,6},{9,8},{10,9},{11,10},{13,12},{... | collective-permute-start | bytes 165896 | tf_op jit(solution)/shard_map/ppermute | solution.py:24
  317.0 81.9 %collective-permute-start.5 = (f32[3,18,1,256]{3,2,1,0:T(1,128)S(1)}, f32[3,18,1,256]{3,2,1,0:T(1,128)}, u32[]{:S(2)}, u32[]{:S(2)}) collective-permute-start(f32[3,18,1,256]{3,2,1,0:T(1,128)S(1)} %get-tuple-element.5), channel_id=1, source_target_pairs={{0,1},{1,2},{2,3},{4,5},{5,6},{6,7},{8,9},{9,10},{10,11},{12,13},{... | collective-permute-start | bytes 165896 | tf_op jit(solution)/shard_map/ppermute | solution.py:23
  409.5 58.9 %all-to-all-start.2 = ((f32[32,1,8192]{2,1,0:T(1,128)}), f32[32,1,8192]{2,1,0:T(1,128)S(1)}, u32[]{:S(2)}, u32[]{:S(2)}) async-start(f32[32,1,8192]{2,1,0:T(1,128)} %reshape.260), calls=%async_computation.2 | async-start | bytes 2097152 | tf_op jit(solution)/shard_map/all_to_all | solution.py:93
  416.4 58.8 %collective-permute-start = (f32[2,128,256]{2,1,0:T(8,128)}, f32[2,128,256]{2,1,0:T(8,128)}, u32[]{:S(2)}, u32[]{:S(2)}) collective-permute-start(f32[2,128,256]{2,1,0:T(8,128)} %broadcast.136), channel_id=1, source_target_pairs={{0,1},{1,2},{2,3},{3,4},{4,5},{5,6},{6,7},{7,8},{8,9},{9,10},{10,1... | collective-permute-start | bytes 786440 | tf_op jit(solution)/shard_map/ppermute | solution.py:38
  420.0 55.2 %collective-permute-start.1 = (f32[2,128,256]{2,1,0:T(8,128)}, f32[2,128,256]{2,1,0:T(8,128)}, u32[]{:S(2)}, u32[]{:S(2)}) collective-permute-start(f32[2,128,256]{2,1,0:T(8,128)} %broadcast.136), channel_id=1, source_target_pairs={{1,0},{2,1},{3,2},{4,3},{5,4},{6,5},{7,6},{8,7},{9,8},{10,9},{11,1... | collective-permute-start | bytes 786440 | tf_op jit(solution)/shard_map/ppermute | solution.py:39
  473.7 10.6 %collective-permute-start.6 = (f32[1,128,256]{2,1,0:T(8,128)S(1)}, f32[1,128,256]{2,1,0:T(8,128)S(1)}, u32[]{:S(2)}, u32[]{:S(2)}) collective-permute-start(f32[1,128,256]{2,1,0:T(8,128)S(1)} %slice.425), channel_id=1, source_target_pairs={{0,1},{1,2},{2,3},{3,4},{4,5},{5,6},{6,7},{7,8},{8,9},{9,10},{10,1... | collective-permute-start | bytes 393224 | tf_op jit(solution)/shard_map/ppermute | solution.py:38
  482.9 5.9 collective-permute-start.7
  495.1 34.4 %all-to-all-start.3 = ((f32[256,8,128]{2,1,0:T(8,128)}), f32[256,8,128]{2,1,0:T(8,128)S(1)}, u32[]{:S(2)}, u32[]{:S(2)}) async-start(f32[256,8,128]{2,1,0:T(8,128)} %copy.275), calls=%async_computation.3 | async-start | bytes 2097152 | tf_op jit(solution)/shard_map/all_to_all | solution.py:48
  529.5 29.9 %all-to-all-start.4 = ((f32[256,8,128]{2,1,0:T(8,128)}), f32[256,8,128]{2,1,0:T(8,128)S(1)}, u32[]{:S(2)}, u32[]{:S(2)}) async-start(f32[256,8,128]{2,1,0:T(8,128)} %copy.282), calls=%async_computation.4 | async-start | bytes 2097152 | tf_op jit(solution)/shard_map/all_to_all | solution.py:48
  536.4 36.9 %collective-permute-start.8 = (f32[2,256,128]{1,2,0:T(8,128)}, f32[2,256,128]{1,2,0:T(8,128)}, u32[]{:S(2)}, u32[]{:S(2)}) collective-permute-start(f32[2,256,128]{1,2,0:T(8,128)} %copy.277), channel_id=1, source_target_pairs={{0,1},{1,2},{2,3},{3,4},{4,5},{5,6},{6,7},{7,8},{8,9},{9,10},{10,1... | collective-permute-start | bytes 786440 | tf_op jit(solution)/shard_map/ppermute | solution.py:38
  542.7 30.6 %collective-permute-start.9 = (f32[2,256,128]{1,2,0:T(8,128)}, f32[2,256,128]{1,2,0:T(8,128)}, u32[]{:S(2)}, u32[]{:S(2)}) collective-permute-start(f32[2,256,128]{1,2,0:T(8,128)} %copy.280), channel_id=1, source_target_pairs={{1,0},{2,1},{3,2},{4,3},{5,4},{6,5},{7,6},{8,7},{9,8},{10,9},{11,1... | collective-permute-start | bytes 786440 | tf_op jit(solution)/shard_map/ppermute | solution.py:39
  565.6 8.8 collective-permute-start.10
  569.2 5.2 collective-permute-start.11
  614.5 19.8 %all-to-all-start.6 = ((f32[16,64,256]{2,1,0:T(8,128)}), f32[16,64,256]{2,1,0:T(8,128)}, u32[]{:S(2)}, u32[]{:S(2)}) async-start(f32[16,64,256]{2,1,0:T(8,128)} %fusion.105), calls=%async_computation.6 | async-start | bytes 2097152 | tf_op jit(solution)/shard_map/all_to_all | solution.py:96
  622.4 30.1 %collective-permute-start.12 = (f32[2,256,256]{1,2,0:T(8,128)}, f32[2,256,256]{1,2,0:T(8,128)}, u32[]{:S(2)}, u32[]{:S(2)}) collective-permute-start(f32[2,256,256]{1,2,0:T(8,128)} %copy.294), channel_id=1, source_target_pairs={{0,1},{1,2},{2,3},{3,4},{4,5},{5,6},{6,7},{7,8},{8,9},{9,10},{10,1... | collective-permute-start | bytes 1572872 | tf_op jit(solution)/shard_map/ppermute | solution.py:38
  629.5 23.1 %collective-permute-start.13 = (f32[2,256,256]{1,2,0:T(8,128)}, f32[2,256,256]{1,2,0:T(8,128)}, u32[]{:S(2)}, u32[]{:S(2)}) collective-permute-start(f32[2,256,256]{1,2,0:T(8,128)} %copy.297), channel_id=1, source_target_pairs={{1,0},{2,1},{3,2},{4,3},{5,4},{6,5},{7,6},{8,7},{9,8},{10,9},{11,1... | collective-permute-start | bytes 1572872 | tf_op jit(solution)/shard_map/ppermute | solution.py:39
  637.9 15.9 %collective-permute-start.14 = (f32[1,256,256]{1,2,0:T(8,128)}, f32[1,256,256]{1,2,0:T(8,128)}, u32[]{:S(2)}, u32[]{:S(2)}) collective-permute-start(f32[1,256,256]{1,2,0:T(8,128)} %copy.299), channel_id=1, source_target_pairs={{0,1},{1,2},{2,3},{3,4},{4,5},{5,6},{6,7},{7,8},{8,9},{9,10},{10,1... | collective-permute-start | bytes 786440 | tf_op jit(solution)/shard_map/ppermute | solution.py:38
  643.8 10.1 %collective-permute-start.15 = (f32[1,256,256]{1,2,0:T(8,128)}, f32[1,256,256]{1,2,0:T(8,128)}, u32[]{:S(2)}, u32[]{:S(2)}) collective-permute-start(f32[1,256,256]{1,2,0:T(8,128)} %copy.301), channel_id=1, source_target_pairs={{1,0},{2,1},{3,2},{4,3},{5,4},{6,5},{7,6},{8,7},{9,8},{10,9},{11,1... | collective-permute-start | bytes 786440 | tf_op jit(solution)/shard_map/ppermute | solution.py:39
  698.2 6.6 collective-permute-start.16
  702.0 4.7 collective-permute-start.17
  751.1 4.6 collective-permute-start.18
  754.0 4.8 collective-permute-start.19
  802.1 4.4 collective-permute-start.20
  804.4 5.7 collective-permute-start.21
  817.4 26.4 %all-to-all-start.10 = ((f32[4,256,256]{2,0,1:T(4,128)}), f32[4,256,256]{2,0,1:T(4,128)S(1)}, u32[]{:S(2)}, u32[]{:S(2)}) async-start(f32[4,256,256]{2,0,1:T(4,128)} %copy.336), calls=%async_computation.10 | async-start | bytes 2097152 | tf_op jit(solution)/shard_map/all_to_all | solution.py:112
  844.7 83.0 %copy-start.19 = (s32[4096,1]{0,1:T(1,128)S(1)}, s32[4096,1]{0,1:T(1,128)}, u32[]{:S(2)}) copy-start(s32[4096,1]{0,1:T(1,128)} %copy-done.18) | copy-start | bytes 49156
  925.2 9.8 all-to-all-start.11
  (26 other events, 267.2 us)

commit v2 on v1

--- a/solution.py
+++ b/solution.py
@@ -1,6 +1,8 @@
 import jax
 import jax.numpy as jnp
 from jax import lax
+from jax.experimental import pallas as pl
+from jax.experimental.pallas import tpu as pltpu
 from jax.sharding import PartitionSpec as P
 
 CX = 16
@@ -13,17 +15,224 @@
 screen_base = 1.0
 
 
-def padded(shard, sides, width):
-    for axis, dim in sides:
-        peers, length = (lax.axis_size(axis), shard.shape[dim])
-        up = [(i, (i + 1) % peers) for i in range(peers - 1)]
-        down = [(j, i) for i, j in up]
-        last = lax.slice_in_dim(shard, length - width, length, axis=dim)
-        initial = lax.slice_in_dim(shard, 0, width, axis=dim)
-        before = lax.ppermute(last, axis, up)
-        after = lax.ppermute(initial, axis, down)
-        shard = jnp.concatenate([before, shard, after], axis=dim)
-    return shard
+def parts_of(value, count):
+    parts = []
+    for _ in range(count):
+        part = value.astype(jnp.bfloat16)
+        parts.append(part)
+        value = value - part.astype(jnp.float32)
+    return parts
+
+
+def rows_iota(rows, columns):
+    return lax.broadcasted_iota(jnp.int32, (rows, columns), 0)
+
+
+def flags(condition):
+    return jnp.where(condition, 1.0, 0.0)
+
+
+def whole_arrays(count):
+    return [pl.BlockSpec(memory_space=pltpu.VMEM)] * count
+
+
+def pack_kernel(owner_ref, cell_ref, normal_ref, send_ref, rank_ref, total_ref):
+    bricks, capacity = send_ref.shape[0], total_ref.shape[1]
+    points = owner_ref.shape[1]
+    block = 256
+    before = flags(rows_iota(block, block) < lax.broadcasted_iota(jnp.int32, (block, block), 1)).astype(jnp.bfloat16)
+    total_ref[...] = jnp.zeros_like(total_ref)
+
+    def step(at, seen):
+        here = pl.ds(pl.multiple_of(at * block, block), block)
+        named = flags(rows_iota(bricks, block) == owner_ref[:, here])
+        inside = jnp.dot(named.astype(jnp.bfloat16), before, preferred_element_type=jnp.float32)
+        rank = jnp.sum(named * (inside + seen), axis=0, keepdims=True)
+        rank_ref[:, here] = rank
+        slot = flags(rows_iota(capacity, block).astype(jnp.float32) == rank).astype(jnp.bfloat16)
+        values = []
+        for k in range(3):
+            values += [part.astype(jnp.float32) for part in parts_of(normal_ref[k : k + 1, here], 3)]
+        cell = cell_ref[:, here] + 1
+        for shift in (16, 8, 0):
+            values.append(((cell >> shift) & 255).astype(jnp.float32))
+        rows = jnp.concatenate([(named * value).astype(jnp.bfloat16) for value in values], axis=0)
+        total_ref[...] += lax.dot_general(
+            rows, slot, (((1,), (1,)), ((), ())), preferred_element_type=jnp.float32
+        )
+        return seen + jnp.sum(named, axis=1, keepdims=True)
+
+    lax.fori_loop(0, points // block, step, jnp.zeros((bricks, 1), jnp.float32))
+    part = lambda i: total_ref[i * bricks : (i + 1) * bricks, :]
+    fields = [part(3 * k) + part(3 * k + 1) + part(3 * k + 2) for k in range(3)]
+    fields.append(part(9) * 65536.0 + part(10) * 256.0 + part(11))
+    row = jnp.concatenate(fields, axis=1)
+    for j in range(send_ref.shape[1]):
+        send_ref[:, j, :] = row[:, 128 * j : 128 * (j + 1)]
+
+
+def pack(owners, cells, normals, bricks, capacity):
+    points = cells.shape[0]
+    return pl.pallas_call(
+        pack_kernel,
+        out_shape=(
+            jax.ShapeDtypeStruct((bricks, 4 * capacity // 128, 128), jnp.float32),
+            jax.ShapeDtypeStruct((1, points), jnp.float32),
+        ),
+        in_specs=whole_arrays(3),
+        out_specs=tuple(whole_arrays(2)),
+        scratch_shapes=[pltpu.VMEM((12 * bricks, capacity), jnp.float32)],
+        compiler_params=pltpu.CompilerParams(vmem_limit_bytes=32 << 20),
+        name="pack",
+    )(owners.reshape(1, points), cells.reshape(1, points), normals)
+
+
+def unpack_kernel(owner_ref, rank_ref, held_ref, out_ref):
+    bricks, capacity = held_ref.shape
+    points = owner_ref.shape[1]
+    block = 512
+    held = jnp.concatenate([part.astype(jnp.float32).T for part in parts_of(held_ref[...], 3)], axis=1)
+    held = held.astype(jnp.bfloat16)
+    for at in range(points // block):
+        here = slice(at * block, (at + 1) * block)
+        named = flags(rows_iota(bricks, block) == owner_ref[:, here]).astype(jnp.bfloat16)
+        named = jnp.concatenate([named] * 3, axis=0)
+        found = jnp.dot(held, named, preferred_element_type=jnp.float32)
+        slot = rows_iota(capacity, block).astype(jnp.float32) == rank_ref[:, here]
+        out_ref[:, here] = jnp.sum(jnp.where(slot, found, 0.0), axis=0, keepdims=True)
+
+
+def unpack(owners, rank, held):
+    points = owners.shape[0]
+    out = pl.pallas_call(
+        unpack_kernel,
+        out_shape=jax.ShapeDtypeStruct((1, points), jnp.float32),
+        in_specs=whole_arrays(3),
+        out_specs=pl.BlockSpec(memory_space=pltpu.VMEM),
+        compiler_params=pltpu.CompilerParams(vmem_limit_bytes=32 << 20),
+        name="unpack",
+    )(owners.reshape(1, points), rank, held)
+    return out.reshape(points)
+
+
+def spread(row):
+    return jnp.broadcast_to(row, (16, 128)).astype(jnp.bfloat16)
+
+
+def times_row(table, row16):
+    rows = table.shape[0]
+    return (table.reshape(rows // 16, 16, 128) * row16[None]).reshape(rows, 128)
+
+
+def places(cell_row):
+    cell = cell_row.astype(jnp.int32) - 1
+    return cell >> 14, (cell >> 8) & (CY - 1), cell & (NZ - 1)
+
+
+def differenced(rows, first, at):
+    index = rows_iota(rows, 128) + first
+    return jnp.where(index == at + 1, 0.5, 0.0) - jnp.where(index == at - 1, 0.5, 0.0)
+
+
+def splat_kernel(used_ref, field_ref, source_ref, x_face_ref, y_face_ref):
+    chunks = field_ref.shape[0] // 4
+    source_ref[...] = jnp.zeros_like(source_ref)
+    x_face_ref[...] = jnp.zeros_like(x_face_ref)
+    y_face_ref[...] = jnp.zeros_like(y_face_ref)
+
+    def product(rows, columns):
+        return lax.dot_general(rows, columns, (((1,), (1,)), ((), ())), preferred_element_type=jnp.float32)
+
+    def step(at, carry):
+        @pl.when(used_ref[at] > 0)
+        def _():
+            x, y, z = places(field_ref[pl.ds(3 * chunks + at, 1), :])
+            y_hot = flags(rows_iota(CY, 128) == y).astype(jnp.bfloat16)
+            y_step = differenced(CY, 0, y).astype(jnp.bfloat16)
+            z_hot = flags(rows_iota(NZ, 128) == z).astype(jnp.bfloat16)
+            z_step = differenced(NZ, 0, z).astype(jnp.bfloat16)
+            columns = []
+            for k in range(3):
+                for part in parts_of(field_ref[pl.ds(k * chunks + at, 1), :], 2):
+                    columns.append(times_row(z_step if k == 2 else z_hot, spread(part.astype(jnp.float32))))
+            columns = jnp.concatenate(columns, axis=1)
+            steps = [spread(jnp.where(x == i - 1, 0.5, 0.0) - jnp.where(x == i + 1, 0.5, 0.0)) for i in range(-1, CX + 1)]
+            hots = [spread(flags(x == i)) for i in range(CX)]
+            along_x = jnp.concatenate([times_row(y_hot, steps[i + 1]) for i in range(CX)], axis=0)
+            along_y = jnp.concatenate([times_row(y_step, hots[i]) for i in range(CX)], axis=0)
+            along_z = jnp.concatenate([times_row(y_hot, hots[i]) for i in range(CX)], axis=0)
+            rows = jnp.concatenate([along_x, along_x, along_y, along_y, along_z, along_z], axis=1)
+            source_ref[...] += product(rows, columns)
+            ends = jnp.concatenate([times_row(y_hot, steps[0]), times_row(y_hot, steps[CX + 1])], axis=0)
+            x_face_ref[...] += product(jnp.concatenate([ends, ends], axis=1), columns[:, :256])
+            x_hot = flags(rows_iota(CX, 128) == x).astype(jnp.bfloat16)
+            ends = jnp.concatenate(
+                [x_hot * spread(jnp.where(y == 0, -0.5, 0.0)), x_hot * spread(jnp.where(y == CY - 1, 0.5, 0.0))], axis=0
+            )
+            y_face_ref[...] += product(jnp.concatenate([ends, ends], axis=1), columns[:, 256:512])
+
+        return carry
+
+    lax.fori_loop(0, chunks, step, 0)
+
+
+def splat(field, used):
+    shapes = ((CX * CY, NZ), (2 * CY, NZ), (2 * CX, NZ))
+    return pl.pallas_call(
+        splat_kernel,
+        out_shape=tuple(jax.ShapeDtypeStruct(shape, jnp.float32) for shape in shapes),
+        in_specs=[pl.BlockSpec(memory_space=pltpu.SMEM), pl.BlockSpec(memory_space=pltpu.VMEM)],
+        out_specs=tuple(whole_arrays(3)),
+        compiler_params=pltpu.CompilerParams(vmem_limit_bytes=32 << 20),
+        name="splat",
+    )(used, field)
+
+
+def sample_kernel(field_ref, iterate_ref, out_ref, turned_ref):
+    chunks = out_ref.shape[0]
+    for i in range(CX * CY // 128):
+        here = slice(128 * i, 128 * (i + 1))
+        block = iterate_ref[here, :].T
+        high, low = parts_of(block, 2)
+        turned_ref[:NZ, here] = high
+        turned_ref[NZ:, here] = low
+
+    def step(at, carry):
+        tables, heights = [], []
+        for half in range(2):
+            x, y, z = places(field_ref[pl.ds(2 * at + half, 1), :])
+            y_hot = flags(rows_iota(CY, 128) == y).astype(jnp.bfloat16)
+            hots = [spread(flags(x == i)) for i in range(CX)]
+            tables.append(jnp.concatenate([times_row(y_hot, hots[i]) for i in range(CX)], axis=0))
+            heights.append(z)
+        found = jnp.dot(turned_ref[...], jnp.concatenate(tables, axis=1), preferred_element_type=jnp.float32)
+        found = found[:NZ] + found[NZ:]
+        level = rows_iota(NZ, 256) == jnp.concatenate(heights, axis=1)
+        row = jnp.sum(jnp.where(level, found, 0.0), axis=0, keepdims=True)
+        out_ref[pl.ds(2 * at, 1), :] = row[:, :128]
+        out_ref[pl.ds(2 * at + 1, 1), :] = row[:, 128:]
+        return carry
+
+    lax.fori_loop(0, chunks // 2, step, 0)
+
+
+def sample(cell_rows, iterate):
+    return pl.pallas_call(
+        sample_kernel,
+        out_shape=jax.ShapeDtypeStruct(cell_rows.shape, jnp.float32),
+        in_specs=whole_arrays(2),
+        out_specs=pl.BlockSpec(memory_space=pltpu.VMEM),
+        scratch_shapes=[pltpu.VMEM((2 * NZ, CX * CY), jnp.bfloat16)],
+        compiler_params=pltpu.CompilerParams(vmem_limit_bytes=32 << 20),
+        name="sample",
+    )(cell_rows, iterate)
+
+
+def neighbours(face, axis, count):
+    peers = lax.axis_size(axis)
+    up = [(i, i + 1) for i in range(peers - 1)]
+    down = [(j, i) for i, j in up]
+    return lax.ppermute(face[count:], axis, up), lax.ppermute(face[:count], axis, down)
 
 
 def slab_halo(slab, width):
@@ -69,14 +278,13 @@
     return iterate[1:-1] + step
 
 
-def relax(source, level, rows_inverse, columns_inverse, depth_inverse):
+def relax(source, levels, rows_inverse, columns_inverse, depth_inverse):
     first_count, second_count = lax.axis_size("bx"), lax.axis_size("by")
     devices = first_count * second_count
     me = lax.axis_index(EVERY)
     nx, ny = first_count * CX, second_count * CY
     thick = (NZ // devices, ny // devices, nx // devices)
-    levels = lax.all_gather(level[0], EVERY, tiled=False).reshape(first_count, second_count)
-    diagonal = 6.0 + screen_base * (1.0 + levels.astype(jnp.float32))
+    diagonal = 6.0 + screen_base * (1.0 + levels.reshape(first_count, second_count))
     diagonal = jnp.repeat(jnp.repeat(diagonal, CX, 0), CY, 1)
     own = lambda n: me * n - 1 + jnp.arange(n + 2)
     inside = []
@@ -113,55 +321,29 @@
 
 
 def local(normals, owners, cells, levels, rows_inverse, columns_inverse, depth_inverse):
-    first_count = lax.axis_size("bx")
-    second_count = lax.axis_size("by")
-    bricks = first_count * second_count
+    bricks = lax.axis_size(EVERY)
     point_count = cells.shape[0]
     capacity = 2 * point_count // bricks
-    brick_cells = CX * CY * NZ
-    target = owners[:, 0]
-    onehot = (target[:, None] == jnp.arange(bricks, dtype=jnp.int32)[None, :]).astype(jnp.int32)
-    ranking = jnp.sum(onehot * (jnp.cumsum(onehot, axis=0) - 1), axis=1)
-    slot_index = target * capacity + ranking
-    send_normals = jnp.zeros((3, bricks * capacity), jnp.float32).at[:, slot_index].set(normals)
-    send_cells = jnp.zeros((bricks * capacity,), jnp.int32).at[slot_index].set(cells)
-    arrived_normals, arrived_cells = (
-        lax.all_to_all(
-            send_normals.reshape(3, bricks, capacity),
-            ("bx", "by"),
-            split_axis=1,
-            concat_axis=1,
-            tiled=True,
-        ),
-        lax.all_to_all(
-            send_cells.reshape(1, bricks, capacity),
-            ("bx", "by"),
-            split_axis=1,
-            concat_axis=1,
-            tiled=True,
-        ),
-    )
-    flat_cells = arrived_cells.reshape(-1)
-    vector_field = (
-        jnp.zeros((3, brick_cells), jnp.float32)
-        .at[:, flat_cells]
-        .add(arrived_normals.reshape(3, -1))
-    )
-    vector_field = vector_field.reshape(3, CX, CY, NZ)
-    stretched = padded(vector_field, (("bx", 1), ("by", 2)), 1)
-    z_padded = jnp.pad(vector_field[2], ((0, 0), (0, 0), (1, 1)))
-    source = -0.5 * (
-        stretched[0, 2:, 1:-1]
-        - stretched[0, :-2, 1:-1]
-        + (stretched[1, 1:-1, 2:] - stretched[1, 1:-1, :-2])
-        + (z_padded[:, :, 2:] - z_padded[:, :, :-2])
-    )
-    iterate = relax(source, levels[0], rows_inverse, columns_inverse, depth_inverse)
-    sampled = iterate.reshape(-1)[flat_cells]
-    returned = lax.all_to_all(
-        sampled.reshape(1, bricks, capacity), ("bx", "by"), split_axis=1, concat_axis=1, tiled=True
-    )
-    implicit = returned.reshape(-1)[slot_index]
+    chunks = bricks * capacity // 128
+    level = jnp.broadcast_to(levels.astype(jnp.float32), (1, 128))
+    levels = lax.all_gather(level, EVERY, tiled=True)[:, 0]
+    send, rank = pack(owners, cells, normals, bricks, capacity)
+    held = lax.all_to_all(send, EVERY, split_axis=0, concat_axis=0, tiled=True)
+    field = held.reshape(bricks, 4, capacity).transpose(1, 0, 2).reshape(4 * chunks, 128)
+    cell_rows = field[3 * chunks :]
+    used = (jnp.max(cell_rows, axis=1) > 0).astype(jnp.int32)
+    source, x_face, y_face = splat(field, used)
+    source = source.reshape(CX, CY, NZ)
+    x_before, x_after = neighbours(x_face, "bx", CY)
+    y_before, y_after = neighbours(y_face, "by", CX)
+    source = source + jnp.pad(x_before[None], ((0, CX - 1), (0, 0), (0, 0)))
+    source = source + jnp.pad(x_after[None], ((CX - 1, 0), (0, 0), (0, 0)))
+    source = source + jnp.pad(y_before[:, None], ((0, 0), (0, CY - 1), (0, 0)))
+    source = source + jnp.pad(y_after[:, None], ((0, 0), (CY - 1, 0), (0, 0)))
+    iterate = relax(source, levels, rows_inverse, columns_inverse, depth_inverse)
+    sampled = sample(cell_rows, iterate.reshape(CX * CY, NZ))
+    returned = lax.all_to_all(sampled.reshape(bricks, capacity), EVERY, split_axis=0, concat_axis=0, tiled=True)
+    implicit = unpack(owners, rank, returned)
     return (iterate, implicit)
 
 

time: 984 us -> 556 us (0.57)
  local copies, waits for them, and re-layouts: 392 us -> 88.2 us
  other arithmetic: 186 us -> 11.3 us
  Pallas kernels: 0 us -> 48 us
  waiting for transfers between devices: 85.1 us -> 69 us
  blocking collectives: 183 us -> 199 us
    scatter-add x3 -> x0, other arithmetic: 160 us -> none  [local(): vector_field = jnp.zeros((3, brick_cells), jnp.float32).at[:, flat_cells]...]
    gather x2 -> x0, local copies, waits for them, and re-layouts: 121 us -> none  [the longest x1 80.4 us: local(): sampled = iterate.reshape(-1)[flat_cells]]
    reshape x3 -> x4, local copies, waits for them, and re-layouts: 82.1 us -> 3.04 us  [the longest x1 2.94 us: relax(): held.reshape(first_count, second_count, thick[0], CX, CY)]
    slice x3 -> x4, local copies, waits for them, and re-layouts: 76.5 us -> 0.02 us  [the longest x2 0.02 us: neighbours(): face[count:]]
    all_to_all x0 -> x3, blocking collectives: none -> 53 us  [the longest x1 28.7 us: relax(): lax.all_to_all(iterate, 'by', split_axis=1, concat_axis=0, tiled=True)]
    pallas_call x0 -> x4, Pallas kernels: none -> 48 us  [the longest x1 24.5 us: splat(): pl.pallas_call(splat_kernel, out_shape=tuple((jax.ShapeDtypeStruct(shape,...]
    all_to_all x4 -> x3, blocking collectives: 137 us -> 102 us  [turn(): held = lax.all_to_all(sent, EVERY, split_axis=0, concat_axis=0, tiled=True)]
    scatter x2 -> x0, local copies, waits for them, and re-layouts: 29.1 us -> none  [the longest x1 16.3 us: local(): jnp.zeros((bricks * capacity,), jnp.int32).at[slot_index].set(cells)]
  transfers between devices with their start and end apart: 30 -> 27, of which waited for: 11 -> 7; matrix products, arithmetic and copies ran while one was open for 17% -> 13% of each run, Pallas kernels for 0% -> 0%
where the time goes in v2:
time: 556 us; the launch traced here: 546 us
  blocking collectives  199 us (36%)
  starting transfers between devices  94.9 us (17%)
  local copies, waits for them, and re-layouts  88.2 us (16%)
  waiting for transfers between devices  69 us (12%)
  Pallas kernels  48 us (9%)
  matrix products  31.9 us (6%)
  other arithmetic  11.3 us (2%)
    all_to_all x3, blocking collectives, turn(): held = lax.all_to_all(sent, EVERY, split_axis=0, concat_axis=0, tiled=True)  102 us
    all_to_all x3, waiting for transfers between devices, turn(): held = lax.all_to_all(sent, EVERY, split_axis=0, concat_axis=0, tiled=True)  63.1 us
    unnamed x1, blocking collectives  44 us
    ppermute x9, starting transfers between devices, slab_halo(): before.insert(0, lax.ppermute(slab[count - part:], EVERY, up))  32 us
    all_to_all x1, blocking collectives, relax(): lax.all_to_all(iterate, 'by', split_axis=1, concat_axis=0, tiled=True)  28.7 us
    pallas_call x1, Pallas kernels, splat(): pl.pallas_call(splat_kernel, out_shape=tuple((jax.ShapeDtypeStruct(shape,...  24.5 us
    ppermute x2, starting transfers between devices, neighbours(): lax.ppermute(face[count:], axis, up)  23 us
    dot_general x6, matrix products, phase(): step = jnp.einsum('ab,nbk->nak', first_matrix, remainder, precision=highest)  20.1 us
  transfers between devices with their start and end apart: 27, of which 7 were waited for; matrix products, arithmetic and copies ran while one was open for 13% of the time, Pallas kernels for 0%

profile of v2, /device:TPU:0, one launch (start us, length us, event | category | flops | bytes accessed | tf_op | source)
XLA Modules:
  0.0 545.5 jit_solution(389627636780824969)
XLA Ops:
  3.0 7.0 %pack.1 = (f32[32,8,128]{2,1,0:T(8,128)S(1)}, f32[1,4096]{1,0:T(1,128)S(1)}) custom-call(s32[1,4096]{1,0:T(1,128)S(1)} %bitcast.168, s32[1,4096]{1,0:T(1,128)S(1)} %bitcast.170, f32[3,4096]{1,0:T(4,128)S(1)} %copy-done.2), custom_call_target="tpu_custom_call" | custom-call | tf_op jit(solution)/shard_map/pack/pallas_call | solution.py:76
  9.9 15.3 %all_to_all.87 = f32[32,8,128]{2,1,0:T(8,128)S(1)} all-to-all(f32[32,8,128]{2,1,0:T(8,128)S(1)} %get-tuple-element.7), channel_id=1, replica_groups=mesh['bx'=8,'by'=4] {'bx','by'}, dimensions={0} | all-to-all | bytes 262144 | tf_op jit(solution)/shard_map/all_to_all | solution.py:331
  25.5 24.5 %splat.1 = (f32[1024,256]{1,0:T(8,128)S(1)}, f32[128,256]{1,0:T(8,128)S(1)}, f32[32,256]{1,0:T(8,128)S(1)}) custom-call(s32[64]{0:T(128)S(1)} %compare_convert_fusion.used_ref, f32[256,128]{1,0:T(8,128)S(1)} %reshape.127.field_ref), custom_call_target="tpu_custom_call" | custom-call | tf_op jit(solution)/shard_map/splat/pallas_call | solution.py:181
  52.6 21.7 %collective-permute-start.4 = (f32[16,256]{1,0:T(8,128)S(1)}, f32[16,256]{1,0:T(8,128)S(1)}, u32[]{:S(2)}, u32[]{:S(2)}) collective-permute-start(f32[16,256]{1,0:T(8,128)S(1)} %get-tuple-element.30), channel_id=1, source_target_pairs={{0,1},{1,2},{2,3},{4,5},{5,6},{6,7},{8,9},{9,10},{10,11},{12,13},{... | collective-permute-start | bytes 49160 | tf_op jit(solution)/shard_map/ppermute | solution.py:235
  84.3 6.4 %all-to-all-start.1 = ((f32[32,1,8192]{2,1,0:T(1,128)}), f32[32,1,8192]{2,1,0:T(1,128)S(1)}, u32[]{:S(2)}, u32[]{:S(2)}) async-start(f32[32,1,8192]{2,1,0:T(1,128)} %reshape.160), calls=%async_computation.1 | async-start | bytes 2097152 | tf_op jit(solution)/shard_map/all_to_all | solution.py:301
  93.4 3.7 collective-permute-start
  97.2 44.0 %all-reduce.19 = f32[32]{0:T(128)S(1)} all-reduce(f32[32]{0:T(128)S(1)} %bitcast_dynamic-update-slice_fusion), channel_id=3, replica_groups=mesh['bx'=8,'by'=4] {'bx','by'}, use_global_device_ids=true, to_apply=%add.19 | all-reduce | flops 32 | bytes 256
  142.8 3.2 reduce
  164.8 3.3 fusion.33
  171.0 6.9 %all-to-all-start.2 = ((f32[256,8,128]{2,1,0:T(8,128)}), f32[256,8,128]{2,1,0:T(8,128)S(1)}, u32[]{:S(2)}, u32[]{:S(2)}) async-start(f32[256,8,128]{2,1,0:T(8,128)} %copy.244), calls=%async_computation.2 | async-start | bytes 2097152 | tf_op jit(solution)/shard_map/all_to_all | solution.py:257
  179.3 24.9 %all-to-all-done.2 = f32[256,8,128]{2,1,0:T(8,128)S(1)} async-done(((f32[256,8,128]{2,1,0:T(8,128)}), f32[256,8,128]{2,1,0:T(8,128)S(1)}, u32[]{:S(2)}, u32[]{:S(2)}) %all-to-all-start.2) | async-done | bytes 1048608 | tf_op jit(solution)/shard_map/all_to_all | solution.py:257
  204.2 3.6 all-to-all-start.3
  215.8 3.7 collective-permute-start.8
  220.5 13.6 %all-to-all-done.3 = f32[256,8,128]{2,1,0:T(8,128)S(1)} async-done(((f32[256,8,128]{2,1,0:T(8,128)}), f32[256,8,128]{2,1,0:T(8,128)S(1)}, u32[]{:S(2)}, u32[]{:S(2)}) %all-to-all-start.3) | async-done | bytes 1048608 | tf_op jit(solution)/shard_map/all_to_all | solution.py:257
  243.2 3.7 collective-permute-start.10
  250.7 3.4 fusion.35
  258.0 4.9 all-to-all-start.4
  264.6 24.6 %all-to-all-done.4 = f32[128,8,256]{2,1,0:T(8,128)} async-done(((f32[128,8,256]{2,1,0:T(8,128)}), f32[128,8,256]{2,1,0:T(8,128)}, u32[]{:S(2)}, u32[]{:S(2)}) %all-to-all-start.4) | async-done | bytes 1048608 | tf_op jit(solution)/shard_map/all_to_all | solution.py:257
  289.2 3.5 all-to-all-start.5
  303.1 3.8 collective-permute-start.12
  318.0 4.2 collective-permute-start.14
  331.0 3.7 bitcast_add_fusion.1
  338.1 33.2 %all_to_all.88 = f32[256,4,256]{2,1,0:T(4,128)S(1)} all-to-all(f32[256,4,256]{2,1,0:T(4,128)S(1)} %copy.280), channel_id=1, replica_groups=mesh['bx'=8,'by'=4] {'bx','by'}, dimensions={0} | all-to-all | bytes 2097152 | tf_op jit(solution)/shard_map/all_to_all | solution.py:257
  377.1 3.7 collective-permute-start.16
  391.6 34.0 %all_to_all.89 = f32[256,8,128]{2,1,0:T(8,128)S(1)} all-to-all(f32[256,8,128]{2,1,0:T(8,128)S(1)} %copy.282), channel_id=1, replica_groups=mesh['bx'=8,'by'=4] {'bx','by'}, dimensions={0} | all-to-all | bytes 2097152 | tf_op jit(solution)/shard_map/all_to_all | solution.py:257
  428.6 4.0 collective-permute-start.18
  434.2 3.4 fusion.39
  440.6 35.2 %all_to_all.90 = f32[128,8,256]{2,1,0:T(8,128)S(1)} all-to-all(f32[128,8,256]{2,1,0:T(8,128)S(1)} %copy.294), channel_id=1, replica_groups=mesh['bx'=8,'by'=4] {'bx','by'}, dimensions={0} | all-to-all | bytes 2097152 | tf_op jit(solution)/shard_map/all_to_all | solution.py:257
  484.2 3.2 bitcast_add_fusion
  490.5 28.7 %all_to_all.91 = f32[4,256,256]{2,0,1:T(4,128)S(1)} all-to-all(f32[4,256,256]{2,0,1:T(4,128)S(1)} %copy.306), channel_id=1, replica_groups=mesh['bx'=8,'by'=4] {'by'}, dimensions={1} | all-to-all | bytes 2097152 | tf_op jit(solution)/shard_map/all_to_all | solution.py:320
  519.5 15.1 %sample.1 = f32[64,128]{1,0:T(8,128)S(1)} custom-call(f32[64,128]{1,0:T(8,128)S(1)} %slice.389.field_ref, f32[1024,256]{1,0:T(8,128)S(1)} %bitcast.163), custom_call_target="tpu_custom_call" | custom-call | tf_op jit(solution)/shard_map/sample/pallas_call | solution.py:220
  534.6 8.9 %all_to_all.92 = f32[32,1,256]{2,1,0:T(1,128)S(1)} all-to-all(f32[32,1,256]{2,1,0:T(1,128)S(1)} %bitcast.166), channel_id=1, replica_groups=mesh['bx'=8,'by'=4] {'bx','by'}, dimensions={0} | all-to-all | bytes 65536 | tf_op jit(solution)/shard_map/all_to_all | solution.py:345
  (204 shorter events, 139.5 us)
Async XLA Ops:
  0.6 167.5 %copy-start = (f32[256,256]{1,0:T(8,128)S(1)}, f32[256,256]{1,0:T(8,128)}, u32[]{:S(2)}) copy-start(f32[256,256]{1,0:T(8,128)} %param.12) | copy-start | bytes 786436
  50.0 25.6 %collective-permute-start.2 = (f32[64,256]{1,0:T(8,128)S(1)}, f32[64,256]{1,0:T(8,128)S(1)}, u32[]{:S(2)}, u32[]{:S(2)}) collective-permute-start(f32[64,256]{1,0:T(8,128)S(1)} %get-tuple-element.28), channel_id=1, source_target_pairs={{0,4},{4,8},{8,12},{12,16},{16,20},{20,24},{24,28},{1,5},{5,9},{9,... | collective-permute-start | bytes 196616 | tf_op jit(solution)/shard_map/ppermute | solution.py:235
  51.3 24.4 %collective-permute-start.3 = (f32[64,256]{1,0:T(8,128)S(1)}, f32[64,256]{1,0:T(8,128)S(1)}, u32[]{:S(2)}, u32[]{:S(2)}) collective-permute-start(f32[64,256]{1,0:T(8,128)S(1)} %get-tuple-element.29), channel_id=1, source_target_pairs={{4,0},{8,4},{12,8},{16,12},{20,16},{24,20},{28,24},{5,1},{9,5},{13... | collective-permute-start | bytes 196616 | tf_op jit(solution)/shard_map/ppermute | solution.py:235
  52.6 23.1 %collective-permute-start.4 = (f32[16,256]{1,0:T(8,128)S(1)}, f32[16,256]{1,0:T(8,128)S(1)}, u32[]{:S(2)}, u32[]{:S(2)}) collective-permute-start(f32[16,256]{1,0:T(8,128)S(1)} %get-tuple-element.30), channel_id=1, source_target_pairs={{0,1},{1,2},{2,3},{4,5},{5,6},{6,7},{8,9},{9,10},{10,11},{12,13},{... | collective-permute-start | bytes 49160 | tf_op jit(solution)/shard_map/ppermute | solution.py:235
  74.4 3.1 collective-permute-start.5
  84.3 58.0 %all-to-all-start.1 = ((f32[32,1,8192]{2,1,0:T(1,128)}), f32[32,1,8192]{2,1,0:T(1,128)S(1)}, u32[]{:S(2)}, u32[]{:S(2)}) async-start(f32[32,1,8192]{2,1,0:T(1,128)} %reshape.160), calls=%async_computation.1 | async-start | bytes 2097152 | tf_op jit(solution)/shard_map/all_to_all | solution.py:301
  91.4 63.4 %collective-permute-start.1 = (f32[2,128,256]{2,1,0:T(8,128)}, f32[2,128,256]{2,1,0:T(8,128)}, u32[]{:S(2)}, u32[]{:S(2)}) collective-permute-start(f32[2,128,256]{2,1,0:T(8,128)} %broadcast.91), channel_id=1, source_target_pairs={{1,0},{2,1},{3,2},{4,3},{5,4},{6,5},{7,6},{8,7},{9,8},{10,9},{11,1... | collective-permute-start | bytes 786440 | tf_op jit(solution)/shard_map/ppermute | solution.py:248
  93.4 61.5 %collective-permute-start = (f32[2,128,256]{2,1,0:T(8,128)}, f32[2,128,256]{2,1,0:T(8,128)}, u32[]{:S(2)}, u32[]{:S(2)}) collective-permute-start(f32[2,128,256]{2,1,0:T(8,128)} %broadcast.91), channel_id=1, source_target_pairs={{0,1},{1,2},{2,3},{3,4},{4,5},{5,6},{6,7},{7,8},{8,9},{9,10},{10,1... | collective-permute-start | bytes 786440 | tf_op jit(solution)/shard_map/ppermute | solution.py:247
  152.8 8.1 %collective-permute-start.6 = (f32[1,128,256]{2,1,0:T(8,128)}, f32[1,128,256]{2,1,0:T(8,128)}, u32[]{:S(2)}, u32[]{:S(2)}) collective-permute-start(f32[1,128,256]{2,1,0:T(8,128)} %slice.395), channel_id=1, source_target_pairs={{0,1},{1,2},{2,3},{3,4},{4,5},{5,6},{6,7},{7,8},{8,9},{9,10},{10,1... | collective-permute-start | bytes 393224 | tf_op jit(solution)/shard_map/ppermute | solution.py:247
  159.4 5.3 copy-start.12
  159.4 5.3 copy-start.16
  159.4 5.3 collective-permute-start.7
  171.0 33.2 %all-to-all-start.2 = ((f32[256,8,128]{2,1,0:T(8,128)}), f32[256,8,128]{2,1,0:T(8,128)S(1)}, u32[]{:S(2)}, u32[]{:S(2)}) async-start(f32[256,8,128]{2,1,0:T(8,128)} %copy.244), calls=%async_computation.2 | async-start | bytes 2097152 | tf_op jit(solution)/shard_map/all_to_all | solution.py:257
  204.2 29.9 %all-to-all-start.3 = ((f32[256,8,128]{2,1,0:T(8,128)}), f32[256,8,128]{2,1,0:T(8,128)S(1)}, u32[]{:S(2)}, u32[]{:S(2)}) async-start(f32[256,8,128]{2,1,0:T(8,128)} %copy.251), calls=%async_computation.3 | async-start | bytes 2097152 | tf_op jit(solution)/shard_map/all_to_all | solution.py:257
  214.5 35.0 %collective-permute-start.9 = (f32[2,256,128]{1,2,0:T(8,128)}, f32[2,256,128]{1,2,0:T(8,128)}, u32[]{:S(2)}, u32[]{:S(2)}) collective-permute-start(f32[2,256,128]{1,2,0:T(8,128)} %copy.249), channel_id=1, source_target_pairs={{1,0},{2,1},{3,2},{4,3},{5,4},{6,5},{7,6},{8,7},{9,8},{10,9},{11,1... | collective-permute-start | bytes 786440 | tf_op jit(solution)/shard_map/ppermute | solution.py:248
  215.8 33.7 %collective-permute-start.8 = (f32[2,256,128]{1,2,0:T(8,128)}, f32[2,256,128]{1,2,0:T(8,128)}, u32[]{:S(2)}, u32[]{:S(2)}) collective-permute-start(f32[2,256,128]{1,2,0:T(8,128)} %copy.246), channel_id=1, source_target_pairs={{0,1},{1,2},{2,3},{3,4},{4,5},{5,6},{6,7},{7,8},{8,9},{9,10},{10,1... | collective-permute-start | bytes 786440 | tf_op jit(solution)/shard_map/ppermute | solution.py:247
  241.9 8.7 %collective-permute-start.11 = (f32[1,256,128]{1,2,0:T(8,128)}, f32[1,256,128]{1,2,0:T(8,128)}, u32[]{:S(2)}, u32[]{:S(2)}) collective-permute-start(f32[1,256,128]{1,2,0:T(8,128)} %copy.254), channel_id=1, source_target_pairs={{1,0},{2,1},{3,2},{4,3},{5,4},{6,5},{7,6},{8,7},{9,8},{10,9},{11,1... | collective-permute-start | bytes 393224 | tf_op jit(solution)/shard_map/ppermute | solution.py:248
  243.2 7.4 %collective-permute-start.10 = (f32[1,256,128]{1,2,0:T(8,128)}, f32[1,256,128]{1,2,0:T(8,128)}, u32[]{:S(2)}, u32[]{:S(2)}) collective-permute-start(f32[1,256,128]{1,2,0:T(8,128)} %copy.252), channel_id=1, source_target_pairs={{0,1},{1,2},{2,3},{3,4},{4,5},{5,6},{6,7},{7,8},{8,9},{9,10},{10,1... | collective-permute-start | bytes 393224 | tf_op jit(solution)/shard_map/ppermute | solution.py:247
  258.0 31.2 %all-to-all-start.4 = ((f32[128,8,256]{2,1,0:T(8,128)}), f32[128,8,256]{2,1,0:T(8,128)}, u32[]{:S(2)}, u32[]{:S(2)}) async-start(f32[128,8,256]{2,1,0:T(8,128)} %copy.261), calls=%async_computation.4 | async-start | bytes 2097152 | tf_op jit(solution)/shard_map/all_to_all | solution.py:257
  289.2 23.1 %all-to-all-start.5 = ((f32[16,64,256]{2,1,0:T(8,128)}), f32[16,64,256]{2,1,0:T(8,128)S(1)}, u32[]{:S(2)}, u32[]{:S(2)}) async-start(f32[16,64,256]{2,1,0:T(8,128)} %copy.268), calls=%async_computation.5 | async-start | bytes 2097152 | tf_op jit(solution)/shard_map/all_to_all | solution.py:304
  301.6 28.0 %collective-permute-start.13 = (f32[2,256,256]{1,2,0:T(8,128)}, f32[2,256,256]{1,2,0:T(8,128)}, u32[]{:S(2)}, u32[]{:S(2)}) collective-permute-start(f32[2,256,256]{1,2,0:T(8,128)} %copy.266), channel_id=1, source_target_pairs={{1,0},{2,1},{3,2},{4,3},{5,4},{6,5},{7,6},{8,7},{9,8},{10,9},{11,1... | collective-permute-start | bytes 1572872 | tf_op jit(solution)/shard_map/ppermute | solution.py:248
  303.1 26.5 %collective-permute-start.12 = (f32[2,256,256]{1,2,0:T(8,128)}, f32[2,256,256]{1,2,0:T(8,128)}, u32[]{:S(2)}, u32[]{:S(2)}) collective-permute-start(f32[2,256,256]{1,2,0:T(8,128)} %copy.263), channel_id=1, source_target_pairs={{0,1},{1,2},{2,3},{3,4},{4,5},{5,6},{6,7},{7,8},{8,9},{9,10},{10,1... | collective-permute-start | bytes 1572872 | tf_op jit(solution)/shard_map/ppermute | solution.py:247
  316.7 14.2 %collective-permute-start.15 = (f32[1,256,256]{1,2,0:T(8,128)}, f32[1,256,256]{1,2,0:T(8,128)}, u32[]{:S(2)}, u32[]{:S(2)}) collective-permute-start(f32[1,256,256]{1,2,0:T(8,128)} %copy.271), channel_id=1, source_target_pairs={{1,0},{2,1},{3,2},{4,3},{5,4},{6,5},{7,6},{8,7},{9,8},{10,9},{11,1... | collective-permute-start | bytes 786440 | tf_op jit(solution)/shard_map/ppermute | solution.py:248
  318.0 13.0 %collective-permute-start.14 = (f32[1,256,256]{1,2,0:T(8,128)}, f32[1,256,256]{1,2,0:T(8,128)}, u32[]{:S(2)}, u32[]{:S(2)}) collective-permute-start(f32[1,256,256]{1,2,0:T(8,128)} %copy.269), channel_id=1, source_target_pairs={{0,1},{1,2},{2,3},{3,4},{4,5},{5,6},{6,7},{7,8},{8,9},{9,10},{10,1... | collective-permute-start | bytes 786440 | tf_op jit(solution)/shard_map/ppermute | solution.py:247
  375.8 6.4 %collective-permute-start.17 = (f32[2,128,256]{2,1,0:T(8,128)}, f32[2,128,256]{2,1,0:T(8,128)}, u32[]{:S(2)}, u32[]{:S(2)}) collective-permute-start(f32[2,128,256]{2,1,0:T(8,128)} %slice.457), channel_id=1, source_target_pairs={{1,0},{2,1},{3,2},{4,3},{5,4},{6,5},{7,6},{8,7},{9,8},{10,9},{11,1... | collective-permute-start | bytes 786440 | tf_op jit(solution)/shard_map/ppermute | solution.py:248
  377.1 5.1 collective-permute-start.16
  427.3 5.7 %collective-permute-start.19 = (f32[2,256,128]{1,2,0:T(8,128)}, f32[2,256,128]{1,2,0:T(8,128)}, u32[]{:S(2)}, u32[]{:S(2)}) collective-permute-start(f32[2,256,128]{1,2,0:T(8,128)} %copy.287), channel_id=1, source_target_pairs={{1,0},{2,1},{3,2},{4,3},{5,4},{6,5},{7,6},{8,7},{9,8},{10,9},{11,1... | collective-permute-start | bytes 786440 | tf_op jit(solution)/shard_map/ppermute | solution.py:248
  428.6 4.5 collective-permute-start.18
  478.0 4.8 collective-permute-start.21
  479.3 4.8 collective-permute-start.20
  519.4 24.1 %copy-start.4 = (s32[4096,1]{0,1:T(1,128)S(1)}, s32[4096,1]{0,1:T(1,128)}, u32[]{:S(2)}) copy-start(s32[4096,1]{0,1:T(1,128)} %param.8) | copy-start | bytes 49156
  519.5 25.6 %copy-start.1 = (f32[4,4,64,256]{3,2,1,0:T(8,128)}, f32[4,4,64,256]{3,2,1,0:T(8,128)S(1)}, u32[]{:S(2)}) copy-start(f32[4,4,64,256]{3,2,1,0:T(8,128)S(1)} %copy.308) | copy-start | bytes 3145732
  (18 other events, 32.5 us)

commit v3 on v2

--- a/solution.py
+++ b/solution.py
@@ -1,3 +1,5 @@
+import functools
+
 import jax
 import jax.numpy as jnp
 from jax import lax
@@ -235,50 +237,250 @@
     return lax.ppermute(face[count:], axis, up), lax.ppermute(face[:count], axis, down)
 
 
-def slab_halo(slab, width):
+def parts_in_rows(value):
+    high, low = parts_of(value, 2)
+    return jnp.concatenate([high, low, high], axis=0)
+
+
+def wide(matrix):
+    high, low = parts_of(matrix, 2)
+    return jnp.concatenate([high, high, low], axis=1)
+
+
+def shifted(value, axis, back):
+    length = value.shape[axis]
+    moved = pltpu.roll(value, length - 1 if back else 1, axis)
+    index = lax.broadcasted_iota(jnp.int32, value.shape, axis)
+    return jnp.where(index == (length - 1 if back else 0), 0.0, moved)
+
+
+def remainder_of(source, before, middle, after, diagonal):
+    beside = before + after
+    beside = beside + shifted(middle, 0, False) + shifted(middle, 0, True)
+    beside = beside + shifted(middle, 1, False) + shifted(middle, 1, True)
+    return source - (diagonal * middle - beside)
+
+
+def pieces(ref, sources, per_source, start, rows, bands, per_band):
+    columns = []
+    for band in range(bands):
+        starts = [i * per_source + band * per_band + start for i in range(sources)]
+        columns.append(jnp.concatenate([ref[at : at + rows, :] for at in starts], axis=0))
+    return jnp.concatenate(columns, axis=1)
+
+
+def put(sent_ref, k, planes, targets, per_block, start, value):
+    turned = value.T
+    per_target = turned.shape[0] // targets
+    for j in range(targets):
+        for band in range(turned.shape[1] // 128):
+            at = j * per_block + start + band * per_target * planes + k
+            part = turned[j * per_target : (j + 1) * per_target, band * 128 : (band + 1) * 128]
+            sent_ref[pl.ds(at, per_target, stride=planes), :] = part
+
+
+def brick_planes(ref, first_count, second_count, planes, k):
+    bands = []
+    lane = lax.broadcasted_iota(jnp.int32, (8, 128), 1)
+    for i in range(first_count):
+        tiles = []
+        for j in range(second_count):
+            start = ((i * second_count + j) * planes + k) * 8
+            tiles.append(ref[start : start + 8, :])
+        turned = [pltpu.roll(tile, 64, 1) for tile in tiles]
+        pairs = range(0, second_count, 2)
+        bands.append(jnp.concatenate([jnp.where(lane < 64, tiles[j], turned[j + 1]) for j in pairs], axis=1))
+        bands.append(jnp.concatenate([jnp.where(lane < 64, turned[j], tiles[j + 1]) for j in pairs], axis=1))
+    return jnp.concatenate(bands, axis=0)
+
+
+def sweep_all(count, step_ref, source_ref, diagonal_ref, matrix_ref, emit):
+    matrix = wide(matrix_ref[...])
+    for k in range(count):
+        diagonal = diagonal_ref[0 if diagonal_ref.shape[0] == 1 else k + 1]
+        middle = step_ref[k + 1]
+        remainder = remainder_of(source_ref[k + 1], step_ref[k], middle, step_ref[k + 2], diagonal)
+        high, low = parts_of(remainder, 2)
+        row = jnp.concatenate([high, low, high], axis=1)
+        step = lax.dot_general(row, matrix, (((1,), (1,)), ((), ())), preferred_element_type=jnp.float32)
+        emit(k, middle + step)
+
+
+def first_kernel(
+    grid, held_ref, before_ref, after_ref, diagonal_ref, first_ref, second_ref, sent_ref, source_ref, step_ref
+):
+    first_count, second_count, planes, per_target = grid
+    for k in range(planes):
+        source_ref[k + 1] = brick_planes(held_ref, first_count, second_count, planes, k)
+    source_ref[0] = brick_planes(before_ref, first_count, second_count, 1, 0)
+    source_ref[planes + 1] = brick_planes(after_ref, first_count, second_count, 1, 0)
+    first = wide(first_ref[...])
+    for k in range(planes + 2):
+        step_ref[k] = jnp.dot(first, parts_in_rows(source_ref[k]), preferred_element_type=jnp.float32)
+    devices = first_count * second_count
+    block = sent_ref.shape[0] // devices
+
+    def emit(k, value):
+        put(sent_ref, k, planes, devices, block, 0, source_ref[k + 1])
+        put(sent_ref, k, planes, devices, block, block // 2, value)
+
+    sweep_all(planes, step_ref, source_ref, diagonal_ref, second_ref, emit)
+
+
+def later_kernel(
+    shape, edge_ref, held_ref, before_ref, after_ref, diagonal_ref, first_ref, second_ref, *refs
+):
+    devices, planes, rows, with_source, last = shape
+    if with_source:
+        sent_ref, source_ref, iterate_ref, step_ref = refs
+    else:
+        source_ref, sent_ref, iterate_ref, step_ref = refs
+    bands = iterate_ref.shape[2] // 128
+    block, edge_block = held_ref.shape[0] // devices, before_ref.shape[0] // devices
+    per_band = planes * rows
+    edge_band = edge_block // bands
+    own = lambda k, start: pieces(held_ref, devices, block, start + k * rows, rows, bands, per_band)
+    edge = lambda ref, k: pieces(ref, devices, edge_block, k * rows, rows, bands, edge_band)
+    if with_source:
+        for k in range(planes):
+            source_ref[k + 1] = own(k, 0)
+        source_ref[0] = edge(before_ref, 0)
+        source_ref[planes + 1] = edge(after_ref, 0)
+    for k in range(2):
+        iterate_ref[k] = edge(before_ref, k + with_source)
+        iterate_ref[planes + 2 + k] = edge(after_ref, k + with_source)
+    for k in range(planes):
+        iterate_ref[k + 2] = own(k, block // 2 if with_source else 0)
+    first = wide(first_ref[...])
+    for k in range(planes + 2):
+        diagonal = diagonal_ref[0 if diagonal_ref.shape[0] == 1 else k]
+        middle = iterate_ref[k + 1]
+        remainder = remainder_of(source_ref[k], iterate_ref[k], middle, iterate_ref[k + 2], diagonal)
+        step = jnp.dot(first, parts_in_rows(remainder), preferred_element_type=jnp.float32)
+        if k == 0:
+            step = step * edge_ref[0]
+        if k == planes + 1:
+            step = step * edge_ref[1]
+        step_ref[k] = middle + step
+
+    def emit(k, value):
+        if last:
+            for j in range(value.shape[0] // CY):
+                sent_ref[j, k] = value[j * CY : (j + 1) * CY, :]
+        else:
+            put(sent_ref, k, planes, devices, sent_ref.shape[0] // devices, 0, value)
+
+    sweep_all(planes, step_ref, source_ref, diagonal_ref, second_ref, emit)
+
+
+SMEM = pl.BlockSpec(memory_space=pltpu.SMEM)
+VMEM = pl.BlockSpec(memory_space=pltpu.VMEM)
+LIMIT = pltpu.CompilerParams(vmem_limit_bytes=48 << 20)
+
+
+def first_phase(grid, held, before, after, diagonal, first, second):
+    rows, columns = diagonal.shape[1:]
+    first_count, second_count, planes, per_target = grid
+    return pl.pallas_call(
+        functools.partial(first_kernel, grid),
+        out_shape=(
+            jax.ShapeDtypeStruct((2 * columns * planes * rows // 128, 128), jnp.float32),
+            jax.ShapeDtypeStruct((planes + 2, rows, columns), jnp.float32),
+        ),
+        in_specs=[VMEM] * 6,
+        out_specs=(VMEM, VMEM),
+        scratch_shapes=[pltpu.VMEM((planes + 2, rows, columns), jnp.float32)],
+        compiler_params=LIMIT,
+        name="first_phase",
+    )(held, before, after, diagonal, first, second)
+
+
+def later_phase(devices, planes, rows, edges, held, before, after, diagonal, first, second, source=None, last=False):
+    columns = second.shape[1]
+    length = devices * rows
+    if last:
+        sent = (length // CY, planes, CY, columns)
+    else:
+        sent = (columns * planes * length // 128, 128)
+    out = [jax.ShapeDtypeStruct(sent, jnp.float32)]
+    operands = [edges, held, before, after, diagonal, first, second]
+    if source is None:
+        out.append(jax.ShapeDtypeStruct((planes + 2, length, columns), jnp.float32))
+    else:
+        operands.append(source)
+    return pl.pallas_call(
+        functools.partial(later_kernel, (devices, planes, rows, source is None, last)),
+        out_shape=tuple(out),
+        in_specs=[SMEM] + [VMEM] * (len(operands) - 1),
+        out_specs=tuple([VMEM] * len(out)),
+        scratch_shapes=[
+            pltpu.VMEM((planes + 4, length, columns), jnp.float32),
+            pltpu.VMEM((planes + 2, length, columns), jnp.float32),
+        ],
+        compiler_params=LIMIT,
+        name="later_phase",
+    )(*operands)
+
+
+def join_kernel(source_ref, x_before_ref, x_after_ref, y_before_ref, y_after_ref, brick_ref, sent_ref):
+    for i in range(CX):
+        here = slice(i * CY, (i + 1) * CY)
+        value = source_ref[here, :]
+        if i == 0:
+            value = value + x_before_ref[...]
+        if i == CX - 1:
+            value = value + x_after_ref[...]
+        row = rows_iota(CY, NZ)
+        value = value + jnp.where(row == 0, y_before_ref[i : i + 1, :], 0.0)
+        brick_ref[here, :] = value + jnp.where(row == CY - 1, y_after_ref[i : i + 1, :], 0.0)
+    half = CX // 2
+    for i in range(half):
+        both = [brick_ref[j * CY : (j + 1) * CY, :] for j in (i, i + half)]
+        sent_ref[pl.ds(i, NZ, stride=half), :] = jnp.concatenate(both, axis=0).T
+
+
+def join(source, *faces):
+    return pl.pallas_call(
+        join_kernel,
+        out_shape=(
+            jax.ShapeDtypeStruct(source.shape, jnp.float32),
+            jax.ShapeDtypeStruct((NZ * CX // 2, 2 * CY), jnp.float32),
+        ),
+        in_specs=[VMEM] * 5,
+        out_specs=(VMEM, VMEM),
+        compiler_params=LIMIT,
+        name="join",
+    )(source, *faces)
+
+
+def along_slabs(to_next, to_previous):
     devices = lax.axis_size(EVERY)
-    count = slab.shape[0]
-    before, after = [], []
-    reach = 1
-    while width > 0:
-        part = min(width, count)
-        up = [(i, i + reach) for i in range(devices - reach)]
-        down = [(j, i) for i, j in up]
-        before.insert(0, lax.ppermute(slab[count - part :], EVERY, up))
-        after.append(lax.ppermute(slab[:part], EVERY, down))
-        width, reach = width - part, reach + 1
-    return jnp.concatenate(before + [slab] + after, axis=0)
-
-
-def turn(slab):
-    devices = lax.axis_size(EVERY)
-    n, first, second = slab.shape
-    sent = slab.transpose(2, 0, 1)
-    held = lax.all_to_all(sent, EVERY, split_axis=0, concat_axis=0, tiled=True)
-    held = held.reshape(devices, second // devices, n, first)
-    return held.transpose(1, 0, 2, 3).reshape(second // devices, devices * n, first)
-
-
-def stencil(field, diagonal):
-    middle = field[1:-1]
-    beside = field[2:] + field[:-2]
-    wide = jnp.pad(middle, ((0, 0), (1, 1), (1, 1)))
-    beside = beside + wide[:, 2:, 1:-1] + wide[:, :-2, 1:-1]
-    beside = beside + wide[:, 1:-1, 2:] + wide[:, 1:-1, :-2]
-    return diagonal * middle - beside
-
-
-def phase(iterate, source, diagonal, inside, first_matrix, second_matrix):
-    highest = lax.Precision.HIGHEST
-    remainder = source - stencil(iterate, diagonal)
-    step = jnp.einsum("ab,nbk->nak", first_matrix, remainder, precision=highest)
-    iterate = iterate[1:-1] + step * inside
-    remainder = source[1:-1] - stencil(iterate, diagonal[1:-1] if diagonal.shape[0] > 1 else diagonal)
-    step = jnp.einsum("ab,nkb->nka", second_matrix, remainder, precision=highest)
-    return iterate[1:-1] + step
-
-
-def relax(source, levels, rows_inverse, columns_inverse, depth_inverse):
+    up = [(i, i + 1) for i in range(devices - 1)]
+    down = [(j, i) for i, j in up]
+    return lax.ppermute(to_next, EVERY, up), lax.ppermute(to_previous, EVERY, down)
+
+
+def exchange(value):
+    return lax.all_to_all(value, EVERY, split_axis=0, concat_axis=0, tiled=True)
+
+
+def x_slab_source(brick):
+    second_count = lax.axis_size("by")
+    mine = lax.axis_index("by")
+    brick = brick.reshape(CX, CY, NZ)
+    thick = CX // second_count
+    slab = jnp.zeros((thick, second_count * CY, NZ), jnp.float32)
+    for turn in range(second_count):
+        partner = mine ^ turn
+        piece = lax.dynamic_slice_in_dim(brick, partner * thick, thick, 0)
+        if turn:
+            piece = lax.ppermute(piece, "by", [(i, i ^ turn) for i in range(second_count)])
+        slab = lax.dynamic_update_slice_in_dim(slab, piece, partner * CY, 1)
+    before, after = along_slabs(slab[-1:], slab[:1])
+    return jnp.concatenate([before, slab, after], axis=0)
+
+
+def relax(brick, sent, levels, rows_inverse, columns_inverse, depth_inverse):
     first_count, second_count = lax.axis_size("bx"), lax.axis_size("by")
     devices = first_count * second_count
     me = lax.axis_index(EVERY)
@@ -286,38 +488,53 @@
     thick = (NZ // devices, ny // devices, nx // devices)
     diagonal = 6.0 + screen_base * (1.0 + levels.reshape(first_count, second_count))
     diagonal = jnp.repeat(jnp.repeat(diagonal, CX, 0), CY, 1)
-    own = lambda n: me * n - 1 + jnp.arange(n + 2)
-    inside = []
-    for n in thick:
-        place = own(n)
-        inside.append(((place >= 0) & (place < n * devices)).astype(jnp.float32)[:, None, None])
-    wide = jnp.pad(diagonal, ((1, 1), (1, 1)), constant_values=1.0)
+    padded = jnp.pad(diagonal, ((1, 1), (1, 1)), constant_values=1.0)
     diagonals = (
         diagonal[None],
-        lax.dynamic_slice_in_dim(wide, me * thick[1], thick[1] + 2, 1).T[:, None, 1:-1],
-        lax.dynamic_slice_in_dim(wide, me * thick[2], thick[2] + 2, 0)[:, 1:-1, None],
+        lax.dynamic_slice_in_dim(padded, me * thick[1], thick[1] + 2, 1).T[:, None, 1:-1],
+        lax.dynamic_slice_in_dim(padded, me * thick[2], thick[2] + 2, 0)[:, 1:-1, None],
     )
-    sent = source.reshape(CX, CY, devices, NZ // devices).transpose(2, 3, 0, 1)
-    held = lax.all_to_all(sent, EVERY, split_axis=0, concat_axis=0, tiled=True)
-    held = held.reshape(first_count, second_count, thick[0], CX, CY).transpose(2, 0, 3, 1, 4)
-    z_source = held.reshape(thick[0], nx, ny)
-    held = lax.all_to_all(source, "by", split_axis=0, concat_axis=1, tiled=True)
-    sources = [slab_halo(z_source, 1), slab_halo(turn(z_source), 1), slab_halo(held, 1)]
+    edges = jnp.stack([me > 0, me < devices - 1]).astype(jnp.float32)
     matrices = (rows_inverse, columns_inverse, depth_inverse)
-    iterate = jnp.zeros((thick[0], nx, ny), jnp.float32)
-    for step in range(3 * ITERS // 2):
+    held, slab, diagonals = lax.optimization_barrier((exchange(sent), x_slab_source(brick), diagonals))
+    blocks = held.reshape(devices, thick[0], CX // 2, 2 * CY)
+    before, after = along_slabs(
+        blocks[:, -1].reshape(-1, 2 * CY), blocks[:, 0].reshape(-1, 2 * CY)
+    )
+    sent, z_source = first_phase(
+        (first_count, second_count, thick[0], thick[1]), held, before, after, diagonals[0], matrices[0], matrices[1]
+    )
+    sources = [z_source, None, slab]
+    for step in range(1, 3 * ITERS // 2):
         at = step % 3
-        iterate = phase(
-            slab_halo(iterate, 2),
-            sources[at],
+        planes, rows = thick[at], thick[(at + 2) % 3]
+        held = exchange(sent)
+        bands = matrices[(2 * step + 1) % 3].shape[1] // 128
+        blocks = held.reshape(devices, -1, bands, planes * rows, 128)
+        to_next, to_previous = blocks[:, -1, :, -2 * rows :], blocks[:, -1, :, : 2 * rows]
+        if sources[at] is None:
+            to_next = jnp.concatenate([blocks[:, 0, :, -rows:], to_next], axis=2)
+            to_previous = jnp.concatenate([blocks[:, 0, :, :rows], to_previous], axis=2)
+        before, after = along_slabs(to_next.reshape(-1, 128), to_previous.reshape(-1, 128))
+        out = later_phase(
+            devices,
+            planes,
+            rows,
+            edges,
+            held,
+            before,
+            after,
             diagonals[at],
-            inside[at],
             matrices[2 * step % 3],
             matrices[(2 * step + 1) % 3],
+            source=sources[at],
+            last=step + 1 == 3 * ITERS // 2,
         )
-        if step + 1 < 3 * ITERS // 2:
-            iterate = turn(iterate)
-    return lax.all_to_all(iterate, "by", split_axis=1, concat_axis=0, tiled=True)
+        sent = out[0]
+        if sources[at] is None:
+            sources[at] = out[1]
+    sent = sent.reshape(second_count * thick[2], CY, NZ)
+    return lax.all_to_all(sent, "by", split_axis=0, concat_axis=0, tiled=True)
 
 
 def local(normals, owners, cells, levels, rows_inverse, columns_inverse, depth_inverse):
@@ -325,22 +542,19 @@
     point_count = cells.shape[0]
     capacity = 2 * point_count // bricks
     chunks = bricks * capacity // 128
-    level = jnp.broadcast_to(levels.astype(jnp.float32), (1, 128))
-    levels = lax.all_gather(level, EVERY, tiled=True)[:, 0]
+    level = jnp.broadcast_to(levels.astype(jnp.float32)[None], (bricks, 1, 128))
+    levels = exchange(level)[:, 0, 0]
     send, rank = pack(owners, cells, normals, bricks, capacity)
+    send, levels = lax.optimization_barrier((send, levels))
     held = lax.all_to_all(send, EVERY, split_axis=0, concat_axis=0, tiled=True)
     field = held.reshape(bricks, 4, capacity).transpose(1, 0, 2).reshape(4 * chunks, 128)
     cell_rows = field[3 * chunks :]
     used = (jnp.max(cell_rows, axis=1) > 0).astype(jnp.int32)
     source, x_face, y_face = splat(field, used)
-    source = source.reshape(CX, CY, NZ)
     x_before, x_after = neighbours(x_face, "bx", CY)
     y_before, y_after = neighbours(y_face, "by", CX)
-    source = source + jnp.pad(x_before[None], ((0, CX - 1), (0, 0), (0, 0)))
-    source = source + jnp.pad(x_after[None], ((CX - 1, 0), (0, 0), (0, 0)))
-    source = source + jnp.pad(y_before[:, None], ((0, 0), (0, CY - 1), (0, 0)))
-    source = source + jnp.pad(y_after[:, None], ((0, 0), (CY - 1, 0), (0, 0)))
-    iterate = relax(source, levels, rows_inverse, columns_inverse, depth_inverse)
+    brick, sent = join(source, x_before, x_after, y_before, y_after)
+    iterate = relax(brick, sent, levels, rows_inverse, columns_inverse, depth_inverse)
     sampled = sample(cell_rows, iterate.reshape(CX * CY, NZ))
     returned = lax.all_to_all(sampled.reshape(bricks, capacity), EVERY, split_axis=0, concat_axis=0, tiled=True)
     implicit = unpack(owners, rank, returned)

time: 556 us -> 456 us (0.82); the launches traced: 546 us -> 455 us
  local copies, waits for them, and re-layouts: 88.2 us -> 18.1 us
  blocking collectives: 199 us -> 255 us
  starting transfers between devices: 94.9 us -> 50 us
  matrix products: 31.9 us -> 0 us
  Pallas kernels: 48 us -> 74.5 us
  waiting for transfers between devices: 69 us -> 52.9 us
  other arithmetic: 11.3 us -> 2.41 us
    all_to_all x4 -> x6, blocking collectives: 131 us -> 233 us  [the longest x5 206 us: exchange(): return lax.all_to_all(value, EVERY, split_axis=0, concat_axis=0, tiled=True)]
    all_to_all x5 -> x2, waiting for transfers between devices: 63.1 us -> 0.01 us  [exchange(): return lax.all_to_all(value, EVERY, split_axis=0, concat_axis=0, tiled=True)]
    unnamed x1 -> x0, blocking collectives: 44 us -> none
    slice x47 -> x11, local copies, waits for them, and re-layouts: 42.1 us -> 3.6 us  [the longest x4 1.32 us: relax(): blocks[:, -1, :, :2 * rows]]
    ppermute x18 -> x17, waiting for transfers between devices: 4.21 us -> 36.9 us  [the longest x3 19.1 us: x_slab_source(): lax.ppermute(piece, 'by', [(i, i ^ turn) for i in range(second_count)])]
    dot_general x12 -> x0, matrix products: 31.9 us -> none  [the longest x6 20.1 us: phase(): step = jnp.einsum('ab,nbk->nak', first_matrix, remainder, precision=highest)]
    pallas_call x0 -> x7, Pallas kernels: none -> 20.6 us  [the longest x5 17.3 us: later_phase(): pl.pallas_call(functools.partial(later_kernel, (devices, planes, rows, so...]
    ppermute x2, starting transfers between devices: 23 us -> 2.58 us  [neighbours(): lax.ppermute(face[count:], axis, up)]
  transfers between devices with their start and end apart: 27 -> 23, of which waited for: 7 -> 12; matrix products, arithmetic and copies ran while one was open for 13% -> 2% of each run, Pallas kernels for 0% -> 2%
where the time goes in v3:
time: 456 us; the launch traced here: 455 us
  blocking collectives  255 us (56%)
  Pallas kernels  74.5 us (16%)
  waiting for transfers between devices  52.9 us (12%)
  starting transfers between devices  50 us (11%)
  local copies, waits for them, and re-layouts  18.1 us (4%)
    all_to_all x5, blocking collectives, exchange(): return lax.all_to_all(value, EVERY, split_axis=0, concat_axis=0, tiled=True)  206 us
    pallas_call x1, Pallas kernels, splat(): pl.pallas_call(splat_kernel, out_shape=tuple((jax.ShapeDtypeStruct(shape,...  30.4 us
    all_to_all x1, blocking collectives, relax(): return lax.all_to_all(sent, 'by', split_axis=0, concat_axis=0, tiled=True)  26.8 us
    ppermute x7, starting transfers between devices, along_slabs(): lax.ppermute(to_next, EVERY, up)  19.5 us
    ppermute x3, waiting for transfers between devices, x_slab_source(): lax.ppermute(piece, 'by', [(i, i ^ turn) for i in range(second_count)])  19.1 us
    pallas_call x5, Pallas kernels, later_phase(): pl.pallas_call(functools.partial(later_kernel, (devices, planes, rows, so...  17.3 us
    ppermute x2, waiting for transfers between devices, neighbours(): lax.ppermute(face[:count], axis, down)  16 us
    ppermute x7, waiting for transfers between devices, along_slabs(): lax.ppermute(to_previous, EVERY, down)  15.1 us
  transfers between devices with their start and end apart: 23, of which 12 were waited for; matrix products, arithmetic and copies ran while one was open for 2% of the time, Pallas kernels for 2%

profile of v3, /device:TPU:0, one launch (start us, length us, event | category | flops | bytes accessed | tf_op | source)
XLA Modules:
  0.0 455.3 jit_solution(4499679627918014485)
XLA Ops:
  1.9 7.3 %all-to-all-start = ((f32[32,1,128]{2,1,0:T(1,128)}), f32[32,1,128]{2,1,0:T(1,128)S(1)}, u32[]{:S(2)}, u32[]{:S(2)}) async-start(f32[32,1,128]{2,1,0:T(1,128)} %broadcast_in_dim.24), calls=%async_computation | async-start | bytes 32768 | tf_op jit(solution)/shard_map/all_to_all | solution.py:464
  11.5 7.0 %pack.1 = (f32[32,8,128]{2,1,0:T(8,128)S(1)}, f32[1,4096]{1,0:T(1,128)S(1)}) custom-call(s32[1,4096]{1,0:T(1,128)S(1)} %bitcast.94, s32[1,4096]{1,0:T(1,128)S(1)} %bitcast.96, f32[3,4096]{1,0:T(4,128)S(1)} %copy-done.16), custom_call_target="tpu_custom_call" | custom-call | tf_op jit(solution)/shard_map/pack/pallas_call | solution.py:78
  19.4 13.9 %all_to_all.93 = f32[32,8,128]{2,1,0:T(8,128)S(1)} all-to-all(f32[32,8,128]{2,1,0:T(8,128)S(1)} %get-tuple-element.21), channel_id=1, replica_groups=mesh['bx'=8,'by'=4] {'bx','by'}, dimensions={0} | all-to-all | bytes 262144 | tf_op jit(solution)/shard_map/all_to_all | solution.py:549
  33.5 30.4 %splat.1 = (f32[1024,256]{1,0:T(8,128)S(1)}, f32[128,256]{1,0:T(8,128)S(1)}, f32[32,256]{1,0:T(8,128)S(1)}) custom-call(s32[64]{0:T(128)S(1)} %compare_convert_fusion.used_ref, f32[256,128]{1,0:T(8,128)S(1)} %reshape.90.field_ref), custom_call_target="tpu_custom_call" | custom-call | tf_op jit(solution)/shard_map/splat/pallas_call | solution.py:183
  69.1 8.4 %collective-permute-done.3.y_after_ref = f32[16,256]{1,0:T(8,128)S(1)} collective-permute-done((f32[16,256]{1,0:T(8,128)S(1)}, f32[16,256]{1,0:T(8,128)S(1)}, u32[]{:S(2)}, u32[]{:S(2)}) %collective-permute-start.3) | collective-permute-done | bytes 16416 | tf_op jit(solution)/shard_map/ppermute | solution.py:237
  77.5 7.6 %collective-permute-done.1.x_after_ref = f32[64,256]{1,0:T(8,128)S(1)} collective-permute-done((f32[64,256]{1,0:T(8,128)S(1)}, f32[64,256]{1,0:T(8,128)S(1)}, u32[]{:S(2)}, u32[]{:S(2)}) %collective-permute-start.1) | collective-permute-done | bytes 65568 | tf_op jit(solution)/shard_map/ppermute | solution.py:237
  86.5 6.7 %all-to-all-start.2 = ((f32[32,64,128]{2,1,0:T(8,128)}), f32[32,64,128]{2,1,0:T(8,128)S(1)}, u32[]{:S(2)}, u32[]{:S(2)}) async-start(f32[32,64,128]{2,1,0:T(8,128)} %bitcast.6), calls=%async_computation.2 | async-start | bytes 2097152 | tf_op jit(solution)/shard_map/all_to_all | solution.py:464
  95.4 1.7 collective-permute-start.5
  97.8 14.2 %collective-permute-done.5 = f32[4,64,256]{2,1,0:T(8,128)S(1)} collective-permute-done((f32[4,64,256]{2,1,0:T(8,128)S(1)}, f32[4,64,256]{2,1,0:T(8,128)S(1)}, u32[]{:S(2)}, u32[]{:S(2)}) %collective-permute-start.5) | collective-permute-done | bytes 262176 | tf_op jit(solution)/shard_map/ppermute | solution.py:477
  112.7 4.9 %collective-permute-done.6 = f32[4,64,256]{2,1,0:T(8,128)S(1)} collective-permute-done((f32[4,64,256]{2,1,0:T(8,128)S(1)}, f32[4,64,256]{2,1,0:T(8,128)S(1)}, u32[]{:S(2)}, u32[]{:S(2)}) %collective-permute-start.6) | collective-permute-done | bytes 262176 | tf_op jit(solution)/shard_map/ppermute | solution.py:477
  119.4 2.6 collective-permute-start.7
  129.1 7.9 %collective-permute-start.9 = (f32[256,128]{1,0:T(8,128)}, f32[256,128]{1,0:T(8,128)S(1)}, u32[]{:S(2)}, u32[]{:S(2)}) collective-permute-start(f32[256,128]{1,0:T(8,128)} %get-tuple-element.51), channel_id=1, source_target_pairs={{0,1},{1,2},{2,3},{3,4},{4,5},{5,6},{6,7},{7,8},{8,9},{9,10},{10,1... | collective-permute-start | bytes 393224 | tf_op jit(solution)/shard_map/ppermute | solution.py:460
  138.1 2.0 first_phase.1
  140.1 61.4 %all_to_all.94 = f32[32,128,128]{2,1,0:T(8,128)S(1)} all-to-all(f32[32,128,128]{2,1,0:T(8,128)S(1)} %bitcast.89), channel_id=1, replica_groups=mesh['bx'=8,'by'=4] {'bx','by'}, dimensions={0} | all-to-all | bytes 4194304 | tf_op jit(solution)/shard_map/all_to_all | solution.py:464
  203.9 3.0 collective-permute-start.11
  210.0 3.5 later_phase.5
  213.6 36.5 %all_to_all.95 = f32[32,64,128]{2,1,0:T(8,128)S(1)} all-to-all(f32[32,64,128]{2,1,0:T(8,128)S(1)} %bitcast.91), channel_id=1, replica_groups=mesh['bx'=8,'by'=4] {'bx','by'}, dimensions={0} | all-to-all | bytes 2097152 | tf_op jit(solution)/shard_map/all_to_all | solution.py:464
  251.2 2.1 collective-permute-start.13
  255.7 2.6 collective-permute-done.14.after_ref
  260.2 3.9 later_phase.6
  264.2 38.4 %all_to_all.96 = f32[32,64,128]{2,1,0:T(8,128)S(1)} all-to-all(f32[32,64,128]{2,1,0:T(8,128)S(1)} %bitcast.88), channel_id=1, replica_groups=mesh['bx'=8,'by'=4] {'bx','by'}, dimensions={0} | all-to-all | bytes 2097152 | tf_op jit(solution)/shard_map/all_to_all | solution.py:464
  305.2 3.8 collective-permute-done.16.after_ref
  309.1 3.3 later_phase.7
  312.3 34.8 %all_to_all.97 = f32[32,64,128]{2,1,0:T(8,128)S(1)} all-to-all(f32[32,64,128]{2,1,0:T(8,128)S(1)} %bitcast.85), channel_id=1, replica_groups=mesh['bx'=8,'by'=4] {'bx','by'}, dimensions={0} | all-to-all | bytes 2097152 | tf_op jit(solution)/shard_map/all_to_all | solution.py:464
  349.8 3.8 collective-permute-done.18.after_ref
  353.6 3.3 later_phase.8
  356.9 34.8 %all_to_all.98 = f32[32,64,128]{2,1,0:T(8,128)S(1)} all-to-all(f32[32,64,128]{2,1,0:T(8,128)S(1)} %bitcast.87), channel_id=1, replica_groups=mesh['bx'=8,'by'=4] {'bx','by'}, dimensions={0} | all-to-all | bytes 2097152 | tf_op jit(solution)/shard_map/all_to_all | solution.py:464
  394.6 4.0 collective-permute-done.20.after_ref
  398.6 3.3 later_phase.9
  401.9 26.8 %all_to_all.99 = f32[16,64,256]{2,1,0:T(8,128)S(1)} all-to-all(f32[16,64,256]{2,1,0:T(8,128)S(1)} %bitcast.86), channel_id=1, replica_groups=mesh['bx'=8,'by'=4] {'by'}, dimensions={0} | all-to-all | bytes 2097152 | tf_op jit(solution)/shard_map/all_to_all | solution.py:537
  428.7 15.0 %sample.1 = f32[64,128]{1,0:T(8,128)S(1)} custom-call(f32[64,128]{1,0:T(8,128)S(1)} %copy-done.15, f32[1024,256]{1,0:T(8,128)S(1)} %bitcast.74), custom_call_target="tpu_custom_call" | custom-call | tf_op jit(solution)/shard_map/sample/pallas_call | solution.py:222
  443.8 8.9 %all_to_all.100 = f32[32,1,256]{2,1,0:T(1,128)S(1)} all-to-all(f32[32,1,256]{2,1,0:T(1,128)S(1)} %bitcast.92), channel_id=1, replica_groups=mesh['bx'=8,'by'=4] {'bx','by'}, dimensions={0} | all-to-all | bytes 65536 | tf_op jit(solution)/shard_map/all_to_all | solution.py:559
  (120 shorter events, 45.7 us)
Async XLA Ops:
  1.9 17.2 %all-to-all-start = ((f32[32,1,128]{2,1,0:T(1,128)}), f32[32,1,128]{2,1,0:T(1,128)S(1)}, u32[]{:S(2)}, u32[]{:S(2)}) async-start(f32[32,1,128]{2,1,0:T(1,128)} %broadcast_in_dim.24), calls=%async_computation | async-start | bytes 32768 | tf_op jit(solution)/shard_map/all_to_all | solution.py:464
  33.4 51.7 %copy-start.14 = (f32[64,128]{1,0:T(8,128)}, f32[64,128]{1,0:T(8,128)S(1)}, u32[]{:S(2)}) copy-start(f32[64,128]{1,0:T(8,128)S(1)} %slice.77.field_ref) | copy-start | bytes 98308
  63.9 13.6 %collective-permute-start = (f32[64,256]{1,0:T(8,128)S(1)}, f32[64,256]{1,0:T(8,128)S(1)}, u32[]{:S(2)}, u32[]{:S(2)}) collective-permute-start(f32[64,256]{1,0:T(8,128)S(1)} %get-tuple-element.59), channel_id=1, source_target_pairs={{0,4},{4,8},{8,12},{12,16},{16,20},{20,24},{24,28},{1,5},{5,9},{9,... | collective-permute-start | bytes 196616 | tf_op jit(solution)/shard_map/ppermute | solution.py:237
  65.2 19.9 %collective-permute-start.1 = (f32[64,256]{1,0:T(8,128)S(1)}, f32[64,256]{1,0:T(8,128)S(1)}, u32[]{:S(2)}, u32[]{:S(2)}) collective-permute-start(f32[64,256]{1,0:T(8,128)S(1)} %get-tuple-element.58), channel_id=1, source_target_pairs={{4,0},{8,4},{12,8},{16,12},{20,16},{24,20},{28,24},{5,1},{9,5},{13... | collective-permute-start | bytes 196616 | tf_op jit(solution)/shard_map/ppermute | solution.py:237
  66.5 2.6 collective-permute-start.2
  67.8 9.7 %collective-permute-start.3 = (f32[16,256]{1,0:T(8,128)S(1)}, f32[16,256]{1,0:T(8,128)S(1)}, u32[]{:S(2)}, u32[]{:S(2)}) collective-permute-start(f32[16,256]{1,0:T(8,128)S(1)} %get-tuple-element.60), channel_id=1, source_target_pairs={{1,0},{2,1},{3,2},{5,4},{6,5},{7,6},{9,8},{10,9},{11,10},{13,12},{... | collective-permute-start | bytes 49160 | tf_op jit(solution)/shard_map/ppermute | solution.py:237
  86.5 40.6 %all-to-all-start.2 = ((f32[32,64,128]{2,1,0:T(8,128)}), f32[32,64,128]{2,1,0:T(8,128)S(1)}, u32[]{:S(2)}, u32[]{:S(2)}) async-start(f32[32,64,128]{2,1,0:T(8,128)} %bitcast.6), calls=%async_computation.2 | async-start | bytes 2097152 | tf_op jit(solution)/shard_map/all_to_all | solution.py:464
  95.2 1.9 collective-permute-start.4
  95.4 16.6 %collective-permute-start.5 = (f32[4,64,256]{2,1,0:T(8,128)S(1)}, f32[4,64,256]{2,1,0:T(8,128)S(1)}, u32[]{:S(2)}, u32[]{:S(2)}) collective-permute-start(f32[4,64,256]{2,1,0:T(8,128)S(1)} %get-tuple-element.55), channel_id=1, source_target_pairs={{0,2},{1,3},{2,0},{3,1},{4,6},{5,7},{6,4},{7,5},{8,10},{9,11},{10,... | collective-permute-start | bytes 786440 | tf_op jit(solution)/shard_map/ppermute | solution.py:477
  97.1 20.5 %collective-permute-start.6 = (f32[4,64,256]{2,1,0:T(8,128)S(1)}, f32[4,64,256]{2,1,0:T(8,128)S(1)}, u32[]{:S(2)}, u32[]{:S(2)}) collective-permute-start(f32[4,64,256]{2,1,0:T(8,128)S(1)} %get-tuple-element.54), channel_id=1, source_target_pairs={{0,3},{1,2},{2,1},{3,0},{4,7},{5,6},{6,5},{7,4},{8,11},{9,10},{10,... | collective-permute-start | bytes 786440 | tf_op jit(solution)/shard_map/ppermute | solution.py:477
  119.4 5.3 %collective-permute-start.7 = (f32[1,256,256]{2,1,0:T(8,128)S(1)}, f32[1,256,256]{2,1,0:T(8,128)S(1)}, u32[]{:S(2)}, u32[]{:S(2)}) collective-permute-start(f32[1,256,256]{2,1,0:T(8,128)S(1)} %get-tuple-element.52), channel_id=1, source_target_pairs={{0,1},{1,2},{2,3},{3,4},{4,5},{5,6},{6,7},{7,8},{8,9},{9,10},{10,1... | collective-permute-start | bytes 786440 | tf_op jit(solution)/shard_map/ppermute | solution.py:460
  122.1 3.6 collective-permute-start.8
  127.8 9.3 %collective-permute-start.10 = (f32[256,128]{1,0:T(8,128)}, f32[256,128]{1,0:T(8,128)S(1)}, u32[]{:S(2)}, u32[]{:S(2)}) collective-permute-start(f32[256,128]{1,0:T(8,128)} %get-tuple-element.50), channel_id=1, source_target_pairs={{1,0},{2,1},{3,2},{4,3},{5,4},{6,5},{7,6},{8,7},{9,8},{10,9},{11,1... | collective-permute-start | bytes 393224 | tf_op jit(solution)/shard_map/ppermute | solution.py:460
  129.1 9.0 %collective-permute-start.9 = (f32[256,128]{1,0:T(8,128)}, f32[256,128]{1,0:T(8,128)S(1)}, u32[]{:S(2)}, u32[]{:S(2)}) collective-permute-start(f32[256,128]{1,0:T(8,128)} %get-tuple-element.51), channel_id=1, source_target_pairs={{0,1},{1,2},{2,3},{3,4},{4,5},{5,6},{6,7},{7,8},{8,9},{9,10},{10,1... | collective-permute-start | bytes 393224 | tf_op jit(solution)/shard_map/ppermute | solution.py:460
  140.1 61.5 %copy-start.8 = (f32[10,128,256]{2,1,0:T(8,128)}, f32[10,128,256]{2,1,0:T(8,128)S(1)}, u32[]{:S(2)}) copy-start(f32[10,128,256]{2,1,0:T(8,128)S(1)} %get-tuple-element.35.refs_0_) | copy-start | bytes 3932164
  201.7 5.3 %collective-permute-start.12 = (f32[768,128]{1,0:T(8,128)S(1)}, f32[768,128]{1,0:T(8,128)S(1)}, u32[]{:S(2)}, u32[]{:S(2)}) collective-permute-start(f32[768,128]{1,0:T(8,128)S(1)} %bitcast.104), channel_id=1, source_target_pairs={{1,0},{2,1},{3,2},{4,3},{5,4},{6,5},{7,6},{8,7},{9,8},{10,9},{11,1... | collective-permute-start | bytes 1179656 | tf_op jit(solution)/shard_map/ppermute | solution.py:460
  203.9 4.6 %collective-permute-start.11 = (f32[768,128]{1,0:T(8,128)}, f32[768,128]{1,0:T(8,128)S(1)}, u32[]{:S(2)}, u32[]{:S(2)}) collective-permute-start(f32[768,128]{1,0:T(8,128)} %bitcast.21), channel_id=1, source_target_pairs={{0,1},{1,2},{2,3},{3,4},{4,5},{5,6},{6,7},{7,8},{8,9},{9,10},{10,1... | collective-permute-start | bytes 1179656 | tf_op jit(solution)/shard_map/ppermute | solution.py:460
  251.2 4.5 collective-permute-start.13
  253.3 5.1 %collective-permute-start.14 = (f32[1024,128]{1,0:T(8,128)}, f32[1024,128]{1,0:T(8,128)}, u32[]{:S(2)}, u32[]{:S(2)}) collective-permute-start(f32[1024,128]{1,0:T(8,128)} %bitcast.29), channel_id=1, source_target_pairs={{1,0},{2,1},{3,2},{4,3},{5,4},{6,5},{7,6},{8,7},{9,8},{10,9},{11,1... | collective-permute-start | bytes 1572872 | tf_op jit(solution)/shard_map/ppermute | solution.py:460
  264.2 44.9 %copy-start.4 = (f32[256,256]{1,0:T(8,128)S(1)}, f32[256,256]{1,0:T(8,128)}, u32[]{:S(2)}) copy-start(f32[256,256]{1,0:T(8,128)} %first_ref.11) | copy-start | bytes 786436
  264.2 44.9 %copy-start.9 = (f32[10,128,256]{2,1,0:T(8,128)S(1)}, f32[10,128,256]{2,1,0:T(8,128)}, u32[]{:S(2)}) copy-start(f32[10,128,256]{2,1,0:T(8,128)} %copy-done.8) | copy-start | bytes 3932164
  264.2 44.9 %copy-start.13 = (f32[128,128]{1,0:T(8,128)S(1)}, f32[128,128]{1,0:T(8,128)}, u32[]{:S(2)}) copy-start(f32[128,128]{1,0:T(8,128)} %second_ref.10) | copy-start | bytes 196612
  302.6 2.6 collective-permute-start.15
  303.9 5.1 %collective-permute-start.16 = (f32[512,128]{1,0:T(8,128)S(1)}, f32[512,128]{1,0:T(8,128)S(1)}, u32[]{:S(2)}, u32[]{:S(2)}) collective-permute-start(f32[512,128]{1,0:T(8,128)S(1)} %bitcast.105), channel_id=1, source_target_pairs={{1,0},{2,1},{3,2},{4,3},{5,4},{6,5},{7,6},{8,7},{9,8},{10,9},{11,1... | collective-permute-start | bytes 786440 | tf_op jit(solution)/shard_map/ppermute | solution.py:460
  312.3 41.3 %copy-start.7 = (f32[256,256]{1,0:T(8,128)S(1)}, f32[256,256]{1,0:T(8,128)}, u32[]{:S(2)}) copy-start(f32[256,256]{1,0:T(8,128)} %second_ref.11) | copy-start | bytes 786436
  312.3 41.3 %copy-start.11 = (f32[10,256,128]{2,1,0:T(8,128)S(1)}, f32[10,256,128]{2,1,0:T(8,128)}, u32[]{:S(2)}) copy-start(f32[10,256,128]{2,1,0:T(8,128)} %copy-done.10) | copy-start | bytes 3932164
  347.1 2.6 collective-permute-start.17
  348.5 5.1 %collective-permute-start.18 = (f32[512,128]{1,0:T(8,128)S(1)}, f32[512,128]{1,0:T(8,128)S(1)}, u32[]{:S(2)}, u32[]{:S(2)}) collective-permute-start(f32[512,128]{1,0:T(8,128)S(1)} %bitcast.106), channel_id=1, source_target_pairs={{1,0},{2,1},{3,2},{4,3},{5,4},{6,5},{7,6},{8,7},{9,8},{10,9},{11,1... | collective-permute-start | bytes 786440 | tf_op jit(solution)/shard_map/ppermute | solution.py:460
  391.8 2.8 collective-permute-start.19
  393.1 5.5 %collective-permute-start.20 = (f32[1024,128]{1,0:T(8,128)S(1)}, f32[1024,128]{1,0:T(8,128)S(1)}, u32[]{:S(2)}, u32[]{:S(2)}) collective-permute-start(f32[1024,128]{1,0:T(8,128)S(1)} %bitcast.102), channel_id=1, source_target_pairs={{1,0},{2,1},{3,2},{4,3},{5,4},{6,5},{7,6},{8,7},{9,8},{10,9},{11,1... | collective-permute-start | bytes 1572872 | tf_op jit(solution)/shard_map/ppermute | solution.py:460
  401.9 50.8 %copy-start.18 = (s32[4096,1]{0,1:T(1,128)S(1)}, s32[4096,1]{0,1:T(1,128)}, u32[]{:S(2)}) copy-start(s32[4096,1]{0,1:T(1,128)} %param.8) | copy-start | bytes 49156
  401.9 50.8 %copy-start.20 = (f32[1,4096]{1,0:T(1,128)S(1)}, f32[1,4096]{1,0:T(1,128)}, u32[]{:S(2)}) copy-start(f32[1,4096]{1,0:T(1,128)} %copy-done.19) | copy-start | bytes 49156
  (13 other events, 106.9 us)

commit v4 on v3

--- a/solution.py
+++ b/solution.py
@@ -38,7 +38,7 @@
     return [pl.BlockSpec(memory_space=pltpu.VMEM)] * count
 
 
-def pack_kernel(owner_ref, cell_ref, normal_ref, send_ref, rank_ref, total_ref):
+def pack_kernel(level_ref, owner_ref, cell_ref, normal_ref, send_ref, rank_ref, total_ref):
     bricks, capacity = send_ref.shape[0], total_ref.shape[1]
     points = owner_ref.shape[1]
     block = 256
@@ -69,24 +69,27 @@
     fields = [part(3 * k) + part(3 * k + 1) + part(3 * k + 2) for k in range(3)]
     fields.append(part(9) * 65536.0 + part(10) * 256.0 + part(11))
     row = jnp.concatenate(fields, axis=1)
-    for j in range(send_ref.shape[1]):
+    used = row.shape[1] // 128
+    for j in range(used):
         send_ref[:, j, :] = row[:, 128 * j : 128 * (j + 1)]
-
-
-def pack(owners, cells, normals, bricks, capacity):
+    level = jnp.full((bricks, send_ref.shape[1] - used, 128), level_ref[0, 0])
+    send_ref[:, used:, :] = level.astype(jnp.float32)
+
+
+def pack(owners, cells, normals, levels, bricks, capacity):
     points = cells.shape[0]
     return pl.pallas_call(
         pack_kernel,
         out_shape=(
-            jax.ShapeDtypeStruct((bricks, 4 * capacity // 128, 128), jnp.float32),
+            jax.ShapeDtypeStruct((bricks, 4 * capacity // 128 // 8 * 8 + 8, 128), jnp.float32),
             jax.ShapeDtypeStruct((1, points), jnp.float32),
         ),
-        in_specs=whole_arrays(3),
+        in_specs=[pl.BlockSpec(memory_space=pltpu.SMEM)] + whole_arrays(3),
         out_specs=tuple(whole_arrays(2)),
         scratch_shapes=[pltpu.VMEM((12 * bricks, capacity), jnp.float32)],
         compiler_params=pltpu.CompilerParams(vmem_limit_bytes=32 << 20),
         name="pack",
-    )(owners.reshape(1, points), cells.reshape(1, points), normals)
+    )(levels, owners.reshape(1, points), cells.reshape(1, points), normals)
 
 
 def unpack_kernel(owner_ref, rank_ref, held_ref, out_ref):
@@ -145,37 +148,50 @@
     def product(rows, columns):
         return lax.dot_general(rows, columns, (((1,), (1,)), ((), ())), preferred_element_type=jnp.float32)
 
+    group = 4
+
+    def tables(at):
+        x, y, z = places(field_ref[pl.ds(3 * chunks + at, 1), :])
+        y_hot = flags(rows_iota(CY, 128) == y).astype(jnp.bfloat16)
+        y_step = differenced(CY, 0, y).astype(jnp.bfloat16)
+        z_hot = flags(rows_iota(NZ, 128) == z).astype(jnp.bfloat16)
+        z_step = differenced(NZ, 0, z).astype(jnp.bfloat16)
+        columns = []
+        for k in range(3):
+            for part in parts_of(field_ref[pl.ds(k * chunks + at, 1), :], 2):
+                columns.append(times_row(z_step if k == 2 else z_hot, spread(part.astype(jnp.float32))))
+        steps = [spread(jnp.where(x == i - 1, 0.5, 0.0) - jnp.where(x == i + 1, 0.5, 0.0)) for i in range(-1, CX + 1)]
+        hots = [spread(flags(x == i)) for i in range(CX)]
+        along_x = jnp.concatenate([times_row(y_hot, steps[i + 1]) for i in range(CX)], axis=0)
+        along_y = jnp.concatenate([times_row(y_step, hots[i]) for i in range(CX)], axis=0)
+        along_z = jnp.concatenate([times_row(y_hot, hots[i]) for i in range(CX)], axis=0)
+        ends_x = jnp.concatenate([times_row(y_hot, steps[0]), times_row(y_hot, steps[CX + 1])], axis=0)
+        x_hot = flags(rows_iota(CX, 128) == x).astype(jnp.bfloat16)
+        ends_y = jnp.concatenate(
+            [x_hot * spread(jnp.where(y == 0, -0.5, 0.0)), x_hot * spread(jnp.where(y == CY - 1, 0.5, 0.0))], axis=0
+        )
+        return columns, along_x, along_y, along_z, ends_x, ends_y
+
     def step(at, carry):
-        @pl.when(used_ref[at] > 0)
+        total = used_ref[group * at]
+        for g in range(1, group):
+            total += used_ref[group * at + g]
+        @pl.when(total > 0)
         def _():
-            x, y, z = places(field_ref[pl.ds(3 * chunks + at, 1), :])
-            y_hot = flags(rows_iota(CY, 128) == y).astype(jnp.bfloat16)
-            y_step = differenced(CY, 0, y).astype(jnp.bfloat16)
-            z_hot = flags(rows_iota(NZ, 128) == z).astype(jnp.bfloat16)
-            z_step = differenced(NZ, 0, z).astype(jnp.bfloat16)
-            columns = []
-            for k in range(3):
-                for part in parts_of(field_ref[pl.ds(k * chunks + at, 1), :], 2):
-                    columns.append(times_row(z_step if k == 2 else z_hot, spread(part.astype(jnp.float32))))
-            columns = jnp.concatenate(columns, axis=1)
-            steps = [spread(jnp.where(x == i - 1, 0.5, 0.0) - jnp.where(x == i + 1, 0.5, 0.0)) for i in range(-1, CX + 1)]
-            hots = [spread(flags(x == i)) for i in range(CX)]
-            along_x = jnp.concatenate([times_row(y_hot, steps[i + 1]) for i in range(CX)], axis=0)
-            along_y = jnp.concatenate([times_row(y_step, hots[i]) for i in range(CX)], axis=0)
-            along_z = jnp.concatenate([times_row(y_hot, hots[i]) for i in range(CX)], axis=0)
-            rows = jnp.concatenate([along_x, along_x, along_y, along_y, along_z, along_z], axis=1)
-            source_ref[...] += product(rows, columns)
-            ends = jnp.concatenate([times_row(y_hot, steps[0]), times_row(y_hot, steps[CX + 1])], axis=0)
-            x_face_ref[...] += product(jnp.concatenate([ends, ends], axis=1), columns[:, :256])
-            x_hot = flags(rows_iota(CX, 128) == x).astype(jnp.bfloat16)
-            ends = jnp.concatenate(
-                [x_hot * spread(jnp.where(y == 0, -0.5, 0.0)), x_hot * spread(jnp.where(y == CY - 1, 0.5, 0.0))], axis=0
-            )
-            y_face_ref[...] += product(jnp.concatenate([ends, ends], axis=1), columns[:, 256:512])
+            cols, rows, cx, ex, cy, ey = [], [], [], [], [], []
+            for g in range(group):
+                c, ax, ay, az, e_x, e_y = tables(group * at + g)
+                cols += c
+                rows += [ax, ax, ay, ay, az, az]
+                cx += c[:2]; ex += [e_x, e_x]; cy += c[2:4]; ey += [e_y, e_y]
+            cat = lambda v: jnp.concatenate(v, axis=1)
+            source_ref[...] += product(cat(rows), cat(cols))
+            x_face_ref[...] += product(cat(ex), cat(cx))
+            y_face_ref[...] += product(cat(ey), cat(cy))
 
         return carry
 
-    lax.fori_loop(0, chunks, step, 0)
+    lax.fori_loop(0, chunks // group, step, 0)
 
 
 def splat(field, used):
@@ -215,7 +231,7 @@
         out_ref[pl.ds(2 * at + 1, 1), :] = row[:, 128:]
         return carry
 
-    lax.fori_loop(0, chunks // 2, step, 0)
+    lax.fori_loop(0, chunks // 2, step, 0, unroll=4)
 
 
 def sample(cell_rows, iterate):
@@ -496,7 +512,7 @@
     )
     edges = jnp.stack([me > 0, me < devices - 1]).astype(jnp.float32)
     matrices = (rows_inverse, columns_inverse, depth_inverse)
-    held, slab, diagonals = lax.optimization_barrier((exchange(sent), x_slab_source(brick), diagonals))
+    held, diagonals = lax.optimization_barrier((exchange(sent), diagonals))
     blocks = held.reshape(devices, thick[0], CX // 2, 2 * CY)
     before, after = along_slabs(
         blocks[:, -1].reshape(-1, 2 * CY), blocks[:, 0].reshape(-1, 2 * CY)
@@ -504,11 +520,13 @@
     sent, z_source = first_phase(
         (first_count, second_count, thick[0], thick[1]), held, before, after, diagonals[0], matrices[0], matrices[1]
     )
-    sources = [z_source, None, slab]
+    sources = [z_source, None, None]
     for step in range(1, 3 * ITERS // 2):
         at = step % 3
         planes, rows = thick[at], thick[(at + 2) % 3]
         held = exchange(sent)
+        if step == 1:
+            held, sources[2] = lax.optimization_barrier((held, x_slab_source(brick)))
         bands = matrices[(2 * step + 1) % 3].shape[1] // 128
         blocks = held.reshape(devices, -1, bands, planes * rows, 128)
         to_next, to_previous = blocks[:, -1, :, -2 * rows :], blocks[:, -1, :, : 2 * rows]
@@ -542,12 +560,10 @@
     point_count = cells.shape[0]
     capacity = 2 * point_count // bricks
     chunks = bricks * capacity // 128
-    level = jnp.broadcast_to(levels.astype(jnp.float32)[None], (bricks, 1, 128))
-    levels = exchange(level)[:, 0, 0]
-    send, rank = pack(owners, cells, normals, bricks, capacity)
-    send, levels = lax.optimization_barrier((send, levels))
-    held = lax.all_to_all(send, EVERY, split_axis=0, concat_axis=0, tiled=True)
-    field = held.reshape(bricks, 4, capacity).transpose(1, 0, 2).reshape(4 * chunks, 128)
+    send, rank = pack(owners, cells, normals, levels, bricks, capacity)
+    held = exchange(send)
+    levels = held[:, 4 * capacity // 128, 0]
+    field = held[:, : 4 * capacity // 128].reshape(bricks, 4, capacity).transpose(1, 0, 2).reshape(4 * chunks, 128)
     cell_rows = field[3 * chunks :]
     used = (jnp.max(cell_rows, axis=1) > 0).astype(jnp.int32)
     source, x_face, y_face = splat(field, used)

time: 456 us -> 430 us (0.943)
  blocking collectives: 255 us -> 202 us
  waiting for transfers between devices: 52.9 us -> 87.3 us
  starting transfers between devices: 50 us -> 44.8 us
    all_to_all x5, blocking collectives: 206 us -> 166 us  [exchange(): return lax.all_to_all(value, EVERY, split_axis=0, concat_axis=0, tiled=True)]
    all_to_all x2, waiting for transfers between devices: 0.01 us -> 33.6 us  [exchange(): return lax.all_to_all(value, EVERY, split_axis=0, concat_axis=0, tiled=True)]
    all_to_all x1 -> x0, blocking collectives: 13.9 us -> none  [local(): held = lax.all_to_all(send, EVERY, split_axis=0, concat_axis=0, tiled=True)]
    ppermute x2, waiting for transfers between devices: 16 us -> 3.04 us  [neighbours(): lax.ppermute(face[:count], axis, down)]
    ppermute x3, waiting for transfers between devices: 19.1 us -> 30.2 us  [x_slab_source(): lax.ppermute(piece, 'by', [(i, i ^ turn) for i in range(second_count)])]
    ppermute x7, starting transfers between devices: 19.5 us -> 13.4 us  [along_slabs(): lax.ppermute(to_next, EVERY, up)]
  transfers between devices with their start and end apart: 23 -> 23, of which waited for: 12 -> 13; matrix products, arithmetic and copies ran while one was open for 2% -> 1% of each run, Pallas kernels for 2% -> 0%
where the time goes in v4:
time: 430 us; the launch traced here: 429 us
  blocking collectives  202 us (47%)
  waiting for transfers between devices  87.3 us (20%)
  Pallas kernels  75.6 us (18%)
  starting transfers between devices  44.8 us (10%)
  local copies, waits for them, and re-layouts  14.3 us (3%)
    all_to_all x5, blocking collectives, exchange(): return lax.all_to_all(value, EVERY, split_axis=0, concat_axis=0, tiled=True)  166 us
    pallas_call x1, Pallas kernels, splat(): pl.pallas_call(splat_kernel, out_shape=tuple((jax.ShapeDtypeStruct(shape,...  34.7 us
    all_to_all x2, waiting for transfers between devices, exchange(): return lax.all_to_all(value, EVERY, split_axis=0, concat_axis=0, tiled=True)  33.6 us
    ppermute x3, waiting for transfers between devices, x_slab_source(): lax.ppermute(piece, 'by', [(i, i ^ turn) for i in range(second_count)])  30.2 us
    all_to_all x1, blocking collectives, relax(): return lax.all_to_all(sent, 'by', split_axis=0, concat_axis=0, tiled=True)  26.8 us
    pallas_call x5, Pallas kernels, later_phase(): pl.pallas_call(functools.partial(later_kernel, (devices, planes, rows, so...  18.1 us
    ppermute x7, waiting for transfers between devices, along_slabs(): lax.ppermute(to_previous, EVERY, down)  17.7 us
    all_to_all x2, starting transfers between devices, exchange(): return lax.all_to_all(value, EVERY, split_axis=0, concat_axis=0, tiled=True)  13.6 us
  transfers between devices with their start and end apart: 23, of which 13 were waited for; matrix products, arithmetic and copies ran while one was open for 1% of the time, Pallas kernels for 0%

profile of v4, /device:TPU:0, one launch (start us, length us, event | category | flops | bytes accessed | tf_op | source)
XLA Modules:
  0.0 428.7 jit_solution(14872226626101935128)
XLA Ops:
  3.6 7.0 %pack.1 = (f32[32,16,128]{2,1,0:T(8,128)S(1)}, f32[1,4096]{1,0:T(1,128)S(1)}) custom-call(s32[1,1]{1,0:T(1,128)S(6)} %copy.61.level_ref, s32[1,4096]{1,0:T(1,128)S(1)} %bitcast.94, s32[1,4096]{1,0:T(1,128)S(1)} %bitcast.96, f32[3,4096]{1,0:T(4,128)S(1)} %copy-done.15), custom_call_target="tpu_custom_call" | custom-call | tf_op jit(solution)/shard_map/pack/pallas_call | solution.py:81
  10.6 17.7 %all_to_all.89 = f32[32,16,128]{2,1,0:T(8,128)S(1)} all-to-all(f32[32,16,128]{2,1,0:T(8,128)S(1)} %get-tuple-element.19), channel_id=1, replica_groups=mesh['bx'=8,'by'=4] {'bx','by'}, dimensions={0} | all-to-all | bytes 524288 | tf_op jit(solution)/shard_map/all_to_all | solution.py:480
  28.6 34.7 %splat.1 = (f32[1024,256]{1,0:T(8,128)S(1)}, f32[128,256]{1,0:T(8,128)S(1)}, f32[32,256]{1,0:T(8,128)S(1)}) custom-call(s32[64]{0:T(128)S(1)} %compare_convert_fusion.used_ref, f32[256,128]{1,0:T(8,128)S(1)} %reshape.85.field_ref), custom_call_target="tpu_custom_call" | custom-call | tf_op jit(solution)/shard_map/splat/pallas_call | solution.py:199
  63.2 2.8 collective-permute-start
  70.0 3.0 collective-permute-done.3.y_after_ref
  74.4 6.0 %all-to-all-start.1 = ((f32[32,64,128]{2,1,0:T(8,128)}), f32[32,64,128]{2,1,0:T(8,128)S(1)}, u32[]{:S(2)}, u32[]{:S(2)}) async-start(f32[32,64,128]{2,1,0:T(8,128)} %bitcast.90), calls=%async_computation.1 | async-start | bytes 2097152 | tf_op jit(solution)/shard_map/all_to_all | solution.py:480
  82.0 24.6 %all-to-all-done.1 = f32[32,64,128]{2,1,0:T(8,128)S(1)} async-done(((f32[32,64,128]{2,1,0:T(8,128)}), f32[32,64,128]{2,1,0:T(8,128)S(1)}, u32[]{:S(2)}, u32[]{:S(2)}) %all-to-all-start.1) | async-done | bytes 1048608 | tf_op jit(solution)/shard_map/all_to_all | solution.py:480
  109.3 3.5 collective-permute-done.5.after_ref
  112.9 3.3 first_phase.1
  117.3 7.6 %all-to-all-start.2 = ((f32[32,128,128]{2,1,0:T(8,128)}), f32[32,128,128]{2,1,0:T(8,128)}, u32[]{:S(2)}, u32[]{:S(2)}) async-start(f32[32,128,128]{2,1,0:T(8,128)} %bitcast.14), calls=%async_computation.2 | async-start | bytes 4194304 | tf_op jit(solution)/shard_map/all_to_all | solution.py:480
  127.8 23.6 %collective-permute-done.7 = f32[4,64,256]{2,1,0:T(8,128)S(1)} collective-permute-done((f32[4,64,256]{2,1,0:T(8,128)}, f32[4,64,256]{2,1,0:T(8,128)S(1)}, u32[]{:S(2)}, u32[]{:S(2)}) %collective-permute-start.7) | collective-permute-done | bytes 262176 | tf_op jit(solution)/shard_map/ppermute | solution.py:493
  151.5 6.6 %collective-permute-done.8 = f32[4,64,256]{2,1,0:T(8,128)S(1)} collective-permute-done((f32[4,64,256]{2,1,0:T(8,128)S(1)}, f32[4,64,256]{2,1,0:T(8,128)S(1)}, u32[]{:S(2)}, u32[]{:S(2)}) %collective-permute-start.8) | collective-permute-done | bytes 262176 | tf_op jit(solution)/shard_map/ppermute | solution.py:493
  159.4 3.0 collective-permute-start.9
  165.0 9.0 %all-to-all-done.2 = f32[32,128,128]{2,1,0:T(8,128)} async-done(((f32[32,128,128]{2,1,0:T(8,128)}), f32[32,128,128]{2,1,0:T(8,128)}, u32[]{:S(2)}, u32[]{:S(2)}) %all-to-all-start.2) | async-done | bytes 2097184 | tf_op jit(solution)/shard_map/all_to_all | solution.py:480
  178.2 3.0 collective-permute-start.11
  182.7 4.3 %later_phase.5 = (f32[2048,128]{1,0:T(8,128)S(1)}, f32[10,256,128]{2,1,0:T(8,128)S(1)}) custom-call(f32[2]{0:T(128)S(1)} %add_convert_fusion.edge_ref, f32[4096,128]{1,0:T(8,128)} %bitcast.15.held_ref, f32[768,128]{1,0:T(8,128)S(1)} %collective-permute-done.11.before_ref, f32[768,128]{1,0:T(8,128)S(1)} %collective-permute-done.12.after_ref, ...), custom_call_target="tpu_custom_call" | custom-call | tf_op jit(solution)/shard_map/later_phase/pallas_call | solution.py:427
  187.1 40.9 %all_to_all.90 = f32[32,64,128]{2,1,0:T(8,128)S(1)} all-to-all(f32[32,64,128]{2,1,0:T(8,128)S(1)} %bitcast.91), channel_id=1, replica_groups=mesh['bx'=8,'by'=4] {'bx','by'}, dimensions={0} | all-to-all | bytes 2097152 | tf_op jit(solution)/shard_map/all_to_all | solution.py:480
  229.1 2.1 collective-permute-start.13
  233.7 2.6 collective-permute-done.14.after_ref
  238.1 3.9 later_phase.6
  242.1 38.4 %all_to_all.91 = f32[32,64,128]{2,1,0:T(8,128)S(1)} all-to-all(f32[32,64,128]{2,1,0:T(8,128)S(1)} %bitcast.88), channel_id=1, replica_groups=mesh['bx'=8,'by'=4] {'bx','by'}, dimensions={0} | all-to-all | bytes 2097152 | tf_op jit(solution)/shard_map/all_to_all | solution.py:480
  283.1 3.8 collective-permute-done.16.after_ref
  287.0 3.3 later_phase.7
  290.3 34.8 %all_to_all.92 = f32[32,64,128]{2,1,0:T(8,128)S(1)} all-to-all(f32[32,64,128]{2,1,0:T(8,128)S(1)} %bitcast.85), channel_id=1, replica_groups=mesh['bx'=8,'by'=4] {'bx','by'}, dimensions={0} | all-to-all | bytes 2097152 | tf_op jit(solution)/shard_map/all_to_all | solution.py:480
  327.7 3.8 collective-permute-done.18.after_ref
  331.5 3.3 later_phase.8
  334.8 34.8 %all_to_all.93 = f32[32,64,128]{2,1,0:T(8,128)S(1)} all-to-all(f32[32,64,128]{2,1,0:T(8,128)S(1)} %bitcast.87), channel_id=1, replica_groups=mesh['bx'=8,'by'=4] {'bx','by'}, dimensions={0} | all-to-all | bytes 2097152 | tf_op jit(solution)/shard_map/all_to_all | solution.py:480
  372.5 4.0 collective-permute-done.20.after_ref
  376.5 3.3 later_phase.9
  379.8 26.8 %all_to_all.94 = f32[16,64,256]{2,1,0:T(8,128)S(1)} all-to-all(f32[16,64,256]{2,1,0:T(8,128)S(1)} %bitcast.86), channel_id=1, replica_groups=mesh['bx'=8,'by'=4] {'by'}, dimensions={0} | all-to-all | bytes 2097152 | tf_op jit(solution)/shard_map/all_to_all | solution.py:555
  406.6 10.6 %sample.1 = f32[64,128]{1,0:T(8,128)S(1)} custom-call(f32[64,128]{1,0:T(8,128)S(1)} %copy-done.14, f32[1024,256]{1,0:T(8,128)S(1)} %bitcast.74), custom_call_target="tpu_custom_call" | custom-call | tf_op jit(solution)/shard_map/sample/pallas_call | solution.py:238
  417.2 8.9 %all_to_all.95 = f32[32,1,256]{2,1,0:T(1,128)S(1)} all-to-all(f32[32,1,256]{2,1,0:T(1,128)S(1)} %bitcast.92), channel_id=1, replica_groups=mesh['bx'=8,'by'=4] {'bx','by'}, dimensions={0} | all-to-all | bytes 65536 | tf_op jit(solution)/shard_map/all_to_all | solution.py:575
  (118 shorter events, 41.8 us)
Async XLA Ops:
  28.4 46.0 %copy-start.13 = (f32[64,128]{1,0:T(8,128)}, f32[64,128]{1,0:T(8,128)S(1)}, u32[]{:S(2)}) copy-start(f32[64,128]{1,0:T(8,128)S(1)} %slice.80.field_ref) | copy-start | bytes 98308
  63.2 9.8 %collective-permute-start = (f32[64,256]{1,0:T(8,128)S(1)}, f32[64,256]{1,0:T(8,128)S(1)}, u32[]{:S(2)}, u32[]{:S(2)}) collective-permute-start(f32[64,256]{1,0:T(8,128)S(1)} %get-tuple-element.57), channel_id=1, source_target_pairs={{0,4},{4,8},{8,12},{12,16},{16,20},{20,24},{24,28},{1,5},{5,9},{9,... | collective-permute-start | bytes 196616 | tf_op jit(solution)/shard_map/ppermute | solution.py:253
  66.0 7.0 %collective-permute-start.1 = (f32[64,256]{1,0:T(8,128)S(1)}, f32[64,256]{1,0:T(8,128)S(1)}, u32[]{:S(2)}, u32[]{:S(2)}) collective-permute-start(f32[64,256]{1,0:T(8,128)S(1)} %get-tuple-element.56), channel_id=1, source_target_pairs={{4,0},{8,4},{12,8},{16,12},{20,16},{24,20},{28,24},{5,1},{9,5},{13... | collective-permute-start | bytes 196616 | tf_op jit(solution)/shard_map/ppermute | solution.py:253
  67.4 2.6 collective-permute-start.2
  68.7 4.3 %collective-permute-start.3 = (f32[16,256]{1,0:T(8,128)S(1)}, f32[16,256]{1,0:T(8,128)S(1)}, u32[]{:S(2)}, u32[]{:S(2)}) collective-permute-start(f32[16,256]{1,0:T(8,128)S(1)} %get-tuple-element.58), channel_id=1, source_target_pairs={{1,0},{2,1},{3,2},{5,4},{6,5},{7,6},{9,8},{10,9},{11,10},{13,12},{... | collective-permute-start | bytes 49160 | tf_op jit(solution)/shard_map/ppermute | solution.py:253
  74.4 32.2 %all-to-all-start.1 = ((f32[32,64,128]{2,1,0:T(8,128)}), f32[32,64,128]{2,1,0:T(8,128)S(1)}, u32[]{:S(2)}, u32[]{:S(2)}) async-start(f32[32,64,128]{2,1,0:T(8,128)} %bitcast.90), calls=%async_computation.1 | async-start | bytes 2097152 | tf_op jit(solution)/shard_map/all_to_all | solution.py:480
  106.6 2.7 collective-permute-start.4
  107.9 4.9 %collective-permute-start.5 = (f32[256,128]{1,0:T(8,128)S(1)}, f32[256,128]{1,0:T(8,128)S(1)}, u32[]{:S(2)}, u32[]{:S(2)}) collective-permute-start(f32[256,128]{1,0:T(8,128)S(1)} %get-tuple-element.54), channel_id=1, source_target_pairs={{1,0},{2,1},{3,2},{4,3},{5,4},{6,5},{7,6},{8,7},{9,8},{10,9},{11,1... | collective-permute-start | bytes 393224 | tf_op jit(solution)/shard_map/ppermute | solution.py:476
  117.3 56.7 %all-to-all-start.2 = ((f32[32,128,128]{2,1,0:T(8,128)}), f32[32,128,128]{2,1,0:T(8,128)}, u32[]{:S(2)}, u32[]{:S(2)}) async-start(f32[32,128,128]{2,1,0:T(8,128)} %bitcast.14), calls=%async_computation.2 | async-start | bytes 4194304 | tf_op jit(solution)/shard_map/all_to_all | solution.py:480
  125.9 1.9 collective-permute-start.6
  126.1 25.4 %collective-permute-start.7 = (f32[4,64,256]{2,1,0:T(8,128)}, f32[4,64,256]{2,1,0:T(8,128)S(1)}, u32[]{:S(2)}, u32[]{:S(2)}) collective-permute-start(f32[4,64,256]{2,1,0:T(8,128)} %get-tuple-element.51), channel_id=1, source_target_pairs={{0,2},{1,3},{2,0},{3,1},{4,6},{5,7},{6,4},{7,5},{8,10},{9,11},{10,... | collective-permute-start | bytes 786440 | tf_op jit(solution)/shard_map/ppermute | solution.py:493
  127.8 30.3 %collective-permute-start.8 = (f32[4,64,256]{2,1,0:T(8,128)S(1)}, f32[4,64,256]{2,1,0:T(8,128)S(1)}, u32[]{:S(2)}, u32[]{:S(2)}) collective-permute-start(f32[4,64,256]{2,1,0:T(8,128)S(1)} %get-tuple-element.50), channel_id=1, source_target_pairs={{0,3},{1,2},{2,1},{3,0},{4,7},{5,6},{6,5},{7,4},{8,11},{9,10},{10,... | collective-permute-start | bytes 786440 | tf_op jit(solution)/shard_map/ppermute | solution.py:493
  158.1 4.4 %collective-permute-start.10 = (f32[1,256,256]{2,1,0:T(8,128)S(1)}, f32[1,256,256]{2,1,0:T(8,128)S(1)}, u32[]{:S(2)}, u32[]{:S(2)}) collective-permute-start(f32[1,256,256]{2,1,0:T(8,128)S(1)} %get-tuple-element.49), channel_id=1, source_target_pairs={{1,0},{2,1},{3,2},{4,3},{5,4},{6,5},{7,6},{8,7},{9,8},{10,9},{11,1... | collective-permute-start | bytes 786440 | tf_op jit(solution)/shard_map/ppermute | solution.py:476
  159.4 4.2 collective-permute-start.9
  176.1 5.2 %collective-permute-start.12 = (f32[768,128]{1,0:T(8,128)S(1)}, f32[768,128]{1,0:T(8,128)S(1)}, u32[]{:S(2)}, u32[]{:S(2)}) collective-permute-start(f32[768,128]{1,0:T(8,128)S(1)} %bitcast.104), channel_id=1, source_target_pairs={{1,0},{2,1},{3,2},{4,3},{5,4},{6,5},{7,6},{8,7},{9,8},{10,9},{11,1... | collective-permute-start | bytes 1179656 | tf_op jit(solution)/shard_map/ppermute | solution.py:476
  178.2 4.6 %collective-permute-start.11 = (f32[768,128]{1,0:T(8,128)}, f32[768,128]{1,0:T(8,128)S(1)}, u32[]{:S(2)}, u32[]{:S(2)}) collective-permute-start(f32[768,128]{1,0:T(8,128)} %bitcast.20), channel_id=1, source_target_pairs={{0,1},{1,2},{2,3},{3,4},{4,5},{5,6},{6,7},{7,8},{8,9},{9,10},{10,1... | collective-permute-start | bytes 1179656 | tf_op jit(solution)/shard_map/ppermute | solution.py:476
  187.1 42.0 %copy-start.8 = (f32[10,256,128]{2,1,0:T(8,128)}, f32[10,256,128]{2,1,0:T(8,128)S(1)}, u32[]{:S(2)}) copy-start(f32[10,256,128]{2,1,0:T(8,128)S(1)} %get-tuple-element.34.refs_0_) | copy-start | bytes 3932164
  229.1 4.5 %collective-permute-start.13 = (f32[1024,128]{1,0:T(8,128)}, f32[1024,128]{1,0:T(8,128)}, u32[]{:S(2)}, u32[]{:S(2)}) collective-permute-start(f32[1024,128]{1,0:T(8,128)} %bitcast.27), channel_id=1, source_target_pairs={{0,1},{1,2},{2,3},{3,4},{4,5},{5,6},{6,7},{7,8},{8,9},{9,10},{10,1... | collective-permute-start | bytes 1572872 | tf_op jit(solution)/shard_map/ppermute | solution.py:476
  231.2 5.0 %collective-permute-start.14 = (f32[1024,128]{1,0:T(8,128)}, f32[1024,128]{1,0:T(8,128)}, u32[]{:S(2)}, u32[]{:S(2)}) collective-permute-start(f32[1024,128]{1,0:T(8,128)} %bitcast.28), channel_id=1, source_target_pairs={{1,0},{2,1},{3,2},{4,3},{5,4},{6,5},{7,6},{8,7},{9,8},{10,9},{11,1... | collective-permute-start | bytes 1572872 | tf_op jit(solution)/shard_map/ppermute | solution.py:476
  242.1 44.9 %copy-start.2 = (f32[256,256]{1,0:T(8,128)S(1)}, f32[256,256]{1,0:T(8,128)}, u32[]{:S(2)}) copy-start(f32[256,256]{1,0:T(8,128)} %first_ref.11) | copy-start | bytes 786436
  242.1 44.9 %copy-start.7 = (f32[10,128,256]{2,1,0:T(8,128)S(1)}, f32[10,128,256]{2,1,0:T(8,128)}, u32[]{:S(2)}) copy-start(f32[10,128,256]{2,1,0:T(8,128)} %copy-done.6) | copy-start | bytes 3932164
  242.1 44.9 %copy-start.11 = (f32[128,128]{1,0:T(8,128)S(1)}, f32[128,128]{1,0:T(8,128)}, u32[]{:S(2)}) copy-start(f32[128,128]{1,0:T(8,128)} %second_ref.10) | copy-start | bytes 196612
  280.5 2.6 collective-permute-start.15
  281.8 5.1 %collective-permute-start.16 = (f32[512,128]{1,0:T(8,128)S(1)}, f32[512,128]{1,0:T(8,128)S(1)}, u32[]{:S(2)}, u32[]{:S(2)}) collective-permute-start(f32[512,128]{1,0:T(8,128)S(1)} %bitcast.105), channel_id=1, source_target_pairs={{1,0},{2,1},{3,2},{4,3},{5,4},{6,5},{7,6},{8,7},{9,8},{10,9},{11,1... | collective-permute-start | bytes 786440 | tf_op jit(solution)/shard_map/ppermute | solution.py:476
  290.2 41.3 %copy-start.5 = (f32[256,256]{1,0:T(8,128)S(1)}, f32[256,256]{1,0:T(8,128)}, u32[]{:S(2)}) copy-start(f32[256,256]{1,0:T(8,128)} %second_ref.11) | copy-start | bytes 786436
  290.2 41.2 %copy-start.9 = (f32[10,256,128]{2,1,0:T(8,128)S(1)}, f32[10,256,128]{2,1,0:T(8,128)}, u32[]{:S(2)}) copy-start(f32[10,256,128]{2,1,0:T(8,128)} %copy-done.8) | copy-start | bytes 3932164
  325.1 2.6 collective-permute-start.17
  326.4 5.1 %collective-permute-start.18 = (f32[512,128]{1,0:T(8,128)S(1)}, f32[512,128]{1,0:T(8,128)S(1)}, u32[]{:S(2)}, u32[]{:S(2)}) collective-permute-start(f32[512,128]{1,0:T(8,128)S(1)} %bitcast.106), channel_id=1, source_target_pairs={{1,0},{2,1},{3,2},{4,3},{5,4},{6,5},{7,6},{8,7},{9,8},{10,9},{11,1... | collective-permute-start | bytes 786440 | tf_op jit(solution)/shard_map/ppermute | solution.py:476
  369.7 2.8 collective-permute-start.19
  371.0 5.5 %collective-permute-start.20 = (f32[1024,128]{1,0:T(8,128)S(1)}, f32[1024,128]{1,0:T(8,128)S(1)}, u32[]{:S(2)}, u32[]{:S(2)}) collective-permute-start(f32[1024,128]{1,0:T(8,128)S(1)} %bitcast.102), channel_id=1, source_target_pairs={{1,0},{2,1},{3,2},{4,3},{5,4},{6,5},{7,6},{8,7},{9,8},{10,9},{11,1... | collective-permute-start | bytes 1572872 | tf_op jit(solution)/shard_map/ppermute | solution.py:476
  379.8 46.4 %copy-start.17 = (s32[4096,1]{0,1:T(1,128)S(1)}, s32[4096,1]{0,1:T(1,128)}, u32[]{:S(2)}) copy-start(s32[4096,1]{0,1:T(1,128)} %param.8) | copy-start | bytes 49156
  379.8 46.3 %copy-start.19 = (f32[1,4096]{1,0:T(1,128)S(1)}, f32[1,4096]{1,0:T(1,128)}, u32[]{:S(2)}) copy-start(f32[1,4096]{1,0:T(1,128)} %copy-done.18) | copy-start | bytes 49156
  (13 other events, 141.0 us)

commit v5 on v4

--- a/solution.py
+++ b/solution.py
@@ -139,78 +139,102 @@
     return jnp.where(index == at + 1, 0.5, 0.0) - jnp.where(index == at - 1, 0.5, 0.0)
 
 
-def splat_kernel(used_ref, field_ref, source_ref, x_face_ref, y_face_ref):
+GROUP = 4
+
+
+def product(rows, columns):
+    rows, columns = jnp.concatenate(rows, axis=1), jnp.concatenate(columns, axis=1)
+    return lax.dot_general(rows, columns, (((1,), (1,)), ((), ())), preferred_element_type=jnp.float32)
+
+
+def columns_of(field_ref, chunks, at, k, table):
+    parts = parts_of(field_ref[pl.ds(k * chunks + at, 1), :], 2)
+    return [times_row(table, spread(part.astype(jnp.float32))) for part in parts]
+
+
+def each_group(used_ref, field_ref, body):
     chunks = field_ref.shape[0] // 4
-    source_ref[...] = jnp.zeros_like(source_ref)
+
+    def step(at, carry):
+        members = [GROUP * at + g for g in range(GROUP)]
+        used = sum([used_ref[member] for member in members])
+
+        @pl.when(used > 0)
+        def _():
+            body(chunks, members)
+
+        return carry
+
+    lax.fori_loop(0, chunks // GROUP, step, 0)
+
+
+def face_kernel(used_ref, field_ref, x_face_ref, y_face_ref):
     x_face_ref[...] = jnp.zeros_like(x_face_ref)
     y_face_ref[...] = jnp.zeros_like(y_face_ref)
 
-    def product(rows, columns):
-        return lax.dot_general(rows, columns, (((1,), (1,)), ((), ())), preferred_element_type=jnp.float32)
-
-    group = 4
-
-    def tables(at):
-        x, y, z = places(field_ref[pl.ds(3 * chunks + at, 1), :])
-        y_hot = flags(rows_iota(CY, 128) == y).astype(jnp.bfloat16)
-        y_step = differenced(CY, 0, y).astype(jnp.bfloat16)
-        z_hot = flags(rows_iota(NZ, 128) == z).astype(jnp.bfloat16)
-        z_step = differenced(NZ, 0, z).astype(jnp.bfloat16)
-        columns = []
-        for k in range(3):
-            for part in parts_of(field_ref[pl.ds(k * chunks + at, 1), :], 2):
-                columns.append(times_row(z_step if k == 2 else z_hot, spread(part.astype(jnp.float32))))
-        steps = [spread(jnp.where(x == i - 1, 0.5, 0.0) - jnp.where(x == i + 1, 0.5, 0.0)) for i in range(-1, CX + 1)]
-        hots = [spread(flags(x == i)) for i in range(CX)]
-        along_x = jnp.concatenate([times_row(y_hot, steps[i + 1]) for i in range(CX)], axis=0)
-        along_y = jnp.concatenate([times_row(y_step, hots[i]) for i in range(CX)], axis=0)
-        along_z = jnp.concatenate([times_row(y_hot, hots[i]) for i in range(CX)], axis=0)
-        ends_x = jnp.concatenate([times_row(y_hot, steps[0]), times_row(y_hot, steps[CX + 1])], axis=0)
-        x_hot = flags(rows_iota(CX, 128) == x).astype(jnp.bfloat16)
-        ends_y = jnp.concatenate(
-            [x_hot * spread(jnp.where(y == 0, -0.5, 0.0)), x_hot * spread(jnp.where(y == CY - 1, 0.5, 0.0))], axis=0
-        )
-        return columns, along_x, along_y, along_z, ends_x, ends_y
-
-    def step(at, carry):
-        total = used_ref[group * at]
-        for g in range(1, group):
-            total += used_ref[group * at + g]
-        @pl.when(total > 0)
-        def _():
-            cols, rows, cx, ex, cy, ey = [], [], [], [], [], []
-            for g in range(group):
-                c, ax, ay, az, e_x, e_y = tables(group * at + g)
-                cols += c
-                rows += [ax, ax, ay, ay, az, az]
-                cx += c[:2]; ex += [e_x, e_x]; cy += c[2:4]; ey += [e_y, e_y]
-            cat = lambda v: jnp.concatenate(v, axis=1)
-            source_ref[...] += product(cat(rows), cat(cols))
-            x_face_ref[...] += product(cat(ex), cat(cx))
-            y_face_ref[...] += product(cat(ey), cat(cy))
-
-        return carry
-
-    lax.fori_loop(0, chunks // group, step, 0)
-
-
-def splat(field, used):
-    shapes = ((CX * CY, NZ), (2 * CY, NZ), (2 * CX, NZ))
+    def body(chunks, members):
+        x_rows, x_columns, y_rows, y_columns = [], [], [], []
+        for at in members:
+            x, y, z = places(field_ref[pl.ds(3 * chunks + at, 1), :])
+            x_hot = flags(rows_iota(CX, 128) == x).astype(jnp.bfloat16)
+            y_hot = flags(rows_iota(CY, 128) == y).astype(jnp.bfloat16)
+            z_hot = flags(rows_iota(NZ, 128) == z).astype(jnp.bfloat16)
+            ends = [jnp.where(x == 0, -0.5, 0.0), jnp.where(x == CX - 1, 0.5, 0.0)]
+            x_rows += [jnp.concatenate([times_row(y_hot, spread(end)) for end in ends], axis=0)] * 2
+            ends = [jnp.where(y == 0, -0.5, 0.0), jnp.where(y == CY - 1, 0.5, 0.0)]
+            y_rows += [jnp.concatenate([x_hot * spread(end) for end in ends], axis=0)] * 2
+            x_columns += columns_of(field_ref, chunks, at, 0, z_hot)
+            y_columns += columns_of(field_ref, chunks, at, 1, z_hot)
+        x_face_ref[...] += product(x_rows, x_columns)
+        y_face_ref[...] += product(y_rows, y_columns)
+
+    each_group(used_ref, field_ref, body)
+
+
+def splat_kernel(used_ref, field_ref, source_ref):
+    source_ref[...] = jnp.zeros_like(source_ref)
+
+    def body(chunks, members):
+        rows, columns = [], []
+        for at in members:
+            x, y, z = places(field_ref[pl.ds(3 * chunks + at, 1), :])
+            y_hot = flags(rows_iota(CY, 128) == y).astype(jnp.bfloat16)
+            y_step = differenced(CY, 0, y).astype(jnp.bfloat16)
+            z_hot = flags(rows_iota(NZ, 128) == z).astype(jnp.bfloat16)
+            z_step = differenced(NZ, 0, z).astype(jnp.bfloat16)
+            for k in range(3):
+                columns += columns_of(field_ref, chunks, at, k, z_step if k == 2 else z_hot)
+            steps = [spread(jnp.where(x == i - 1, 0.5, 0.0) - jnp.where(x == i + 1, 0.5, 0.0)) for i in range(CX)]
+            hots = [spread(flags(x == i)) for i in range(CX)]
+            for table, by_x in ((y_hot, steps), (y_step, hots), (y_hot, hots)):
+                rows += [jnp.concatenate([times_row(table, row) for row in by_x], axis=0)] * 2
+        source_ref[...] += product(rows, columns)
+
+    each_group(used_ref, field_ref, body)
+
+
+def splat(kernel, field, used, *rows):
     return pl.pallas_call(
-        splat_kernel,
-        out_shape=tuple(jax.ShapeDtypeStruct(shape, jnp.float32) for shape in shapes),
+        kernel,
+        out_shape=tuple(jax.ShapeDtypeStruct((count, NZ), jnp.float32) for count in rows),
         in_specs=[pl.BlockSpec(memory_space=pltpu.SMEM), pl.BlockSpec(memory_space=pltpu.VMEM)],
-        out_specs=tuple(whole_arrays(3)),
+        out_specs=tuple(whole_arrays(len(rows))),
         compiler_params=pltpu.CompilerParams(vmem_limit_bytes=32 << 20),
+        cost_estimate=pl.CostEstimate(flops=2 * 49152 * NZ * sum(rows), bytes_accessed=4 << 20, transcendentals=0),
         name="splat",
     )(used, field)
 
 
-def sample_kernel(field_ref, iterate_ref, out_ref, turned_ref):
+def sample_kernel(blocks, flip_ref, field_ref, held_ref, out_ref, iterate_ref, turned_ref):
     chunks = out_ref.shape[0]
     for i in range(CX * CY // 128):
         here = slice(128 * i, 128 * (i + 1))
-        block = iterate_ref[here, :].T
+        per_block = CX * CY // 128 // blocks
+        place = i // per_block
+        place = jnp.where(flip_ref[0] > 0, blocks - 1 - place, place) * per_block + i % per_block
+        block = held_ref[pl.ds(pl.multiple_of(place * 128, 128), 128), :]
+        iterate_ref[here, :] = block
+        block = block.T
         high, low = parts_of(block, 2)
         turned_ref[:NZ, here] = high
         turned_ref[NZ:, here] = low
@@ -234,16 +258,17 @@
     lax.fori_loop(0, chunks // 2, step, 0, unroll=4)
 
 
-def sample(cell_rows, iterate):
+def sample(cell_rows, held, flip, blocks):
+    shapes = (cell_rows.shape, held.shape)
     return pl.pallas_call(
-        sample_kernel,
-        out_shape=jax.ShapeDtypeStruct(cell_rows.shape, jnp.float32),
-        in_specs=whole_arrays(2),
-        out_specs=pl.BlockSpec(memory_space=pltpu.VMEM),
+        functools.partial(sample_kernel, blocks),
+        out_shape=tuple(jax.ShapeDtypeStruct(shape, jnp.float32) for shape in shapes),
+        in_specs=[pl.BlockSpec(memory_space=pltpu.SMEM)] + whole_arrays(2),
+        out_specs=tuple(whole_arrays(2)),
         scratch_shapes=[pltpu.VMEM((2 * NZ, CX * CY), jnp.bfloat16)],
         compiler_params=pltpu.CompilerParams(vmem_limit_bytes=32 << 20),
         name="sample",
-    )(cell_rows, iterate)
+    )(flip, cell_rows, held)
 
 
 def neighbours(face, axis, count):
@@ -277,20 +302,20 @@
     return source - (diagonal * middle - beside)
 
 
-def pieces(ref, sources, per_source, start, rows, bands, per_band):
+def pieces(ref, order, per_source, start, rows, bands, per_band):
     columns = []
     for band in range(bands):
-        starts = [i * per_source + band * per_band + start for i in range(sources)]
+        starts = [i * per_source + band * per_band + start for i in order]
         columns.append(jnp.concatenate([ref[at : at + rows, :] for at in starts], axis=0))
     return jnp.concatenate(columns, axis=1)
 
 
-def put(sent_ref, k, planes, targets, per_block, start, value):
+def put(sent_ref, k, planes, order, per_block, start, value):
     turned = value.T
-    per_target = turned.shape[0] // targets
-    for j in range(targets):
+    per_target = turned.shape[0] // len(order)
+    for j, target in enumerate(order):
         for band in range(turned.shape[1] // 128):
-            at = j * per_block + start + band * per_target * planes + k
+            at = target * per_block + start + band * per_target * planes + k
             part = turned[j * per_target : (j + 1) * per_target, band * 128 : (band + 1) * 128]
             sent_ref[pl.ds(at, per_target, stride=planes), :] = part
 
@@ -323,48 +348,52 @@
 
 
 def first_kernel(
-    grid, held_ref, before_ref, after_ref, diagonal_ref, first_ref, second_ref, sent_ref, source_ref, step_ref
+    grid, held_ref, diagonal_ref, first_ref, second_ref, sent_ref, source_ref, step_ref
 ):
     first_count, second_count, planes, per_target = grid
-    for k in range(planes):
-        source_ref[k + 1] = brick_planes(held_ref, first_count, second_count, planes, k)
-    source_ref[0] = brick_planes(before_ref, first_count, second_count, 1, 0)
-    source_ref[planes + 1] = brick_planes(after_ref, first_count, second_count, 1, 0)
+    for k in range(planes + 2):
+        source_ref[k] = brick_planes(held_ref, first_count, second_count, planes + 2, k)
     first = wide(first_ref[...])
     for k in range(planes + 2):
         step_ref[k] = jnp.dot(first, parts_in_rows(source_ref[k]), preferred_element_type=jnp.float32)
-    devices = first_count * second_count
-    block = sent_ref.shape[0] // devices
+    order = slab_order(first_count, second_count)
+    block = sent_ref.shape[0] // len(order)
 
     def emit(k, value):
-        put(sent_ref, k, planes, devices, block, 0, source_ref[k + 1])
-        put(sent_ref, k, planes, devices, block, block // 2, value)
+        put(sent_ref, k, planes, order, block, 0, source_ref[k + 1])
+        put(sent_ref, k, planes, order, block, block // 2, value)
 
     sweep_all(planes, step_ref, source_ref, diagonal_ref, second_ref, emit)
 
 
 def later_kernel(
-    shape, edge_ref, held_ref, before_ref, after_ref, diagonal_ref, first_ref, second_ref, *refs
+    shape, edge_ref, held_ref, pair_ref, other_ref, diagonal_ref, first_ref, second_ref, *refs
 ):
-    devices, planes, rows, with_source, last = shape
+    order, planes, rows, with_source, last = shape
+    devices = len(order)
+    even = edge_ref[2] > 0
     if with_source:
         sent_ref, source_ref, iterate_ref, step_ref = refs
     else:
         source_ref, sent_ref, iterate_ref, step_ref = refs
     bands = iterate_ref.shape[2] // 128
-    block, edge_block = held_ref.shape[0] // devices, before_ref.shape[0] // devices
+    block, edge_block = held_ref.shape[0] // devices, pair_ref.shape[0] // devices
     per_band = planes * rows
     edge_band = edge_block // bands
-    own = lambda k, start: pieces(held_ref, devices, block, start + k * rows, rows, bands, per_band)
-    edge = lambda ref, k: pieces(ref, devices, edge_block, k * rows, rows, bands, edge_band)
+    own = lambda k, start: pieces(held_ref, order, block, start + k * rows, rows, bands, per_band)
+
+    def edge(after, k):
+        pair, other = [pieces(ref, order, edge_block, k * rows, rows, bands, edge_band) for ref in (pair_ref, other_ref)]
+        return jnp.where(even, pair, other) if after else jnp.where(even, other, pair)
+
     if with_source:
         for k in range(planes):
             source_ref[k + 1] = own(k, 0)
-        source_ref[0] = edge(before_ref, 0)
-        source_ref[planes + 1] = edge(after_ref, 0)
+        source_ref[0] = edge(False, 0)
+        source_ref[planes + 1] = edge(True, 0)
     for k in range(2):
-        iterate_ref[k] = edge(before_ref, k + with_source)
-        iterate_ref[planes + 2 + k] = edge(after_ref, k + with_source)
+        iterate_ref[k] = edge(False, k + with_source)
+        iterate_ref[planes + 2 + k] = edge(True, k + with_source)
     for k in range(planes):
         iterate_ref[k + 2] = own(k, block // 2 if with_source else 0)
     first = wide(first_ref[...])
@@ -384,7 +413,7 @@
             for j in range(value.shape[0] // CY):
                 sent_ref[j, k] = value[j * CY : (j + 1) * CY, :]
         else:
-            put(sent_ref, k, planes, devices, sent_ref.shape[0] // devices, 0, value)
+            put(sent_ref, k, planes, order, sent_ref.shape[0] // devices, 0, value)
 
     sweep_all(planes, step_ref, source_ref, diagonal_ref, second_ref, emit)
 
@@ -394,7 +423,7 @@
 LIMIT = pltpu.CompilerParams(vmem_limit_bytes=48 << 20)
 
 
-def first_phase(grid, held, before, after, diagonal, first, second):
+def first_phase(grid, held, diagonal, first, second):
     rows, columns = diagonal.shape[1:]
     first_count, second_count, planes, per_target = grid
     return pl.pallas_call(
@@ -403,29 +432,29 @@
             jax.ShapeDtypeStruct((2 * columns * planes * rows // 128, 128), jnp.float32),
             jax.ShapeDtypeStruct((planes + 2, rows, columns), jnp.float32),
         ),
-        in_specs=[VMEM] * 6,
+        in_specs=[VMEM] * 4,
         out_specs=(VMEM, VMEM),
         scratch_shapes=[pltpu.VMEM((planes + 2, rows, columns), jnp.float32)],
         compiler_params=LIMIT,
         name="first_phase",
-    )(held, before, after, diagonal, first, second)
-
-
-def later_phase(devices, planes, rows, edges, held, before, after, diagonal, first, second, source=None, last=False):
+    )(held, diagonal, first, second)
+
+
+def later_phase(order, planes, rows, edges, held, pair, other, diagonal, first, second, source=None, last=False):
     columns = second.shape[1]
-    length = devices * rows
+    length = len(order) * rows
     if last:
         sent = (length // CY, planes, CY, columns)
     else:
         sent = (columns * planes * length // 128, 128)
     out = [jax.ShapeDtypeStruct(sent, jnp.float32)]
-    operands = [edges, held, before, after, diagonal, first, second]
+    operands = [edges, held, pair, other, diagonal, first, second]
     if source is None:
         out.append(jax.ShapeDtypeStruct((planes + 2, length, columns), jnp.float32))
     else:
         operands.append(source)
     return pl.pallas_call(
-        functools.partial(later_kernel, (devices, planes, rows, source is None, last)),
+        functools.partial(later_kernel, (order, planes, rows, source is None, last)),
         out_shape=tuple(out),
         in_specs=[SMEM] + [VMEM] * (len(operands) - 1),
         out_specs=tuple([VMEM] * len(out)),
@@ -438,7 +467,7 @@
     )(*operands)
 
 
-def join_kernel(source_ref, x_before_ref, x_after_ref, y_before_ref, y_after_ref, brick_ref, sent_ref):
+def join_kernel(order, source_ref, x_before_ref, x_after_ref, y_before_ref, y_after_ref, brick_ref, sent_ref, turned_ref):
     for i in range(CX):
         here = slice(i * CY, (i + 1) * CY)
         value = source_ref[here, :]
@@ -450,37 +479,58 @@
         value = value + jnp.where(row == 0, y_before_ref[i : i + 1, :], 0.0)
         brick_ref[here, :] = value + jnp.where(row == CY - 1, y_after_ref[i : i + 1, :], 0.0)
     half = CX // 2
+    planes = sent_ref.shape[1] // half
+    turned_ref[:8, :] = jnp.zeros((8, 2 * CY), jnp.float32)
+    turned_ref[NZ + 8 :, :] = jnp.zeros((8, 2 * CY), jnp.float32)
     for i in range(half):
         both = [brick_ref[j * CY : (j + 1) * CY, :] for j in (i, i + half)]
-        sent_ref[pl.ds(i, NZ, stride=half), :] = jnp.concatenate(both, axis=0).T
-
-
-def join(source, *faces):
+        turned_ref[8 : NZ + 8, :] = jnp.concatenate(both, axis=0).T
+        for j, target in enumerate(order):
+            first = 7 + j * (planes - 2)
+            sent_ref[target, pl.ds(i, planes, stride=half), :] = turned_ref[first : first + planes, :]
+
+
+def join(source, order, *faces):
     return pl.pallas_call(
-        join_kernel,
+        functools.partial(join_kernel, order),
         out_shape=(
             jax.ShapeDtypeStruct(source.shape, jnp.float32),
-            jax.ShapeDtypeStruct((NZ * CX // 2, 2 * CY), jnp.float32),
+            jax.ShapeDtypeStruct((len(order), (NZ // len(order) + 2) * CX // 2, 2 * CY), jnp.float32),
         ),
         in_specs=[VMEM] * 5,
         out_specs=(VMEM, VMEM),
+        scratch_shapes=[pltpu.VMEM((NZ + 16, 2 * CY), jnp.float32)],
         compiler_params=LIMIT,
         name="join",
     )(source, *faces)
 
 
-def along_slabs(to_next, to_previous):
-    devices = lax.axis_size(EVERY)
-    up = [(i, i + 1) for i in range(devices - 1)]
-    down = [(j, i) for i, j in up]
-    return lax.ppermute(to_next, EVERY, up), lax.ppermute(to_previous, EVERY, down)
+def slab_order(first_count, second_count):
+    order = []
+    for i in range(first_count):
+        row = [i * second_count + j for j in range(second_count)]
+        order += row if i % 2 == 0 else row[::-1]
+    return order
+
+
+def place_in_row(j):
+    return jnp.where(lax.axis_index("bx") % 2 == 0, j, lax.axis_size("by") - 1 - j)
+
+
+def beside(to_next, to_previous, even):
+    order = slab_order(lax.axis_size("bx"), lax.axis_size("by"))
+    got = []
+    for start, value in ((0, jnp.where(even, to_next, to_previous)), (1, jnp.where(even, to_previous, to_next))):
+        pairs = [(order[i], order[i + 1]) for i in range(start, len(order) - 1, 2)]
+        got.append(lax.ppermute(value, EVERY, pairs + [(j, i) for i, j in pairs]))
+    return got
 
 
 def exchange(value):
     return lax.all_to_all(value, EVERY, split_axis=0, concat_axis=0, tiled=True)
 
 
-def x_slab_source(brick):
+def x_slab_source(brick, even):
     second_count = lax.axis_size("by")
     mine = lax.axis_index("by")
     brick = brick.reshape(CX, CY, NZ)
@@ -488,18 +538,20 @@
     slab = jnp.zeros((thick, second_count * CY, NZ), jnp.float32)
     for turn in range(second_count):
         partner = mine ^ turn
-        piece = lax.dynamic_slice_in_dim(brick, partner * thick, thick, 0)
+        piece = lax.dynamic_slice_in_dim(brick, place_in_row(partner) * thick, thick, 0)
         if turn:
             piece = lax.ppermute(piece, "by", [(i, i ^ turn) for i in range(second_count)])
         slab = lax.dynamic_update_slice_in_dim(slab, piece, partner * CY, 1)
-    before, after = along_slabs(slab[-1:], slab[:1])
-    return jnp.concatenate([before, slab, after], axis=0)
+    pair, other = beside(slab[-1:], slab[:1], even)
+    return jnp.concatenate([jnp.where(even, other, pair), slab, jnp.where(even, pair, other)], axis=0)
 
 
 def relax(brick, sent, levels, rows_inverse, columns_inverse, depth_inverse):
     first_count, second_count = lax.axis_size("bx"), lax.axis_size("by")
     devices = first_count * second_count
-    me = lax.axis_index(EVERY)
+    order = slab_order(first_count, second_count)
+    me = lax.axis_index("bx") * second_count + place_in_row(lax.axis_index("by"))
+    even = me % 2 == 0
     nx, ny = first_count * CX, second_count * CY
     thick = (NZ // devices, ny // devices, nx // devices)
     diagonal = 6.0 + screen_base * (1.0 + levels.reshape(first_count, second_count))
@@ -510,15 +562,11 @@
         lax.dynamic_slice_in_dim(padded, me * thick[1], thick[1] + 2, 1).T[:, None, 1:-1],
         lax.dynamic_slice_in_dim(padded, me * thick[2], thick[2] + 2, 0)[:, 1:-1, None],
     )
-    edges = jnp.stack([me > 0, me < devices - 1]).astype(jnp.float32)
+    edges = jnp.stack([me > 0, me < devices - 1, even]).astype(jnp.float32)
     matrices = (rows_inverse, columns_inverse, depth_inverse)
     held, diagonals = lax.optimization_barrier((exchange(sent), diagonals))
-    blocks = held.reshape(devices, thick[0], CX // 2, 2 * CY)
-    before, after = along_slabs(
-        blocks[:, -1].reshape(-1, 2 * CY), blocks[:, 0].reshape(-1, 2 * CY)
-    )
     sent, z_source = first_phase(
-        (first_count, second_count, thick[0], thick[1]), held, before, after, diagonals[0], matrices[0], matrices[1]
+        (first_count, second_count, thick[0], thick[1]), held.reshape(-1, 2 * CY), diagonals[0], matrices[0], matrices[1]
     )
     sources = [z_source, None, None]
     for step in range(1, 3 * ITERS // 2):
@@ -526,22 +574,22 @@
         planes, rows = thick[at], thick[(at + 2) % 3]
         held = exchange(sent)
         if step == 1:
-            held, sources[2] = lax.optimization_barrier((held, x_slab_source(brick)))
+            held, sources[2] = lax.optimization_barrier((held, x_slab_source(brick, even)))
         bands = matrices[(2 * step + 1) % 3].shape[1] // 128
         blocks = held.reshape(devices, -1, bands, planes * rows, 128)
         to_next, to_previous = blocks[:, -1, :, -2 * rows :], blocks[:, -1, :, : 2 * rows]
         if sources[at] is None:
             to_next = jnp.concatenate([blocks[:, 0, :, -rows:], to_next], axis=2)
             to_previous = jnp.concatenate([blocks[:, 0, :, :rows], to_previous], axis=2)
-        before, after = along_slabs(to_next.reshape(-1, 128), to_previous.reshape(-1, 128))
+        pair, other = beside(to_next.reshape(-1, 128), to_previous.reshape(-1, 128), even)
         out = later_phase(
-            devices,
+            order,
             planes,
             rows,
             edges,
             held,
-            before,
-            after,
+            pair,
+            other,
             diagonals[at],
             matrices[2 * step % 3],
             matrices[(2 * step + 1) % 3],
@@ -566,15 +614,17 @@
     field = held[:, : 4 * capacity // 128].reshape(bricks, 4, capacity).transpose(1, 0, 2).reshape(4 * chunks, 128)
     cell_rows = field[3 * chunks :]
     used = (jnp.max(cell_rows, axis=1) > 0).astype(jnp.int32)
-    source, x_face, y_face = splat(field, used)
+    x_face, y_face = splat(face_kernel, field, used, 2 * CY, 2 * CX)
+    (source,) = splat(splat_kernel, field, used, CX * CY)
     x_before, x_after = neighbours(x_face, "bx", CY)
     y_before, y_after = neighbours(y_face, "by", CX)
-    brick, sent = join(source, x_before, x_after, y_before, y_after)
-    iterate = relax(brick, sent, levels, rows_inverse, columns_inverse, depth_inverse)
-    sampled = sample(cell_rows, iterate.reshape(CX * CY, NZ))
+    brick, sent = join(source, slab_order(lax.axis_size("bx"), lax.axis_size("by")), x_before, x_after, y_before, y_after)
+    held = relax(brick, sent, levels, rows_inverse, columns_inverse, depth_inverse)
+    flip = (lax.axis_index("bx") % 2).astype(jnp.int32).reshape(1)
+    sampled, iterate = sample(cell_rows, held.reshape(CX * CY, NZ), flip, lax.axis_size("by"))
     returned = lax.all_to_all(sampled.reshape(bricks, capacity), EVERY, split_axis=0, concat_axis=0, tiled=True)
     implicit = unpack(owners, rank, returned)
-    return (iterate, implicit)
+    return (iterate.reshape(CX, CY, NZ), implicit)
 
 
 def solution(mesh):

time: 430 us -> 405 us (0.942)
  starting transfers between devices: 44.8 us -> 29.2 us
  waiting for transfers between devices: 87.3 us -> 76.7 us
    ppermute x14 -> x12, waiting for transfers between devices: 20.4 us -> 5.32 us  [beside(): got.append(lax.ppermute(value, EVERY, pairs + [(j, i) for i, j in pairs]))]
    ppermute x14 -> x12, starting transfers between devices: 22.6 us -> 9.65 us  [beside(): got.append(lax.ppermute(value, EVERY, pairs + [(j, i) for i, j in pairs]))]
    all_to_all x2, waiting for transfers between devices: 33.6 us -> 41.1 us  [exchange(): return lax.all_to_all(value, EVERY, split_axis=0, concat_axis=0, tiled=True)]
    pallas_call x8 -> x9, Pallas kernels: 63.7 us -> 68.1 us  [the longest x2 38.2 us: splat(): pl.pallas_call(kernel, out_shape=tuple((jax.ShapeDtypeStruct((count, NZ),...]
  transfers between devices with their start and end apart: 23 -> 21, of which waited for: 13 -> 9; matrix products, arithmetic and copies ran while one was open for 1% -> 1% of each run, Pallas kernels for 0% -> 7%
where the time goes in v5:
time: 405 us; the launch traced here: 404 us
  blocking collectives  202 us (50%)
  Pallas kernels  78.4 us (19%)
  waiting for transfers between devices  76.7 us (19%)
  starting transfers between devices  29.2 us (7%)
  local copies, waits for them, and re-layouts  12.3 us (3%)
  other arithmetic  4.09 us (1%)
    all_to_all x5, blocking collectives, exchange(): return lax.all_to_all(value, EVERY, split_axis=0, concat_axis=0, tiled=True)  166 us
    all_to_all x2, waiting for transfers between devices, exchange(): return lax.all_to_all(value, EVERY, split_axis=0, concat_axis=0, tiled=True)  41.1 us
    pallas_call x2, Pallas kernels, splat(): pl.pallas_call(kernel, out_shape=tuple((jax.ShapeDtypeStruct((count, NZ),...  38.2 us
    ppermute x3, waiting for transfers between devices, x_slab_source(): lax.ppermute(piece, 'by', [(i, i ^ turn) for i in range(second_count)])  30.2 us
    all_to_all x1, blocking collectives, relax(): return lax.all_to_all(sent, 'by', split_axis=0, concat_axis=0, tiled=True)  25.7 us
    pallas_call x5, Pallas kernels, later_phase(): pl.pallas_call(functools.partial(later_kernel, (order, planes, rows, sour...  17.6 us
    all_to_all x2, starting transfers between devices, exchange(): return lax.all_to_all(value, EVERY, split_axis=0, concat_axis=0, tiled=True)  11 us
    pallas_call x1, Pallas kernels, sample(): pl.pallas_call(functools.partial(sample_kernel, blocks), out_shape=tuple(...  10.6 us
  transfers between devices with their start and end apart: 21, of which 9 were waited for; matrix products, arithmetic and copies ran while one was open for 1% of the time, Pallas kernels for 7%

profile of v5, /device:TPU:0, one launch (start us, length us, event | category | flops | bytes accessed | tf_op | source)
XLA Modules:
  0.0 404.2 jit_solution(1184328734289135677)
XLA Ops:
  3.6 7.0 %pack.1 = (f32[32,16,128]{2,1,0:T(8,128)S(1)}, f32[1,4096]{1,0:T(1,128)S(1)}) custom-call(s32[1,1]{1,0:T(1,128)S(6)} %copy.52.level_ref, s32[1,4096]{1,0:T(1,128)S(1)} %bitcast.85, s32[1,4096]{1,0:T(1,128)S(1)} %bitcast.88, f32[3,4096]{1,0:T(4,128)S(1)} %copy-done.15), custom_call_target="tpu_custom_call" | custom-call | tf_op jit(solution)/shard_map/pack/pallas_call | solution.py:81
  10.6 17.7 %all_to_all.82 = f32[32,16,128]{2,1,0:T(8,128)S(1)} all-to-all(f32[32,16,128]{2,1,0:T(8,128)S(1)} %get-tuple-element.20), channel_id=1, replica_groups=mesh['bx'=8,'by'=4] {'bx','by'}, dimensions={0} | all-to-all | bytes 524288 | tf_op jit(solution)/shard_map/all_to_all | solution.py:530
  28.6 8.1 %splat.3 = (f32[128,256]{1,0:T(8,128)S(1)}, f32[32,256]{1,0:T(8,128)S(1)}) custom-call(s32[64]{0:T(128)S(1)} %compare_convert_fusion.used_ref, f32[256,128]{1,0:T(8,128)S(1)} %reshape.106.field_ref), custom_call_target="tpu_custom_call" | custom-call | flops 4026531840 | bytes 4194304 | tf_op jit(solution)/shard_map/splat/pallas_call | solution.py:217
  36.7 2.8 collective-permute-start
  43.4 30.1 %splat.2.source_ref = f32[1024,256]{1,0:T(8,128)S(1)} custom-call(s32[64]{0:T(128)S(1)} %compare_convert_fusion.used_ref, f32[256,128]{1,0:T(8,128)S(1)} %reshape.106.field_ref), custom_call_target="tpu_custom_call" | custom-call | flops 25769803776 | bytes 4194304 | tf_op jit(solution)/shard_map/splat/pallas_call | solution.py:217
  73.6 1.7 join.1
  75.3 7.3 %all-to-all-start.1 = ((f32[32,80,128]{2,1,0:T(8,128)}), f32[32,80,128]{2,1,0:T(8,128)S(1)}, u32[]{:S(2)}, u32[]{:S(2)}) async-start(f32[32,80,128]{2,1,0:T(8,128)} %get-tuple-element.23), calls=%async_computation.1 | async-start | bytes 2621440 | tf_op jit(solution)/shard_map/all_to_all | solution.py:530
  84.3 30.5 %all-to-all-done.1 = f32[32,80,128]{2,1,0:T(8,128)S(1)} async-done(((f32[32,80,128]{2,1,0:T(8,128)}), f32[32,80,128]{2,1,0:T(8,128)S(1)}, u32[]{:S(2)}, u32[]{:S(2)}) %all-to-all-start.1) | async-done | bytes 1310752 | tf_op jit(solution)/shard_map/all_to_all | solution.py:530
  114.9 1.8 first_phase.1
  116.7 1.4 copy-done.6
  119.1 3.7 all-to-all-start.2
  124.0 1.7 collective-permute-start.5
  125.8 23.6 %collective-permute-done.5 = f32[4,64,256]{2,1,0:T(8,128)S(1)} collective-permute-done((f32[4,64,256]{2,1,0:T(8,128)}, f32[4,64,256]{2,1,0:T(8,128)S(1)}, u32[]{:S(2)}, u32[]{:S(2)}) %collective-permute-start.5) | collective-permute-done | bytes 262176 | tf_op jit(solution)/shard_map/ppermute | solution.py:543
  149.4 6.6 %collective-permute-done.6 = f32[4,64,256]{2,1,0:T(8,128)S(1)} collective-permute-done((f32[4,64,256]{2,1,0:T(8,128)S(1)}, f32[4,64,256]{2,1,0:T(8,128)S(1)}, u32[]{:S(2)}, u32[]{:S(2)}) %collective-permute-start.6) | collective-permute-done | bytes 262176 | tf_op jit(solution)/shard_map/ppermute | solution.py:543
  156.8 1.9 collective-permute-start.8
  159.9 1.4 pad_maximum_fusion.refs_0_
  161.2 10.6 %all-to-all-done.2 = f32[32,128,128]{2,1,0:T(8,128)} async-done(((f32[32,128,128]{2,1,0:T(8,128)}), f32[32,128,128]{2,1,0:T(8,128)}, u32[]{:S(2)}, u32[]{:S(2)}) %all-to-all-start.2) | async-done | bytes 2097184 | tf_op jit(solution)/shard_map/all_to_all | solution.py:530
  175.5 2.7 collective-permute-start.9
  179.5 4.2 %later_phase.5 = (f32[2048,128]{1,0:T(8,128)S(1)}, f32[10,256,128]{2,1,0:T(8,128)S(1)}) custom-call(f32[3]{0:T(128)S(1)} %add_convert_fusion.edge_ref, f32[4096,128]{1,0:T(8,128)} %bitcast.13.held_ref, f32[768,128]{1,0:T(8,128)S(1)} %collective-permute-done.9.pair_ref, f32[768,128]{1,0:T(8,128)S(1)} %collective-permute-done.10.other_ref, ...), custom_call_target="tpu_custom_call" | custom-call | tf_op jit(solution)/shard_map/later_phase/pallas_call | solution.py:456
  183.8 38.1 %all_to_all.83 = f32[32,64,128]{2,1,0:T(8,128)S(1)} all-to-all(f32[32,64,128]{2,1,0:T(8,128)S(1)} %bitcast.83), channel_id=1, replica_groups=mesh['bx'=8,'by'=4] {'bx','by'}, dimensions={0} | all-to-all | bytes 2097152 | tf_op jit(solution)/shard_map/all_to_all | solution.py:530
  223.0 1.5 collective-permute-start.12
  227.3 3.9 later_phase.6
  231.3 38.1 %all_to_all.84 = f32[32,64,128]{2,1,0:T(8,128)S(1)} all-to-all(f32[32,64,128]{2,1,0:T(8,128)S(1)} %bitcast.80), channel_id=1, replica_groups=mesh['bx'=8,'by'=4] {'bx','by'}, dimensions={0} | all-to-all | bytes 2097152 | tf_op jit(solution)/shard_map/all_to_all | solution.py:530
  271.0 3.2 later_phase.7
  274.2 35.9 %all_to_all.85 = f32[32,64,128]{2,1,0:T(8,128)S(1)} all-to-all(f32[32,64,128]{2,1,0:T(8,128)S(1)} %bitcast.76), channel_id=1, replica_groups=mesh['bx'=8,'by'=4] {'bx','by'}, dimensions={0} | all-to-all | bytes 2097152 | tf_op jit(solution)/shard_map/all_to_all | solution.py:530
  311.8 3.2 later_phase.8
  314.9 35.9 %all_to_all.86 = f32[32,64,128]{2,1,0:T(8,128)S(1)} all-to-all(f32[32,64,128]{2,1,0:T(8,128)S(1)} %bitcast.79), channel_id=1, replica_groups=mesh['bx'=8,'by'=4] {'bx','by'}, dimensions={0} | all-to-all | bytes 2097152 | tf_op jit(solution)/shard_map/all_to_all | solution.py:530
  352.9 3.1 later_phase.9
  356.1 25.7 %all_to_all.87 = f32[16,64,256]{2,1,0:T(8,128)S(1)} all-to-all(f32[16,64,256]{2,1,0:T(8,128)S(1)} %bitcast.78), channel_id=1, replica_groups=mesh['bx'=8,'by'=4] {'by'}, dimensions={0} | all-to-all | bytes 2097152 | tf_op jit(solution)/shard_map/all_to_all | solution.py:603
  381.8 10.6 %sample.1 = (f32[64,128]{1,0:T(8,128)S(1)}, f32[1024,256]{1,0:T(8,128)}) custom-call(s32[1]{0:T(128)} %bitcast.flip_ref, f32[64,128]{1,0:T(8,128)S(1)} %copy-done.14, f32[1024,256]{1,0:T(8,128)S(1)} %bitcast.77), custom_call_target="tpu_custom_call" | custom-call | tf_op jit(solution)/shard_map/sample/pallas_call | solution.py:263
  392.4 10.3 %all_to_all.88 = f32[32,1,256]{2,1,0:T(1,128)S(1)} all-to-all(f32[32,1,256]{2,1,0:T(1,128)S(1)} %bitcast.87), channel_id=1, replica_groups=mesh['bx'=8,'by'=4] {'bx','by'}, dimensions={0} | all-to-all | bytes 65536 | tf_op jit(solution)/shard_map/all_to_all | solution.py:625
  402.7 1.6 unpack.1
  (113 shorter events, 26.7 us)
Async XLA Ops:
  36.7 36.9 %collective-permute-start = (f32[64,256]{1,0:T(8,128)S(1)}, f32[64,256]{1,0:T(8,128)S(1)}, u32[]{:S(2)}, u32[]{:S(2)}) collective-permute-start(f32[64,256]{1,0:T(8,128)S(1)} %get-tuple-element.61), channel_id=1, source_target_pairs={{0,4},{4,8},{8,12},{12,16},{16,20},{20,24},{24,28},{1,5},{5,9},{9,... | collective-permute-start | bytes 196616 | tf_op jit(solution)/shard_map/ppermute | solution.py:278
  39.5 34.1 %collective-permute-start.1 = (f32[64,256]{1,0:T(8,128)S(1)}, f32[64,256]{1,0:T(8,128)S(1)}, u32[]{:S(2)}, u32[]{:S(2)}) collective-permute-start(f32[64,256]{1,0:T(8,128)S(1)} %get-tuple-element.60), channel_id=1, source_target_pairs={{4,0},{8,4},{12,8},{16,12},{20,16},{24,20},{28,24},{5,1},{9,5},{13... | collective-permute-start | bytes 196616 | tf_op jit(solution)/shard_map/ppermute | solution.py:278
  40.8 32.7 %collective-permute-start.2 = (f32[16,256]{1,0:T(8,128)S(1)}, f32[16,256]{1,0:T(8,128)S(1)}, u32[]{:S(2)}, u32[]{:S(2)}) collective-permute-start(f32[16,256]{1,0:T(8,128)S(1)} %get-tuple-element.63), channel_id=1, source_target_pairs={{0,1},{1,2},{2,3},{4,5},{5,6},{6,7},{8,9},{9,10},{10,11},{12,13},{... | collective-permute-start | bytes 49160 | tf_op jit(solution)/shard_map/ppermute | solution.py:278
  42.1 31.4 %collective-permute-start.3 = (f32[16,256]{1,0:T(8,128)S(1)}, f32[16,256]{1,0:T(8,128)S(1)}, u32[]{:S(2)}, u32[]{:S(2)}) collective-permute-start(f32[16,256]{1,0:T(8,128)S(1)} %get-tuple-element.62), channel_id=1, source_target_pairs={{1,0},{2,1},{3,2},{5,4},{6,5},{7,6},{9,8},{10,9},{11,10},{13,12},{... | collective-permute-start | bytes 49160 | tf_op jit(solution)/shard_map/ppermute | solution.py:278
  75.3 39.6 %copy-start = (f32[256,256]{1,0:T(8,128)S(1)}, f32[256,256]{1,0:T(8,128)}, u32[]{:S(2)}) copy-start(f32[256,256]{1,0:T(8,128)} %first_ref.11) | copy-start | bytes 786436
  75.3 39.6 %copy-start.11 = (f32[128,128]{1,0:T(8,128)S(1)}, f32[128,128]{1,0:T(8,128)}, u32[]{:S(2)}) copy-start(f32[128,128]{1,0:T(8,128)} %second_ref.10) | copy-start | bytes 196612
  75.3 39.5 %all-to-all-start.1 = ((f32[32,80,128]{2,1,0:T(8,128)}), f32[32,80,128]{2,1,0:T(8,128)S(1)}, u32[]{:S(2)}, u32[]{:S(2)}) async-start(f32[32,80,128]{2,1,0:T(8,128)} %get-tuple-element.23), calls=%async_computation.1 | async-start | bytes 2621440 | tf_op jit(solution)/shard_map/all_to_all | solution.py:530
  119.1 52.7 %all-to-all-start.2 = ((f32[32,128,128]{2,1,0:T(8,128)}), f32[32,128,128]{2,1,0:T(8,128)}, u32[]{:S(2)}, u32[]{:S(2)}) async-start(f32[32,128,128]{2,1,0:T(8,128)} %bitcast.81), calls=%async_computation.2 | async-start | bytes 4194304 | tf_op jit(solution)/shard_map/all_to_all | solution.py:530
  123.9 1.9 collective-permute-start.4
  124.0 25.3 %collective-permute-start.5 = (f32[4,64,256]{2,1,0:T(8,128)}, f32[4,64,256]{2,1,0:T(8,128)S(1)}, u32[]{:S(2)}, u32[]{:S(2)}) collective-permute-start(f32[4,64,256]{2,1,0:T(8,128)} %get-tuple-element.53), channel_id=1, source_target_pairs={{0,2},{1,3},{2,0},{3,1},{4,6},{5,7},{6,4},{7,5},{8,10},{9,11},{10,... | collective-permute-start | bytes 786440 | tf_op jit(solution)/shard_map/ppermute | solution.py:543
  125.7 30.3 %collective-permute-start.6 = (f32[4,64,256]{2,1,0:T(8,128)S(1)}, f32[4,64,256]{2,1,0:T(8,128)S(1)}, u32[]{:S(2)}, u32[]{:S(2)}) collective-permute-start(f32[4,64,256]{2,1,0:T(8,128)S(1)} %get-tuple-element.52), channel_id=1, source_target_pairs={{0,3},{1,2},{2,1},{3,0},{4,7},{5,6},{6,5},{7,4},{8,11},{9,10},{10,... | collective-permute-start | bytes 786440 | tf_op jit(solution)/shard_map/ppermute | solution.py:543
  156.1 2.6 collective-permute-start.7
  156.8 3.1 collective-permute-start.8
  174.8 3.5 collective-permute-start.10
  175.5 4.0 collective-permute-start.9
  183.7 39.2 %copy-start.9 = (f32[10,256,128]{2,1,0:T(8,128)}, f32[10,256,128]{2,1,0:T(8,128)S(1)}, u32[]{:S(2)}) copy-start(f32[10,256,128]{2,1,0:T(8,128)S(1)} %get-tuple-element.34.refs_0_) | copy-start | bytes 3932164
  223.0 2.4 collective-permute-start.11
  223.0 2.5 collective-permute-start.12
  231.2 39.8 %copy-start.2 = (f32[256,256]{1,0:T(8,128)S(1)}, f32[256,256]{1,0:T(8,128)}, u32[]{:S(2)}) copy-start(f32[256,256]{1,0:T(8,128)} %first_ref.11) | copy-start | bytes 786436
  231.2 39.7 %copy-start.8 = (f32[10,128,256]{2,1,0:T(8,128)S(1)}, f32[10,128,256]{2,1,0:T(8,128)}, u32[]{:S(2)}) copy-start(f32[10,128,256]{2,1,0:T(8,128)} %copy-done.7) | copy-start | bytes 3932164
  231.3 39.7 %copy-start.12 = (f32[128,128]{1,0:T(8,128)S(1)}, f32[128,128]{1,0:T(8,128)}, u32[]{:S(2)}) copy-start(f32[128,128]{1,0:T(8,128)} %second_ref.10) | copy-start | bytes 196612
  269.4 1.6 collective-permute-start.13
  269.5 1.5 collective-permute-start.14
  274.2 37.5 %copy-start.5 = (f32[256,256]{1,0:T(8,128)S(1)}, f32[256,256]{1,0:T(8,128)}, u32[]{:S(2)}) copy-start(f32[256,256]{1,0:T(8,128)} %second_ref.11) | copy-start | bytes 786436
  274.2 37.5 %copy-start.10 = (f32[10,256,128]{2,1,0:T(8,128)S(1)}, f32[10,256,128]{2,1,0:T(8,128)}, u32[]{:S(2)}) copy-start(f32[10,256,128]{2,1,0:T(8,128)} %copy-done.9) | copy-start | bytes 3932164
  310.1 1.6 collective-permute-start.15
  310.2 1.5 collective-permute-start.16
  351.0 2.0 collective-permute-start.17
  351.0 1.9 collective-permute-start.18
  356.0 25.8 %copy-start.14 = (f32[64,128]{1,0:T(8,128)S(1)}, f32[64,128]{1,0:T(8,128)}, u32[]{:S(2)}) copy-start(f32[64,128]{1,0:T(8,128)} %copy-done.13) | copy-start | bytes 98308
  356.0 46.6 %copy-start.17 = (s32[4096,1]{0,1:T(1,128)S(1)}, s32[4096,1]{0,1:T(1,128)}, u32[]{:S(2)}) copy-start(s32[4096,1]{0,1:T(1,128)} %param.8) | copy-start | bytes 49156
  356.1 46.6 %copy-start.19 = (f32[1,4096]{1,0:T(1,128)S(1)}, f32[1,4096]{1,0:T(1,128)}, u32[]{:S(2)}) copy-start(f32[1,4096]{1,0:T(1,128)} %copy-done.18) | copy-start | bytes 49156
  (11 other events, 44.1 us)

commit v6 on v5

--- a/solution.py
+++ b/solution.py
@@ -38,20 +38,50 @@
     return [pl.BlockSpec(memory_space=pltpu.VMEM)] * count
 
 
-def pack_kernel(level_ref, owner_ref, cell_ref, normal_ref, send_ref, rank_ref, total_ref):
+def product(rows, columns):
+    rows, columns = jnp.concatenate(rows, axis=1), jnp.concatenate(columns, axis=1)
+    return lax.dot_general(rows, columns, (((1,), (1,)), ((), ())), preferred_element_type=jnp.float32)
+
+
+def pack_kernel(level_ref, owner_ref, cell_ref, normal_ref, send_ref, slot_ref, total_ref):
     bricks, capacity = send_ref.shape[0], total_ref.shape[1]
     points = owner_ref.shape[1]
     block = 256
-    before = flags(rows_iota(block, block) < lax.broadcasted_iota(jnp.int32, (block, block), 1)).astype(jnp.bfloat16)
+    earlier = rows_iota(block, block) < lax.broadcasted_iota(jnp.int32, (block, block), 1)
     total_ref[...] = jnp.zeros_like(total_ref)
 
-    def step(at, seen):
+    def names(at):
         here = pl.ds(pl.multiple_of(at * block, block), block)
         named = flags(rows_iota(bricks, block) == owner_ref[:, here])
-        inside = jnp.dot(named.astype(jnp.bfloat16), before, preferred_element_type=jnp.float32)
-        rank = jnp.sum(named * (inside + seen), axis=0, keepdims=True)
-        rank_ref[:, here] = rank
-        slot = flags(rows_iota(capacity, block).astype(jnp.float32) == rank).astype(jnp.bfloat16)
+        x = cell_ref[:, here] >> 14
+        return here, named, x, flags(rows_iota(CX, block) == x)
+
+    def tally(named, x_hot):
+        return product([named.astype(jnp.bfloat16)], [x_hot.astype(jnp.bfloat16)])
+
+    def count(at, counts):
+        _, named, _, x_hot = names(at)
+        return counts + tally(named, x_hot)
+
+    counts = lax.fori_loop(0, points // block, count, jnp.zeros((bricks, CX), jnp.float32), unroll=4)
+    per_brick = jnp.sum(counts, axis=1, keepdims=True)
+
+    def step(at, seen):
+        here, named, x, x_hot = names(at)
+        x_less = flags(rows_iota(CX, block) < x)
+        ahead = jnp.dot(
+            jnp.concatenate([counts, seen], axis=1).astype(jnp.bfloat16),
+            jnp.concatenate([x_less, x_hot], axis=0).astype(jnp.bfloat16),
+            preferred_element_type=jnp.float32,
+        )
+        key = (owner_ref[:, here] * CX + x).astype(jnp.float32)
+        column = jnp.broadcast_to(key, (128, block)).T
+        same = (jnp.concatenate([column] * (block // 128), axis=1) == key) & earlier
+        rank = jnp.sum(named * ahead, axis=0, keepdims=True) + jnp.sum(flags(same), axis=0, keepdims=True)
+        used = jnp.sum(named * per_brick, axis=0, keepdims=True)
+        place = jnp.floor((rank * capacity + 0.5) / used)
+        slot_ref[:, here] = place
+        slot = flags(rows_iota(capacity, block).astype(jnp.float32) == place).astype(jnp.bfloat16)
         values = []
         for k in range(3):
             values += [part.astype(jnp.float32) for part in parts_of(normal_ref[k : k + 1, here], 3)]
@@ -59,12 +89,10 @@
         for shift in (16, 8, 0):
             values.append(((cell >> shift) & 255).astype(jnp.float32))
         rows = jnp.concatenate([(named * value).astype(jnp.bfloat16) for value in values], axis=0)
-        total_ref[...] += lax.dot_general(
-            rows, slot, (((1,), (1,)), ((), ())), preferred_element_type=jnp.float32
-        )
-        return seen + jnp.sum(named, axis=1, keepdims=True)
-
-    lax.fori_loop(0, points // block, step, jnp.zeros((bricks, 1), jnp.float32))
+        total_ref[...] += product([rows], [slot])
+        return seen + tally(named, x_hot)
+
+    lax.fori_loop(0, points // block, step, jnp.zeros((bricks, CX), jnp.float32), unroll=2)
     part = lambda i: total_ref[i * bricks : (i + 1) * bricks, :]
     fields = [part(3 * k) + part(3 * k + 1) + part(3 * k + 2) for k in range(3)]
     fields.append(part(9) * 65536.0 + part(10) * 256.0 + part(11))
@@ -134,99 +162,127 @@
     return cell >> 14, (cell >> 8) & (CY - 1), cell & (NZ - 1)
 
 
-def differenced(rows, first, at):
-    index = rows_iota(rows, 128) + first
-    return jnp.where(index == at + 1, 0.5, 0.0) - jnp.where(index == at - 1, 0.5, 0.0)
-
-
 GROUP = 4
-
-
-def product(rows, columns):
-    rows, columns = jnp.concatenate(rows, axis=1), jnp.concatenate(columns, axis=1)
-    return lax.dot_general(rows, columns, (((1,), (1,)), ((), ())), preferred_element_type=jnp.float32)
-
-
-def columns_of(field_ref, chunks, at, k, table):
-    parts = parts_of(field_ref[pl.ds(k * chunks + at, 1), :], 2)
-    return [times_row(table, spread(part.astype(jnp.float32))) for part in parts]
-
-
-def each_group(used_ref, field_ref, body):
+WINDOW = 6
+
+
+def units_turned(tile):
+    row = rows_iota(8, 128)
+    unit = lax.broadcasted_iota(jnp.int32, (8, 128), 1) // 16
+    for bit in (4, 2, 1):
+        low, high = (row & bit) == 0, (unit & bit) != 0
+        from_below = pltpu.roll(pltpu.roll(tile, 8 - bit, 0), 16 * bit, 1)
+        from_above = pltpu.roll(pltpu.roll(tile, bit, 0), 128 - 16 * bit, 1)
+        tile = jnp.where(low & high, from_below, jnp.where(low | high, tile, from_above))
+    return tile
+
+
+def regroup_kernel(held_ref, field_ref):
+    bricks = held_ref.shape[0]
     chunks = field_ref.shape[0] // 4
-
-    def step(at, carry):
-        members = [GROUP * at + g for g in range(GROUP)]
-        used = sum([used_ref[member] for member in members])
-
-        @pl.when(used > 0)
-        def _():
-            body(chunks, members)
-
+    halves, blocks = chunks // bricks, bricks // 8
+    for k in range(4):
+        for half in range(halves):
+            for block in range(blocks):
+                tile = held_ref[8 * block : 8 * (block + 1), halves * k + half, :]
+                here = pl.ds(k * chunks + 8 * half * blocks + block, 8, stride=blocks)
+                field_ref[here, :] = units_turned(tile)
+
+
+def regroup(held, bricks, capacity):
+    chunks = bricks * capacity // 128
+    if capacity % 128 or bricks % 8:
+        field = held[:, : 4 * capacity // 128].reshape(bricks, 4, capacity)
+        return field.transpose(1, 0, 2).reshape(4 * chunks, 128)
+    return pl.pallas_call(
+        regroup_kernel,
+        out_shape=jax.ShapeDtypeStruct((4 * chunks, 128), jnp.float32),
+        in_specs=whole_arrays(1),
+        out_specs=pl.BlockSpec(memory_space=pltpu.VMEM),
+        name="regroup",
+    )(held)
+
+
+def splat_kernel(
+    bound_ref, even_ref, field_ref, source_ref, x_pair_ref, x_other_ref, y_pair_ref, y_other_ref, sum_ref, column_ref
+):
+    chunks = field_ref.shape[0] // 4
+    points = 128 * GROUP
+    sum_ref[...] = jnp.zeros_like(sum_ref)
+
+    def group(at, carry):
+        first, last = bound_ref[at, 0], bound_ref[at, 1]
+        cells = []
+        for member in range(GROUP):
+            chunk = GROUP * at + member
+            x, y, z = places(field_ref[pl.ds(3 * chunks + chunk, 1), :])
+            z_hot = flags(rows_iota(NZ, 128) == z).astype(jnp.bfloat16)
+            for k in range(3):
+                parts = parts_of(field_ref[pl.ds(k * chunks + chunk, 1), :], 2)
+                for j, part in enumerate(parts):
+                    here = slice(j * points + 128 * member, j * points + 128 * (member + 1))
+                    column_ref[k * NZ : (k + 1) * NZ, here] = times_row(z_hot, spread(part.astype(jnp.float32)))
+            cells.append((x, flags(rows_iota(CY, 128) == y).astype(jnp.bfloat16)))
+
+        def window(turn, carry):
+            start = first + turn * WINDOW
+            rows = []
+            for x, y_hot in cells:
+                hots = [spread(flags(x == start + i)) for i in range(WINDOW)]
+                rows.append(jnp.concatenate([times_row(y_hot, hot) for hot in hots], axis=0))
+            here = pl.ds(pl.multiple_of(start * CY, CY), WINDOW * CY)
+            sum_ref[here, :] += product(rows * 2, [column_ref[...]])
+            return carry
+
+        window(0, 0)
+        lax.fori_loop(1, jnp.maximum(last - first, 0) // WINDOW + 1, window, 0)
         return carry
 
-    lax.fori_loop(0, chunks // GROUP, step, 0)
-
-
-def face_kernel(used_ref, field_ref, x_face_ref, y_face_ref):
-    x_face_ref[...] = jnp.zeros_like(x_face_ref)
-    y_face_ref[...] = jnp.zeros_like(y_face_ref)
-
-    def body(chunks, members):
-        x_rows, x_columns, y_rows, y_columns = [], [], [], []
-        for at in members:
-            x, y, z = places(field_ref[pl.ds(3 * chunks + at, 1), :])
-            x_hot = flags(rows_iota(CX, 128) == x).astype(jnp.bfloat16)
-            y_hot = flags(rows_iota(CY, 128) == y).astype(jnp.bfloat16)
-            z_hot = flags(rows_iota(NZ, 128) == z).astype(jnp.bfloat16)
-            ends = [jnp.where(x == 0, -0.5, 0.0), jnp.where(x == CX - 1, 0.5, 0.0)]
-            x_rows += [jnp.concatenate([times_row(y_hot, spread(end)) for end in ends], axis=0)] * 2
-            ends = [jnp.where(y == 0, -0.5, 0.0), jnp.where(y == CY - 1, 0.5, 0.0)]
-            y_rows += [jnp.concatenate([x_hot * spread(end) for end in ends], axis=0)] * 2
-            x_columns += columns_of(field_ref, chunks, at, 0, z_hot)
-            y_columns += columns_of(field_ref, chunks, at, 1, z_hot)
-        x_face_ref[...] += product(x_rows, x_columns)
-        y_face_ref[...] += product(y_rows, y_columns)
-
-    each_group(used_ref, field_ref, body)
-
-
-def splat_kernel(used_ref, field_ref, source_ref):
-    source_ref[...] = jnp.zeros_like(source_ref)
-
-    def body(chunks, members):
-        rows, columns = [], []
-        for at in members:
-            x, y, z = places(field_ref[pl.ds(3 * chunks + at, 1), :])
-            y_hot = flags(rows_iota(CY, 128) == y).astype(jnp.bfloat16)
-            y_step = differenced(CY, 0, y).astype(jnp.bfloat16)
-            z_hot = flags(rows_iota(NZ, 128) == z).astype(jnp.bfloat16)
-            z_step = differenced(NZ, 0, z).astype(jnp.bfloat16)
-            for k in range(3):
-                columns += columns_of(field_ref, chunks, at, k, z_step if k == 2 else z_hot)
-            steps = [spread(jnp.where(x == i - 1, 0.5, 0.0) - jnp.where(x == i + 1, 0.5, 0.0)) for i in range(CX)]
-            hots = [spread(flags(x == i)) for i in range(CX)]
-            for table, by_x in ((y_hot, steps), (y_step, hots), (y_hot, hots)):
-                rows += [jnp.concatenate([times_row(table, row) for row in by_x], axis=0)] * 2
-        source_ref[...] += product(rows, columns)
-
-    each_group(used_ref, field_ref, body)
-
-
-def splat(kernel, field, used, *rows):
+    lax.fori_loop(0, chunks // GROUP, group, 0)
+    row = rows_iota(CY, NZ)
+    lane = lax.broadcasted_iota(jnp.int32, (CY, NZ), 1)
+
+    def part(i, k):
+        return sum_ref[i * CY : (i + 1) * CY, k * NZ : (k + 1) * NZ]
+
+    for i in range(CX):
+        y_part, z_part = part(i, 1), part(i, 2)
+        value = jnp.where(row == CY - 1, 0.0, pltpu.roll(y_part, CY - 1, 0)) - jnp.where(row == 0, 0.0, pltpu.roll(y_part, 1, 0))
+        value += jnp.where(lane == NZ - 1, 0.0, pltpu.roll(z_part, NZ - 1, 1)) - jnp.where(lane == 0, 0.0, pltpu.roll(z_part, 1, 1))
+        if i < CX - 1:
+            value += part(i + 1, 0)
+        if i > 0:
+            value -= part(i - 1, 0)
+        source_ref[i * CY : (i + 1) * CY, :] = -0.5 * value
+    before, after = -0.5 * part(0, 0), 0.5 * part(CX - 1, 0)
+    x_pair_ref[...] = jnp.where(even_ref[0] > 0, after, before)
+    x_other_ref[...] = jnp.where(even_ref[0] > 0, before, after)
+    y_part = slice(NZ, 2 * NZ)
+    before = -0.5 * jnp.concatenate([sum_ref[i * CY : i * CY + 1, y_part] for i in range(CX)], axis=0)
+    after = 0.5 * jnp.concatenate([sum_ref[(i + 1) * CY - 1 : (i + 1) * CY, y_part] for i in range(CX)], axis=0)
+    y_pair_ref[...] = jnp.where(even_ref[1] > 0, after, before)
+    y_other_ref[...] = jnp.where(even_ref[1] > 0, before, after)
+
+
+def splat(field, bounds, even):
+    shapes = [(CX * CY, NZ), (CY, NZ), (CY, NZ), (CX, NZ), (CX, NZ)]
     return pl.pallas_call(
-        kernel,
-        out_shape=tuple(jax.ShapeDtypeStruct((count, NZ), jnp.float32) for count in rows),
-        in_specs=[pl.BlockSpec(memory_space=pltpu.SMEM), pl.BlockSpec(memory_space=pltpu.VMEM)],
-        out_specs=tuple(whole_arrays(len(rows))),
+        splat_kernel,
+        out_shape=tuple(jax.ShapeDtypeStruct(shape, jnp.float32) for shape in shapes),
+        in_specs=[pl.BlockSpec(memory_space=pltpu.SMEM)] * 2 + whole_arrays(1),
+        out_specs=tuple(whole_arrays(5)),
+        scratch_shapes=[
+            pltpu.VMEM(((CX + WINDOW) * CY, 3 * NZ), jnp.float32),
+            pltpu.VMEM((3 * NZ, 2 * GROUP * 128), jnp.bfloat16),
+        ],
         compiler_params=pltpu.CompilerParams(vmem_limit_bytes=32 << 20),
-        cost_estimate=pl.CostEstimate(flops=2 * 49152 * NZ * sum(rows), bytes_accessed=4 << 20, transcendentals=0),
         name="splat",
-    )(used, field)
-
-
-def sample_kernel(blocks, flip_ref, field_ref, held_ref, out_ref, iterate_ref, turned_ref):
-    chunks = out_ref.shape[0]
+    )(bounds, even, field)
+
+
+def sample_kernel(blocks, flip_ref, bound_ref, field_ref, held_ref, out_ref, iterate_ref, turned_ref, sampled_ref):
+    chunks = field_ref.shape[0]
+    turned_ref[:, CX * CY :] = jnp.zeros((2 * NZ, turned_ref.shape[1] - CX * CY), jnp.bfloat16)
     for i in range(CX * CY // 128):
         here = slice(128 * i, 128 * (i + 1))
         per_block = CX * CY // 128 // blocks
@@ -234,48 +290,70 @@
         place = jnp.where(flip_ref[0] > 0, blocks - 1 - place, place) * per_block + i % per_block
         block = held_ref[pl.ds(pl.multiple_of(place * 128, 128), 128), :]
         iterate_ref[here, :] = block
-        block = block.T
-        high, low = parts_of(block, 2)
+        high, low = parts_of(block.T, 2)
         turned_ref[:NZ, here] = high
         turned_ref[NZ:, here] = low
-
-    def step(at, carry):
-        tables, heights = [], []
-        for half in range(2):
-            x, y, z = places(field_ref[pl.ds(2 * at + half, 1), :])
-            y_hot = flags(rows_iota(CY, 128) == y).astype(jnp.bfloat16)
-            hots = [spread(flags(x == i)) for i in range(CX)]
-            tables.append(jnp.concatenate([times_row(y_hot, hots[i]) for i in range(CX)], axis=0))
-            heights.append(z)
-        found = jnp.dot(turned_ref[...], jnp.concatenate(tables, axis=1), preferred_element_type=jnp.float32)
-        found = found[:NZ] + found[NZ:]
-        level = rows_iota(NZ, 256) == jnp.concatenate(heights, axis=1)
-        row = jnp.sum(jnp.where(level, found, 0.0), axis=0, keepdims=True)
-        out_ref[pl.ds(2 * at, 1), :] = row[:, :128]
-        out_ref[pl.ds(2 * at + 1, 1), :] = row[:, 128:]
+    width = 8
+
+    def group(at, carry):
+        first, last = bound_ref[at, 0] // 2 * 2, bound_ref[at, 1]
+        cells = [places(field_ref[pl.ds(GROUP * at + member, 1), :]) for member in range(GROUP)]
+        level = rows_iota(NZ, 128 * GROUP) == jnp.concatenate([z for _, _, z in cells], axis=1)
+
+        def window(turn, total):
+            start = first + turn * width
+            tables = []
+            for x, y, _ in cells:
+                y_hot = flags(rows_iota(CY, 128) == y).astype(jnp.bfloat16)
+                hots = [spread(flags(x == start + i)) for i in range(width)]
+                tables.append(jnp.concatenate([times_row(y_hot, hot) for hot in hots], axis=0))
+            here = pl.ds(pl.multiple_of(start * CY, 128), width * CY)
+            found = jnp.dot(turned_ref[:, here], jnp.concatenate(tables, axis=1), preferred_element_type=jnp.float32)
+            found = jnp.where(level, found[:NZ] + found[NZ:], 0.0)
+            return total + jnp.sum(found, axis=0, keepdims=True)
+
+        turns = jnp.maximum(last - first, 0) // width + 1
+        row = lax.fori_loop(1, turns, window, window(0, jnp.zeros((1, 128 * GROUP), jnp.float32)))
+        for member in range(GROUP):
+            sampled_ref[pl.ds(GROUP * at + member, 1), :] = row[:, 128 * member : 128 * (member + 1)]
         return carry
 
-    lax.fori_loop(0, chunks // 2, step, 0, unroll=4)
-
-
-def sample(cell_rows, held, flip, blocks):
-    shapes = (cell_rows.shape, held.shape)
+    lax.fori_loop(0, chunks // GROUP, group, 0)
+    if len(out_ref.shape) == 2:
+        out_ref[...] = sampled_ref[...]
+        return
+    bricks, halves = out_ref.shape[:2]
+    for half in range(halves):
+        for block in range(bricks // 8):
+            tile = sampled_ref[pl.ds(8 * half * (bricks // 8) + block, 8, stride=bricks // 8), :]
+            out_ref[8 * block : 8 * (block + 1), half, :] = units_turned(tile)
+
+
+def sample(cell_rows, bounds, held, flip, blocks, bricks, capacity):
+    turned = (bricks, capacity // 128, 128)
+    if capacity % 128 or bricks % 8:
+        turned = cell_rows.shape
     return pl.pallas_call(
         functools.partial(sample_kernel, blocks),
-        out_shape=tuple(jax.ShapeDtypeStruct(shape, jnp.float32) for shape in shapes),
-        in_specs=[pl.BlockSpec(memory_space=pltpu.SMEM)] + whole_arrays(2),
+        out_shape=tuple(jax.ShapeDtypeStruct(shape, jnp.float32) for shape in (turned, held.shape)),
+        in_specs=[pl.BlockSpec(memory_space=pltpu.SMEM)] * 2 + whole_arrays(2),
         out_specs=tuple(whole_arrays(2)),
-        scratch_shapes=[pltpu.VMEM((2 * NZ, CX * CY), jnp.bfloat16)],
+        scratch_shapes=[
+            pltpu.VMEM((2 * NZ, CX * CY + 512), jnp.bfloat16),
+            pltpu.VMEM(cell_rows.shape, jnp.float32),
+        ],
         compiler_params=pltpu.CompilerParams(vmem_limit_bytes=32 << 20),
         name="sample",
-    )(flip, cell_rows, held)
-
-
-def neighbours(face, axis, count):
+    )(flip, bounds, cell_rows, held)
+
+
+def swaps(pair, other, axis):
     peers = lax.axis_size(axis)
-    up = [(i, i + 1) for i in range(peers - 1)]
-    down = [(j, i) for i, j in up]
-    return lax.ppermute(face[count:], axis, up), lax.ppermute(face[:count], axis, down)
+    got = []
+    for start, value in ((0, pair), (1, other)):
+        pairs = [(i, i + 1) for i in range(start, peers - 1, 2)]
+        got.append(lax.ppermute(value, axis, pairs + [(j, i) for i, j in pairs]))
+    return got
 
 
 def parts_in_rows(value):
@@ -467,17 +545,20 @@
     )(*operands)
 
 
-def join_kernel(order, source_ref, x_before_ref, x_after_ref, y_before_ref, y_after_ref, brick_ref, sent_ref, turned_ref):
+def join_kernel(order, even_ref, source_ref, x_pair_ref, x_other_ref, y_pair_ref, y_other_ref, brick_ref, sent_ref, turned_ref):
+    x_even, y_even = even_ref[0] > 0, even_ref[1] > 0
+    y_before = jnp.where(y_even, y_other_ref[...], y_pair_ref[...])
+    y_after = jnp.where(y_even, y_pair_ref[...], y_other_ref[...])
     for i in range(CX):
         here = slice(i * CY, (i + 1) * CY)
         value = source_ref[here, :]
         if i == 0:
-            value = value + x_before_ref[...]
+            value = value + jnp.where(x_even, x_other_ref[...], x_pair_ref[...])
         if i == CX - 1:
-            value = value + x_after_ref[...]
+            value = value + jnp.where(x_even, x_pair_ref[...], x_other_ref[...])
         row = rows_iota(CY, NZ)
-        value = value + jnp.where(row == 0, y_before_ref[i : i + 1, :], 0.0)
-        brick_ref[here, :] = value + jnp.where(row == CY - 1, y_after_ref[i : i + 1, :], 0.0)
+        value = value + jnp.where(row == 0, y_before[i : i + 1, :], 0.0)
+        brick_ref[here, :] = value + jnp.where(row == CY - 1, y_after[i : i + 1, :], 0.0)
     half = CX // 2
     planes = sent_ref.shape[1] // half
     turned_ref[:8, :] = jnp.zeros((8, 2 * CY), jnp.float32)
@@ -490,19 +571,19 @@
             sent_ref[target, pl.ds(i, planes, stride=half), :] = turned_ref[first : first + planes, :]
 
 
-def join(source, order, *faces):
+def join(source, even, order, *faces):
     return pl.pallas_call(
         functools.partial(join_kernel, order),
         out_shape=(
             jax.ShapeDtypeStruct(source.shape, jnp.float32),
             jax.ShapeDtypeStruct((len(order), (NZ // len(order) + 2) * CX // 2, 2 * CY), jnp.float32),
         ),
-        in_specs=[VMEM] * 5,
+        in_specs=[SMEM] + [VMEM] * 5,
         out_specs=(VMEM, VMEM),
         scratch_shapes=[pltpu.VMEM((NZ + 16, 2 * CY), jnp.float32)],
         compiler_params=LIMIT,
         name="join",
-    )(source, *faces)
+    )(even, source, *faces)
 
 
 def slab_order(first_count, second_count):
@@ -608,22 +689,26 @@
     point_count = cells.shape[0]
     capacity = 2 * point_count // bricks
     chunks = bricks * capacity // 128
-    send, rank = pack(owners, cells, normals, levels, bricks, capacity)
+    send, slot = pack(owners, cells, normals, levels, bricks, capacity)
     held = exchange(send)
     levels = held[:, 4 * capacity // 128, 0]
-    field = held[:, : 4 * capacity // 128].reshape(bricks, 4, capacity).transpose(1, 0, 2).reshape(4 * chunks, 128)
+    field = regroup(held, bricks, capacity)
     cell_rows = field[3 * chunks :]
-    used = (jnp.max(cell_rows, axis=1) > 0).astype(jnp.int32)
-    x_face, y_face = splat(face_kernel, field, used, 2 * CY, 2 * CX)
-    (source,) = splat(splat_kernel, field, used, CX * CY)
-    x_before, x_after = neighbours(x_face, "bx", CY)
-    y_before, y_after = neighbours(y_face, "by", CX)
-    brick, sent = join(source, slab_order(lax.axis_size("bx"), lax.axis_size("by")), x_before, x_after, y_before, y_after)
+    grouped = cell_rows.reshape(chunks // GROUP, -1)
+    x = (grouped.astype(jnp.int32) - 1) >> 14
+    bounds = [jnp.min(jnp.where(grouped > 0, x, CX), axis=1), jnp.max(jnp.where(grouped > 0, x, -1), axis=1)]
+    bounds = jnp.stack(bounds, axis=1)
+    even = jnp.stack([lax.axis_index("bx") % 2 == 0, lax.axis_index("by") % 2 == 0]).astype(jnp.int32)
+    source, x_pair, x_other, y_pair, y_other = splat(field, bounds, even)
+    faces = swaps(x_pair, x_other, "bx") + swaps(y_pair, y_other, "by")
+    brick, sent = join(source, even, slab_order(lax.axis_size("bx"), lax.axis_size("by")), *faces)
     held = relax(brick, sent, levels, rows_inverse, columns_inverse, depth_inverse)
     flip = (lax.axis_index("bx") % 2).astype(jnp.int32).reshape(1)
-    sampled, iterate = sample(cell_rows, held.reshape(CX * CY, NZ), flip, lax.axis_size("by"))
-    returned = lax.all_to_all(sampled.reshape(bricks, capacity), EVERY, split_axis=0, concat_axis=0, tiled=True)
-    implicit = unpack(owners, rank, returned)
+    held = held.reshape(CX * CY, NZ)
+    sampled, iterate = sample(cell_rows, bounds, held, flip, lax.axis_size("by"), bricks, capacity)
+    if sampled.ndim == 2:
+        sampled = sampled.reshape(bricks, capacity)
+    implicit = unpack(owners, slot, exchange(sampled).reshape(bricks, capacity))
     return (iterate.reshape(CX, CY, NZ), implicit)
 
 

time: 405 us -> 393 us (0.970)
  blocking collectives: 202 us -> 162 us
  waiting for transfers between devices: 76.7 us -> 103 us
  Pallas kernels: 78.4 us -> 59.6 us
  starting transfers between devices: 29.2 us -> 46.1 us
    all_to_all x2 -> x0, blocking collectives: 36 us -> none  [the longest x1 25.7 us: relax(): return lax.all_to_all(sent, 'by', split_axis=0, concat_axis=0, tiled=True)]
    pallas_call x2, Pallas kernels: 38.2 us -> 18.8 us  [the longest x1 16.8 us: splat(): pl.pallas_call(splat_kernel, out_shape=tuple((jax.ShapeDtypeStruct(shape,...]
    all_to_all x0 -> x1, waiting for transfers between devices: none -> 13.9 us  [relax(): return lax.all_to_all(sent, 'by', split_axis=0, concat_axis=0, tiled=True)]
    all_to_all x2 -> x3, starting transfers between devices: 11 us -> 24.3 us  [exchange(): return lax.all_to_all(value, EVERY, split_axis=0, concat_axis=0, tiled=True)]
    all_to_all x0 -> x1, starting transfers between devices: none -> 11.5 us  [relax(): return lax.all_to_all(sent, 'by', split_axis=0, concat_axis=0, tiled=True)]
    all_to_all x2 -> x3, waiting for transfers between devices: 41.1 us -> 50.7 us  [exchange(): return lax.all_to_all(value, EVERY, split_axis=0, concat_axis=0, tiled=True)]
    ppermute x4, starting transfers between devices: 6.67 us -> 1.53 us  [swaps(): got.append(lax.ppermute(value, axis, pairs + [(j, i) for i, j in pairs]))]
    unnamed x45 -> x51, local copies, waits for them, and re-layouts: 6.68 us -> 9.5 us
  transfers between devices with their start and end apart: 21 -> 23, of which waited for: 9 -> 13; matrix products, arithmetic and copies ran while one was open for 1% -> 2% of each run, Pallas kernels for 7% -> 0%
where the time goes in v6:
time: 393 us; the launch traced here: 394 us
  blocking collectives  162 us (41%)
  waiting for transfers between devices  103 us (26%)
  Pallas kernels  59.6 us (15%)
  starting transfers between devices  46.1 us (12%)
  local copies, waits for them, and re-layouts  16 us (4%)
  other arithmetic  6.09 us (2%)
    all_to_all x5, blocking collectives, exchange(): return lax.all_to_all(value, EVERY, split_axis=0, concat_axis=0, tiled=True)  162 us
    all_to_all x3, waiting for transfers between devices, exchange(): return lax.all_to_all(value, EVERY, split_axis=0, concat_axis=0, tiled=True)  50.7 us
    ppermute x3, waiting for transfers between devices, x_slab_source(): lax.ppermute(piece, 'by', [(i, i ^ turn) for i in range(second_count)])  30.2 us
    all_to_all x3, starting transfers between devices, exchange(): return lax.all_to_all(value, EVERY, split_axis=0, concat_axis=0, tiled=True)  24.3 us
    pallas_call x5, Pallas kernels, later_phase(): pl.pallas_call(functools.partial(later_kernel, (order, planes, rows, sour...  18.6 us
    pallas_call x1, Pallas kernels, splat(): pl.pallas_call(splat_kernel, out_shape=tuple((jax.ShapeDtypeStruct(shape,...  16.8 us
    all_to_all x1, waiting for transfers between devices, relax(): return lax.all_to_all(sent, 'by', split_axis=0, concat_axis=0, tiled=True)  13.9 us
    all_to_all x1, starting transfers between devices, relax(): return lax.all_to_all(sent, 'by', split_axis=0, concat_axis=0, tiled=True)  11.5 us
  transfers between devices with their start and end apart: 23, of which 13 were waited for; matrix products, arithmetic and copies ran while one was open for 2% of the time, Pallas kernels for 0%

profile of v6, /device:TPU:0, one launch (start us, length us, event | category | flops | bytes accessed | tf_op | source)
XLA Modules:
  0.0 394.3 jit_solution(3399306168319997721)
XLA Ops:
  3.6 6.9 %pack.1 = (f32[32,16,128]{2,1,0:T(8,128)}, f32[1,4096]{1,0:T(1,128)S(1)}) custom-call(s32[1,1]{1,0:T(1,128)S(6)} %copy.52.level_ref, s32[1,4096]{1,0:T(1,128)S(1)} %bitcast.85, s32[1,4096]{1,0:T(1,128)S(1)} %bitcast.87, f32[3,4096]{1,0:T(4,128)S(1)} %copy-done.14), custom_call_target="tpu_custom_call" | custom-call | tf_op jit(solution)/shard_map/pack/pallas_call | solution.py:109
  11.1 7.3 %all-to-all-start = ((f32[32,16,128]{2,1,0:T(8,128)}), f32[32,16,128]{2,1,0:T(8,128)S(1)}, u32[]{:S(2)}, u32[]{:S(2)}) async-start(f32[32,16,128]{2,1,0:T(8,128)} %get-tuple-element.23), calls=%async_computation | async-start | bytes 524288 | tf_op jit(solution)/shard_map/all_to_all | solution.py:611
  18.5 10.5 %all-to-all-done.held_ref = f32[32,16,128]{2,1,0:T(8,128)S(1)} async-done(((f32[32,16,128]{2,1,0:T(8,128)}), f32[32,16,128]{2,1,0:T(8,128)S(1)}, u32[]{:S(2)}, u32[]{:S(2)}) %all-to-all-start) | async-done | bytes 262176 | tf_op jit(solution)/shard_map/all_to_all | solution.py:611
  29.7 1.9 regroup.1.field_ref
  33.9 16.8 %splat.1 = (f32[1024,256]{1,0:T(8,128)S(1)}, f32[64,256]{1,0:T(8,128)S(1)}, f32[64,256]{1,0:T(8,128)S(1)}, f32[16,256]{1,0:T(8,128)S(1)}, f32[16,256]{1,0:T(8,128)S(1)}) custom-call(s32[16,2]{1,0:T(8,128)S(1)} %copy.40.bound_ref, s32[2]{0:T(128)S(1)} %add_convert_fusion.1.even_ref, f32[256,128]{1,0:T(8,128)S(1)} %copy-done.13), custom_call_target="tpu_custom_call" | custom-call | tf_op jit(solution)/shard_map/splat/pallas_call | solution.py:269
  52.8 2.3 collective-permute-done.x_pair_ref
  55.1 2.3 join.1
  57.4 13.3 %all-to-all-start.1 = ((f32[32,80,128]{2,1,0:T(8,128)}), f32[32,80,128]{2,1,0:T(8,128)S(1)}, u32[]{:S(2)}, u32[]{:S(2)}) async-start(f32[32,80,128]{2,1,0:T(8,128)} %get-tuple-element.29), calls=%async_computation.1 | async-start | bytes 2621440 | tf_op jit(solution)/shard_map/all_to_all | solution.py:611
  73.2 29.6 %all-to-all-done.1 = f32[32,80,128]{2,1,0:T(8,128)S(1)} async-done(((f32[32,80,128]{2,1,0:T(8,128)}), f32[32,80,128]{2,1,0:T(8,128)S(1)}, u32[]{:S(2)}, u32[]{:S(2)}) %all-to-all-start.1) | async-done | bytes 1310752 | tf_op jit(solution)/shard_map/all_to_all | solution.py:611
  102.9 1.8 first_phase.1
  104.7 1.4 copy-done.6
  107.2 3.7 all-to-all-start.2
  112.1 1.7 collective-permute-start.5
  113.8 23.6 %collective-permute-done.5 = f32[4,64,256]{2,1,0:T(8,128)S(1)} collective-permute-done((f32[4,64,256]{2,1,0:T(8,128)}, f32[4,64,256]{2,1,0:T(8,128)S(1)}, u32[]{:S(2)}, u32[]{:S(2)}) %collective-permute-start.5) | collective-permute-done | bytes 262176 | tf_op jit(solution)/shard_map/ppermute | solution.py:624
  137.4 6.6 %collective-permute-done.6 = f32[4,64,256]{2,1,0:T(8,128)S(1)} collective-permute-done((f32[4,64,256]{2,1,0:T(8,128)S(1)}, f32[4,64,256]{2,1,0:T(8,128)S(1)}, u32[]{:S(2)}, u32[]{:S(2)}) %collective-permute-start.6) | collective-permute-done | bytes 262176 | tf_op jit(solution)/shard_map/ppermute | solution.py:624
  144.8 1.9 collective-permute-start.8
  149.2 10.6 %all-to-all-done.2 = f32[32,128,128]{2,1,0:T(8,128)} async-done(((f32[32,128,128]{2,1,0:T(8,128)}), f32[32,128,128]{2,1,0:T(8,128)}, u32[]{:S(2)}, u32[]{:S(2)}) %all-to-all-start.2) | async-done | bytes 2097184 | tf_op jit(solution)/shard_map/all_to_all | solution.py:611
  164.7 4.3 %later_phase.5 = (f32[2048,128]{1,0:T(8,128)S(1)}, f32[10,256,128]{2,1,0:T(8,128)S(1)}) custom-call(f32[3]{0:T(128)S(1)} %add_convert_fusion.edge_ref, f32[4096,128]{1,0:T(8,128)} %bitcast.16.held_ref, f32[768,128]{1,0:T(8,128)S(1)} %collective-permute-done.9.pair_ref, f32[768,128]{1,0:T(8,128)S(1)} %collective-permute-done.10.other_ref, ...), custom_call_target="tpu_custom_call" | custom-call | tf_op jit(solution)/shard_map/later_phase/pallas_call | solution.py:534
  169.0 40.6 %all_to_all.76 = f32[32,64,128]{2,1,0:T(8,128)S(1)} all-to-all(f32[32,64,128]{2,1,0:T(8,128)S(1)} %bitcast.83), channel_id=1, replica_groups=mesh['bx'=8,'by'=4] {'bx','by'}, dimensions={0} | all-to-all | bytes 2097152 | tf_op jit(solution)/shard_map/all_to_all | solution.py:611
  210.8 1.4 collective-permute-start.12
  215.8 3.9 later_phase.6
  219.7 38.1 %all_to_all.77 = f32[32,64,128]{2,1,0:T(8,128)S(1)} all-to-all(f32[32,64,128]{2,1,0:T(8,128)S(1)} %bitcast.80), channel_id=1, replica_groups=mesh['bx'=8,'by'=4] {'bx','by'}, dimensions={0} | all-to-all | bytes 2097152 | tf_op jit(solution)/shard_map/all_to_all | solution.py:611
  259.5 3.2 later_phase.7
  262.7 35.9 %all_to_all.78 = f32[32,64,128]{2,1,0:T(8,128)S(1)} all-to-all(f32[32,64,128]{2,1,0:T(8,128)S(1)} %bitcast.77), channel_id=1, replica_groups=mesh['bx'=8,'by'=4] {'bx','by'}, dimensions={0} | all-to-all | bytes 2097152 | tf_op jit(solution)/shard_map/all_to_all | solution.py:611
  300.2 3.2 later_phase.8
  303.4 35.9 %all_to_all.79 = f32[32,64,128]{2,1,0:T(8,128)S(1)} all-to-all(f32[32,64,128]{2,1,0:T(8,128)S(1)} %bitcast.79), channel_id=1, replica_groups=mesh['bx'=8,'by'=4] {'bx','by'}, dimensions={0} | all-to-all | bytes 2097152 | tf_op jit(solution)/shard_map/all_to_all | solution.py:611
  341.4 4.1 %later_phase.9 = f32[4,4,64,256]{3,2,1,0:T(8,128)} custom-call(f32[3]{0:T(128)S(1)} %copy-done.19, f32[2048,128]{1,0:T(8,128)S(1)} %bitcast.69, f32[1024,128]{1,0:T(8,128)S(1)} %collective-permute-done.17.pair_ref, f32[1024,128]{1,0:T(8,128)S(1)} %collective-permute-done.18.other_ref, f32[6,256,1]{2,1,0:T(8,128)S(1)} %copy.37.diagonal_ref, ...), custom_call_target="tpu_custom_call" | custom-call | tf_op jit(solution)/shard_map/later_phase/pallas_call | solution.py:534
  345.5 11.5 %all-to-all-start.7 = ((f32[16,64,256]{2,1,0:T(8,128)}), f32[16,64,256]{2,1,0:T(8,128)S(1)}, u32[]{:S(2)}, u32[]{:S(2)}) async-start(f32[16,64,256]{2,1,0:T(8,128)} %bitcast.45), calls=%async_computation.7 | async-start | bytes 2097152 | tf_op jit(solution)/shard_map/all_to_all | solution.py:684
  357.7 13.9 %all-to-all-done.7 = f32[16,64,256]{2,1,0:T(8,128)S(1)} async-done(((f32[16,64,256]{2,1,0:T(8,128)}), f32[16,64,256]{2,1,0:T(8,128)S(1)}, u32[]{:S(2)}, u32[]{:S(2)}) %all-to-all-start.7) | async-done | bytes 1048608 | tf_op jit(solution)/shard_map/all_to_all | solution.py:684
  371.6 9.7 %sample.1 = (f32[32,2,128]{2,1,0:T(2,128)S(1)}, f32[1024,256]{1,0:T(8,128)}) custom-call(s32[1]{0:T(128)} %bitcast.flip_ref, s32[16,2]{1,0:T(8,128)S(1)} %copy.40.bound_ref, f32[64,128]{1,0:T(8,128)S(1)} %slice.72.field_ref, f32[1024,256]{1,0:T(8,128)S(1)} %bitcast.78), custom_call_target="tpu_custom_call" | custom-call | tf_op jit(solution)/shard_map/sample/pallas_call | solution.py:336
  381.3 11.4 %all_to_all.80 = f32[32,2,128]{2,1,0:T(2,128)S(1)} all-to-all(f32[32,2,128]{2,1,0:T(2,128)S(1)} %get-tuple-element.43), channel_id=1, replica_groups=mesh['bx'=8,'by'=4] {'bx','by'}, dimensions={0} | all-to-all | bytes 65536 | tf_op jit(solution)/shard_map/all_to_all | solution.py:611
  392.8 1.6 unpack.1
  (120 shorter events, 31.8 us)
Async XLA Ops:
  11.1 17.9 %all-to-all-start = ((f32[32,16,128]{2,1,0:T(8,128)}), f32[32,16,128]{2,1,0:T(8,128)S(1)}, u32[]{:S(2)}, u32[]{:S(2)}) async-start(f32[32,16,128]{2,1,0:T(8,128)} %get-tuple-element.23), calls=%async_computation | async-start | bytes 524288 | tf_op jit(solution)/shard_map/all_to_all | solution.py:611
  50.8 4.3 %collective-permute-start = (f32[64,256]{1,0:T(8,128)S(1)}, f32[64,256]{1,0:T(8,128)S(1)}, u32[]{:S(2)}, u32[]{:S(2)}) collective-permute-start(f32[64,256]{1,0:T(8,128)S(1)} %get-tuple-element.25), channel_id=1, source_target_pairs={{0,4},{8,12},{16,20},{24,28},{4,0},{12,8},{20,16},{28,24},{1,5},{9... | collective-permute-start | bytes 196616 | tf_op jit(solution)/shard_map/ppermute | solution.py:355
  50.9 4.2 %collective-permute-start.1 = (f32[64,256]{1,0:T(8,128)S(1)}, f32[64,256]{1,0:T(8,128)S(1)}, u32[]{:S(2)}, u32[]{:S(2)}) collective-permute-start(f32[64,256]{1,0:T(8,128)S(1)} %get-tuple-element.26), channel_id=1, source_target_pairs={{4,8},{12,16},{20,24},{8,4},{16,12},{24,20},{5,9},{13,17},{21,25},... | collective-permute-start | bytes 196616 | tf_op jit(solution)/shard_map/ppermute | solution.py:355
  51.6 1.2 collective-permute-start.2
  51.7 1.2 collective-permute-start.3
  57.4 45.5 %copy-start = (f32[256,256]{1,0:T(8,128)S(1)}, f32[256,256]{1,0:T(8,128)}, u32[]{:S(2)}) copy-start(f32[256,256]{1,0:T(8,128)} %first_ref.11) | copy-start | bytes 786436
  57.4 45.5 %copy-start.11 = (f32[128,128]{1,0:T(8,128)S(1)}, f32[128,128]{1,0:T(8,128)}, u32[]{:S(2)}) copy-start(f32[128,128]{1,0:T(8,128)} %second_ref.10) | copy-start | bytes 196612
  57.4 45.4 %all-to-all-start.1 = ((f32[32,80,128]{2,1,0:T(8,128)}), f32[32,80,128]{2,1,0:T(8,128)S(1)}, u32[]{:S(2)}, u32[]{:S(2)}) async-start(f32[32,80,128]{2,1,0:T(8,128)} %get-tuple-element.29), calls=%async_computation.1 | async-start | bytes 2621440 | tf_op jit(solution)/shard_map/all_to_all | solution.py:611
  107.2 52.7 %all-to-all-start.2 = ((f32[32,128,128]{2,1,0:T(8,128)}), f32[32,128,128]{2,1,0:T(8,128)}, u32[]{:S(2)}, u32[]{:S(2)}) async-start(f32[32,128,128]{2,1,0:T(8,128)} %bitcast.81), calls=%async_computation.2 | async-start | bytes 4194304 | tf_op jit(solution)/shard_map/all_to_all | solution.py:611
  111.9 1.9 collective-permute-start.4
  112.1 25.3 %collective-permute-start.5 = (f32[4,64,256]{2,1,0:T(8,128)}, f32[4,64,256]{2,1,0:T(8,128)S(1)}, u32[]{:S(2)}, u32[]{:S(2)}) collective-permute-start(f32[4,64,256]{2,1,0:T(8,128)} %get-tuple-element.61), channel_id=1, source_target_pairs={{0,2},{1,3},{2,0},{3,1},{4,6},{5,7},{6,4},{7,5},{8,10},{9,11},{10,... | collective-permute-start | bytes 786440 | tf_op jit(solution)/shard_map/ppermute | solution.py:624
  113.7 30.3 %collective-permute-start.6 = (f32[4,64,256]{2,1,0:T(8,128)S(1)}, f32[4,64,256]{2,1,0:T(8,128)S(1)}, u32[]{:S(2)}, u32[]{:S(2)}) collective-permute-start(f32[4,64,256]{2,1,0:T(8,128)S(1)} %get-tuple-element.60), channel_id=1, source_target_pairs={{0,3},{1,2},{2,1},{3,0},{4,7},{5,6},{6,5},{7,4},{8,11},{9,10},{10,... | collective-permute-start | bytes 786440 | tf_op jit(solution)/shard_map/ppermute | solution.py:624
  144.1 2.6 collective-permute-start.7
  144.8 3.1 collective-permute-start.8
  162.8 1.9 collective-permute-start.9
  162.8 1.9 collective-permute-start.10
  169.0 41.8 %copy-start.9 = (f32[10,256,128]{2,1,0:T(8,128)}, f32[10,256,128]{2,1,0:T(8,128)S(1)}, u32[]{:S(2)}) copy-start(f32[10,256,128]{2,1,0:T(8,128)S(1)} %get-tuple-element.40.refs_0_) | copy-start | bytes 3932164
  210.8 2.4 collective-permute-start.11
  210.8 2.5 collective-permute-start.12
  219.7 39.8 %copy-start.2 = (f32[256,256]{1,0:T(8,128)S(1)}, f32[256,256]{1,0:T(8,128)}, u32[]{:S(2)}) copy-start(f32[256,256]{1,0:T(8,128)} %first_ref.11) | copy-start | bytes 786436
  219.7 39.8 %copy-start.8 = (f32[10,128,256]{2,1,0:T(8,128)S(1)}, f32[10,128,256]{2,1,0:T(8,128)}, u32[]{:S(2)}) copy-start(f32[10,128,256]{2,1,0:T(8,128)} %copy-done.7) | copy-start | bytes 3932164
  219.7 39.8 %copy-start.12 = (f32[128,128]{1,0:T(8,128)S(1)}, f32[128,128]{1,0:T(8,128)}, u32[]{:S(2)}) copy-start(f32[128,128]{1,0:T(8,128)} %second_ref.10) | copy-start | bytes 196612
  219.7 39.8 %copy-start.19 = (f32[3]{0:T(128)S(1)}, f32[3]{0:T(128)}, u32[]{:S(2)}) copy-start(f32[3]{0:T(128)} %copy-done.17) | copy-start | bytes 40
  257.8 1.6 collective-permute-start.13
  257.9 1.5 collective-permute-start.14
  298.6 1.6 collective-permute-start.15
  298.7 1.5 collective-permute-start.16
  339.4 2.0 collective-permute-start.17
  339.5 1.9 collective-permute-start.18
  345.5 47.3 %copy-start.16 = (s32[4096,1]{0,1:T(1,128)S(1)}, s32[4096,1]{0,1:T(1,128)}, u32[]{:S(2)}) copy-start(s32[4096,1]{0,1:T(1,128)} %param.8) | copy-start | bytes 49156
  345.5 47.3 %copy-start.21 = (f32[1,4096]{1,0:T(1,128)S(1)}, f32[1,4096]{1,0:T(1,128)}, u32[]{:S(2)}) copy-start(f32[1,4096]{1,0:T(1,128)} %copy-done.20) | copy-start | bytes 49156
  345.5 26.1 %all-to-all-start.7 = ((f32[16,64,256]{2,1,0:T(8,128)}), f32[16,64,256]{2,1,0:T(8,128)S(1)}, u32[]{:S(2)}, u32[]{:S(2)}) async-start(f32[16,64,256]{2,1,0:T(8,128)} %bitcast.45), calls=%async_computation.7 | async-start | bytes 2097152 | tf_op jit(solution)/shard_map/all_to_all | solution.py:684
  (16 other events, 98.7 us)

commit v7 on v6

--- a/solution.py
+++ b/solution.py
@@ -57,29 +57,35 @@
         return here, named, x, flags(rows_iota(CX, block) == x)
 
     def tally(named, x_hot):
-        return product([named.astype(jnp.bfloat16)], [x_hot.astype(jnp.bfloat16)])
+        return product([x_hot.astype(jnp.bfloat16)], [named.astype(jnp.bfloat16)])
 
     def count(at, counts):
         _, named, _, x_hot = names(at)
         return counts + tally(named, x_hot)
 
-    counts = lax.fori_loop(0, points // block, count, jnp.zeros((bricks, CX), jnp.float32), unroll=4)
-    per_brick = jnp.sum(counts, axis=1, keepdims=True)
+    counts = lax.fori_loop(0, points // block, count, jnp.zeros((CX, bricks), jnp.float32), unroll=4)
+    ahead, shift, shifts = jnp.zeros((1, bricks), jnp.float32), jnp.zeros((1, bricks), jnp.float32), []
+    for i in range(CX):
+        shift = jnp.maximum(shift, float(i * capacity // CX) - ahead)
+        shifts.append(shift)
+        ahead = ahead + counts[i : i + 1, :]
+    shifts = jnp.concatenate(shifts, axis=0)
 
     def step(at, seen):
         here, named, x, x_hot = names(at)
         x_less = flags(rows_iota(CX, block) < x)
-        ahead = jnp.dot(
-            jnp.concatenate([counts, seen], axis=1).astype(jnp.bfloat16),
-            jnp.concatenate([x_less, x_hot], axis=0).astype(jnp.bfloat16),
+        own = jnp.dot(
+            jnp.concatenate([counts, seen, shifts], axis=0).astype(jnp.bfloat16),
+            named.astype(jnp.bfloat16),
             preferred_element_type=jnp.float32,
         )
+        ahead = jnp.sum(x_less * own[:CX] + x_hot * own[CX : 2 * CX], axis=0, keepdims=True)
+        used = jnp.sum(own[:CX], axis=0, keepdims=True)
+        moved = jnp.minimum(jnp.sum(x_hot * own[2 * CX :], axis=0, keepdims=True), capacity - used)
         key = (owner_ref[:, here] * CX + x).astype(jnp.float32)
         column = jnp.broadcast_to(key, (128, block)).T
         same = (jnp.concatenate([column] * (block // 128), axis=1) == key) & earlier
-        rank = jnp.sum(named * ahead, axis=0, keepdims=True) + jnp.sum(flags(same), axis=0, keepdims=True)
-        used = jnp.sum(named * per_brick, axis=0, keepdims=True)
-        place = jnp.floor((rank * capacity + 0.5) / used)
+        place = ahead + jnp.sum(flags(same), axis=0, keepdims=True) + moved
         slot_ref[:, here] = place
         slot = flags(rows_iota(capacity, block).astype(jnp.float32) == place).astype(jnp.bfloat16)
         values = []
@@ -92,7 +98,7 @@
         total_ref[...] += product([rows], [slot])
         return seen + tally(named, x_hot)
 
-    lax.fori_loop(0, points // block, step, jnp.zeros((bricks, CX), jnp.float32), unroll=2)
+    lax.fori_loop(0, points // block, step, jnp.zeros((CX, bricks), jnp.float32), unroll=2)
     part = lambda i: total_ref[i * bricks : (i + 1) * bricks, :]
     fields = [part(3 * k) + part(3 * k + 1) + part(3 * k + 2) for k in range(3)]
     fields.append(part(9) * 65536.0 + part(10) * 256.0 + part(11))
@@ -115,7 +121,7 @@
         in_specs=[pl.BlockSpec(memory_space=pltpu.SMEM)] + whole_arrays(3),
         out_specs=tuple(whole_arrays(2)),
         scratch_shapes=[pltpu.VMEM((12 * bricks, capacity), jnp.float32)],
-        compiler_params=pltpu.CompilerParams(vmem_limit_bytes=32 << 20),
+        compiler_params=pltpu.CompilerParams(vmem_limit_bytes=16 << 20),
         name="pack",
     )(levels, owners.reshape(1, points), cells.reshape(1, points), normals)
 
@@ -142,7 +148,7 @@
         out_shape=jax.ShapeDtypeStruct((1, points), jnp.float32),
         in_specs=whole_arrays(3),
         out_specs=pl.BlockSpec(memory_space=pltpu.VMEM),
-        compiler_params=pltpu.CompilerParams(vmem_limit_bytes=32 << 20),
+        compiler_params=pltpu.CompilerParams(vmem_limit_bytes=16 << 20),
         name="unpack",
     )(owners.reshape(1, points), rank, held)
     return out.reshape(points)
@@ -163,7 +169,7 @@
 
 
 GROUP = 4
-WINDOW = 6
+WINDOW = 4
 
 
 def units_turned(tile):
@@ -177,7 +183,11 @@
     return tile
 
 
-def regroup_kernel(held_ref, field_ref):
+def grouped(bricks, capacity):
+    return capacity % 128 == 0 and bricks % 8 == 0
+
+
+def regroup(held_ref, field_ref):
     bricks = held_ref.shape[0]
     chunks = field_ref.shape[0] // 4
     halves, blocks = chunks // bricks, bricks // 8
@@ -189,25 +199,32 @@
                 field_ref[here, :] = units_turned(tile)
 
 
-def regroup(held, bricks, capacity):
-    chunks = bricks * capacity // 128
-    if capacity % 128 or bricks % 8:
-        field = held[:, : 4 * capacity // 128].reshape(bricks, 4, capacity)
-        return field.transpose(1, 0, 2).reshape(4 * chunks, 128)
-    return pl.pallas_call(
-        regroup_kernel,
-        out_shape=jax.ShapeDtypeStruct((4 * chunks, 128), jnp.float32),
-        in_specs=whole_arrays(1),
-        out_specs=pl.BlockSpec(memory_space=pltpu.VMEM),
-        name="regroup",
-    )(held)
-
-
 def splat_kernel(
-    bound_ref, even_ref, field_ref, source_ref, x_pair_ref, x_other_ref, y_pair_ref, y_other_ref, sum_ref, column_ref
+    even_ref,
+    held_ref,
+    source_ref,
+    x_pair_ref,
+    x_other_ref,
+    y_pair_ref,
+    y_other_ref,
+    cell_ref,
+    bound_ref,
+    field_ref,
+    sum_ref,
+    column_ref,
 ):
     chunks = field_ref.shape[0] // 4
     points = 128 * GROUP
+    if len(held_ref.shape) == 3:
+        regroup(held_ref, field_ref)
+    else:
+        field_ref[...] = held_ref[...]
+    cell_ref[...] = field_ref[3 * chunks :, :]
+    for at in range(chunks // GROUP):
+        cell = cell_ref[GROUP * at : GROUP * (at + 1), :]
+        x = places(cell)[0].astype(jnp.float32)
+        bound_ref[at, 0] = jnp.min(jnp.where(cell > 0, x, float(CX))).astype(jnp.int32)
+        bound_ref[at, 1] = jnp.max(jnp.where(cell > 0, x, -1.0)).astype(jnp.int32)
     sum_ref[...] = jnp.zeros_like(sum_ref)
 
     def group(at, carry):
@@ -264,20 +281,22 @@
     y_other_ref[...] = jnp.where(even_ref[1] > 0, before, after)
 
 
-def splat(field, bounds, even):
-    shapes = [(CX * CY, NZ), (CY, NZ), (CY, NZ), (CX, NZ), (CX, NZ)]
+def splat(held, even, chunks):
+    shapes = [(CX * CY, NZ), (CY, NZ), (CY, NZ), (CX, NZ), (CX, NZ), (chunks, 128)]
+    out = [jax.ShapeDtypeStruct(shape, jnp.float32) for shape in shapes]
     return pl.pallas_call(
         splat_kernel,
-        out_shape=tuple(jax.ShapeDtypeStruct(shape, jnp.float32) for shape in shapes),
-        in_specs=[pl.BlockSpec(memory_space=pltpu.SMEM)] * 2 + whole_arrays(1),
-        out_specs=tuple(whole_arrays(5)),
+        out_shape=tuple(out + [jax.ShapeDtypeStruct((chunks // GROUP, 2), jnp.int32)]),
+        in_specs=[pl.BlockSpec(memory_space=pltpu.SMEM)] + whole_arrays(1),
+        out_specs=tuple(whole_arrays(6) + [pl.BlockSpec(memory_space=pltpu.SMEM)]),
         scratch_shapes=[
+            pltpu.VMEM((4 * chunks, 128), jnp.float32),
             pltpu.VMEM(((CX + WINDOW) * CY, 3 * NZ), jnp.float32),
             pltpu.VMEM((3 * NZ, 2 * GROUP * 128), jnp.bfloat16),
         ],
-        compiler_params=pltpu.CompilerParams(vmem_limit_bytes=32 << 20),
+        compiler_params=pltpu.CompilerParams(vmem_limit_bytes=16 << 20),
         name="splat",
-    )(bounds, even, field)
+    )(even, held)
 
 
 def sample_kernel(blocks, flip_ref, bound_ref, field_ref, held_ref, out_ref, iterate_ref, turned_ref, sampled_ref):
@@ -293,7 +312,7 @@
         high, low = parts_of(block.T, 2)
         turned_ref[:NZ, here] = high
         turned_ref[NZ:, here] = low
-    width = 8
+    width = 4
 
     def group(at, carry):
         first, last = bound_ref[at, 0] // 2 * 2, bound_ref[at, 1]
@@ -331,7 +350,7 @@
 
 def sample(cell_rows, bounds, held, flip, blocks, bricks, capacity):
     turned = (bricks, capacity // 128, 128)
-    if capacity % 128 or bricks % 8:
+    if not grouped(bricks, capacity):
         turned = cell_rows.shape
     return pl.pallas_call(
         functools.partial(sample_kernel, blocks),
@@ -339,10 +358,10 @@
         in_specs=[pl.BlockSpec(memory_space=pltpu.SMEM)] * 2 + whole_arrays(2),
         out_specs=tuple(whole_arrays(2)),
         scratch_shapes=[
-            pltpu.VMEM((2 * NZ, CX * CY + 512), jnp.bfloat16),
+            pltpu.VMEM((2 * NZ, CX * CY + 256), jnp.bfloat16),
             pltpu.VMEM(cell_rows.shape, jnp.float32),
         ],
-        compiler_params=pltpu.CompilerParams(vmem_limit_bytes=32 << 20),
+        compiler_params=pltpu.CompilerParams(vmem_limit_bytes=16 << 20),
         name="sample",
     )(flip, bounds, cell_rows, held)
 
@@ -388,14 +407,17 @@
     return jnp.concatenate(columns, axis=1)
 
 
-def put(sent_ref, k, planes, order, per_block, start, value):
+def put(sent_ref, k, planes, order, per_block, runs, value):
     turned = value.T
     per_target = turned.shape[0] // len(order)
     for j, target in enumerate(order):
         for band in range(turned.shape[1] // 128):
-            at = target * per_block + start + band * per_target * planes + k
-            part = turned[j * per_target : (j + 1) * per_target, band * 128 : (band + 1) * 128]
-            sent_ref[pl.ds(at, per_target, stride=planes), :] = part
+            columns = slice(band * 128, (band + 1) * 128)
+            start = target * per_block + band * (per_block * 128 // turned.shape[1]) + k
+            for place, first, count in runs:
+                if count:
+                    part = turned[j * per_target + first : j * per_target + first + count, columns]
+                    sent_ref[pl.ds(start + place * planes, count, stride=planes), :] = part
 
 
 def brick_planes(ref, first_count, second_count, planes, k):
@@ -413,11 +435,27 @@
     return jnp.concatenate(bands, axis=0)
 
 
-def sweep_all(count, step_ref, source_ref, diagonal_ref, matrix_ref, emit):
+def diagonal_of(ref, k, turned, shape):
+    if ref.shape[0] == 1:
+        return ref[0]
+    if not turned:
+        return ref[k]
+    column = jnp.broadcast_to(ref[k], (128, shape[0])).T
+    return jnp.concatenate([column] * (shape[1] // 128), axis=1)
+
+
+def fetch(pairs, sem_ref):
+    copies = [pltpu.make_async_copy(source, held, sem_ref.at[i]) for i, (source, held) in enumerate(pairs)]
+    for copy in copies:
+        copy.start()
+    return copies
+
+
+def sweep_all(count, step_ref, source_ref, diagonal_ref, turned, matrix_ref, emit):
     matrix = wide(matrix_ref[...])
     for k in range(count):
-        diagonal = diagonal_ref[0 if diagonal_ref.shape[0] == 1 else k + 1]
         middle = step_ref[k + 1]
+        diagonal = diagonal_of(diagonal_ref, k + 1, turned, middle.shape)
         remainder = remainder_of(source_ref[k + 1], step_ref[k], middle, step_ref[k + 2], diagonal)
         high, low = parts_of(remainder, 2)
         row = jnp.concatenate([high, low, high], axis=1)
@@ -426,11 +464,13 @@
 
 
 def first_kernel(
-    grid, held_ref, diagonal_ref, first_ref, second_ref, sent_ref, source_ref, step_ref
+    grid, held_ref, diagonal_ref, first_any, second_any, sent_ref, source_ref, step_ref, first_ref, second_ref, sem_ref
 ):
+    copies = fetch([(first_any, first_ref), (second_any, second_ref)], sem_ref)
     first_count, second_count, planes, per_target = grid
     for k in range(planes + 2):
         source_ref[k] = brick_planes(held_ref, first_count, second_count, planes + 2, k)
+    copies[0].wait()
     first = wide(first_ref[...])
     for k in range(planes + 2):
         step_ref[k] = jnp.dot(first, parts_in_rows(source_ref[k]), preferred_element_type=jnp.float32)
@@ -438,17 +478,21 @@
     block = sent_ref.shape[0] // len(order)
 
     def emit(k, value):
-        put(sent_ref, k, planes, order, block, 0, source_ref[k + 1])
-        put(sent_ref, k, planes, order, block, block // 2, value)
-
-    sweep_all(planes, step_ref, source_ref, diagonal_ref, second_ref, emit)
+        last = sent_ref.shape[0] * 128 // (2 * planes * len(order) * value.shape[0]) - 1
+        put(sent_ref, k, planes, order, block, [(0, 0, 1), (last + 2, last, 1), (last + 3, 1, last - 1)], source_ref[k + 1])
+        put(sent_ref, k, planes, order, block, [(1, 0, last + 1)], value)
+
+    copies[1].wait()
+    sweep_all(planes, step_ref, source_ref, diagonal_ref, False, second_ref, emit)
 
 
 def later_kernel(
-    shape, edge_ref, held_ref, pair_ref, other_ref, diagonal_ref, first_ref, second_ref, *refs
+    shape, edge_ref, held_ref, pair_ref, other_ref, diagonal_ref, first_any, second_any, *refs
 ):
-    order, planes, rows, with_source, last = shape
+    order, planes, rows, with_source, last, turned = shape
     devices = len(order)
+    *refs, first_ref, second_ref, sem_ref = refs
+    copies = fetch([(first_any, first_ref), (second_any, second_ref)], sem_ref)
     even = edge_ref[2] > 0
     if with_source:
         sent_ref, source_ref, iterate_ref, step_ref = refs
@@ -456,9 +500,9 @@
         source_ref, sent_ref, iterate_ref, step_ref = refs
     bands = iterate_ref.shape[2] // 128
     block, edge_block = held_ref.shape[0] // devices, pair_ref.shape[0] // devices
-    per_band = planes * rows
+    per_band = block // bands
     edge_band = edge_block // bands
-    own = lambda k, start: pieces(held_ref, order, block, start + k * rows, rows, bands, per_band)
+    own = lambda place: pieces(held_ref, order, block, place * rows, rows, bands, per_band)
 
     def edge(after, k):
         pair, other = [pieces(ref, order, edge_block, k * rows, rows, bands, edge_band) for ref in (pair_ref, other_ref)]
@@ -466,18 +510,19 @@
 
     if with_source:
         for k in range(planes):
-            source_ref[k + 1] = own(k, 0)
-        source_ref[0] = edge(False, 0)
+            source_ref[k + 1] = own(0 if k == 0 else planes + 1 if k == planes - 1 else planes + 1 + k)
+        source_ref[0] = edge(False, 2)
         source_ref[planes + 1] = edge(True, 0)
     for k in range(2):
-        iterate_ref[k] = edge(False, k + with_source)
+        iterate_ref[k] = edge(False, k)
         iterate_ref[planes + 2 + k] = edge(True, k + with_source)
     for k in range(planes):
-        iterate_ref[k + 2] = own(k, block // 2 if with_source else 0)
+        iterate_ref[k + 2] = own(k + with_source)
+    copies[0].wait()
     first = wide(first_ref[...])
     for k in range(planes + 2):
-        diagonal = diagonal_ref[0 if diagonal_ref.shape[0] == 1 else k]
         middle = iterate_ref[k + 1]
+        diagonal = diagonal_of(diagonal_ref, k, turned, middle.shape)
         remainder = remainder_of(source_ref[k], iterate_ref[k], middle, iterate_ref[k + 2], diagonal)
         step = jnp.dot(first, parts_in_rows(remainder), preferred_element_type=jnp.float32)
         if k == 0:
@@ -491,14 +536,21 @@
             for j in range(value.shape[0] // CY):
                 sent_ref[j, k] = value[j * CY : (j + 1) * CY, :]
         else:
-            put(sent_ref, k, planes, order, sent_ref.shape[0] // devices, 0, value)
-
-    sweep_all(planes, step_ref, source_ref, diagonal_ref, second_ref, emit)
-
-
+            per_target = value.shape[1] // devices
+            put(sent_ref, k, planes, order, sent_ref.shape[0] // devices, [(0, 0, per_target)], value)
+
+    copies[1].wait()
+    sweep_all(planes, step_ref, source_ref, diagonal_ref, turned, second_ref, emit)
+
+
+ANY = pl.BlockSpec(memory_space=pl.ANY)
 SMEM = pl.BlockSpec(memory_space=pltpu.SMEM)
 VMEM = pl.BlockSpec(memory_space=pltpu.VMEM)
-LIMIT = pltpu.CompilerParams(vmem_limit_bytes=48 << 20)
+LIMIT = pltpu.CompilerParams(vmem_limit_bytes=20 << 20)
+
+
+def matrix_scratch(first, second):
+    return [pltpu.VMEM(matrix.shape, jnp.float32) for matrix in (first, second)] + [pltpu.SemaphoreType.DMA((2,))]
 
 
 def first_phase(grid, held, diagonal, first, second):
@@ -510,15 +562,17 @@
             jax.ShapeDtypeStruct((2 * columns * planes * rows // 128, 128), jnp.float32),
             jax.ShapeDtypeStruct((planes + 2, rows, columns), jnp.float32),
         ),
-        in_specs=[VMEM] * 4,
+        in_specs=[VMEM] * 2 + [ANY] * 2,
         out_specs=(VMEM, VMEM),
-        scratch_shapes=[pltpu.VMEM((planes + 2, rows, columns), jnp.float32)],
+        scratch_shapes=[pltpu.VMEM((planes + 2, rows, columns), jnp.float32)] + matrix_scratch(first, second),
         compiler_params=LIMIT,
         name="first_phase",
     )(held, diagonal, first, second)
 
 
-def later_phase(order, planes, rows, edges, held, pair, other, diagonal, first, second, source=None, last=False):
+def later_phase(
+    order, planes, rows, turned, edges, held, pair, other, diagonal, first, second, source=None, last=False
+):
     columns = second.shape[1]
     length = len(order) * rows
     if last:
@@ -532,14 +586,15 @@
     else:
         operands.append(source)
     return pl.pallas_call(
-        functools.partial(later_kernel, (order, planes, rows, source is None, last)),
+        functools.partial(later_kernel, (order, planes, rows, source is None, last, turned)),
         out_shape=tuple(out),
-        in_specs=[SMEM] + [VMEM] * (len(operands) - 1),
+        in_specs=[SMEM] + [VMEM] * 4 + [ANY] * 2 + [VMEM] * (len(operands) - 7),
         out_specs=tuple([VMEM] * len(out)),
         scratch_shapes=[
             pltpu.VMEM((planes + 4, length, columns), jnp.float32),
             pltpu.VMEM((planes + 2, length, columns), jnp.float32),
-        ],
+        ]
+        + matrix_scratch(first, second),
         compiler_params=LIMIT,
         name="later_phase",
     )(*operands)
@@ -641,7 +696,7 @@
     diagonals = (
         diagonal[None],
         lax.dynamic_slice_in_dim(padded, me * thick[1], thick[1] + 2, 1).T[:, None, 1:-1],
-        lax.dynamic_slice_in_dim(padded, me * thick[2], thick[2] + 2, 0)[:, 1:-1, None],
+        lax.dynamic_slice_in_dim(padded, me * thick[2], thick[2] + 2, 0)[:, None, 1:-1],
     )
     edges = jnp.stack([me > 0, me < devices - 1, even]).astype(jnp.float32)
     matrices = (rows_inverse, columns_inverse, depth_inverse)
@@ -657,16 +712,16 @@
         if step == 1:
             held, sources[2] = lax.optimization_barrier((held, x_slab_source(brick, even)))
         bands = matrices[(2 * step + 1) % 3].shape[1] // 128
-        blocks = held.reshape(devices, -1, bands, planes * rows, 128)
-        to_next, to_previous = blocks[:, -1, :, -2 * rows :], blocks[:, -1, :, : 2 * rows]
+        blocks = held.reshape(devices, bands, -1, 128)
+        to_next, to_previous = blocks[:, :, -2 * rows :], blocks[:, :, : 2 * rows]
         if sources[at] is None:
-            to_next = jnp.concatenate([blocks[:, 0, :, -rows:], to_next], axis=2)
-            to_previous = jnp.concatenate([blocks[:, 0, :, :rows], to_previous], axis=2)
+            to_next, to_previous = blocks[:, :, (planes - 1) * rows : (planes + 2) * rows], blocks[:, :, : 3 * rows]
         pair, other = beside(to_next.reshape(-1, 128), to_previous.reshape(-1, 128), even)
         out = later_phase(
             order,
             planes,
             rows,
+            at == 2,
             edges,
             held,
             pair,
@@ -692,14 +747,11 @@
     send, slot = pack(owners, cells, normals, levels, bricks, capacity)
     held = exchange(send)
     levels = held[:, 4 * capacity // 128, 0]
-    field = regroup(held, bricks, capacity)
-    cell_rows = field[3 * chunks :]
-    grouped = cell_rows.reshape(chunks // GROUP, -1)
-    x = (grouped.astype(jnp.int32) - 1) >> 14
-    bounds = [jnp.min(jnp.where(grouped > 0, x, CX), axis=1), jnp.max(jnp.where(grouped > 0, x, -1), axis=1)]
-    bounds = jnp.stack(bounds, axis=1)
+    if not grouped(bricks, capacity):
+        held = held[:, : 4 * capacity // 128].reshape(bricks, 4, capacity)
+        held = held.transpose(1, 0, 2).reshape(4 * chunks, 128)
     even = jnp.stack([lax.axis_index("bx") % 2 == 0, lax.axis_index("by") % 2 == 0]).astype(jnp.int32)
-    source, x_pair, x_other, y_pair, y_other = splat(field, bounds, even)
+    source, x_pair, x_other, y_pair, y_other, cell_rows, bounds = splat(held, even, chunks)
     faces = swaps(x_pair, x_other, "bx") + swaps(y_pair, y_other, "by")
     brick, sent = join(source, even, slab_order(lax.axis_size("bx"), lax.axis_size("by")), *faces)
     held = relax(brick, sent, levels, rows_inverse, columns_inverse, depth_inverse)

time: 393 us -> 378 us (0.962)
  blocking collectives: 162 us -> 185 us
  waiting for transfers between devices: 103 us -> 85.4 us
  starting transfers between devices: 46.1 us -> 30.4 us
  Pallas kernels: 59.6 us -> 53.6 us
    all_to_all x0 -> x1, blocking collectives: none -> 25.7 us  [relax(): return lax.all_to_all(sent, 'by', split_axis=0, concat_axis=0, tiled=True)]
    all_to_all x1 -> x0, waiting for transfers between devices: 13.9 us -> none  [relax(): return lax.all_to_all(sent, 'by', split_axis=0, concat_axis=0, tiled=True)]
    all_to_all x1 -> x0, starting transfers between devices: 11.5 us -> none  [relax(): return lax.all_to_all(sent, 'by', split_axis=0, concat_axis=0, tiled=True)]
    pallas_call x2 -> x1, Pallas kernels: 18.8 us -> 13.2 us  [splat(): pl.pallas_call(splat_kernel, out_shape=tuple(out + [jax.ShapeDtypeStruct(...]
    all_to_all x3, starting transfers between devices: 24.3 us -> 18.8 us  [exchange(): return lax.all_to_all(value, EVERY, split_axis=0, concat_axis=0, tiled=True)]
    unnamed x51 -> x41, local copies, waits for them, and re-layouts: 9.5 us -> 9.96 us
  transfers between devices with their start and end apart: 23 -> 22, of which waited for: 13 -> 12; matrix products, arithmetic and copies ran while one was open for 2% -> 2% of each run, Pallas kernels for 0% -> 0%
where the time goes in v7:
time: 378 us; the launch traced here: 376 us
  blocking collectives  185 us (49%)
  waiting for transfers between devices  85.4 us (23%)
  Pallas kernels  53.6 us (14%)
  starting transfers between devices  30.4 us (8%)
  local copies, waits for them, and re-layouts  14.6 us (4%)
  other arithmetic  4.71 us (1%)
    all_to_all x5, blocking collectives, exchange(): return lax.all_to_all(value, EVERY, split_axis=0, concat_axis=0, tiled=True)  160 us
    all_to_all x3, waiting for transfers between devices, exchange(): return lax.all_to_all(value, EVERY, split_axis=0, concat_axis=0, tiled=True)  51.1 us
    ppermute x3, waiting for transfers between devices, x_slab_source(): lax.ppermute(piece, 'by', [(i, i ^ turn) for i in range(second_count)])  27.5 us
    all_to_all x1, blocking collectives, relax(): return lax.all_to_all(sent, 'by', split_axis=0, concat_axis=0, tiled=True)  25.7 us
    pallas_call x5, Pallas kernels, later_phase(): pl.pallas_call(functools.partial(later_kernel, (order, planes, rows, sour...  20.3 us
    all_to_all x3, starting transfers between devices, exchange(): return lax.all_to_all(value, EVERY, split_axis=0, concat_axis=0, tiled=True)  18.8 us
    pallas_call x1, Pallas kernels, splat(): pl.pallas_call(splat_kernel, out_shape=tuple(out + [jax.ShapeDtypeStruct(...  13.2 us
    unnamed x41, local copies, waits for them, and re-layouts  9.96 us
  transfers between devices with their start and end apart: 22, of which 12 were waited for; matrix products, arithmetic and copies ran while one was open for 2% of the time, Pallas kernels for 0%

profile of v7, /device:TPU:0, one launch (start us, length us, event | category | flops | bytes accessed | tf_op | source)
XLA Modules:
  0.0 375.8 jit_solution(5169800358380951894)
XLA Ops:
  3.6 5.8 %pack.1 = (f32[32,16,128]{2,1,0:T(8,128)}, f32[1,4096]{1,0:T(1,128)S(1)}) custom-call(s32[1,1]{1,0:T(1,128)S(6)} %copy.24.level_ref, s32[1,4096]{1,0:T(1,128)S(1)} %bitcast.69, s32[1,4096]{1,0:T(1,128)S(1)} %bitcast.71, f32[3,4096]{1,0:T(4,128)S(1)} %copy-done.7), custom_call_target="tpu_custom_call" | custom-call | tf_op jit(solution)/shard_map/pack/pallas_call | solution.py:115
  9.9 7.3 %all-to-all-start = ((f32[32,16,128]{2,1,0:T(8,128)}), f32[32,16,128]{2,1,0:T(8,128)S(1)}, u32[]{:S(2)}, u32[]{:S(2)}) async-start(f32[32,16,128]{2,1,0:T(8,128)} %get-tuple-element.25), calls=%async_computation | async-start | bytes 524288 | tf_op jit(solution)/shard_map/all_to_all | solution.py:666
  17.3 10.5 %all-to-all-done.held_ref = f32[32,16,128]{2,1,0:T(8,128)S(1)} async-done(((f32[32,16,128]{2,1,0:T(8,128)}), f32[32,16,128]{2,1,0:T(8,128)S(1)}, u32[]{:S(2)}, u32[]{:S(2)}) %all-to-all-start) | async-done | bytes 262176 | tf_op jit(solution)/shard_map/all_to_all | solution.py:666
  27.8 13.2 %splat.1 = (f32[1024,256]{1,0:T(8,128)S(1)}, f32[64,256]{1,0:T(8,128)S(1)}, f32[64,256]{1,0:T(8,128)S(1)}, f32[16,256]{1,0:T(8,128)S(1)}, f32[16,256]{1,0:T(8,12...) custom-call(s32[2]{0:T(128)S(1)} %add_convert_fusion.even_ref, f32[32,16,128]{2,1,0:T(8,128)S(1)} %all-to-all-done.held_ref), custom_call_target="tpu_custom_call" | custom-call | tf_op jit(solution)/shard_map/splat/pallas_call | solution.py:287
  45.0 1.5 collective-permute-done.x_pair_ref
  46.5 2.3 join.1
  49.7 7.8 %all-to-all-start.1 = ((f32[32,80,128]{2,1,0:T(8,128)}), f32[32,80,128]{2,1,0:T(8,128)S(1)}, u32[]{:S(2)}, u32[]{:S(2)}) async-start(f32[32,80,128]{2,1,0:T(8,128)} %get-tuple-element.33), calls=%async_computation.1 | async-start | bytes 2621440 | tf_op jit(solution)/shard_map/all_to_all | solution.py:666
  59.2 30.5 %all-to-all-done.1 = f32[32,80,128]{2,1,0:T(8,128)S(1)} async-done(((f32[32,80,128]{2,1,0:T(8,128)}), f32[32,80,128]{2,1,0:T(8,128)S(1)}, u32[]{:S(2)}, u32[]{:S(2)}) %all-to-all-start.1) | async-done | bytes 1310752 | tf_op jit(solution)/shard_map/all_to_all | solution.py:666
  89.8 2.7 first_phase.1
  92.6 1.3 copy-done.2
  93.9 3.7 all-to-all-start.2
  100.1 1.7 collective-permute-start.5
  102.5 21.6 %collective-permute-done.5 = f32[4,64,256]{2,1,0:T(8,128)S(1)} collective-permute-done((f32[4,64,256]{2,1,0:T(8,128)S(1)}, f32[4,64,256]{2,1,0:T(8,128)S(1)}, u32[]{:S(2)}, u32[]{:S(2)}) %collective-permute-start.5) | collective-permute-done | bytes 262176 | tf_op jit(solution)/shard_map/ppermute | solution.py:679
  124.9 5.9 %collective-permute-done.6 = f32[4,64,256]{2,1,0:T(8,128)S(1)} collective-permute-done((f32[4,64,256]{2,1,0:T(8,128)S(1)}, f32[4,64,256]{2,1,0:T(8,128)S(1)}, u32[]{:S(2)}, u32[]{:S(2)}) %collective-permute-start.6) | collective-permute-done | bytes 262176 | tf_op jit(solution)/shard_map/ppermute | solution.py:679
  133.3 1.9 collective-permute-start.8
  135.2 1.2 collective-permute-done.8
  136.6 10.1 %all-to-all-done.2 = f32[32,128,128]{2,1,0:T(8,128)} async-done(((f32[32,128,128]{2,1,0:T(8,128)}), f32[32,128,128]{2,1,0:T(8,128)}, u32[]{:S(2)}, u32[]{:S(2)}) %all-to-all-start.2) | async-done | bytes 2097184 | tf_op jit(solution)/shard_map/all_to_all | solution.py:666
  146.6 2.1 slice_select_fusion.4
  148.7 1.4 collective-permute-start.10
  153.2 4.6 %later_phase.5 = (f32[2048,128]{1,0:T(8,128)S(1)}, f32[10,256,128]{2,1,0:T(8,128)S(1)}) custom-call(f32[3]{0:T(128)S(1)} %copy-done.12, f32[4096,128]{1,0:T(8,128)} %bitcast.14.held_ref, f32[768,128]{1,0:T(8,128)} %collective-permute-done.9.pair_ref, f32[768,128]{1,0:T(8,128)} %collective-permute-done.10.other_ref, f32[10,1,128]{2,1,0:T(1,128)S(1)} %copy.14.diagonal_ref, ...), custom_call_target="tpu_custom_call" | custom-call | tf_op jit(solution)/shard_map/later_phase/pallas_call | solution.py:588
  157.8 38.7 %all_to_all.76 = f32[32,64,128]{2,1,0:T(8,128)S(1)} all-to-all(f32[32,64,128]{2,1,0:T(8,128)S(1)} %bitcast.67), channel_id=1, replica_groups=mesh['bx'=8,'by'=4] {'bx','by'}, dimensions={0} | all-to-all | bytes 2097152 | tf_op jit(solution)/shard_map/all_to_all | solution.py:666
  198.6 4.7 %later_phase.6 = f32[2048,128]{1,0:T(8,128)S(1)} custom-call(f32[3]{0:T(128)S(1)} %copy-done.12, f32[2048,128]{1,0:T(8,128)S(1)} %bitcast.54, f32[1024,128]{1,0:T(8,128)S(1)} %collective-permute-done.11.pair_ref, f32[1024,128]{1,0:T(8,128)S(1)} %collective-permute-done.12.other_ref, f32[6,1,256]{2,1,0:T(1,128)S(1)} %broadcast_in_dim.18.diagonal_ref, ...), custom_call_target="tpu_custom_call" | custom-call | tf_op jit(solution)/shard_map/later_phase/pallas_call | solution.py:588
  203.4 38.3 %all_to_all.77 = f32[32,64,128]{2,1,0:T(8,128)S(1)} all-to-all(f32[32,64,128]{2,1,0:T(8,128)S(1)} %bitcast.64), channel_id=1, replica_groups=mesh['bx'=8,'by'=4] {'bx','by'}, dimensions={0} | all-to-all | bytes 2097152 | tf_op jit(solution)/shard_map/all_to_all | solution.py:666
  243.3 3.7 later_phase.7
  247.0 35.9 %all_to_all.78 = f32[32,64,128]{2,1,0:T(8,128)S(1)} all-to-all(f32[32,64,128]{2,1,0:T(8,128)S(1)} %bitcast.60), channel_id=1, replica_groups=mesh['bx'=8,'by'=4] {'bx','by'}, dimensions={0} | all-to-all | bytes 2097152 | tf_op jit(solution)/shard_map/all_to_all | solution.py:666
  284.5 3.3 later_phase.8
  287.8 35.9 %all_to_all.79 = f32[32,64,128]{2,1,0:T(8,128)S(1)} all-to-all(f32[32,64,128]{2,1,0:T(8,128)S(1)} %bitcast.63), channel_id=1, replica_groups=mesh['bx'=8,'by'=4] {'bx','by'}, dimensions={0} | all-to-all | bytes 2097152 | tf_op jit(solution)/shard_map/all_to_all | solution.py:666
  325.8 4.0 %later_phase.9 = f32[4,4,64,256]{3,2,1,0:T(8,128)S(1)} custom-call(f32[3]{0:T(128)S(1)} %copy-done.12, f32[2048,128]{1,0:T(8,128)S(1)} %bitcast.52, f32[1024,128]{1,0:T(8,128)S(1)} %collective-permute-done.17.pair_ref, f32[1024,128]{1,0:T(8,128)S(1)} %collective-permute-done.18.other_ref, f32[6,1,256]{2,1,0:T(1,128)S(1)} %broadcast_in_dim.18.diagonal_ref, ...), custom_call_target="tpu_custom_call" | custom-call | tf_op jit(solution)/shard_map/later_phase/pallas_call | solution.py:588
  329.9 25.7 %all_to_all.80 = f32[16,64,256]{2,1,0:T(8,128)S(1)} all-to-all(f32[16,64,256]{2,1,0:T(8,128)S(1)} %bitcast.62), channel_id=1, replica_groups=mesh['bx'=8,'by'=4] {'by'}, dimensions={0} | all-to-all | bytes 2097152 | tf_op jit(solution)/shard_map/all_to_all | solution.py:739
  355.6 7.8 %sample.1 = (f32[32,2,128]{2,1,0:T(2,128)S(1)}, f32[1024,256]{1,0:T(8,128)}) custom-call(s32[1]{0:T(128)} %bitcast.flip_ref, s32[16,2]{1,0:T(8,128)S(1)} %copy-done.17, f32[64,128]{1,0:T(8,128)S(1)} %copy-done.11, f32[1024,256]{1,0:T(8,128)S(1)} %bitcast.61), custom_call_target="tpu_custom_call" | custom-call | tf_op jit(solution)/shard_map/sample/pallas_call | solution.py:355
  363.4 10.9 %all_to_all.81 = f32[32,2,128]{2,1,0:T(2,128)S(1)} all-to-all(f32[32,2,128]{2,1,0:T(2,128)S(1)} %get-tuple-element.47), channel_id=1, replica_groups=mesh['bx'=8,'by'=4] {'bx','by'}, dimensions={0} | all-to-all | bytes 65536 | tf_op jit(solution)/shard_map/all_to_all | solution.py:666
  374.3 1.6 unpack.1
  (98 shorter events, 26.6 us)
Async XLA Ops:
  9.9 17.9 %all-to-all-start = ((f32[32,16,128]{2,1,0:T(8,128)}), f32[32,16,128]{2,1,0:T(8,128)S(1)}, u32[]{:S(2)}, u32[]{:S(2)}) async-start(f32[32,16,128]{2,1,0:T(8,128)} %get-tuple-element.25), calls=%async_computation | async-start | bytes 524288 | tf_op jit(solution)/shard_map/all_to_all | solution.py:666
  42.2 4.3 %collective-permute-start = (f32[64,256]{1,0:T(8,128)S(1)}, f32[64,256]{1,0:T(8,128)S(1)}, u32[]{:S(2)}, u32[]{:S(2)}) collective-permute-start(f32[64,256]{1,0:T(8,128)S(1)} %get-tuple-element.29), channel_id=1, source_target_pairs={{0,4},{8,12},{16,20},{24,28},{4,0},{12,8},{20,16},{28,24},{1,5},{9... | collective-permute-start | bytes 196616 | tf_op jit(solution)/shard_map/ppermute | solution.py:374
  43.1 3.4 collective-permute-start.1
  43.8 1.2 collective-permute-start.2
  43.9 1.2 collective-permute-start.3
  49.7 40.1 %copy-start = (f32[256,256]{1,0:T(8,128)S(1)}, f32[256,256]{1,0:T(8,128)}, u32[]{:S(2)}) copy-start(f32[256,256]{1,0:T(8,128)} %first_any.11) | copy-start | bytes 786436
  49.7 40.1 %copy-start.3 = (f32[128,128]{1,0:T(8,128)S(1)}, f32[128,128]{1,0:T(8,128)}, u32[]{:S(2)}) copy-start(f32[128,128]{1,0:T(8,128)} %second_any.10) | copy-start | bytes 196612
  49.7 40.0 %all-to-all-start.1 = ((f32[32,80,128]{2,1,0:T(8,128)}), f32[32,80,128]{2,1,0:T(8,128)S(1)}, u32[]{:S(2)}, u32[]{:S(2)}) async-start(f32[32,80,128]{2,1,0:T(8,128)} %get-tuple-element.33), calls=%async_computation.1 | async-start | bytes 2621440 | tf_op jit(solution)/shard_map/all_to_all | solution.py:666
  92.6 1.4 copy-start.2
  93.9 52.7 %all-to-all-start.2 = ((f32[32,128,128]{2,1,0:T(8,128)}), f32[32,128,128]{2,1,0:T(8,128)}, u32[]{:S(2)}, u32[]{:S(2)}) async-start(f32[32,128,128]{2,1,0:T(8,128)} %bitcast.65), calls=%async_computation.2 | async-start | bytes 4194304 | tf_op jit(solution)/shard_map/all_to_all | solution.py:666
  97.6 1.2 copy-start.6
  99.9 1.9 collective-permute-start.4
  100.1 24.1 %collective-permute-start.5 = (f32[4,64,256]{2,1,0:T(8,128)S(1)}, f32[4,64,256]{2,1,0:T(8,128)S(1)}, u32[]{:S(2)}, u32[]{:S(2)}) collective-permute-start(f32[4,64,256]{2,1,0:T(8,128)S(1)} %get-tuple-element.61), channel_id=1, source_target_pairs={{0,2},{1,3},{2,0},{3,1},{4,6},{5,7},{6,4},{7,5},{8,10},{9,11},{10,... | collective-permute-start | bytes 786440 | tf_op jit(solution)/shard_map/ppermute | solution.py:679
  101.8 29.0 %collective-permute-start.6 = (f32[4,64,256]{2,1,0:T(8,128)S(1)}, f32[4,64,256]{2,1,0:T(8,128)S(1)}, u32[]{:S(2)}, u32[]{:S(2)}) collective-permute-start(f32[4,64,256]{2,1,0:T(8,128)S(1)} %get-tuple-element.60), channel_id=1, source_target_pairs={{0,3},{1,2},{2,1},{3,0},{4,7},{5,6},{6,5},{7,4},{8,11},{9,10},{10,... | collective-permute-start | bytes 786440 | tf_op jit(solution)/shard_map/ppermute | solution.py:679
  131.5 4.9 %copy-start.19 = (f32[4,256,256]{2,1,0:T(8,128)S(1)}, f32[4,256,256]{2,1,0:T(8,128)}, u32[]{:S(2)}) copy-start(f32[4,256,256]{2,1,0:T(8,128)} %constant_dynamic-update-slice_fusion.2) | copy-start | bytes 3145732
  132.6 2.6 collective-permute-start.7
  133.3 3.1 collective-permute-start.8
  136.5 15.1 %copy-start.1 = (f32[256,256]{1,0:T(8,128)S(1)}, f32[256,256]{1,0:T(8,128)}, u32[]{:S(2)}) copy-start(f32[256,256]{1,0:T(8,128)} %second_any.11) | copy-start | bytes 786436
  148.7 2.9 collective-permute-start.9
  148.7 2.9 collective-permute-start.10
  196.6 2.0 collective-permute-start.11
  196.7 1.9 collective-permute-start.12
  241.7 1.6 collective-permute-start.13
  241.8 1.5 collective-permute-start.14
  282.9 1.6 collective-permute-start.15
  283.0 1.5 collective-permute-start.16
  323.9 2.0 collective-permute-start.17
  323.9 1.9 collective-permute-start.18
  329.8 25.8 %copy-start.11 = (f32[64,128]{1,0:T(8,128)S(1)}, f32[64,128]{1,0:T(8,128)}, u32[]{:S(2)}) copy-start(f32[64,128]{1,0:T(8,128)} %copy-done.10) | copy-start | bytes 98308
  329.8 25.8 %copy-start.17 = (s32[16,2]{1,0:T(8,128)S(1)}, s32[16,2]{1,0:T(8,128)}, u32[]{:S(2)}) copy-start(s32[16,2]{1,0:T(8,128)} %copy-done.16) | copy-start | bytes 388
  329.9 44.4 %copy-start.9 = (s32[4096,1]{0,1:T(1,128)S(1)}, s32[4096,1]{0,1:T(1,128)}, u32[]{:S(2)}) copy-start(s32[4096,1]{0,1:T(1,128)} %param.8) | copy-start | bytes 49156
  329.9 44.4 %copy-start.14 = (f32[1,4096]{1,0:T(1,128)S(1)}, f32[1,4096]{1,0:T(1,128)}, u32[]{:S(2)}) copy-start(f32[1,4096]{1,0:T(1,128)} %copy-done.13) | copy-start | bytes 49156
  (10 other events, 7.5 us)

commit v8 on v7

--- a/solution.py
+++ b/solution.py
@@ -43,12 +43,17 @@
     return lax.dot_general(rows, columns, (((1,), (1,)), ((), ())), preferred_element_type=jnp.float32)
 
 
-def pack_kernel(level_ref, owner_ref, cell_ref, normal_ref, send_ref, slot_ref, total_ref):
+def pack_kernel(
+    level_ref, owner_any, cell_any, normal_any, send_ref, slot_ref, total_ref, owner_ref, cell_ref, normal_ref, sem_ref
+):
     bricks, capacity = send_ref.shape[0], total_ref.shape[1]
     points = owner_ref.shape[1]
     block = 256
+    copies = fetch([(owner_any, owner_ref), (cell_any, cell_ref), (normal_any, normal_ref)], sem_ref)
     earlier = rows_iota(block, block) < lax.broadcasted_iota(jnp.int32, (block, block), 1)
     total_ref[...] = jnp.zeros_like(total_ref)
+    for copy in copies:
+        copy.wait()
 
     def names(at):
         here = pl.ds(pl.multiple_of(at * block, block), block)
@@ -118,9 +123,15 @@
             jax.ShapeDtypeStruct((bricks, 4 * capacity // 128 // 8 * 8 + 8, 128), jnp.float32),
             jax.ShapeDtypeStruct((1, points), jnp.float32),
         ),
-        in_specs=[pl.BlockSpec(memory_space=pltpu.SMEM)] + whole_arrays(3),
+        in_specs=[pl.BlockSpec(memory_space=pltpu.SMEM)] + [pl.BlockSpec(memory_space=pl.ANY)] * 3,
         out_specs=tuple(whole_arrays(2)),
-        scratch_shapes=[pltpu.VMEM((12 * bricks, capacity), jnp.float32)],
+        scratch_shapes=[
+            pltpu.VMEM((12 * bricks, capacity), jnp.float32),
+            pltpu.VMEM((1, points), jnp.int32),
+            pltpu.VMEM((1, points), jnp.int32),
+            pltpu.VMEM((3, points), jnp.float32),
+            pltpu.SemaphoreType.DMA((3,)),
+        ],
         compiler_params=pltpu.CompilerParams(vmem_limit_bytes=16 << 20),
         name="pack",
     )(levels, owners.reshape(1, points), cells.reshape(1, points), normals)
@@ -435,13 +446,31 @@
     return jnp.concatenate(bands, axis=0)
 
 
-def diagonal_of(ref, k, turned, shape):
-    if ref.shape[0] == 1:
-        return ref[0]
-    if not turned:
-        return ref[k]
-    column = jnp.broadcast_to(ref[k], (128, shape[0])).T
-    return jnp.concatenate([column] * (shape[1] // 128), axis=1)
+def diagonals(layout, counts, planes, level_ref, me, shape):
+    first_count, second_count = counts
+
+    def row(count, width, at):
+        block = lax.broadcasted_iota(jnp.int32, (1, count * width), 1) // width
+        value = jnp.zeros((1, count * width), jnp.float32)
+        for i in range(count):
+            value = jnp.where(block == i, level_ref[at(i)], value)
+        return 6.0 + screen_base * (1.0 + value)
+
+    if layout == 0:
+        rows = [row(second_count, CY, lambda j: i * second_count + j) for i in range(first_count)]
+        whole = jnp.concatenate([jnp.broadcast_to(value, (CX, shape[1])) for value in rows], axis=0)
+        return lambda k: whole
+
+    def along_x(k):
+        i = jnp.clip(me * planes - 1 + k, 0, first_count * CX - 1) // CX
+        column = jnp.broadcast_to(row(second_count, CY, lambda j: i * second_count + j), (128, shape[0])).T
+        return jnp.concatenate([column] * (shape[1] // 128), axis=1)
+
+    def along_y(k):
+        j = jnp.clip(me * planes - 1 + k, 0, second_count * CY - 1) // CY
+        return row(first_count, CX, lambda i: i * second_count + j)
+
+    return along_x if layout == 2 else along_y
 
 
 def fetch(pairs, sem_ref):
@@ -451,12 +480,11 @@
     return copies
 
 
-def sweep_all(count, step_ref, source_ref, diagonal_ref, turned, matrix_ref, emit):
+def sweep_all(count, step_ref, source_ref, diagonal, matrix_ref, emit):
     matrix = wide(matrix_ref[...])
     for k in range(count):
         middle = step_ref[k + 1]
-        diagonal = diagonal_of(diagonal_ref, k + 1, turned, middle.shape)
-        remainder = remainder_of(source_ref[k + 1], step_ref[k], middle, step_ref[k + 2], diagonal)
+        remainder = remainder_of(source_ref[k + 1], step_ref[k], middle, step_ref[k + 2], diagonal(k + 1))
         high, low = parts_of(remainder, 2)
         row = jnp.concatenate([high, low, high], axis=1)
         step = lax.dot_general(row, matrix, (((1,), (1,)), ((), ())), preferred_element_type=jnp.float32)
@@ -464,7 +492,7 @@
 
 
 def first_kernel(
-    grid, held_ref, diagonal_ref, first_any, second_any, sent_ref, source_ref, step_ref, first_ref, second_ref, sem_ref
+    grid, level_ref, held_ref, first_any, second_any, sent_ref, source_ref, step_ref, first_ref, second_ref, sem_ref
 ):
     copies = fetch([(first_any, first_ref), (second_any, second_ref)], sem_ref)
     first_count, second_count, planes, per_target = grid
@@ -483,13 +511,14 @@
         put(sent_ref, k, planes, order, block, [(1, 0, last + 1)], value)
 
     copies[1].wait()
-    sweep_all(planes, step_ref, source_ref, diagonal_ref, False, second_ref, emit)
+    diagonal = diagonals(0, grid[:2], planes, level_ref, 0, step_ref.shape[1:])
+    sweep_all(planes, step_ref, source_ref, diagonal, second_ref, emit)
 
 
 def later_kernel(
-    shape, edge_ref, held_ref, pair_ref, other_ref, diagonal_ref, first_any, second_any, *refs
+    shape, edge_ref, level_ref, held_ref, pair_ref, other_ref, first_any, second_any, *refs
 ):
-    order, planes, rows, with_source, last, turned = shape
+    order, planes, rows, with_source, last, layout, counts = shape
     devices = len(order)
     *refs, first_ref, second_ref, sem_ref = refs
     copies = fetch([(first_any, first_ref), (second_any, second_ref)], sem_ref)
@@ -518,17 +547,17 @@
         iterate_ref[planes + 2 + k] = edge(True, k + with_source)
     for k in range(planes):
         iterate_ref[k + 2] = own(k + with_source)
+    diagonal = diagonals(layout, counts, planes, level_ref, edge_ref[3], step_ref.shape[1:])
     copies[0].wait()
     first = wide(first_ref[...])
     for k in range(planes + 2):
         middle = iterate_ref[k + 1]
-        diagonal = diagonal_of(diagonal_ref, k, turned, middle.shape)
-        remainder = remainder_of(source_ref[k], iterate_ref[k], middle, iterate_ref[k + 2], diagonal)
+        remainder = remainder_of(source_ref[k], iterate_ref[k], middle, iterate_ref[k + 2], diagonal(k))
         step = jnp.dot(first, parts_in_rows(remainder), preferred_element_type=jnp.float32)
         if k == 0:
-            step = step * edge_ref[0]
+            step = step * edge_ref[0].astype(jnp.float32)
         if k == planes + 1:
-            step = step * edge_ref[1]
+            step = step * edge_ref[1].astype(jnp.float32)
         step_ref[k] = middle + step
 
     def emit(k, value):
@@ -540,7 +569,7 @@
             put(sent_ref, k, planes, order, sent_ref.shape[0] // devices, [(0, 0, per_target)], value)
 
     copies[1].wait()
-    sweep_all(planes, step_ref, source_ref, diagonal_ref, turned, second_ref, emit)
+    sweep_all(planes, step_ref, source_ref, diagonal, second_ref, emit)
 
 
 ANY = pl.BlockSpec(memory_space=pl.ANY)
@@ -553,8 +582,8 @@
     return [pltpu.VMEM(matrix.shape, jnp.float32) for matrix in (first, second)] + [pltpu.SemaphoreType.DMA((2,))]
 
 
-def first_phase(grid, held, diagonal, first, second):
-    rows, columns = diagonal.shape[1:]
+def first_phase(grid, levels, held, first, second):
+    rows, columns = len(first), len(second)
     first_count, second_count, planes, per_target = grid
     return pl.pallas_call(
         functools.partial(first_kernel, grid),
@@ -562,16 +591,16 @@
             jax.ShapeDtypeStruct((2 * columns * planes * rows // 128, 128), jnp.float32),
             jax.ShapeDtypeStruct((planes + 2, rows, columns), jnp.float32),
         ),
-        in_specs=[VMEM] * 2 + [ANY] * 2,
+        in_specs=[SMEM, VMEM] + [ANY] * 2,
         out_specs=(VMEM, VMEM),
         scratch_shapes=[pltpu.VMEM((planes + 2, rows, columns), jnp.float32)] + matrix_scratch(first, second),
         compiler_params=LIMIT,
         name="first_phase",
-    )(held, diagonal, first, second)
+    )(levels, held, first, second)
 
 
 def later_phase(
-    order, planes, rows, turned, edges, held, pair, other, diagonal, first, second, source=None, last=False
+    order, planes, rows, layout, counts, edges, levels, held, pair, other, first, second, source=None, last=False
 ):
     columns = second.shape[1]
     length = len(order) * rows
@@ -580,15 +609,15 @@
     else:
         sent = (columns * planes * length // 128, 128)
     out = [jax.ShapeDtypeStruct(sent, jnp.float32)]
-    operands = [edges, held, pair, other, diagonal, first, second]
+    operands = [edges, levels, held, pair, other, first, second]
     if source is None:
         out.append(jax.ShapeDtypeStruct((planes + 2, length, columns), jnp.float32))
     else:
         operands.append(source)
     return pl.pallas_call(
-        functools.partial(later_kernel, (order, planes, rows, source is None, last, turned)),
+        functools.partial(later_kernel, (order, planes, rows, source is None, last, layout, counts)),
         out_shape=tuple(out),
-        in_specs=[SMEM] + [VMEM] * 4 + [ANY] * 2 + [VMEM] * (len(operands) - 7),
+        in_specs=[SMEM] * 2 + [VMEM] * 3 + [ANY] * 2 + [VMEM] * (len(operands) - 7),
         out_specs=tuple([VMEM] * len(out)),
         scratch_shapes=[
             pltpu.VMEM((planes + 4, length, columns), jnp.float32),
@@ -656,10 +685,10 @@
 def beside(to_next, to_previous, even):
     order = slab_order(lax.axis_size("bx"), lax.axis_size("by"))
     got = []
-    for start, value in ((0, jnp.where(even, to_next, to_previous)), (1, jnp.where(even, to_previous, to_next))):
+    for start, value in ((1, jnp.where(even, to_previous, to_next)), (0, jnp.where(even, to_next, to_previous))):
         pairs = [(order[i], order[i + 1]) for i in range(start, len(order) - 1, 2)]
         got.append(lax.ppermute(value, EVERY, pairs + [(j, i) for i, j in pairs]))
-    return got
+    return got[::-1]
 
 
 def exchange(value):
@@ -690,19 +719,11 @@
     even = me % 2 == 0
     nx, ny = first_count * CX, second_count * CY
     thick = (NZ // devices, ny // devices, nx // devices)
-    diagonal = 6.0 + screen_base * (1.0 + levels.reshape(first_count, second_count))
-    diagonal = jnp.repeat(jnp.repeat(diagonal, CX, 0), CY, 1)
-    padded = jnp.pad(diagonal, ((1, 1), (1, 1)), constant_values=1.0)
-    diagonals = (
-        diagonal[None],
-        lax.dynamic_slice_in_dim(padded, me * thick[1], thick[1] + 2, 1).T[:, None, 1:-1],
-        lax.dynamic_slice_in_dim(padded, me * thick[2], thick[2] + 2, 0)[:, None, 1:-1],
-    )
-    edges = jnp.stack([me > 0, me < devices - 1, even]).astype(jnp.float32)
+    edges = jnp.stack([me > 0, me < devices - 1, even, me]).astype(jnp.int32)
     matrices = (rows_inverse, columns_inverse, depth_inverse)
-    held, diagonals = lax.optimization_barrier((exchange(sent), diagonals))
+    held = exchange(sent)
     sent, z_source = first_phase(
-        (first_count, second_count, thick[0], thick[1]), held.reshape(-1, 2 * CY), diagonals[0], matrices[0], matrices[1]
+        (first_count, second_count, thick[0], thick[1]), levels, held.reshape(-1, 2 * CY), matrices[0], matrices[1]
     )
     sources = [z_source, None, None]
     for step in range(1, 3 * ITERS // 2):
@@ -721,12 +742,13 @@
             order,
             planes,
             rows,
-            at == 2,
+            at,
+            (first_count, second_count),
             edges,
+            levels,
             held,
             pair,
             other,
-            diagonals[at],
             matrices[2 * step % 3],
             matrices[(2 * step + 1) % 3],
             source=sources[at],

time: 378 us -> 374 us (0.989)
  local copies, waits for them, and re-layouts: 14.6 us -> 9.3 us
    unnamed x41 -> x25, local copies, waits for them, and re-layouts: 9.96 us -> 6.65 us
  transfers between devices with their start and end apart: 22 -> 22, of which waited for: 12 -> 13; matrix products, arithmetic and copies ran while one was open for 2% -> 1% of each run, Pallas kernels for 0% -> 0%
where the time goes in v8:
time: 374 us
  blocking collectives  186 us (50%)
  waiting for transfers between devices  87.3 us (23%)
  Pallas kernels  54.5 us (15%)
  starting transfers between devices  30.9 us (8%)
  local copies, waits for them, and re-layouts  9.3 us (2%)
  other arithmetic  3.82 us (1%)
    all_to_all x5, blocking collectives, exchange(): return lax.all_to_all(value, EVERY, split_axis=0, concat_axis=0, tiled=True)  161 us
    all_to_all x3, waiting for transfers between devices, exchange(): return lax.all_to_all(value, EVERY, split_axis=0, concat_axis=0, tiled=True)  52.4 us
    ppermute x3, waiting for transfers between devices, x_slab_source(): lax.ppermute(piece, 'by', [(i, i ^ turn) for i in range(second_count)])  27.5 us
    all_to_all x1, blocking collectives, relax(): return lax.all_to_all(sent, 'by', split_axis=0, concat_axis=0, tiled=True)  25.6 us
    pallas_call x5, Pallas kernels, later_phase(): pl.pallas_call(functools.partial(later_kernel, (order, planes, rows, sour...  20.3 us
    all_to_all x3, starting transfers between devices, exchange(): return lax.all_to_all(value, EVERY, split_axis=0, concat_axis=0, tiled=True)  19.3 us
    pallas_call x1, Pallas kernels, splat(): pl.pallas_call(splat_kernel, out_shape=tuple(out + [jax.ShapeDtypeStruct(...  13.3 us
    pallas_call x1, Pallas kernels, sample(): pl.pallas_call(functools.partial(sample_kernel, blocks), out_shape=tuple(...  8.09 us
  transfers between devices with their start and end apart: 22, of which 13 were waited for; matrix products, arithmetic and copies ran while one was open for 1% of the time, Pallas kernels for 0%

profile of v8, /device:TPU:0, one launch (start us, length us, event | category | flops | bytes accessed | tf_op | source)
XLA Modules:
  0.0 374.0 jit_solution(10474029031817617276)
XLA Ops:
  3.6 5.9 %pack.1 = (f32[32,16,128]{2,1,0:T(8,128)}, f32[1,4096]{1,0:T(1,128)S(1)}) custom-call(s32[1,1]{1,0:T(1,128)S(6)} %copy.16.level_ref, s32[1,4096]{1,0:T(1,128)S(1)} %bitcast.62, s32[1,4096]{1,0:T(1,128)S(1)} %bitcast.64, f32[3,4096]{1,0:T(4,128)S(1)} %copy-done.6), custom_call_target="tpu_custom_call" | custom-call | tf_op jit(solution)/shard_map/pack/pallas_call | solution.py:120
  9.5 7.3 %all-to-all-start = ((f32[32,16,128]{2,1,0:T(8,128)}), f32[32,16,128]{2,1,0:T(8,128)S(1)}, u32[]{:S(2)}, u32[]{:S(2)}) async-start(f32[32,16,128]{2,1,0:T(8,128)} %get-tuple-element.21), calls=%async_computation | async-start | bytes 524288 | tf_op jit(solution)/shard_map/all_to_all | solution.py:695
  16.9 10.5 %all-to-all-done.held_ref = f32[32,16,128]{2,1,0:T(8,128)S(1)} async-done(((f32[32,16,128]{2,1,0:T(8,128)}), f32[32,16,128]{2,1,0:T(8,128)S(1)}, u32[]{:S(2)}, u32[]{:S(2)}) %all-to-all-start) | async-done | bytes 262176 | tf_op jit(solution)/shard_map/all_to_all | solution.py:695
  27.4 13.3 %splat.1 = (f32[1024,256]{1,0:T(8,128)S(1)}, f32[64,256]{1,0:T(8,128)S(1)}, f32[64,256]{1,0:T(8,128)S(1)}, f32[16,256]{1,0:T(8,128)S(1)}, f32[16,256]{1,0:T(8,12...) custom-call(s32[2]{0:T(128)S(1)} %add_convert_fusion.even_ref, f32[32,16,128]{2,1,0:T(8,128)S(1)} %all-to-all-done.held_ref), custom_call_target="tpu_custom_call" | custom-call | tf_op jit(solution)/shard_map/splat/pallas_call | solution.py:298
  43.5 1.5 collective-permute-done.x_pair_ref
  45.0 2.3 join.1
  48.2 8.3 %all-to-all-start.1 = ((f32[32,80,128]{2,1,0:T(8,128)}), f32[32,80,128]{2,1,0:T(8,128)S(1)}, u32[]{:S(2)}, u32[]{:S(2)}) async-start(f32[32,80,128]{2,1,0:T(8,128)} %get-tuple-element.29), calls=%async_computation.1 | async-start | bytes 2621440 | tf_op jit(solution)/shard_map/all_to_all | solution.py:695
  56.9 31.8 %all-to-all-done.1 = f32[32,80,128]{2,1,0:T(8,128)S(1)} async-done(((f32[32,80,128]{2,1,0:T(8,128)}), f32[32,80,128]{2,1,0:T(8,128)S(1)}, u32[]{:S(2)}, u32[]{:S(2)}) %all-to-all-start.1) | async-done | bytes 1310752 | tf_op jit(solution)/shard_map/all_to_all | solution.py:695
  88.7 3.2 first_phase.1
  91.9 1.3 copy-done.2
  93.2 3.7 all-to-all-start.2
  99.4 1.7 collective-permute-start.5
  101.8 21.6 %collective-permute-done.5 = f32[4,64,256]{2,1,0:T(8,128)S(1)} collective-permute-done((f32[4,64,256]{2,1,0:T(8,128)S(1)}, f32[4,64,256]{2,1,0:T(8,128)S(1)}, u32[]{:S(2)}, u32[]{:S(2)}) %collective-permute-start.5) | collective-permute-done | bytes 262176 | tf_op jit(solution)/shard_map/ppermute | solution.py:708
  124.2 5.9 %collective-permute-done.6 = f32[4,64,256]{2,1,0:T(8,128)S(1)} collective-permute-done((f32[4,64,256]{2,1,0:T(8,128)S(1)}, f32[4,64,256]{2,1,0:T(8,128)S(1)}, u32[]{:S(2)}, u32[]{:S(2)}) %collective-permute-start.6) | collective-permute-done | bytes 262176 | tf_op jit(solution)/shard_map/ppermute | solution.py:708
  132.6 1.9 collective-permute-start.8
  134.5 1.2 collective-permute-done.8
  135.9 10.1 %all-to-all-done.2 = f32[32,128,128]{2,1,0:T(8,128)} async-done(((f32[32,128,128]{2,1,0:T(8,128)}), f32[32,128,128]{2,1,0:T(8,128)}, u32[]{:S(2)}, u32[]{:S(2)}) %all-to-all-start.2) | async-done | bytes 2097184 | tf_op jit(solution)/shard_map/all_to_all | solution.py:695
  145.9 2.0 slice_select_fusion.4
  148.0 1.4 collective-permute-start.10
  150.1 4.6 %later_phase.5 = (f32[2048,128]{1,0:T(8,128)S(1)}, f32[10,256,128]{2,1,0:T(8,128)S(1)}) custom-call(s32[4]{0:T(128)S(1)} %pad_add_fusion.edge_ref, f32[32]{0:T(128)S(1)} %slice_reduce_fusion.level_ref, f32[4096,128]{1,0:T(8,128)} %bitcast.11.held_ref, f32[768,128]{1,0:T(8,128)} %collective-permute-done.9.pair_ref, ...), custom_call_target="tpu_custom_call" | custom-call | tf_op jit(solution)/shard_map/later_phase/pallas_call | solution.py:617
  154.6 39.6 %all_to_all.76 = f32[32,64,128]{2,1,0:T(8,128)S(1)} all-to-all(f32[32,64,128]{2,1,0:T(8,128)S(1)} %bitcast.60), channel_id=1, replica_groups=mesh['bx'=8,'by'=4] {'bx','by'}, dimensions={0} | all-to-all | bytes 2097152 | tf_op jit(solution)/shard_map/all_to_all | solution.py:695
  196.4 4.8 %later_phase.6 = f32[2048,128]{1,0:T(8,128)S(1)} custom-call(s32[4]{0:T(128)S(1)} %pad_add_fusion.edge_ref, f32[32]{0:T(128)S(1)} %slice_reduce_fusion.level_ref, f32[2048,128]{1,0:T(8,128)S(1)} %bitcast.47, f32[1024,128]{1,0:T(8,128)S(1)} %collective-permute-done.11.pair_ref, f32[1024,128]{1,0:T(8,128)S(1)} %collective-permute-done.12.other_ref, ...), custom_call_target="tpu_custom_call" | custom-call | tf_op jit(solution)/shard_map/later_phase/pallas_call | solution.py:617
  201.1 38.3 %all_to_all.77 = f32[32,64,128]{2,1,0:T(8,128)S(1)} all-to-all(f32[32,64,128]{2,1,0:T(8,128)S(1)} %bitcast.57), channel_id=1, replica_groups=mesh['bx'=8,'by'=4] {'bx','by'}, dimensions={0} | all-to-all | bytes 2097152 | tf_op jit(solution)/shard_map/all_to_all | solution.py:695
  241.1 3.6 later_phase.7
  244.7 35.9 %all_to_all.78 = f32[32,64,128]{2,1,0:T(8,128)S(1)} all-to-all(f32[32,64,128]{2,1,0:T(8,128)S(1)} %bitcast.53), channel_id=1, replica_groups=mesh['bx'=8,'by'=4] {'bx','by'}, dimensions={0} | all-to-all | bytes 2097152 | tf_op jit(solution)/shard_map/all_to_all | solution.py:695
  282.3 3.3 later_phase.8
  285.6 35.9 %all_to_all.79 = f32[32,64,128]{2,1,0:T(8,128)S(1)} all-to-all(f32[32,64,128]{2,1,0:T(8,128)S(1)} %bitcast.54), channel_id=1, replica_groups=mesh['bx'=8,'by'=4] {'bx','by'}, dimensions={0} | all-to-all | bytes 2097152 | tf_op jit(solution)/shard_map/all_to_all | solution.py:695
  323.6 4.0 %later_phase.9 = f32[4,4,64,256]{3,2,1,0:T(8,128)S(1)} custom-call(s32[4]{0:T(128)S(1)} %pad_add_fusion.edge_ref, f32[32]{0:T(128)S(1)} %slice_reduce_fusion.level_ref, f32[2048,128]{1,0:T(8,128)S(1)} %bitcast.45, f32[1024,128]{1,0:T(8,128)S(1)} %collective-permute-done.17.pair_ref, f32[1024,128]{1,0:T(8,128)S(1)} %collective-permute-done.18.other_ref, ...), custom_call_target="tpu_custom_call" | custom-call | tf_op jit(solution)/shard_map/later_phase/pallas_call | solution.py:617
  327.6 25.6 %all_to_all.80 = f32[16,64,256]{2,1,0:T(8,128)S(1)} all-to-all(f32[16,64,256]{2,1,0:T(8,128)S(1)} %bitcast.56), channel_id=1, replica_groups=mesh['bx'=8,'by'=4] {'by'}, dimensions={0} | all-to-all | bytes 2097152 | tf_op jit(solution)/shard_map/all_to_all | solution.py:761
  353.2 8.1 %sample.1 = (f32[32,2,128]{2,1,0:T(2,128)S(1)}, f32[1024,256]{1,0:T(8,128)}) custom-call(s32[1]{0:T(128)} %bitcast.flip_ref, s32[16,2]{1,0:T(8,128)S(1)} %get-tuple-element.22.bound_ref, f32[64,128]{1,0:T(8,128)S(1)} %get-tuple-element.23.field_ref, f32[1024,256]{1,0:T(8,128)S(1)} %bitcast.55), custom_call_target="tpu_custom_call" | custom-call | tf_op jit(solution)/shard_map/sample/pallas_call | solution.py:366
  361.3 11.1 %all_to_all.81 = f32[32,2,128]{2,1,0:T(2,128)S(1)} all-to-all(f32[32,2,128]{2,1,0:T(2,128)S(1)} %get-tuple-element.39), channel_id=1, replica_groups=mesh['bx'=8,'by'=4] {'bx','by'}, dimensions={0} | all-to-all | bytes 65536 | tf_op jit(solution)/shard_map/all_to_all | solution.py:695
  372.4 1.5 unpack.1
  (70 shorter events, 21.2 us)
Async XLA Ops:
  1.3 0.8 copy-start.6
  9.5 17.9 %all-to-all-start = ((f32[32,16,128]{2,1,0:T(8,128)}), f32[32,16,128]{2,1,0:T(8,128)S(1)}, u32[]{:S(2)}, u32[]{:S(2)}) async-start(f32[32,16,128]{2,1,0:T(8,128)} %get-tuple-element.21), calls=%async_computation | async-start | bytes 524288 | tf_op jit(solution)/shard_map/all_to_all | solution.py:695
  40.6 4.3 %collective-permute-start = (f32[64,256]{1,0:T(8,128)S(1)}, f32[64,256]{1,0:T(8,128)S(1)}, u32[]{:S(2)}, u32[]{:S(2)}) collective-permute-start(f32[64,256]{1,0:T(8,128)S(1)} %get-tuple-element.25), channel_id=1, source_target_pairs={{0,4},{8,12},{16,20},{24,28},{4,0},{12,8},{20,16},{28,24},{1,5},{9... | collective-permute-start | bytes 196616 | tf_op jit(solution)/shard_map/ppermute | solution.py:385
  41.6 3.4 collective-permute-start.1
  42.3 1.2 collective-permute-start.2
  42.3 1.2 collective-permute-start.3
  47.2 1.0 copy-start.4
  48.2 40.5 %copy-start.1 = (f32[256,256]{1,0:T(8,128)S(1)}, f32[256,256]{1,0:T(8,128)}, u32[]{:S(2)}) copy-start(f32[256,256]{1,0:T(8,128)} %first_any.11) | copy-start | bytes 786436
  48.2 40.5 %copy-start.3 = (f32[128,128]{1,0:T(8,128)S(1)}, f32[128,128]{1,0:T(8,128)}, u32[]{:S(2)}) copy-start(f32[128,128]{1,0:T(8,128)} %second_any.10) | copy-start | bytes 196612
  48.2 40.5 %all-to-all-start.1 = ((f32[32,80,128]{2,1,0:T(8,128)}), f32[32,80,128]{2,1,0:T(8,128)S(1)}, u32[]{:S(2)}, u32[]{:S(2)}) async-start(f32[32,80,128]{2,1,0:T(8,128)} %get-tuple-element.29), calls=%async_computation.1 | async-start | bytes 2621440 | tf_op jit(solution)/shard_map/all_to_all | solution.py:695
  91.9 1.3 copy-start.2
  93.2 52.7 %all-to-all-start.2 = ((f32[32,128,128]{2,1,0:T(8,128)}), f32[32,128,128]{2,1,0:T(8,128)}, u32[]{:S(2)}, u32[]{:S(2)}) async-start(f32[32,128,128]{2,1,0:T(8,128)} %bitcast.58), calls=%async_computation.2 | async-start | bytes 4194304 | tf_op jit(solution)/shard_map/all_to_all | solution.py:695
  96.9 1.2 copy-start.5
  98.2 1.0 copy-start.10
  99.2 1.9 collective-permute-start.4
  99.4 24.1 %collective-permute-start.5 = (f32[4,64,256]{2,1,0:T(8,128)S(1)}, f32[4,64,256]{2,1,0:T(8,128)S(1)}, u32[]{:S(2)}, u32[]{:S(2)}) collective-permute-start(f32[4,64,256]{2,1,0:T(8,128)S(1)} %get-tuple-element.53), channel_id=1, source_target_pairs={{0,2},{1,3},{2,0},{3,1},{4,6},{5,7},{6,4},{7,5},{8,10},{9,11},{10,... | collective-permute-start | bytes 786440 | tf_op jit(solution)/shard_map/ppermute | solution.py:708
  101.1 29.0 %collective-permute-start.6 = (f32[4,64,256]{2,1,0:T(8,128)S(1)}, f32[4,64,256]{2,1,0:T(8,128)S(1)}, u32[]{:S(2)}, u32[]{:S(2)}) collective-permute-start(f32[4,64,256]{2,1,0:T(8,128)S(1)} %get-tuple-element.52), channel_id=1, source_target_pairs={{0,3},{1,2},{2,1},{3,0},{4,7},{5,6},{6,5},{7,4},{8,11},{9,10},{10,... | collective-permute-start | bytes 786440 | tf_op jit(solution)/shard_map/ppermute | solution.py:708
  130.8 4.9 %copy-start.11 = (f32[4,256,256]{2,1,0:T(8,128)S(1)}, f32[4,256,256]{2,1,0:T(8,128)}, u32[]{:S(2)}) copy-start(f32[4,256,256]{2,1,0:T(8,128)} %constant_dynamic-update-slice_fusion) | copy-start | bytes 3145732
  131.9 2.6 collective-permute-start.7
  132.6 3.1 collective-permute-start.8
  135.8 14.2 %copy-start = (f32[256,256]{1,0:T(8,128)S(1)}, f32[256,256]{1,0:T(8,128)}, u32[]{:S(2)}) copy-start(f32[256,256]{1,0:T(8,128)} %second_any.11) | copy-start | bytes 786436
  148.0 2.1 collective-permute-start.9
  148.0 2.1 collective-permute-start.10
  194.4 2.0 collective-permute-start.11
  194.5 1.9 collective-permute-start.12
  239.5 1.6 collective-permute-start.13
  239.6 1.5 collective-permute-start.14
  280.7 1.6 collective-permute-start.15
  280.7 1.5 collective-permute-start.16
  321.6 2.0 collective-permute-start.17
  321.7 1.9 collective-permute-start.18
  327.6 44.8 %copy-start.8 = (s32[4096,1]{0,1:T(1,128)S(1)}, s32[4096,1]{0,1:T(1,128)}, u32[]{:S(2)}) copy-start(s32[4096,1]{0,1:T(1,128)} %param.8) | copy-start | bytes 49156
  (2 other events, 1.4 us)

commit v9 on v8

--- a/solution.py
+++ b/solution.py
@@ -137,11 +137,22 @@
     )(levels, owners.reshape(1, points), cells.reshape(1, points), normals)
 
 
-def unpack_kernel(owner_ref, rank_ref, held_ref, out_ref):
-    bricks, capacity = held_ref.shape
+def unpack_kernel(second_count, owner_ref, rank_ref, held_ref, out_ref):
+    bricks = held_ref.shape[0]
     points = owner_ref.shape[1]
     block = 512
-    held = jnp.concatenate([part.astype(jnp.float32).T for part in parts_of(held_ref[...], 3)], axis=1)
+    held = held_ref[...]
+    if len(held.shape) == 3:
+        halves = held.shape[1] // second_count
+        rows = []
+        for i in range(0, bricks, second_count):
+            rows.append(sum([held_ref[i + j] for j in range(second_count)]))
+        part = lambda row, half: row[half * second_count : (half + 1) * second_count, :]
+        held = jnp.concatenate(
+            [jnp.concatenate([part(row, half) for row in rows], axis=0) for half in range(halves)], axis=1
+        )
+    capacity = held.shape[1]
+    held = jnp.concatenate([part.astype(jnp.float32).T for part in parts_of(held, 3)], axis=1)
     held = held.astype(jnp.bfloat16)
     for at in range(points // block):
         here = slice(at * block, (at + 1) * block)
@@ -152,10 +163,10 @@
         out_ref[:, here] = jnp.sum(jnp.where(slot, found, 0.0), axis=0, keepdims=True)
 
 
-def unpack(owners, rank, held):
+def unpack(owners, rank, held, second_count):
     points = owners.shape[0]
     out = pl.pallas_call(
-        unpack_kernel,
+        functools.partial(unpack_kernel, second_count),
         out_shape=jax.ShapeDtypeStruct((1, points), jnp.float32),
         in_specs=whole_arrays(3),
         out_specs=pl.BlockSpec(memory_space=pltpu.VMEM),
@@ -230,12 +241,16 @@
         regroup(held_ref, field_ref)
     else:
         field_ref[...] = held_ref[...]
-    cell_ref[...] = field_ref[3 * chunks :, :]
+    cell_ref[:chunks, :] = field_ref[3 * chunks :, :]
+    lane = lax.broadcasted_iota(jnp.int32, (8, 128), 1)
+    bounds = jnp.zeros((8, 128), jnp.float32)
     for at in range(chunks // GROUP):
-        cell = cell_ref[GROUP * at : GROUP * (at + 1), :]
+        cell = field_ref[3 * chunks + GROUP * at : 3 * chunks + GROUP * (at + 1), :]
         x = places(cell)[0].astype(jnp.float32)
-        bound_ref[at, 0] = jnp.min(jnp.where(cell > 0, x, float(CX))).astype(jnp.int32)
-        bound_ref[at, 1] = jnp.max(jnp.where(cell > 0, x, -1.0)).astype(jnp.int32)
+        least, most = jnp.min(jnp.where(cell > 0, x, float(CX))), jnp.max(jnp.where(cell > 0, x, -1.0))
+        bound_ref[at, 0], bound_ref[at, 1] = least.astype(jnp.int32), most.astype(jnp.int32)
+        bounds = jnp.where(lane == at, jnp.where(rows_iota(8, 128) == 0, least, most), bounds)
+    cell_ref[chunks:, :] = bounds
     sum_ref[...] = jnp.zeros_like(sum_ref)
 
     def group(at, carry):
@@ -293,14 +308,15 @@
 
 
 def splat(held, even, chunks):
-    shapes = [(CX * CY, NZ), (CY, NZ), (CY, NZ), (CX, NZ), (CX, NZ), (chunks, 128)]
+    shapes = [(CX * CY, NZ), (CY, NZ), (CY, NZ), (CX, NZ), (CX, NZ), (chunks + 8, 128)]
     out = [jax.ShapeDtypeStruct(shape, jnp.float32) for shape in shapes]
     return pl.pallas_call(
         splat_kernel,
-        out_shape=tuple(out + [jax.ShapeDtypeStruct((chunks // GROUP, 2), jnp.int32)]),
+        out_shape=tuple(out),
         in_specs=[pl.BlockSpec(memory_space=pltpu.SMEM)] + whole_arrays(1),
-        out_specs=tuple(whole_arrays(6) + [pl.BlockSpec(memory_space=pltpu.SMEM)]),
+        out_specs=tuple(whole_arrays(6)),
         scratch_shapes=[
+            pltpu.SMEM((chunks // GROUP, 2), jnp.int32),
             pltpu.VMEM((4 * chunks, 128), jnp.float32),
             pltpu.VMEM(((CX + WINDOW) * CY, 3 * NZ), jnp.float32),
             pltpu.VMEM((3 * NZ, 2 * GROUP * 128), jnp.bfloat16),
@@ -310,71 +326,70 @@
     )(even, held)
 
 
-def sample_kernel(blocks, flip_ref, bound_ref, field_ref, held_ref, out_ref, iterate_ref, turned_ref, sampled_ref):
-    chunks = field_ref.shape[0]
-    turned_ref[:, CX * CY :] = jnp.zeros((2 * NZ, turned_ref.shape[1] - CX * CY), jnp.bfloat16)
-    for i in range(CX * CY // 128):
-        here = slice(128 * i, 128 * (i + 1))
-        per_block = CX * CY // 128 // blocks
-        place = i // per_block
-        place = jnp.where(flip_ref[0] > 0, blocks - 1 - place, place) * per_block + i % per_block
-        block = held_ref[pl.ds(pl.multiple_of(place * 128, 128), 128), :]
-        iterate_ref[here, :] = block
+def sample_kernel(place_ref, bound_ref, cell_ref, slab_ref, out_ref, turned_ref, sampled_ref):
+    second_count, thick = slab_ref.shape[:2]
+    chunks = sampled_ref.shape[1]
+    columns = thick * CY
+    start = place_ref[0] * thick
+    for j in range(second_count):
+        block = jnp.concatenate([slab_ref[j, i] for i in range(thick)], axis=0)
         high, low = parts_of(block.T, 2)
-        turned_ref[:NZ, here] = high
-        turned_ref[NZ:, here] = low
-    width = 4
-
-    def group(at, carry):
-        first, last = bound_ref[at, 0] // 2 * 2, bound_ref[at, 1]
-        cells = [places(field_ref[pl.ds(GROUP * at + member, 1), :]) for member in range(GROUP)]
-        level = rows_iota(NZ, 128 * GROUP) == jnp.concatenate([z for _, _, z in cells], axis=1)
-
-        def window(turn, total):
-            start = first + turn * width
-            tables = []
-            for x, y, _ in cells:
-                y_hot = flags(rows_iota(CY, 128) == y).astype(jnp.bfloat16)
-                hots = [spread(flags(x == start + i)) for i in range(width)]
-                tables.append(jnp.concatenate([times_row(y_hot, hot) for hot in hots], axis=0))
-            here = pl.ds(pl.multiple_of(start * CY, 128), width * CY)
-            found = jnp.dot(turned_ref[:, here], jnp.concatenate(tables, axis=1), preferred_element_type=jnp.float32)
-            found = jnp.where(level, found[:NZ] + found[NZ:], 0.0)
-            return total + jnp.sum(found, axis=0, keepdims=True)
-
-        turns = jnp.maximum(last - first, 0) // width + 1
-        row = lax.fori_loop(1, turns, window, window(0, jnp.zeros((1, 128 * GROUP), jnp.float32)))
-        for member in range(GROUP):
-            sampled_ref[pl.ds(GROUP * at + member, 1), :] = row[:, 128 * member : 128 * (member + 1)]
-        return carry
-
-    lax.fori_loop(0, chunks // GROUP, group, 0)
-    if len(out_ref.shape) == 2:
+        turned_ref[:NZ, j * columns : (j + 1) * columns] = high
+        turned_ref[NZ:, j * columns : (j + 1) * columns] = low
+    sampled_ref[...] = jnp.zeros_like(sampled_ref)
+    for j in range(second_count):
+
+        def group(at, carry, j=j):
+            @pl.when((bound_ref[j, 0, at] < start + thick) & (bound_ref[j, 1, at] >= start))
+            def _():
+                tables, heights = [], []
+                for member in range(GROUP):
+                    x, y, z = places(cell_ref[j, pl.ds(GROUP * at + member, 1), :])
+                    y_hot = flags(rows_iota(CY, 128) == y).astype(jnp.bfloat16)
+                    hots = [spread(flags(x == start + i)) for i in range(thick)]
+                    tables.append(jnp.concatenate([times_row(y_hot, hot) for hot in hots], axis=0))
+                    heights.append(z)
+                level = rows_iota(NZ, 128 * GROUP) == jnp.concatenate(heights, axis=1)
+                values = turned_ref[:, j * columns : (j + 1) * columns]
+                found = jnp.dot(values, jnp.concatenate(tables, axis=1), preferred_element_type=jnp.float32)
+                row = jnp.sum(jnp.where(level, found[:NZ] + found[NZ:], 0.0), axis=0, keepdims=True)
+                for member in range(GROUP):
+                    here = slice(128 * member, 128 * (member + 1))
+                    sampled_ref[j, pl.ds(GROUP * at + member, 1), :] = row[:, here]
+
+            return carry
+
+        lax.fori_loop(0, chunks // GROUP, group, 0)
+    if len(out_ref.shape) == 3 and out_ref.shape == sampled_ref.shape:
         out_ref[...] = sampled_ref[...]
         return
-    bricks, halves = out_ref.shape[:2]
-    for half in range(halves):
-        for block in range(bricks // 8):
-            tile = sampled_ref[pl.ds(8 * half * (bricks // 8) + block, 8, stride=bricks // 8), :]
-            out_ref[8 * block : 8 * (block + 1), half, :] = units_turned(tile)
-
-
-def sample(cell_rows, bounds, held, flip, blocks, bricks, capacity):
-    turned = (bricks, capacity // 128, 128)
-    if not grouped(bricks, capacity):
-        turned = cell_rows.shape
+    bricks = out_ref.shape[0]
+    blocks = bricks // 8
+    for j in range(second_count):
+        for half in range(chunks // bricks):
+            for block in range(blocks):
+                tile = sampled_ref[j, pl.ds(8 * half * blocks + block, 8, stride=blocks), :]
+                out_ref[8 * block : 8 * (block + 1), half * second_count + j, :] = units_turned(tile)
+
+
+def sample(place, bounds, cells, slab, chunks, bricks, capacity):
+    second_count, thick = slab.shape[:2]
+    shape = (second_count, chunks, 128)
+    if grouped(bricks, capacity):
+        shape = (bricks, second_count * capacity // 128, 128)
     return pl.pallas_call(
-        functools.partial(sample_kernel, blocks),
-        out_shape=tuple(jax.ShapeDtypeStruct(shape, jnp.float32) for shape in (turned, held.shape)),
+        sample_kernel,
+        out_shape=jax.ShapeDtypeStruct(shape, jnp.float32),
         in_specs=[pl.BlockSpec(memory_space=pltpu.SMEM)] * 2 + whole_arrays(2),
-        out_specs=tuple(whole_arrays(2)),
+        out_specs=pl.BlockSpec(memory_space=pltpu.VMEM),
         scratch_shapes=[
-            pltpu.VMEM((2 * NZ, CX * CY + 256), jnp.bfloat16),
-            pltpu.VMEM(cell_rows.shape, jnp.float32),
+            pltpu.VMEM((2 * NZ, second_count * thick * CY), jnp.bfloat16),
+            pltpu.VMEM((second_count, chunks, 128), jnp.float32),
         ],
         compiler_params=pltpu.CompilerParams(vmem_limit_bytes=16 << 20),
+        cost_estimate=pl.CostEstimate(flops=8 << 30, bytes_accessed=4 << 20, transcendentals=0),
         name="sample",
-    )(flip, bounds, cell_rows, held)
+    )(place, bounds, cells, slab)
 
 
 def swaps(pair, other, axis):
@@ -695,6 +710,17 @@
     return lax.all_to_all(value, EVERY, split_axis=0, concat_axis=0, tiled=True)
 
 
+def of_row(value):
+    second_count, mine = lax.axis_size("by"), lax.axis_index("by")
+    held = jnp.zeros((second_count,) + value.shape, value.dtype)
+    for turn in range(second_count):
+        piece = value
+        if turn:
+            piece = lax.ppermute(value, "by", [(i, i ^ turn) for i in range(second_count)])
+        held = lax.dynamic_update_slice_in_dim(held, piece[None], mine ^ turn, 0)
+    return held
+
+
 def x_slab_source(brick, even):
     second_count = lax.axis_size("by")
     mine = lax.axis_index("by")
@@ -711,7 +737,7 @@
     return jnp.concatenate([jnp.where(even, other, pair), slab, jnp.where(even, pair, other)], axis=0)
 
 
-def relax(brick, sent, levels, rows_inverse, columns_inverse, depth_inverse):
+def relax(brick, sent, cells, levels, rows_inverse, columns_inverse, depth_inverse):
     first_count, second_count = lax.axis_size("bx"), lax.axis_size("by")
     devices = first_count * second_count
     order = slab_order(first_count, second_count)
@@ -731,7 +757,7 @@
         planes, rows = thick[at], thick[(at + 2) % 3]
         held = exchange(sent)
         if step == 1:
-            held, sources[2] = lax.optimization_barrier((held, x_slab_source(brick, even)))
+            held, sources[2], cells = lax.optimization_barrier((held, x_slab_source(brick, even), of_row(cells)))
         bands = matrices[(2 * step + 1) % 3].shape[1] // 128
         blocks = held.reshape(devices, bands, -1, 128)
         to_next, to_previous = blocks[:, :, -2 * rows :], blocks[:, :, : 2 * rows]
@@ -757,8 +783,7 @@
         sent = out[0]
         if sources[at] is None:
             sources[at] = out[1]
-    sent = sent.reshape(second_count * thick[2], CY, NZ)
-    return lax.all_to_all(sent, "by", split_axis=0, concat_axis=0, tiled=True)
+    return sent, cells
 
 
 def local(normals, owners, cells, levels, rows_inverse, columns_inverse, depth_inverse):
@@ -773,17 +798,25 @@
         held = held[:, : 4 * capacity // 128].reshape(bricks, 4, capacity)
         held = held.transpose(1, 0, 2).reshape(4 * chunks, 128)
     even = jnp.stack([lax.axis_index("bx") % 2 == 0, lax.axis_index("by") % 2 == 0]).astype(jnp.int32)
-    source, x_pair, x_other, y_pair, y_other, cell_rows, bounds = splat(held, even, chunks)
+    source, x_pair, x_other, y_pair, y_other, cells = splat(held, even, chunks)
     faces = swaps(x_pair, x_other, "bx") + swaps(y_pair, y_other, "by")
     brick, sent = join(source, even, slab_order(lax.axis_size("bx"), lax.axis_size("by")), *faces)
-    held = relax(brick, sent, levels, rows_inverse, columns_inverse, depth_inverse)
-    flip = (lax.axis_index("bx") % 2).astype(jnp.int32).reshape(1)
-    held = held.reshape(CX * CY, NZ)
-    sampled, iterate = sample(cell_rows, bounds, held, flip, lax.axis_size("by"), bricks, capacity)
-    if sampled.ndim == 2:
-        sampled = sampled.reshape(bricks, capacity)
-    implicit = unpack(owners, slot, exchange(sampled).reshape(bricks, capacity))
-    return (iterate.reshape(CX, CY, NZ), implicit)
+    slab, cells = relax(brick, sent, cells, levels, rows_inverse, columns_inverse, depth_inverse)
+    bounds = cells[:, chunks : chunks + 2, : chunks // GROUP].astype(jnp.int32)
+    second_count, thick = slab.shape[:2]
+    pieces_of = slab.reshape(second_count * thick, CY, NZ)
+    held = lax.all_to_all(pieces_of, "by", split_axis=0, concat_axis=0, tiled=True).reshape(slab.shape)
+    place = place_in_row(lax.axis_index("by")).astype(jnp.int32).reshape(1)
+    sampled = sample(place, bounds, cells, slab, chunks, bricks, capacity)
+    if not grouped(bricks, capacity):
+        sampled = sampled.reshape(second_count, bricks, capacity).transpose(1, 0, 2)
+    sampled, held = lax.optimization_barrier((sampled, held))
+    returned = exchange(sampled)
+    iterate = jnp.where(lax.axis_index("bx") % 2 == 0, held, held[::-1]).reshape(CX, CY, NZ)
+    if not grouped(bricks, capacity):
+        returned = jnp.sum(returned.reshape(-1, second_count, second_count, capacity), axis=1).reshape(bricks, capacity)
+    implicit = unpack(owners, slot, returned, second_count)
+    return (iterate, implicit)
 
 
 def solution(mesh):

time: 374 us -> 368 us (0.984)
  blocking collectives: 186 us -> 150 us
  starting transfers between devices: 30.9 us -> 47.5 us
  waiting for transfers between devices: 87.3 us -> 103 us
  local copies, waits for them, and re-layouts: 9.3 us -> 5.22 us
    all_to_all x1 -> x0, blocking collectives: 25.6 us -> none  [relax(): return lax.all_to_all(sent, 'by', split_axis=0, concat_axis=0, tiled=True)]
    all_to_all x0 -> x1, starting transfers between devices: none -> 11.3 us  [local(): lax.all_to_all(pieces_of, 'by', split_axis=0, concat_axis=0, tiled=True)]
    all_to_all x5 -> x4, blocking collectives: 161 us -> 150 us  [exchange(): return lax.all_to_all(value, EVERY, split_axis=0, concat_axis=0, tiled=True)]
    all_to_all x3 -> x4, waiting for transfers between devices: 52.4 us -> 59.7 us  [exchange(): return lax.all_to_all(value, EVERY, split_axis=0, concat_axis=0, tiled=True)]
    all_to_all x0 -> x1, waiting for transfers between devices: none -> 5.99 us  [local(): lax.all_to_all(pieces_of, 'by', split_axis=0, concat_axis=0, tiled=True)]
    all_to_all x3 -> x4, starting transfers between devices: 19.3 us -> 22.1 us  [exchange(): return lax.all_to_all(value, EVERY, split_axis=0, concat_axis=0, tiled=True)]
  transfers between devices with their start and end apart: 22 -> 27, of which waited for: 13 -> 15; matrix products, arithmetic and copies ran while one was open for 1% -> 1% of each run, Pallas kernels for 0% -> 2%
where the time goes in v9:
time: 368 us; the launch traced here: 367 us
  blocking collectives  150 us (41%)
  waiting for transfers between devices  103 us (28%)
  Pallas kernels  55.8 us (15%)
  starting transfers between devices  47.5 us (13%)
  local copies, waits for them, and re-layouts  5.22 us (1%)
  other arithmetic  3.82 us (1%)
    all_to_all x4, blocking collectives, exchange(): return lax.all_to_all(value, EVERY, split_axis=0, concat_axis=0, tiled=True)  150 us
    all_to_all x4, waiting for transfers between devices, exchange(): return lax.all_to_all(value, EVERY, split_axis=0, concat_axis=0, tiled=True)  59.7 us
    ppermute x3, waiting for transfers between devices, x_slab_source(): lax.ppermute(piece, 'by', [(i, i ^ turn) for i in range(second_count)])  30.1 us
    all_to_all x4, starting transfers between devices, exchange(): return lax.all_to_all(value, EVERY, split_axis=0, concat_axis=0, tiled=True)  22.1 us
    pallas_call x5, Pallas kernels, later_phase(): pl.pallas_call(functools.partial(later_kernel, (order, planes, rows, sour...  21.1 us
    pallas_call x1, Pallas kernels, splat(): pl.pallas_call(splat_kernel, out_shape=tuple(out), in_specs=[pl.BlockSpec...  13.2 us
    all_to_all x1, starting transfers between devices, local(): lax.all_to_all(pieces_of, 'by', split_axis=0, concat_axis=0, tiled=True)  11.3 us
    pallas_call x1, Pallas kernels, sample(): pl.pallas_call(sample_kernel, out_shape=jax.ShapeDtypeStruct(shape, jnp.f...  8.64 us
  transfers between devices with their start and end apart: 27, of which 15 were waited for; matrix products, arithmetic and copies ran while one was open for 1% of the time, Pallas kernels for 2%

profile of v9, /device:TPU:0, one launch (start us, length us, event | category | flops | bytes accessed | tf_op | source)
XLA Modules:
  0.0 366.9 jit_solution(12230305189056010972)
XLA Ops:
  3.6 5.9 %pack.1 = (f32[32,16,128]{2,1,0:T(8,128)}, f32[1,4096]{1,0:T(1,128)S(1)}) custom-call(s32[1,1]{1,0:T(1,128)S(6)} %copy.17.level_ref, s32[1,4096]{1,0:T(1,128)S(1)} %bitcast.63, s32[1,4096]{1,0:T(1,128)S(1)} %bitcast.65, f32[3,4096]{1,0:T(4,128)S(1)} %copy-done.8), custom_call_target="tpu_custom_call" | custom-call | tf_op jit(solution)/shard_map/pack/pallas_call | solution.py:120
  9.5 7.3 %all-to-all-start = ((f32[32,16,128]{2,1,0:T(8,128)}), f32[32,16,128]{2,1,0:T(8,128)S(1)}, u32[]{:S(2)}, u32[]{:S(2)}) async-start(f32[32,16,128]{2,1,0:T(8,128)} %get-tuple-element.21), calls=%async_computation | async-start | bytes 524288 | tf_op jit(solution)/shard_map/all_to_all | solution.py:710
  16.9 10.5 %all-to-all-done.held_ref = f32[32,16,128]{2,1,0:T(8,128)S(1)} async-done(((f32[32,16,128]{2,1,0:T(8,128)}), f32[32,16,128]{2,1,0:T(8,128)S(1)}, u32[]{:S(2)}, u32[]{:S(2)}) %all-to-all-start) | async-done | bytes 262176 | tf_op jit(solution)/shard_map/all_to_all | solution.py:710
  27.4 13.2 %splat.1 = (f32[1024,256]{1,0:T(8,128)S(1)}, f32[64,256]{1,0:T(8,128)S(1)}, f32[64,256]{1,0:T(8,128)S(1)}, f32[16,256]{1,0:T(8,128)S(1)}, f32[16,256]{1,0:T(8,128)S(1)}, /*index=5*/f32[72,128]{1,0:T(8,128)S(1)}) custom-call(s32[2]{0:T(128)S(1)} %add_convert_fusion.even_ref, f32[32,16,128]{2,1,0:T(8,128)S(1)} %all-to-all-done.held_ref), custom_call_target="tpu_custom_call" | custom-call | tf_op jit(solution)/shard_map/splat/pallas_call | solution.py:313
  43.4 1.5 collective-permute-done.x_pair_ref
  44.9 2.3 join.1
  48.1 7.2 %all-to-all-start.1 = ((f32[32,80,128]{2,1,0:T(8,128)}), f32[32,80,128]{2,1,0:T(8,128)S(1)}, u32[]{:S(2)}, u32[]{:S(2)}) async-start(f32[32,80,128]{2,1,0:T(8,128)} %get-tuple-element.27), calls=%async_computation.1 | async-start | bytes 2621440 | tf_op jit(solution)/shard_map/all_to_all | solution.py:710
  55.7 31.8 %all-to-all-done.1 = f32[32,80,128]{2,1,0:T(8,128)S(1)} async-done(((f32[32,80,128]{2,1,0:T(8,128)}), f32[32,80,128]{2,1,0:T(8,128)S(1)}, u32[]{:S(2)}, u32[]{:S(2)}) %all-to-all-start.1) | async-done | bytes 1310752 | tf_op jit(solution)/shard_map/all_to_all | solution.py:710
  87.5 3.1 first_phase.1
  92.0 3.7 %all-to-all-start.2 = ((f32[32,128,128]{2,1,0:T(8,128)}), f32[32,128,128]{2,1,0:T(8,128)}, u32[]{:S(2)}, u32[]{:S(2)}) async-start(f32[32,128,128]{2,1,0:T(8,128)} %bitcast.60), calls=%async_computation.2 | async-start | bytes 4194304 | tf_op jit(solution)/shard_map/all_to_all | solution.py:710
  96.0 1.7 collective-permute-start.10
  98.5 1.7 collective-permute-start.5
  100.3 24.2 %collective-permute-done.5 = f32[4,64,256]{2,1,0:T(8,128)S(1)} collective-permute-done((f32[4,64,256]{2,1,0:T(8,128)S(1)}, f32[4,64,256]{2,1,0:T(8,128)S(1)}, u32[]{:S(2)}, u32[]{:S(2)}) %collective-permute-start.5) | collective-permute-done | bytes 262176 | tf_op jit(solution)/shard_map/ppermute | solution.py:734
  124.5 5.9 %collective-permute-done.6 = f32[4,64,256]{2,1,0:T(8,128)S(1)} collective-permute-done((f32[4,64,256]{2,1,0:T(8,128)S(1)}, f32[4,64,256]{2,1,0:T(8,128)S(1)}, u32[]{:S(2)}, u32[]{:S(2)}) %collective-permute-start.6) | collective-permute-done | bytes 262176 | tf_op jit(solution)/shard_map/ppermute | solution.py:734
  131.2 2.0 collective-permute-start.8
  134.5 10.2 %all-to-all-done.2 = f32[32,128,128]{2,1,0:T(8,128)} async-done(((f32[32,128,128]{2,1,0:T(8,128)}), f32[32,128,128]{2,1,0:T(8,128)}, u32[]{:S(2)}, u32[]{:S(2)}) %all-to-all-start.2) | async-done | bytes 2097184 | tf_op jit(solution)/shard_map/all_to_all | solution.py:710
  144.7 2.1 slice_select_fusion.4
  148.9 4.7 %later_phase.5 = (f32[2048,128]{1,0:T(8,128)S(1)}, f32[10,256,128]{2,1,0:T(8,128)S(1)}) custom-call(s32[4]{0:T(128)S(1)} %pad_add_fusion.edge_ref, f32[32]{0:T(128)S(1)} %slice_reduce_fusion.level_ref, f32[4096,128]{1,0:T(8,128)} %bitcast.7.held_ref, f32[768,128]{1,0:T(8,128)} %collective-permute-done.12.pair_ref, ...), custom_call_target="tpu_custom_call" | custom-call | tf_op jit(solution)/shard_map/later_phase/pallas_call | solution.py:632
  153.6 39.6 %all_to_all.76 = f32[32,64,128]{2,1,0:T(8,128)S(1)} all-to-all(f32[32,64,128]{2,1,0:T(8,128)S(1)} %bitcast.62), channel_id=1, replica_groups=mesh['bx'=8,'by'=4] {'bx','by'}, dimensions={0} | all-to-all | bytes 2097152 | tf_op jit(solution)/shard_map/all_to_all | solution.py:710
  195.3 4.7 %later_phase.6 = f32[2048,128]{1,0:T(8,128)S(1)} custom-call(s32[4]{0:T(128)S(1)} %pad_add_fusion.edge_ref, f32[32]{0:T(128)S(1)} %slice_reduce_fusion.level_ref, f32[2048,128]{1,0:T(8,128)S(1)} %bitcast.51, f32[1024,128]{1,0:T(8,128)S(1)} %collective-permute-done.14.pair_ref, f32[1024,128]{1,0:T(8,128)S(1)} %collective-permute-done.15.other_ref, ...), custom_call_target="tpu_custom_call" | custom-call | tf_op jit(solution)/shard_map/later_phase/pallas_call | solution.py:632
  200.0 38.3 %all_to_all.77 = f32[32,64,128]{2,1,0:T(8,128)S(1)} all-to-all(f32[32,64,128]{2,1,0:T(8,128)S(1)} %bitcast.59), channel_id=1, replica_groups=mesh['bx'=8,'by'=4] {'bx','by'}, dimensions={0} | all-to-all | bytes 2097152 | tf_op jit(solution)/shard_map/all_to_all | solution.py:710
  239.9 3.6 later_phase.7
  243.5 35.9 %all_to_all.78 = f32[32,64,128]{2,1,0:T(8,128)S(1)} all-to-all(f32[32,64,128]{2,1,0:T(8,128)S(1)} %bitcast.57), channel_id=1, replica_groups=mesh['bx'=8,'by'=4] {'bx','by'}, dimensions={0} | all-to-all | bytes 2097152 | tf_op jit(solution)/shard_map/all_to_all | solution.py:710
  281.0 3.4 later_phase.8
  284.4 35.9 %all_to_all.79 = f32[32,64,128]{2,1,0:T(8,128)S(1)} all-to-all(f32[32,64,128]{2,1,0:T(8,128)S(1)} %bitcast.58), channel_id=1, replica_groups=mesh['bx'=8,'by'=4] {'bx','by'}, dimensions={0} | all-to-all | bytes 2097152 | tf_op jit(solution)/shard_map/all_to_all | solution.py:710
  322.4 4.9 %later_phase.9.slab_ref = f32[4,4,64,256]{3,2,1,0:T(8,128)} custom-call(s32[4]{0:T(128)S(1)} %pad_add_fusion.edge_ref, f32[32]{0:T(128)S(1)} %slice_reduce_fusion.level_ref, f32[2048,128]{1,0:T(8,128)S(1)} %bitcast.49, f32[1024,128]{1,0:T(8,128)S(1)} %collective-permute-done.20.pair_ref, f32[1024,128]{1,0:T(8,128)S(1)} %collective-permute-done.21.other_ref, ...), custom_call_target="tpu_custom_call" | custom-call | tf_op jit(solution)/shard_map/later_phase/pallas_call | solution.py:632
  327.2 11.3 %all-to-all-start.7 = ((f32[16,64,256]{2,1,0:T(8,128)}), f32[16,64,256]{2,1,0:T(8,128)S(1)}, u32[]{:S(2)}, u32[]{:S(2)}) async-start(f32[16,64,256]{2,1,0:T(8,128)} %bitcast.40), calls=%async_computation.7 | async-start | bytes 2097152 | tf_op jit(solution)/shard_map/all_to_all | solution.py:808
  338.6 8.6 %sample.1 = f32[32,8,128]{2,1,0:T(8,128)} custom-call(s32[1]{0:T(128)} %bitcast.place_ref, s32[4,2,16]{2,1,0:T(2,128)S(1)} %slice_convert_fusion.bound_ref, f32[4,72,128]{2,1,0:T(8,128)S(1)} %copy-done.7, f32[4,4,64,256]{3,2,1,0:T(8,128)} %later_phase.9.slab_ref), custom_call_target="tpu_custom_call" | custom-call | flops 8589934592 | bytes 4194304 | tf_op jit(solution)/shard_map/sample/pallas_call | solution.py:380
  347.2 6.0 %all-to-all-done.7 = f32[16,64,256]{2,1,0:T(8,128)S(1)} async-done(((f32[16,64,256]{2,1,0:T(8,128)}), f32[16,64,256]{2,1,0:T(8,128)S(1)}, u32[]{:S(2)}, u32[]{:S(2)}) %all-to-all-start.7) | async-done | bytes 1048608 | tf_op jit(solution)/shard_map/all_to_all | solution.py:808
  353.2 3.9 %all-to-all-start.8 = ((f32[32,8,128]{2,1,0:T(8,128)}), f32[32,8,128]{2,1,0:T(8,128)S(1)}, u32[]{:S(2)}, u32[]{:S(2)}) async-start(f32[32,8,128]{2,1,0:T(8,128)} %sample.1), calls=%async_computation.8 | async-start | bytes 262144 | tf_op jit(solution)/shard_map/all_to_all | solution.py:710
  358.2 7.2 %all-to-all-done.8.held_ref = f32[32,8,128]{2,1,0:T(8,128)S(1)} async-done(((f32[32,8,128]{2,1,0:T(8,128)}), f32[32,8,128]{2,1,0:T(8,128)S(1)}, u32[]{:S(2)}, u32[]{:S(2)}) %all-to-all-start.8) | async-done | bytes 131104 | tf_op jit(solution)/shard_map/all_to_all | solution.py:710
  365.4 1.6 unpack.1
  (84 shorter events, 21.4 us)
Async XLA Ops:
  9.5 17.9 %all-to-all-start = ((f32[32,16,128]{2,1,0:T(8,128)}), f32[32,16,128]{2,1,0:T(8,128)S(1)}, u32[]{:S(2)}, u32[]{:S(2)}) async-start(f32[32,16,128]{2,1,0:T(8,128)} %get-tuple-element.21), calls=%async_computation | async-start | bytes 524288 | tf_op jit(solution)/shard_map/all_to_all | solution.py:710
  40.6 4.3 %collective-permute-start = (f32[64,256]{1,0:T(8,128)S(1)}, f32[64,256]{1,0:T(8,128)S(1)}, u32[]{:S(2)}, u32[]{:S(2)}) collective-permute-start(f32[64,256]{1,0:T(8,128)S(1)} %get-tuple-element.23), channel_id=1, source_target_pairs={{0,4},{8,12},{16,20},{24,28},{4,0},{12,8},{20,16},{28,24},{1,5},{9... | collective-permute-start | bytes 196616 | tf_op jit(solution)/shard_map/ppermute | solution.py:400
  41.5 3.4 collective-permute-start.1
  42.2 1.2 collective-permute-start.2
  42.3 1.2 collective-permute-start.3
  48.1 39.4 %copy-start.1 = (f32[256,256]{1,0:T(8,128)S(1)}, f32[256,256]{1,0:T(8,128)}, u32[]{:S(2)}) copy-start(f32[256,256]{1,0:T(8,128)} %first_any.11) | copy-start | bytes 786436
  48.1 39.4 %copy-start.3 = (f32[128,128]{1,0:T(8,128)S(1)}, f32[128,128]{1,0:T(8,128)}, u32[]{:S(2)}) copy-start(f32[128,128]{1,0:T(8,128)} %second_any.10) | copy-start | bytes 196612
  48.1 39.4 %all-to-all-start.1 = ((f32[32,80,128]{2,1,0:T(8,128)}), f32[32,80,128]{2,1,0:T(8,128)S(1)}, u32[]{:S(2)}, u32[]{:S(2)}) async-start(f32[32,80,128]{2,1,0:T(8,128)} %get-tuple-element.27), calls=%async_computation.1 | async-start | bytes 2621440 | tf_op jit(solution)/shard_map/all_to_all | solution.py:710
  92.0 52.7 %all-to-all-start.2 = ((f32[32,128,128]{2,1,0:T(8,128)}), f32[32,128,128]{2,1,0:T(8,128)}, u32[]{:S(2)}, u32[]{:S(2)}) async-start(f32[32,128,128]{2,1,0:T(8,128)} %bitcast.60), calls=%async_computation.2 | async-start | bytes 4194304 | tf_op jit(solution)/shard_map/all_to_all | solution.py:710
  95.7 2.1 copy-start.5
  95.8 4.4 %collective-permute-start.9 = (f32[72,128]{1,0:T(8,128)S(1)}, f32[72,128]{1,0:T(8,128)S(1)}, u32[]{:S(2)}, u32[]{:S(2)}) collective-permute-start(f32[72,128]{1,0:T(8,128)S(1)} %get-tuple-element.30), channel_id=1, source_target_pairs={{0,1},{1,0},{2,3},{3,2},{4,5},{5,4},{6,7},{7,6},{8,9},{9,8},{10,11... | collective-permute-start | bytes 110600 | tf_op jit(solution)/shard_map/ppermute | solution.py:719
  96.0 37.2 %collective-permute-start.10 = (f32[72,128]{1,0:T(8,128)S(1)}, f32[72,128]{1,0:T(8,128)S(1)}, u32[]{:S(2)}, u32[]{:S(2)}) collective-permute-start(f32[72,128]{1,0:T(8,128)S(1)} %get-tuple-element.30), channel_id=1, source_target_pairs={{0,2},{1,3},{2,0},{3,1},{4,6},{5,7},{6,4},{7,5},{8,10},{9,11},{10,... | collective-permute-start | bytes 110600 | tf_op jit(solution)/shard_map/ppermute | solution.py:719
  97.7 35.5 %collective-permute-start.11 = (f32[72,128]{1,0:T(8,128)S(1)}, f32[72,128]{1,0:T(8,128)S(1)}, u32[]{:S(2)}, u32[]{:S(2)}) collective-permute-start(f32[72,128]{1,0:T(8,128)S(1)} %get-tuple-element.30), channel_id=1, source_target_pairs={{0,3},{1,2},{2,1},{3,0},{4,7},{5,6},{6,5},{7,4},{8,11},{9,10},{10,... | collective-permute-start | bytes 110600 | tf_op jit(solution)/shard_map/ppermute | solution.py:719
  97.9 2.3 collective-permute-start.4
  98.5 26.0 %collective-permute-start.5 = (f32[4,64,256]{2,1,0:T(8,128)S(1)}, f32[4,64,256]{2,1,0:T(8,128)S(1)}, u32[]{:S(2)}, u32[]{:S(2)}) collective-permute-start(f32[4,64,256]{2,1,0:T(8,128)S(1)} %get-tuple-element.53), channel_id=1, source_target_pairs={{0,2},{1,3},{2,0},{3,1},{4,6},{5,7},{6,4},{7,5},{8,10},{9,11},{10,... | collective-permute-start | bytes 786440 | tf_op jit(solution)/shard_map/ppermute | solution.py:734
  100.2 30.2 %collective-permute-start.6 = (f32[4,64,256]{2,1,0:T(8,128)S(1)}, f32[4,64,256]{2,1,0:T(8,128)S(1)}, u32[]{:S(2)}, u32[]{:S(2)}) collective-permute-start(f32[4,64,256]{2,1,0:T(8,128)S(1)} %get-tuple-element.52), channel_id=1, source_target_pairs={{0,3},{1,2},{2,1},{3,0},{4,7},{5,6},{6,5},{7,4},{8,11},{9,10},{10,... | collective-permute-start | bytes 786440 | tf_op jit(solution)/shard_map/ppermute | solution.py:734
  130.5 2.8 collective-permute-start.7
  131.2 3.2 collective-permute-start.8
  134.5 14.3 %copy-start = (f32[256,256]{1,0:T(8,128)S(1)}, f32[256,256]{1,0:T(8,128)}, u32[]{:S(2)}) copy-start(f32[256,256]{1,0:T(8,128)} %second_any.11) | copy-start | bytes 786436
  146.8 2.1 collective-permute-start.12
  146.8 2.1 collective-permute-start.13
  193.3 2.0 collective-permute-start.14
  193.4 1.9 collective-permute-start.15
  238.3 1.6 collective-permute-start.16
  238.4 1.5 collective-permute-start.17
  279.4 1.6 collective-permute-start.18
  279.5 1.5 collective-permute-start.19
  320.4 2.0 collective-permute-start.20
  320.5 1.9 collective-permute-start.21
  327.2 26.0 %all-to-all-start.7 = ((f32[16,64,256]{2,1,0:T(8,128)}), f32[16,64,256]{2,1,0:T(8,128)S(1)}, u32[]{:S(2)}, u32[]{:S(2)}) async-start(f32[16,64,256]{2,1,0:T(8,128)} %bitcast.40), calls=%async_computation.7 | async-start | bytes 2097152 | tf_op jit(solution)/shard_map/all_to_all | solution.py:808
  347.2 18.1 %copy-start.10 = (s32[4096,1]{0,1:T(1,128)S(1)}, s32[4096,1]{0,1:T(1,128)}, u32[]{:S(2)}) copy-start(s32[4096,1]{0,1:T(1,128)} %param.8) | copy-start | bytes 49156
  353.2 12.2 %all-to-all-start.8 = ((f32[32,8,128]{2,1,0:T(8,128)}), f32[32,8,128]{2,1,0:T(8,128)S(1)}, u32[]{:S(2)}, u32[]{:S(2)}) async-start(f32[32,8,128]{2,1,0:T(8,128)} %sample.1), calls=%async_computation.8 | async-start | bytes 262144 | tf_op jit(solution)/shard_map/all_to_all | solution.py:710
  (7 other events, 6.9 us)

commit v10 on v9

--- a/solution.py
+++ b/solution.py
@@ -478,8 +478,8 @@
 
     def along_x(k):
         i = jnp.clip(me * planes - 1 + k, 0, first_count * CX - 1) // CX
-        column = jnp.broadcast_to(row(second_count, CY, lambda j: i * second_count + j), (128, shape[0])).T
-        return jnp.concatenate([column] * (shape[1] // 128), axis=1)
+        values = [6.0 + screen_base * (1.0 + level_ref[i * second_count + j]) for j in range(second_count)]
+        return jnp.concatenate([jnp.full((CY, shape[1]), value) for value in values], axis=0)
 
     def along_y(k):
         j = jnp.clip(me * planes - 1 + k, 0, second_count * CY - 1) // CY

time: 368 us -> 367 us (level)
  no operation moved by 1% of the time
where the time goes in v10:
time: 367 us; the launch traced here: 365 us
  blocking collectives  150 us (41%)
  waiting for transfers between devices  103 us (28%)
  Pallas kernels  54.4 us (15%)
  starting transfers between devices  47.5 us (13%)
  local copies, waits for them, and re-layouts  5.22 us (1%)
  other arithmetic  3.82 us (1%)
    all_to_all x4, blocking collectives, exchange(): return lax.all_to_all(value, EVERY, split_axis=0, concat_axis=0, tiled=True)  150 us
    all_to_all x4, waiting for transfers between devices, exchange(): return lax.all_to_all(value, EVERY, split_axis=0, concat_axis=0, tiled=True)  59.7 us
    ppermute x3, waiting for transfers between devices, x_slab_source(): lax.ppermute(piece, 'by', [(i, i ^ turn) for i in range(second_count)])  30.1 us
    all_to_all x4, starting transfers between devices, exchange(): return lax.all_to_all(value, EVERY, split_axis=0, concat_axis=0, tiled=True)  22.1 us
    pallas_call x5, Pallas kernels, later_phase(): pl.pallas_call(functools.partial(later_kernel, (order, planes, rows, sour...  19.4 us
    pallas_call x1, Pallas kernels, splat(): pl.pallas_call(splat_kernel, out_shape=tuple(out), in_specs=[pl.BlockSpec...  13.2 us
    all_to_all x1, starting transfers between devices, local(): lax.all_to_all(pieces_of, 'by', split_axis=0, concat_axis=0, tiled=True)  11.3 us
    pallas_call x1, Pallas kernels, sample(): pl.pallas_call(sample_kernel, out_shape=jax.ShapeDtypeStruct(shape, jnp.f...  8.97 us
  transfers between devices with their start and end apart: 27, of which 15 were waited for; matrix products, arithmetic and copies ran while one was open for 1% of the time, Pallas kernels for 2%

profile of v10, /device:TPU:0, one launch (start us, length us, event | category | flops | bytes accessed | tf_op | source)
XLA Modules:
  0.0 365.3 jit_solution(13847924713947636554)
XLA Ops:
  3.6 5.9 %pack.1 = (f32[32,16,128]{2,1,0:T(8,128)}, f32[1,4096]{1,0:T(1,128)S(1)}) custom-call(s32[1,1]{1,0:T(1,128)S(6)} %copy.17.level_ref, s32[1,4096]{1,0:T(1,128)S(1)} %bitcast.63, s32[1,4096]{1,0:T(1,128)S(1)} %bitcast.65, f32[3,4096]{1,0:T(4,128)S(1)} %copy-done.8), custom_call_target="tpu_custom_call" | custom-call | tf_op jit(solution)/shard_map/pack/pallas_call | solution.py:120
  9.5 7.3 %all-to-all-start = ((f32[32,16,128]{2,1,0:T(8,128)}), f32[32,16,128]{2,1,0:T(8,128)S(1)}, u32[]{:S(2)}, u32[]{:S(2)}) async-start(f32[32,16,128]{2,1,0:T(8,128)} %get-tuple-element.21), calls=%async_computation | async-start | bytes 524288 | tf_op jit(solution)/shard_map/all_to_all | solution.py:710
  16.9 10.5 %all-to-all-done.held_ref = f32[32,16,128]{2,1,0:T(8,128)S(1)} async-done(((f32[32,16,128]{2,1,0:T(8,128)}), f32[32,16,128]{2,1,0:T(8,128)S(1)}, u32[]{:S(2)}, u32[]{:S(2)}) %all-to-all-start) | async-done | bytes 262176 | tf_op jit(solution)/shard_map/all_to_all | solution.py:710
  27.4 13.2 %splat.1 = (f32[1024,256]{1,0:T(8,128)S(1)}, f32[64,256]{1,0:T(8,128)S(1)}, f32[64,256]{1,0:T(8,128)S(1)}, f32[16,256]{1,0:T(8,128)S(1)}, f32[16,256]{1,0:T(8,128)S(1)}, /*index=5*/f32[72,128]{1,0:T(8,128)S(1)}) custom-call(s32[2]{0:T(128)S(1)} %add_convert_fusion.even_ref, f32[32,16,128]{2,1,0:T(8,128)S(1)} %all-to-all-done.held_ref), custom_call_target="tpu_custom_call" | custom-call | tf_op jit(solution)/shard_map/splat/pallas_call | solution.py:313
  43.4 1.5 collective-permute-done.x_pair_ref
  44.9 2.3 join.1
  48.1 7.2 %all-to-all-start.1 = ((f32[32,80,128]{2,1,0:T(8,128)}), f32[32,80,128]{2,1,0:T(8,128)S(1)}, u32[]{:S(2)}, u32[]{:S(2)}) async-start(f32[32,80,128]{2,1,0:T(8,128)} %get-tuple-element.27), calls=%async_computation.1 | async-start | bytes 2621440 | tf_op jit(solution)/shard_map/all_to_all | solution.py:710
  55.7 31.8 %all-to-all-done.1 = f32[32,80,128]{2,1,0:T(8,128)S(1)} async-done(((f32[32,80,128]{2,1,0:T(8,128)}), f32[32,80,128]{2,1,0:T(8,128)S(1)}, u32[]{:S(2)}, u32[]{:S(2)}) %all-to-all-start.1) | async-done | bytes 1310752 | tf_op jit(solution)/shard_map/all_to_all | solution.py:710
  87.5 3.1 first_phase.1
  92.0 3.7 %all-to-all-start.2 = ((f32[32,128,128]{2,1,0:T(8,128)}), f32[32,128,128]{2,1,0:T(8,128)}, u32[]{:S(2)}, u32[]{:S(2)}) async-start(f32[32,128,128]{2,1,0:T(8,128)} %bitcast.60), calls=%async_computation.2 | async-start | bytes 4194304 | tf_op jit(solution)/shard_map/all_to_all | solution.py:710
  96.0 1.7 collective-permute-start.10
  98.5 1.7 collective-permute-start.5
  100.3 24.2 %collective-permute-done.5 = f32[4,64,256]{2,1,0:T(8,128)S(1)} collective-permute-done((f32[4,64,256]{2,1,0:T(8,128)S(1)}, f32[4,64,256]{2,1,0:T(8,128)S(1)}, u32[]{:S(2)}, u32[]{:S(2)}) %collective-permute-start.5) | collective-permute-done | bytes 262176 | tf_op jit(solution)/shard_map/ppermute | solution.py:734
  124.5 5.9 %collective-permute-done.6 = f32[4,64,256]{2,1,0:T(8,128)S(1)} collective-permute-done((f32[4,64,256]{2,1,0:T(8,128)S(1)}, f32[4,64,256]{2,1,0:T(8,128)S(1)}, u32[]{:S(2)}, u32[]{:S(2)}) %collective-permute-start.6) | collective-permute-done | bytes 262176 | tf_op jit(solution)/shard_map/ppermute | solution.py:734
  131.2 2.0 collective-permute-start.8
  134.5 10.2 %all-to-all-done.2 = f32[32,128,128]{2,1,0:T(8,128)} async-done(((f32[32,128,128]{2,1,0:T(8,128)}), f32[32,128,128]{2,1,0:T(8,128)}, u32[]{:S(2)}, u32[]{:S(2)}) %all-to-all-start.2) | async-done | bytes 2097184 | tf_op jit(solution)/shard_map/all_to_all | solution.py:710
  144.7 2.1 slice_select_fusion.4
  148.9 4.7 %later_phase.5 = (f32[2048,128]{1,0:T(8,128)S(1)}, f32[10,256,128]{2,1,0:T(8,128)S(1)}) custom-call(s32[4]{0:T(128)S(1)} %pad_add_fusion.edge_ref, f32[32]{0:T(128)S(1)} %slice_reduce_fusion.level_ref, f32[4096,128]{1,0:T(8,128)} %bitcast.7.held_ref, f32[768,128]{1,0:T(8,128)} %collective-permute-done.12.pair_ref, ...), custom_call_target="tpu_custom_call" | custom-call | tf_op jit(solution)/shard_map/later_phase/pallas_call | solution.py:632
  153.6 39.6 %all_to_all.76 = f32[32,64,128]{2,1,0:T(8,128)S(1)} all-to-all(f32[32,64,128]{2,1,0:T(8,128)S(1)} %bitcast.62), channel_id=1, replica_groups=mesh['bx'=8,'by'=4] {'bx','by'}, dimensions={0} | all-to-all | bytes 2097152 | tf_op jit(solution)/shard_map/all_to_all | solution.py:710
  195.3 3.5 later_phase.6
  198.8 38.3 %all_to_all.77 = f32[32,64,128]{2,1,0:T(8,128)S(1)} all-to-all(f32[32,64,128]{2,1,0:T(8,128)S(1)} %bitcast.59), channel_id=1, replica_groups=mesh['bx'=8,'by'=4] {'bx','by'}, dimensions={0} | all-to-all | bytes 2097152 | tf_op jit(solution)/shard_map/all_to_all | solution.py:710
  238.8 3.6 later_phase.7
  242.4 35.9 %all_to_all.78 = f32[32,64,128]{2,1,0:T(8,128)S(1)} all-to-all(f32[32,64,128]{2,1,0:T(8,128)S(1)} %bitcast.57), channel_id=1, replica_groups=mesh['bx'=8,'by'=4] {'bx','by'}, dimensions={0} | all-to-all | bytes 2097152 | tf_op jit(solution)/shard_map/all_to_all | solution.py:710
  279.9 3.4 later_phase.8
  283.3 35.9 %all_to_all.79 = f32[32,64,128]{2,1,0:T(8,128)S(1)} all-to-all(f32[32,64,128]{2,1,0:T(8,128)S(1)} %bitcast.58), channel_id=1, replica_groups=mesh['bx'=8,'by'=4] {'bx','by'}, dimensions={0} | all-to-all | bytes 2097152 | tf_op jit(solution)/shard_map/all_to_all | solution.py:710
  321.2 4.3 %later_phase.9.slab_ref = f32[4,4,64,256]{3,2,1,0:T(8,128)} custom-call(s32[4]{0:T(128)S(1)} %pad_add_fusion.edge_ref, f32[32]{0:T(128)S(1)} %slice_reduce_fusion.level_ref, f32[2048,128]{1,0:T(8,128)S(1)} %bitcast.49, f32[1024,128]{1,0:T(8,128)S(1)} %collective-permute-done.20.pair_ref, f32[1024,128]{1,0:T(8,128)S(1)} %collective-permute-done.21.other_ref, ...), custom_call_target="tpu_custom_call" | custom-call | tf_op jit(solution)/shard_map/later_phase/pallas_call | solution.py:632
  325.6 11.3 %all-to-all-start.7 = ((f32[16,64,256]{2,1,0:T(8,128)}), f32[16,64,256]{2,1,0:T(8,128)S(1)}, u32[]{:S(2)}, u32[]{:S(2)}) async-start(f32[16,64,256]{2,1,0:T(8,128)} %bitcast.40), calls=%async_computation.7 | async-start | bytes 2097152 | tf_op jit(solution)/shard_map/all_to_all | solution.py:808
  336.9 9.0 %sample.1 = f32[32,8,128]{2,1,0:T(8,128)} custom-call(s32[1]{0:T(128)} %bitcast.place_ref, s32[4,2,16]{2,1,0:T(2,128)S(1)} %slice_convert_fusion.bound_ref, f32[4,72,128]{2,1,0:T(8,128)S(1)} %copy-done.7, f32[4,4,64,256]{3,2,1,0:T(8,128)} %later_phase.9.slab_ref), custom_call_target="tpu_custom_call" | custom-call | flops 8589934592 | bytes 4194304 | tf_op jit(solution)/shard_map/sample/pallas_call | solution.py:380
  345.9 5.7 %all-to-all-done.7 = f32[16,64,256]{2,1,0:T(8,128)S(1)} async-done(((f32[16,64,256]{2,1,0:T(8,128)}), f32[16,64,256]{2,1,0:T(8,128)S(1)}, u32[]{:S(2)}, u32[]{:S(2)}) %all-to-all-start.7) | async-done | bytes 1048608 | tf_op jit(solution)/shard_map/all_to_all | solution.py:808
  351.5 3.9 %all-to-all-start.8 = ((f32[32,8,128]{2,1,0:T(8,128)}), f32[32,8,128]{2,1,0:T(8,128)S(1)}, u32[]{:S(2)}, u32[]{:S(2)}) async-start(f32[32,8,128]{2,1,0:T(8,128)} %sample.1), calls=%async_computation.8 | async-start | bytes 262144 | tf_op jit(solution)/shard_map/all_to_all | solution.py:710
  356.5 7.2 %all-to-all-done.8.held_ref = f32[32,8,128]{2,1,0:T(8,128)S(1)} async-done(((f32[32,8,128]{2,1,0:T(8,128)}), f32[32,8,128]{2,1,0:T(8,128)S(1)}, u32[]{:S(2)}, u32[]{:S(2)}) %all-to-all-start.8) | async-done | bytes 131104 | tf_op jit(solution)/shard_map/all_to_all | solution.py:710
  363.7 1.6 unpack.1
  (84 shorter events, 21.4 us)
Async XLA Ops:
  9.5 17.9 %all-to-all-start = ((f32[32,16,128]{2,1,0:T(8,128)}), f32[32,16,128]{2,1,0:T(8,128)S(1)}, u32[]{:S(2)}, u32[]{:S(2)}) async-start(f32[32,16,128]{2,1,0:T(8,128)} %get-tuple-element.21), calls=%async_computation | async-start | bytes 524288 | tf_op jit(solution)/shard_map/all_to_all | solution.py:710
  40.6 4.3 %collective-permute-start = (f32[64,256]{1,0:T(8,128)S(1)}, f32[64,256]{1,0:T(8,128)S(1)}, u32[]{:S(2)}, u32[]{:S(2)}) collective-permute-start(f32[64,256]{1,0:T(8,128)S(1)} %get-tuple-element.23), channel_id=1, source_target_pairs={{0,4},{8,12},{16,20},{24,28},{4,0},{12,8},{20,16},{28,24},{1,5},{9... | collective-permute-start | bytes 196616 | tf_op jit(solution)/shard_map/ppermute | solution.py:400
  41.5 3.4 collective-permute-start.1
  42.2 1.2 collective-permute-start.2
  42.3 1.2 collective-permute-start.3
  48.1 39.4 %copy-start.1 = (f32[256,256]{1,0:T(8,128)S(1)}, f32[256,256]{1,0:T(8,128)}, u32[]{:S(2)}) copy-start(f32[256,256]{1,0:T(8,128)} %first_any.11) | copy-start | bytes 786436
  48.1 39.4 %copy-start.3 = (f32[128,128]{1,0:T(8,128)S(1)}, f32[128,128]{1,0:T(8,128)}, u32[]{:S(2)}) copy-start(f32[128,128]{1,0:T(8,128)} %second_any.10) | copy-start | bytes 196612
  48.1 39.4 %all-to-all-start.1 = ((f32[32,80,128]{2,1,0:T(8,128)}), f32[32,80,128]{2,1,0:T(8,128)S(1)}, u32[]{:S(2)}, u32[]{:S(2)}) async-start(f32[32,80,128]{2,1,0:T(8,128)} %get-tuple-element.27), calls=%async_computation.1 | async-start | bytes 2621440 | tf_op jit(solution)/shard_map/all_to_all | solution.py:710
  92.0 52.7 %all-to-all-start.2 = ((f32[32,128,128]{2,1,0:T(8,128)}), f32[32,128,128]{2,1,0:T(8,128)}, u32[]{:S(2)}, u32[]{:S(2)}) async-start(f32[32,128,128]{2,1,0:T(8,128)} %bitcast.60), calls=%async_computation.2 | async-start | bytes 4194304 | tf_op jit(solution)/shard_map/all_to_all | solution.py:710
  95.7 2.1 copy-start.5
  95.8 4.4 %collective-permute-start.9 = (f32[72,128]{1,0:T(8,128)S(1)}, f32[72,128]{1,0:T(8,128)S(1)}, u32[]{:S(2)}, u32[]{:S(2)}) collective-permute-start(f32[72,128]{1,0:T(8,128)S(1)} %get-tuple-element.30), channel_id=1, source_target_pairs={{0,1},{1,0},{2,3},{3,2},{4,5},{5,4},{6,7},{7,6},{8,9},{9,8},{10,11... | collective-permute-start | bytes 110600 | tf_op jit(solution)/shard_map/ppermute | solution.py:719
  96.0 37.2 %collective-permute-start.10 = (f32[72,128]{1,0:T(8,128)S(1)}, f32[72,128]{1,0:T(8,128)S(1)}, u32[]{:S(2)}, u32[]{:S(2)}) collective-permute-start(f32[72,128]{1,0:T(8,128)S(1)} %get-tuple-element.30), channel_id=1, source_target_pairs={{0,2},{1,3},{2,0},{3,1},{4,6},{5,7},{6,4},{7,5},{8,10},{9,11},{10,... | collective-permute-start | bytes 110600 | tf_op jit(solution)/shard_map/ppermute | solution.py:719
  97.7 35.5 %collective-permute-start.11 = (f32[72,128]{1,0:T(8,128)S(1)}, f32[72,128]{1,0:T(8,128)S(1)}, u32[]{:S(2)}, u32[]{:S(2)}) collective-permute-start(f32[72,128]{1,0:T(8,128)S(1)} %get-tuple-element.30), channel_id=1, source_target_pairs={{0,3},{1,2},{2,1},{3,0},{4,7},{5,6},{6,5},{7,4},{8,11},{9,10},{10,... | collective-permute-start | bytes 110600 | tf_op jit(solution)/shard_map/ppermute | solution.py:719
  97.9 2.3 collective-permute-start.4
  98.5 26.0 %collective-permute-start.5 = (f32[4,64,256]{2,1,0:T(8,128)S(1)}, f32[4,64,256]{2,1,0:T(8,128)S(1)}, u32[]{:S(2)}, u32[]{:S(2)}) collective-permute-start(f32[4,64,256]{2,1,0:T(8,128)S(1)} %get-tuple-element.53), channel_id=1, source_target_pairs={{0,2},{1,3},{2,0},{3,1},{4,6},{5,7},{6,4},{7,5},{8,10},{9,11},{10,... | collective-permute-start | bytes 786440 | tf_op jit(solution)/shard_map/ppermute | solution.py:734
  100.2 30.2 %collective-permute-start.6 = (f32[4,64,256]{2,1,0:T(8,128)S(1)}, f32[4,64,256]{2,1,0:T(8,128)S(1)}, u32[]{:S(2)}, u32[]{:S(2)}) collective-permute-start(f32[4,64,256]{2,1,0:T(8,128)S(1)} %get-tuple-element.52), channel_id=1, source_target_pairs={{0,3},{1,2},{2,1},{3,0},{4,7},{5,6},{6,5},{7,4},{8,11},{9,10},{10,... | collective-permute-start | bytes 786440 | tf_op jit(solution)/shard_map/ppermute | solution.py:734
  130.5 2.8 collective-permute-start.7
  131.2 3.2 collective-permute-start.8
  134.5 14.3 %copy-start = (f32[256,256]{1,0:T(8,128)S(1)}, f32[256,256]{1,0:T(8,128)}, u32[]{:S(2)}) copy-start(f32[256,256]{1,0:T(8,128)} %second_any.11) | copy-start | bytes 786436
  146.8 2.1 collective-permute-start.12
  146.8 2.1 collective-permute-start.13
  193.3 2.0 collective-permute-start.14
  193.4 1.9 collective-permute-start.15
  237.2 1.6 collective-permute-start.16
  237.3 1.5 collective-permute-start.17
  278.3 1.6 collective-permute-start.18
  278.4 1.5 collective-permute-start.19
  319.3 2.0 collective-permute-start.20
  319.3 1.9 collective-permute-start.21
  325.6 26.0 %all-to-all-start.7 = ((f32[16,64,256]{2,1,0:T(8,128)}), f32[16,64,256]{2,1,0:T(8,128)S(1)}, u32[]{:S(2)}, u32[]{:S(2)}) async-start(f32[16,64,256]{2,1,0:T(8,128)} %bitcast.40), calls=%async_computation.7 | async-start | bytes 2097152 | tf_op jit(solution)/shard_map/all_to_all | solution.py:808
  345.9 17.8 %copy-start.10 = (s32[4096,1]{0,1:T(1,128)S(1)}, s32[4096,1]{0,1:T(1,128)}, u32[]{:S(2)}) copy-start(s32[4096,1]{0,1:T(1,128)} %param.8) | copy-start | bytes 49156
  351.5 12.2 %all-to-all-start.8 = ((f32[32,8,128]{2,1,0:T(8,128)}), f32[32,8,128]{2,1,0:T(8,128)S(1)}, u32[]{:S(2)}, u32[]{:S(2)}) async-start(f32[32,8,128]{2,1,0:T(8,128)} %sample.1), calls=%async_computation.8 | async-start | bytes 262144 | tf_op jit(solution)/shard_map/all_to_all | solution.py:710
  (7 other events, 6.9 us)
